TPU v7x, 32 devices: a whole 2x2x4 slice. The times are simulated.
32 devices in a mesh: morton: 8 (over z, x), sib: 4 (over y, core).
Axes of the slice: x: 2, y: 2, z: 4, core: 2. Of those that a mesh axis runs over, the one named last changes fastest.
Arguments:
- velocity: bfloat16 [4096, 3, 512], P(('morton', 'sib')), may hold values from -6 to 6
- pressure: bfloat16 [4096, 512], P(('morton', 'sib')), may hold values from -96 to 96
- viscosity: float32 [4096, 512], P(('morton', 'sib')), may hold values from 0.25 to 8
- levels: int32 [4096], P(('morton', 'sib')), may hold values from 3 to 7
- morton_keys: int32 [4096], P(('morton', 'sib')), may hold values from 0 to 2097151, as said below
- counts: int32 [32], replicated, may hold values from 32 to 128, as said below
- neighbors: int32 [4096, 6], P(('morton', 'sib')), may hold values from -1 to 4095, as said below
Outputs:
- stokes_force: float32 [4096, 3, 512], P(('morton', 'sib'))
- continuity: float32 [4096, 512], P(('morton', 'sib'))
- box_multipoles: float32 [8, 3, 216], P('morton')
- root_multipole: float32 [8, 3, 216], P('morton')
Inputs may be any that keep to these rules, and one draw needn't show every extreme that they name: counts[r] live leaves occupy slots 0 to counts[r] - 1 of range r; some range is full in every draw. `morton_keys`: the key of a leaf of range r lies in that range's key block. `neighbors`: -1 marks the domain's boundary and every face of a padded slot. Otherwise the entry is a live leaf of the same Morton index m (any range), or one of the last 32 live leaves of a range of Morton index m - 1, or one of the first 32 leaves of a range of Morton index m + 1; in every draw the outermost leaf of both bands is referenced for every m that has such a neighbour.
All inputs are finite; a program needn't handle non-finite values.
Results may differ from a plain program's by a relative error of at most 0.0068.
Values may be sent and summed in bfloat16 or wider, within the bound.
No kernel may reach another device: no remote copies, remote signals or barrier semaphores. Data moves between devices by JAX's collectives and lax.ppermute only.
A program may use at most 64 MiB of HBM per device.

v0:
```python
import math

import jax
import jax.numpy as jnp
import numpy as np
from jax import lax
from jax.sharding import PartitionSpec as P

DEG = 5
LMAX = 7
MOMENTS = 216


penalty = 256.0
out_scale = 1.0 / 1024.0
mass_scale = 1.0 / 32.0
highest = lax.Precision.HIGHEST


def padded(block, sides, width):
    for axis, dim in sides:
        count = lax.axis_size(axis)
        forward = [(i, i + 1) for i in range(count - 1)]
        backward = [(target, source) for source, target in forward]
        low = lax.ppermute(
            lax.slice_in_dim(block, block.shape[dim] - width, None, axis=dim), axis, forward
        )
        high = lax.ppermute(lax.slice_in_dim(block, 0, width, axis=dim), axis, backward)
        block = jnp.concatenate([low, block, high], axis=dim)
    return block


def partner(block, axis, apart):
    count = lax.axis_size(axis)
    route = []
    for low in range(count):
        high = low | 1 << apart
        if high != low and high < count:
            route += [(low, high), (high, low)]
    return lax.ppermute(block, axis, route)


def cheb_tables():
    points = -np.cos(np.pi * np.arange(8) / 7.0)
    bary_weights = np.array([(-1.0) ** node_idx for node_idx in range(8)])
    bary_weights[0] = bary_weights[0] * 0.5
    bary_weights[7] = bary_weights[7] * 0.5
    derivative = np.zeros((8, 8))
    for row_idx in range(8):
        for col_idx in range(8):
            if row_idx != col_idx:
                derivative[row_idx, col_idx] = (
                    bary_weights[col_idx]
                    / bary_weights[row_idx]
                    / (points[row_idx] - points[col_idx])
                )
        derivative[row_idx, row_idx] = -np.sum(derivative[row_idx])
    identity = np.eye(8)
    directional = [
        np.kron(np.kron(derivative, identity), identity),
        np.kron(np.kron(identity, derivative), identity),
        np.kron(np.kron(identity, identity), derivative),
    ]
    wide_np = np.concatenate([matrix_one.T for matrix_one in directional], axis=1)
    tall_np = np.concatenate([matrix_one.T for matrix_one in directional], axis=0)
    face_pick = np.zeros((512, 384))
    for face_idx in range(6):
        face_dim = face_idx // 2
        face_side = face_idx % 2
        for first_idx in range(8):
            for second_idx in range(8):
                coords = [first_idx, second_idx]
                coords.insert(face_dim, 7 * face_side)
                face_pick[
                    64 * coords[0] + 8 * coords[1] + coords[2],
                    face_idx * 64 + first_idx * 8 + second_idx,
                ] = 1.0
    return (points, wide_np, tall_np, face_pick)


def power_table(values):
    power_terms = [jnp.ones_like(values)]
    for power_idx in range(DEG):
        power_terms.append(power_terms[-1] * values)
    return jnp.stack(power_terms, axis=-1)


def leaf_geometry(morton_keys, levels):
    shift_bits = 3 * (LMAX - levels)
    anchor = jnp.left_shift(jnp.right_shift(morton_keys, shift_bits), shift_bits)
    leaf_span = jnp.left_shift(jnp.ones_like(levels), LMAX - levels).astype(jnp.float32)
    finest = 1.0 / float(2**LMAX)
    cell_coords = []
    for offset in (2, 1, 0):
        coordinate = jnp.zeros_like(anchor)
        for bit_idx in range(LMAX):
            coordinate = coordinate + jnp.left_shift(
                jnp.bitwise_and(jnp.right_shift(anchor, 3 * bit_idx + offset), 1), bit_idx
            )
        cell_coords.append((coordinate.astype(jnp.float32) + 0.5 * leaf_span) * finest)
    return (jnp.stack(cell_coords, axis=-1), 0.5 * leaf_span * finest)


def box_geometry(base_key, key_bits):
    finest = 1.0 / float(2**LMAX)
    centers = []
    side_lengths = []
    for offset in (2, 1, 0):
        free_bits = max(0, min(LMAX, (key_bits - offset + 2) // 3))
        coordinate = jnp.zeros_like(base_key)
        for bit_idx in range(LMAX):
            coordinate = coordinate + jnp.left_shift(
                jnp.bitwise_and(jnp.right_shift(base_key, 3 * bit_idx + offset), 1), bit_idx
            )
        side_len = float(2**free_bits) * finest
        centers.append(coordinate.astype(jnp.float32) * finest + 0.5 * side_len)
        side_lengths.append(side_len)
    return (jnp.stack(centers, axis=-1), 0.5 * max(side_lengths))


def moments(forces, centers, radius, box_center, box_scale, points):
    leaf_count = forces.shape[0]
    nodal_field = forces.reshape(leaf_count, 3, 8, 8, 8)
    tables = []
    for dim_idx in range(3):
        position = centers[:, dim_idx][:, None] + radius[:, None] * points[None, :]
        tables.append(power_table((position - box_center[dim_idx]) / box_scale))
    step_one = jnp.einsum("liabc,lcz->liabz", nodal_field, tables[2], precision=highest)
    step_two = jnp.einsum("liabz,lby->liayz", step_one, tables[1], precision=highest)
    moment_sum = jnp.einsum("liayz,lax->ixyz", step_two, tables[0], precision=highest)
    return (moment_sum / 512.0).reshape(3, MOMENTS)


def shift_tables(child_center, child_scale, parent_center, parent_scale):
    width_deg = DEG + 1
    binomials = np.zeros((width_deg, width_deg))
    for alpha_idx in range(width_deg):
        for beta_idx in range(alpha_idx + 1):
            binomials[alpha_idx, beta_idx] = float(math.comb(alpha_idx, beta_idx))
    scale_ratio = child_scale / parent_scale
    scale_pows = np.array([scale_ratio**beta_idx for beta_idx in range(width_deg)])
    weights_np = (binomials * scale_pows[None, :]).astype(np.float32)
    gap_index = np.clip(np.arange(width_deg)[:, None] - np.arange(width_deg)[None, :], 0, DEG)
    shift_mats = []
    for dim_idx in range(3):
        offset = (child_center[..., dim_idx] - parent_center[dim_idx]) / parent_scale
        offset_pows = power_table(offset)
        shift_mats.append(jnp.asarray(weights_np) * offset_pows[..., gap_index])
    return shift_mats


def translate(moment_rows, shift_mats):
    width_deg = DEG + 1
    shaped = moment_rows.reshape(3, width_deg, width_deg, width_deg)
    shaped = jnp.einsum("ixyz,Xx->iXyz", shaped, shift_mats[0], precision=highest)
    shaped = jnp.einsum("iXyz,Yy->iXYz", shaped, shift_mats[1], precision=highest)
    shaped = jnp.einsum("iXYz,Zz->iXYZ", shaped, shift_mats[2], precision=highest)
    return shaped.reshape(3, MOMENTS)


def on_device(velocity, pressure, viscosity, levels, morton_keys, counts, neighbors):
    points_np, wide_np, tall_np, pick_np = cheb_tables()
    points = jnp.asarray(points_np.astype(np.float32))
    wide_table = jnp.asarray(wide_np.astype(np.float32)).astype(jnp.bfloat16)
    tall_table = jnp.asarray(tall_np.astype(np.float32)).astype(jnp.bfloat16)
    pick_low = jnp.asarray(pick_np.astype(np.float32)).astype(jnp.bfloat16)
    spread_table = jnp.asarray(pick_np.T.astype(np.float32)).astype(jnp.bfloat16)
    leaf_count = velocity.shape[0]
    sib_count = lax.axis_size("sib")
    morton_count = lax.axis_size("morton")
    morton_idx = lax.axis_index("morton")
    sib_idx = lax.axis_index("sib")
    local_counts = lax.dynamic_slice_in_dim(counts, morton_idx * sib_count, sib_count, 0)
    own_count = jnp.sum(
        jnp.where(jnp.arange(sib_count, dtype=jnp.int32) == sib_idx, local_counts, 0)
    )
    flat_velocity = velocity.reshape(leaf_count * 3, 512)
    own_faces = jnp.dot(flat_velocity, pick_low, preferred_element_type=jnp.float32).astype(
        jnp.bfloat16
    )
    face_rows = own_faces.reshape(leaf_count, 1152)
    sib_rows = lax.all_gather(face_rows, "sib", axis=0, tiled=True)
    valid_ref = neighbors >= 0
    owner_morton = neighbors // (sib_count * leaf_count)
    owner_sib = neighbors // leaf_count % sib_count
    owner_slot = neighbors % leaf_count
    morton_step = owner_morton - morton_idx
    window = padded(sib_rows, (("morton", 0),), sib_count * leaf_count)
    position = (morton_step + 1) * (sib_count * leaf_count) + owner_sib * leaf_count + owner_slot
    window_rows = window.shape[0]
    by_face = window.reshape(window_rows, 3, 6, 64)
    fetched_faces = []
    for face_idx in range(6):
        chosen = by_face[:, :, face_idx ^ 1, :].reshape(window_rows, 192)
        fetched = jnp.take(chosen, jnp.clip(position[:, face_idx], 0, window_rows - 1), axis=0)
        fetched_faces.append(
            jnp.where(valid_ref[:, face_idx][:, None], fetched, jnp.zeros_like(fetched))
        )
    neighbour_rows = jnp.stack(fetched_faces)
    neighbour_faces = (
        neighbour_rows.reshape(6, leaf_count, 3, 64)
        .transpose(1, 2, 0, 3)
        .reshape(leaf_count * 3, 384)
    )
    block_size = min(leaf_count, 64)
    block_count = leaf_count // block_size
    live_slots = jnp.arange(leaf_count, dtype=jnp.int32) < own_count

    def one_block(inputs):
        vel_block, press_block, visc_block, own_block, nbr_block, live_block = inputs
        block_rows = visc_block.shape[0]
        gradient = jnp.dot(vel_block, wide_table, preferred_element_type=jnp.float32).reshape(
            block_rows, 3, 3, 512
        )
        press_grad = jnp.dot(press_block, wide_table, preferred_element_type=jnp.float32).reshape(
            block_rows, 3, 512
        )
        stress = (visc_block[:, None, None, :] * (gradient + jnp.swapaxes(gradient, 1, 2))).astype(
            jnp.bfloat16
        )
        divergence = jnp.dot(
            stress.reshape(block_rows * 3, 1536), tall_table, preferred_element_type=jnp.float32
        ).reshape(block_rows, 3, 512)
        own_spread = jnp.dot(own_block, spread_table, preferred_element_type=jnp.float32)
        nbr_spread = jnp.dot(nbr_block, spread_table, preferred_element_type=jnp.float32)
        face_jump = (own_spread - nbr_spread).reshape(block_rows, 3, 512)
        momentum = (
            penalty * visc_block[:, None, :] * face_jump - divergence + press_grad
        ) * out_scale
        mass_rows = -(gradient[:, 0, 0] + gradient[:, 1, 1] + gradient[:, 2, 2]) * mass_scale
        return (
            jnp.where(live_block[:, None, None], momentum, 0.0),
            jnp.where(live_block[:, None], mass_rows, 0.0),
        )

    forces, masses = lax.map(
        one_block,
        (
            flat_velocity.reshape(block_count, block_size * 3, 512),
            pressure.reshape(block_count, block_size, 512),
            viscosity.reshape(block_count, block_size, 512),
            own_faces.reshape(block_count, block_size * 3, 384),
            neighbour_faces.reshape(block_count, block_size * 3, 384),
            live_slots.reshape(block_count, block_size),
        ),
    )
    stokes_force = forces.reshape(leaf_count, 3, 512)
    continuity = masses.reshape(leaf_count, 512)
    key_range = 2 ** (3 * LMAX) // (morton_count * sib_count)
    group_keys = sib_count * key_range
    morton_bits = morton_count.bit_length() - 1
    box_bits = 3 * LMAX - morton_bits
    centers, radius = leaf_geometry(morton_keys, levels)
    box_center, box_scale = box_geometry(morton_idx * group_keys, box_bits)
    local_moments = moments(stokes_force, centers, radius, box_center, box_scale, points)
    box_total = lax.psum(local_moments, "sib")
    current = box_total
    for bit_idx in range(morton_bits):
        child_base = jnp.left_shift(jnp.right_shift(morton_idx, bit_idx), bit_idx) * group_keys
        parent_base = (
            jnp.left_shift(jnp.right_shift(morton_idx, bit_idx + 1), bit_idx + 1) * group_keys
        )
        child_center, child_scale = box_geometry(child_base, box_bits + bit_idx)
        parent_center, parent_scale = box_geometry(parent_base, box_bits + bit_idx + 1)
        current = translate(
            current, shift_tables(child_center, child_scale, parent_center, parent_scale)
        )
        current = current + partner(current, "morton", bit_idx)
    return (stokes_force, continuity, box_total[None], current[None])


def solution(mesh):
    in_specs = (
        P(("morton", "sib"), None, None),
        P(("morton", "sib"), None),
        P(("morton", "sib"), None),
        P(("morton", "sib")),
        P(("morton", "sib")),
        P(),
        P(("morton", "sib"), None),
    )
    out_specs = (
        P(("morton", "sib"), None, None),
        P(("morton", "sib"), None),
        P("morton", None, None),
        P("morton", None, None),
    )
    return jax.shard_map(
        on_device, mesh=mesh, in_specs=in_specs, out_specs=out_specs, check_vma=False
    )
```

profile of v0, /device:TPU:0, one launch (start us, length us, event | category | flops | bytes accessed | tf_op | source)
XLA Modules:
  0.0 206.5 jit_solution(8710949076509617139)
XLA Ops:
  7.3 1.3 copy.135
  8.9 1.4 convolution_convert_fusion
  10.5 0.9 copy.136
  12.2 19.6 %all-gather.2.cloned.1.call-done = bf16[512,1152]{0,1:T(8,128)(2,1)} async-done(((bf16[128,1152]{0,1:T(8,128)(2,1)}), bf16[512,1152]{0,1:T(8,128)(2,1)}) %all-gather.2.cloned.1.call-update) | async-done | bytes 1179664 | tf_op jit(solution)/shard_map/all_gather | solution.py:182
  31.8 3.4 %collective-permute-start = (bf16[512,1152]{0,1:T(8,128)(2,1)}, bf16[512,1152]{0,1:T(8,128)(2,1)S(1)}, u32[]{:S(2)}, u32[]{:S(2)}) collective-permute-start(bf16[512,1152]{0,1:T(8,128)(2,1)} %all-gather.2.cloned.1.call-done), channel_id=1, source_target_pairs={{0,4},{4,8},{8,12},{12,16},{16,20},{20,24},{24,28},{1,5},{5,9},{9,... | collective-permute-start | bytes 3538952 | tf_op jit(solution)/shard_map/ppermute | solution.py:25
  35.3 1.3 collective-permute-start.1
  36.6 1.1 reshape_reshape.10
  37.7 1.0 copy.167
  38.7 1.0 copy.168
  41.6 0.8 gather_fusion.6
  46.2 0.8 gather_fusion
  47.9 1.4 gather_fusion.2
  49.3 1.4 gather_fusion.3
  51.4 1.1 add_compare_fusion
  52.6 33.8 %collective-permute-done = bf16[512,1152]{0,1:T(8,128)(2,1)S(1)} collective-permute-done((bf16[512,1152]{0,1:T(8,128)(2,1)}, bf16[512,1152]{0,1:T(8,128)(2,1)S(1)}, u32[]{:S(2)}, u32[]{:S(2)}) %collective-permute-start) | collective-permute-done | bytes 1179680 | tf_op jit(solution)/shard_map/ppermute | solution.py:25
  86.4 1.4 pad_maximum_fusion
  87.8 1.2 fusion.84
  89.1 2.2 %copy.139 = bf16[1536,192]{1,0:T(8,128)(2,1)} copy(bf16[1536,192]{0,1:T(8,128)(2,1)} %bitcast.250) | data formatting | bytes 1179648 | tf_op jit(solution)/shard_map/reshape;squeeze | solution.py:194
  91.3 2.0 gather_fusion.10
  93.5 1.2 copy.137
  94.7 2.0 gather_fusion.9
  97.2 0.8 gather_fusion.11
  98.5 0.8 gather_fusion.12
  99.6 2.4 %copy.145 = bf16[1536,192]{1,0:T(8,128)(2,1)} copy(bf16[1536,192]{0,1:T(8,128)(2,1)} %bitcast.246) | data formatting | bytes 1179648 | tf_op jit(solution)/shard_map/reshape;squeeze | solution.py:194
  102.0 2.0 gather_fusion.13
  104.2 1.2 copy.147
  105.4 2.0 gather_fusion.14
  108.7 16.2 %while.13 = (s32[]{:T(128)}, f32[2,64,3,512]{3,1,2,0:T(8,128)}, f32[2,64,512]{2,1,0:T(8,128)}, pred[2,64]{1,0:T(4,128)(4,1)}, f32[2,64,512]{2,1,0:T(8,128)}, /*i...) while((s32[]{:T(128)}, f32[2,64,3,512]{3,1,2,0:T(8,128)}, ...), condition=%wide.region_2.4_spmd.clone, body=%wide.region_1.3_spmd.clone.sunk | while | flops 857309184 | bytes 31623144 | solution.py:236
  109.4 0.9 constant_dynamic-slice_fusion.3
  110.5 2.2 %fusion.129 = f32[64,3,3,512]{3,0,2,1:T(8,128)S(1)} fusion(bf16[3,512,512,1]{2,1,0,3:T(8,128)(2,1)} %get-tuple-element.294, bf16[64,3,512,1]{2,1,0,3:T(4,128)(2,1)S(1)} %bitcast.241), kind=kOutput, calls=%fused_computation.30.clone.1 | convolution fusion | flops 301989888 | bytes 2949120 | tf_op jit(solution)/shard_map/while/body/eval_jaxpr/dot_general | solution.py:212
  112.7 0.9 broadcast_multiply_fusion.2
  115.1 0.9 copy-done.5
  117.4 0.9 constant_dynamic-slice_fusion.3
  118.6 2.2 %fusion.129 = f32[64,3,3,512]{3,0,2,1:T(8,128)S(1)} fusion(bf16[3,512,512,1]{2,1,0,3:T(8,128)(2,1)} %get-tuple-element.294, bf16[64,3,512,1]{2,1,0,3:T(4,128)(2,1)S(1)} %bitcast.241), kind=kOutput, calls=%fused_computation.30.clone.1 | convolution fusion | flops 301989888 | bytes 2949120 | tf_op jit(solution)/shard_map/while/body/eval_jaxpr/dot_general | solution.py:212
  120.8 0.9 broadcast_multiply_fusion.2
  123.2 0.9 copy-done.5
  124.8 1.7 copy.184
  126.5 8.8 %reshape.1297 = f32[128,3,8,8,8]{4,3,2,1,0:T(8,128)} reshape(f32[2,64,3,512]{3,2,1,0:T(4,128)S(1)} %copy.184) | data formatting | bytes 1572864 | tf_op jit(solution)/shard_map/reshape;reshape | solution.py:123
  135.3 14.8 %fusion.87 = f32[128,3,8,8,6]{4,3,2,1,0:T(8,128)S(1)} fusion(f32[128,3,8,8,8]{4,3,2,1,0:T(8,128)} %reshape.1297, f32[128,8,6,1,1]{2,1,4,3,0:T(8,128)S(1)} %copy-done.3), kind=kOutput, calls=%fused_computation.196 | convolution fusion | flops 14155776 | bytes 1400832 | tf_op jit(solution)/shard_map/liabc,lcz->liabz/dot_general | solution.py:128
  150.1 13.5 %convolution_bitcast_fusion = f32[128,3,8,6,6]{4,3,2,1,0:T(8,128)} fusion(f32[128,8,6,1,1]{1,2,4,3,0:T(8,128)S(1)} %copy-done.7, f32[128,3,8,8,6]{4,3,2,1,0:T(8,128)S(1)} %fusion.87), kind=kOutput, calls=%fused_computation.56 | convolution fusion | flops 10616832 | bytes 1056768 | tf_op jit(solution)/shard_map/liabz,lby->liayz/dot_general | solution.py:129
  163.7 13.4 %fusion.39 = f32[3,6,6,6]{3,1,2,0:T(8,128)S(1)} fusion(f32[128,3,8,6,6]{4,3,2,1,0:T(8,128)} %convolution_bitcast_fusion, f32[128,8,6,1,1]{0,1,2,4,3:T(8,128)S(1)} %bitcast.261), kind=kOutput, calls=%fused_computation.67 | convolution fusion | flops 7963272 | bytes 469536 | tf_op jit(solution)/shard_map/liayz,lax->ixyz/dot_general | solution.py:130
  177.3 6.0 %psum.7 = f32[3,216]{1,0:T(4,128)S(1)} all-reduce(f32[3,216]{1,0:T(4,128)S(1)} %reshape.1107), channel_id=1, replica_groups=mesh['morton'=8,'sib'=4] {'sib'}, use_global_device_ids=true, to_apply=%region_3.5 | all-reduce | flops 648 | bytes 5184 | tf_op jit(solution)/shard_map/psum | solution.py:256
  184.1 2.4 %collective-permute-start.2 = (f32[3,216]{1,0:T(4,128)S(1)}, f32[3,216]{1,0:T(4,128)S(1)}, u32[]{:S(2)}, u32[]{:S(2)}) collective-permute-start(f32[3,216]{1,0:T(4,128)S(1)} %reshape.1109), channel_id=1, source_target_pairs={{0,4},{4,0},{8,12},{12,8},{16,20},{20,16},{24,28},{28,24},{1,5},{5... | collective-permute-start | bytes 7784 | tf_op jit(solution)/shard_map/ppermute | solution.py:40
  186.8 1.3 collective-permute-done.2
  189.0 3.1 %collective-permute-start.3 = (f32[3,216]{1,0:T(4,128)S(1)}, f32[3,216]{1,0:T(4,128)S(1)}, u32[]{:S(2)}, u32[]{:S(2)}) collective-permute-start(f32[3,216]{1,0:T(4,128)S(1)} %reshape.1111), channel_id=1, source_target_pairs={{0,8},{8,0},{4,12},{12,4},{16,24},{24,16},{20,28},{28,20},{1,9},{9... | collective-permute-start | bytes 7784 | tf_op jit(solution)/shard_map/ppermute | solution.py:40
  192.3 1.4 collective-permute-done.3
  194.5 3.0 %collective-permute-start.4 = (f32[3,216]{1,0:T(4,128)S(1)}, f32[3,216]{1,0:T(4,128)S(1)}, u32[]{:S(2)}, u32[]{:S(2)}) collective-permute-start(f32[3,216]{1,0:T(4,128)S(1)} %reshape.1113), channel_id=1, source_target_pairs={{0,16},{16,0},{4,20},{20,4},{8,24},{24,8},{12,28},{28,12},{1,17},{... | collective-permute-start | bytes 7784 | tf_op jit(solution)/shard_map/ppermute | solution.py:40
  197.5 0.9 copy.151
  (186 shorter events, 21.6 us)
Async XLA Ops:
  7.2 4.4 %copy-start.14 = (f32[8]{0:T(128)S(1)}, f32[8]{0:T(128)}, u32[]{:S(2)}) copy-start(f32[8]{0:T(128)} %constant.261.clone) | copy-start | bytes 100
  7.2 29.4 %copy-start.21 = (s32[36]{0:T(128)S(1)}, s32[36]{0:T(128)}, u32[]{:S(2)}) copy-start(s32[36]{0:T(128)} %constant.275) | copy-start | bytes 436
  7.2 4.2 %copy-start.19 = (s32[128]{0:T(128)S(1)}, s32[128]{0:T(128)}, u32[]{:S(2)}) copy-start(s32[128]{0:T(128)} %param.34) | copy-start | bytes 1540
  7.2 4.2 %copy-start.22 = (s32[128]{0:T(128)S(1)}, s32[128]{0:T(128)}, u32[]{:S(2)}) copy-start(s32[128]{0:T(128)} %param.35) | copy-start | bytes 1540
  7.2 4.3 %copy-start.18 = (s32[128,6]{0,1:T(8,128)S(1)}, s32[128,6]{0,1:T(8,128)}, u32[]{:S(2)}) copy-start(s32[128,6]{0,1:T(8,128)} %param.37) | copy-start | bytes 9220
  7.2 24.6 %all-gather.2.cloned.1.call-start = ((), (), s32[]{:S(2)}) async-start(), calls=%async_computation | async-start | bytes 1474560 | tf_op jit(solution)/shard_map/all_gather | solution.py:182
  12.0 28.6 %copy-start.10 = (f32[128,8,6]{0,1,2:T(8,128)}, f32[128,8,6]{0,1,2:T(8,128)S(1)}, u32[]{:S(2)}) copy-start(f32[128,8,6]{0,1,2:T(8,128)S(1)} %get-tuple-element.158) | copy-start | bytes 73732
  31.8 54.6 %collective-permute-start = (bf16[512,1152]{0,1:T(8,128)(2,1)}, bf16[512,1152]{0,1:T(8,128)(2,1)S(1)}, u32[]{:S(2)}, u32[]{:S(2)}) collective-permute-start(bf16[512,1152]{0,1:T(8,128)(2,1)} %all-gather.2.cloned.1.call-done), channel_id=1, source_target_pairs={{0,4},{4,8},{8,12},{12,16},{16,20},{20,24},{24,28},{1,5},{5,9},{9,... | collective-permute-start | bytes 3538952 | tf_op jit(solution)/shard_map/ppermute | solution.py:25
  35.3 51.1 %collective-permute-start.1 = (bf16[512,1152]{0,1:T(8,128)(2,1)}, bf16[512,1152]{0,1:T(8,128)(2,1)}, u32[]{:S(2)}, u32[]{:S(2)}) collective-permute-start(bf16[512,1152]{0,1:T(8,128)(2,1)} %all-gather.2.cloned.1.call-done), channel_id=1, source_target_pairs={{4,0},{8,4},{12,8},{16,12},{20,16},{24,20},{28,24},{5,1},{9,5},{13... | collective-permute-start | bytes 3538952 | tf_op jit(solution)/shard_map/ppermute | solution.py:28
  40.7 1.6 copy-start.20
  47.9 2.8 %copy-start.23 = (s32[32]{0:T(128)S(1)}, s32[32]{0:T(128)}, u32[]{:S(2)}) copy-start(s32[32]{0:T(128)} %param.36) | copy-start | bytes 388
  47.9 38.5 %copy-start.8 = (bf16[512,1152]{0,1:T(8,128)(2,1)S(1)}, bf16[512,1152]{0,1:T(8,128)(2,1)}, u32[]{:S(2)}) copy-start(bf16[512,1152]{0,1:T(8,128)(2,1)} %all-gather.2.cloned.1.call-done) | copy-start | bytes 3538948
  99.6 9.0 %copy-start = (bf16[3,512,512]{2,1,0:T(8,128)(2,1)S(1)}, bf16[3,512,512]{2,1,0:T(8,128)(2,1)}, u32[]{:S(2)}) copy-start(bf16[3,512,512]{2,1,0:T(8,128)(2,1)} %constant.513) | copy-start | bytes 4718596
  99.6 9.0 %copy-start.2 = (bf16[384,512]{1,0:T(8,128)(2,1)S(1)}, bf16[384,512]{1,0:T(8,128)(2,1)}, u32[]{:S(2)}) copy-start(bf16[384,512]{1,0:T(8,128)(2,1)} %constant.516) | copy-start | bytes 1179652
  110.4 3.4 %copy-start.9 = (bf16[2,64,512]{2,1,0:T(8,128)(2,1)S(1)}, bf16[2,64,512]{2,1,0:T(8,128)(2,1)}, u32[]{:S(2)}) copy-start(bf16[2,64,512]{2,1,0:T(8,128)(2,1)} %get-tuple-element.291) | copy-start | bytes 393220 | tf_op jit(solution)/shard_map/while
  110.5 4.0 %copy-start.27 = (pred[2,64]{1,0:T(4,128)(4,1)S(1)}, pred[2,64]{1,0:T(4,128)(4,1)}, u32[]{:S(2)}) copy-start(pred[2,64]{1,0:T(4,128)(4,1)} %get-tuple-element.286) | copy-start | bytes 388 | tf_op jit(solution)/shard_map/while
  110.5 4.1 %copy-start.1 = (bf16[1536,512,1]{1,0,2:T(8,128)(2,1)S(1)}, bf16[1536,512,1]{1,0,2:T(8,128)(2,1)}, u32[]{:S(2)}) copy-start(bf16[1536,512,1]{1,0,2:T(8,128)(2,1)} %get-tuple-element.295) | copy-start | bytes 4718596 | tf_op jit(solution)/shard_map/while
  110.5 4.0 %copy-start.4 = (f32[2,64,3,512]{3,1,2,0:T(8,128)S(1)}, f32[2,64,3,512]{3,1,2,0:T(8,128)}, u32[]{:S(2)}) copy-start(f32[2,64,3,512]{3,1,2,0:T(8,128)} %get-tuple-element.270) | copy-start | bytes 2359300 | tf_op jit(solution)/shard_map/while
  113.8 2.1 %copy-start.25 = (f32[2,64,512]{2,1,0:T(8,128)S(1)}, f32[2,64,512]{2,1,0:T(8,128)}, u32[]{:S(2)}) copy-start(f32[2,64,512]{2,1,0:T(8,128)} %get-tuple-element.271) | copy-start | bytes 786436 | tf_op jit(solution)/shard_map/while
  115.1 0.9 copy-start.5
  116.0 0.7 copy-start.26
  118.5 3.4 %copy-start.9 = (bf16[2,64,512]{2,1,0:T(8,128)(2,1)S(1)}, bf16[2,64,512]{2,1,0:T(8,128)(2,1)}, u32[]{:S(2)}) copy-start(bf16[2,64,512]{2,1,0:T(8,128)(2,1)} %get-tuple-element.291) | copy-start | bytes 393220 | tf_op jit(solution)/shard_map/while
  118.5 4.0 %copy-start.27 = (pred[2,64]{1,0:T(4,128)(4,1)S(1)}, pred[2,64]{1,0:T(4,128)(4,1)}, u32[]{:S(2)}) copy-start(pred[2,64]{1,0:T(4,128)(4,1)} %get-tuple-element.286) | copy-start | bytes 388 | tf_op jit(solution)/shard_map/while
  118.5 4.1 %copy-start.1 = (bf16[1536,512,1]{1,0,2:T(8,128)(2,1)S(1)}, bf16[1536,512,1]{1,0,2:T(8,128)(2,1)}, u32[]{:S(2)}) copy-start(bf16[1536,512,1]{1,0,2:T(8,128)(2,1)} %get-tuple-element.295) | copy-start | bytes 4718596 | tf_op jit(solution)/shard_map/while
  118.5 4.0 %copy-start.4 = (f32[2,64,3,512]{3,1,2,0:T(8,128)S(1)}, f32[2,64,3,512]{3,1,2,0:T(8,128)}, u32[]{:S(2)}) copy-start(f32[2,64,3,512]{3,1,2,0:T(8,128)} %get-tuple-element.270) | copy-start | bytes 2359300 | tf_op jit(solution)/shard_map/while
  121.9 2.1 %copy-start.25 = (f32[2,64,512]{2,1,0:T(8,128)S(1)}, f32[2,64,512]{2,1,0:T(8,128)}, u32[]{:S(2)}) copy-start(f32[2,64,512]{2,1,0:T(8,128)} %get-tuple-element.271) | copy-start | bytes 786436 | tf_op jit(solution)/shard_map/while
  123.1 0.9 copy-start.5
  124.1 0.7 copy-start.26
  126.5 8.8 %copy-start.3 = (f32[128,8,6,1,1]{2,1,4,3,0:T(8,128)S(1)}, f32[128,8,6,1,1]{2,1,4,3,0:T(8,128)}, u32[]{:S(2)}) copy-start(f32[128,8,6,1,1]{2,1,4,3,0:T(8,128)} %copy.167) | copy-start | bytes 73732
  135.3 14.8 %copy-start.7 = (f32[128,8,6,1,1]{1,2,4,3,0:T(8,128)S(1)}, f32[128,8,6,1,1]{1,2,4,3,0:T(8,128)}, u32[]{:S(2)}) copy-start(f32[128,8,6,1,1]{1,2,4,3,0:T(8,128)} %copy.168) | copy-start | bytes 73732
  150.1 13.6 %copy-start.11 = (f32[128,8,6]{0,1,2:T(8,128)S(1)}, f32[128,8,6]{0,1,2:T(8,128)}, u32[]{:S(2)}) copy-start(f32[128,8,6]{0,1,2:T(8,128)} %copy-done.10) | copy-start | bytes 73732
  163.7 19.7 %copy-start.17 = (f32[6,6,1,1]{1,0,2,3:T(8,128)S(1)}, f32[6,6,1,1]{1,0,2,3:T(8,128)}, u32[]{:S(2)}) copy-start(f32[6,6,1,1]{1,0,2,3:T(8,128)} %reshape.1288) | copy-start | bytes 436
  163.7 19.9 %copy-start.15 = (f32[6,6,1,1]{1,0,2,3:T(8,128)S(1)}, f32[6,6,1,1]{1,0,2,3:T(8,128)}, u32[]{:S(2)}) copy-start(f32[6,6,1,1]{1,0,2,3:T(8,128)} %reshape.1289) | copy-start | bytes 436
  163.7 20.1 %copy-start.16 = (f32[6,6,1,1]{1,0,2,3:T(8,128)S(1)}, f32[6,6,1,1]{1,0,2,3:T(8,128)}, u32[]{:S(2)}) copy-start(f32[6,6,1,1]{1,0,2,3:T(8,128)} %reshape.1290) | copy-start | bytes 436
  163.7 22.9 %copy-start.12 = (f32[36]{0:T(128)S(1)}, f32[36]{0:T(128)}, u32[]{:S(2)}) copy-start(f32[36]{0:T(128)} %gather_fusion.2) | copy-start | bytes 436
  163.7 22.9 %copy-start.13 = (f32[36]{0:T(128)S(1)}, f32[36]{0:T(128)}, u32[]{:S(2)}) copy-start(f32[36]{0:T(128)} %gather_fusion.3) | copy-start | bytes 436
  163.7 22.9 %copy-start.24 = (f32[36]{0:T(128)S(1)}, f32[36]{0:T(128)}, u32[]{:S(2)}) copy-start(f32[36]{0:T(128)} %constant.284) | copy-start | bytes 436
  163.7 33.8 %copy-start.6 = (f32[2,64,3,512]{3,1,2,0:T(8,128)S(1)}, f32[2,64,3,512]{3,1,2,0:T(8,128)}, u32[]{:S(2)}) copy-start(f32[2,64,3,512]{3,1,2,0:T(8,128)} %get-tuple-element.68) | copy-start | bytes 2359300
  184.1 4.0 %collective-permute-start.2 = (f32[3,216]{1,0:T(4,128)S(1)}, f32[3,216]{1,0:T(4,128)S(1)}, u32[]{:S(2)}, u32[]{:S(2)}) collective-permute-start(f32[3,216]{1,0:T(4,128)S(1)} %reshape.1109), channel_id=1, source_target_pairs={{0,4},{4,0},{8,12},{12,8},{16,20},{20,16},{24,28},{28,24},{1,5},{5... | collective-permute-start | bytes 7784 | tf_op jit(solution)/shard_map/ppermute | solution.py:40
  189.0 4.7 %collective-permute-start.3 = (f32[3,216]{1,0:T(4,128)S(1)}, f32[3,216]{1,0:T(4,128)S(1)}, u32[]{:S(2)}, u32[]{:S(2)}) collective-permute-start(f32[3,216]{1,0:T(4,128)S(1)} %reshape.1111), channel_id=1, source_target_pairs={{0,8},{8,0},{4,12},{12,4},{16,24},{24,16},{20,28},{28,20},{1,9},{9... | collective-permute-start | bytes 7784 | tf_op jit(solution)/shard_map/ppermute | solution.py:40
  194.5 4.6 %collective-permute-start.4 = (f32[3,216]{1,0:T(4,128)S(1)}, f32[3,216]{1,0:T(4,128)S(1)}, u32[]{:S(2)}, u32[]{:S(2)}) collective-permute-start(f32[3,216]{1,0:T(4,128)S(1)} %reshape.1113), channel_id=1, source_target_pairs={{0,16},{16,0},{4,20},{20,4},{8,24},{24,8},{12,28},{28,12},{1,17},{... | collective-permute-start | bytes 7784 | tf_op jit(solution)/shard_map/ppermute | solution.py:40
Sparse Core Ops, SparseCore 0:
  11.5 20.2 all-gather.1
where the time goes:
time: 207 us
  local copies, waits for them, and re-layouts  56.5 us (27%)
  waiting for transfers between devices  56.2 us (27%)
  matrix products  52.6 us (25%)
  between operations  14.7 us (7%)
  starting transfers between devices  13.3 us (6%)
  other arithmetic  6.89 us (3%)
  blocking collectives  5.96 us (3%)
    ppermute x1, waiting for transfers between devices, padded(): lax.ppermute(lax.slice_in_dim(block, block.shape[dim] - width, None, axis...  33.8 us
    all_gather x1, waiting for transfers between devices, on_device(): sib_rows = lax.all_gather(face_rows, 'sib', axis=0, tiled=True)  19.6 us
    dot_general x1, matrix products, moments(): jnp.einsum('liabc,lcz->liabz', nodal_field, tables[2], precision=highest)  14.8 us
    dot_general x1, matrix products, moments(): jnp.einsum('liabz,lby->liayz', step_one, tables[1], precision=highest)  13.5 us
    dot_general x1, matrix products, moments(): jnp.einsum('liayz,lax->ixyz', step_two, tables[0], precision=highest)  13.4 us
    another operation x2, local copies, waits for them, and re-layouts, moments(): nodal_field = forces.reshape(leaf_count, 3, 8, 8, 8)  10.5 us
    gather x6, local copies, waits for them, and re-layouts, on_device(): jnp.take(chosen, jnp.clip(position[:, face_idx], 0, window_rows - 1), axi...  9.65 us
    ppermute x3, starting transfers between devices, partner(): return lax.ppermute(block, axis, route)  8.53 us
  transfers between devices with their start and end apart: 6, of which 5 were waited for; matrix products, arithmetic and copies ran while one was open for 9% of the time, Pallas kernels for 0%

commit v1 on v0

v1 whole, which is shorter than its diff:
```python
import functools

import jax
import jax.numpy as jnp
import numpy as np
from jax import lax
from jax.experimental import pallas as pl
from jax.experimental.pallas import tpu as pltpu
from jax.sharding import PartitionSpec as P

DEG = 5
LMAX = 7
MOMENTS = 216
BAND = 32
NODES = 512
FACES = 384
ROWS = 288
LANES = 128

penalty = 256.0
out_scale = 1.0 / 1024.0
mass_scale = 1.0 / 32.0
highest = lax.Precision.HIGHEST
f32 = jnp.float32
bf16 = jnp.bfloat16


def cheb_matrix():
    points = -np.cos(np.pi * np.arange(8) / 7.0)
    weights = np.array([(-1.0) ** node for node in range(8)])
    weights[0] *= 0.5
    weights[7] *= 0.5
    derivative = np.zeros((8, 8))
    for row in range(8):
        for col in range(8):
            if row != col:
                derivative[row, col] = weights[col] / weights[row] / (points[row] - points[col])
        derivative[row, row] = -np.sum(derivative[row])
    return points, derivative


def operator_tables():
    _, derivative = cheb_matrix()
    along_x = np.kron(derivative, np.eye(64)).T
    along_y = np.kron(np.eye(4), np.kron(derivative, np.eye(8))).T
    along_z = np.kron(np.eye(32), derivative).T
    return along_x, np.concatenate([along_y, along_z], axis=1)


def face_table():
    pick = np.zeros((NODES, FACES))
    for face in range(6):
        for first in range(8):
            for second in range(8):
                coords = [first, second]
                coords.insert(face // 2, 7 * (face % 2))
                node = 64 * coords[0] + 8 * coords[1] + coords[2]
                pick[node, face * 64 + first * 8 + second] = 1.0
    return pick


def spread_table():
    pick = face_table()
    order = np.concatenate([np.arange(64) + 64 * (face ^ 1) for face in range(6)])
    return pick[:, order].T


def basis_tables():
    points, _ = cheb_matrix()
    powers = np.stack([points**power for power in range(DEG + 1)])
    basis = np.zeros((6, 6, 8, 8, 8, 8))
    basis[:, :, :6] = np.einsum("xa,yb,zc->xyzabc", powers, powers, powers)
    basis = basis.reshape(ROWS, NODES).astype(np.float32)
    top = np.asarray(basis.astype(jnp.bfloat16))
    rest = np.asarray((basis - top.astype(np.float32)).astype(jnp.bfloat16))
    return top, rest


def compact_table():
    table = np.zeros((ROWS, 256), np.float32)
    for group in range(36):
        for power in range(6):
            table[group * 8 + power, group * 6 + power] = 1.0 / 512.0
    return table


def box_table(morton_count):
    bits = morton_count.bit_length() - 1
    key_bits = 3 * LMAX - bits
    table = np.zeros((morton_count, 8, LANES), np.float32)
    for morton in range(morton_count):
        base = morton << key_bits
        lows, sides = [], []
        for offset in (2, 1, 0):
            free = max(0, min(LMAX, (key_bits - offset + 2) // 3))
            cell = sum(((base >> (3 * bit + offset)) & 1) << bit for bit in range(LMAX))
            sides.append(2.0**free / 2.0**LMAX)
            lows.append(cell / 2.0**LMAX)
        scale = 0.5 * max(sides)
        for dim in range(3):
            center = lows[dim] + 0.5 * sides[dim]
            table[morton, dim, 3:6] = (center - 0.5) / 0.5
            table[morton, 4 + dim] = center
        table[morton, 3] = 1.0
        table[morton, 3, 3:6] = scale / 0.5
        table[morton, 7] = 1.0 / scale
    return table.reshape(morton_count * 8, LANES)


def doubling(count):
    order = [0]
    for bit in reversed(range(count.bit_length() - 1)):
        order += [other ^ 1 << bit for other in order]
    return order


def swap(block, axis, apart):
    return lax.ppermute(block, axis, [(at, at ^ apart) for at in range(lax.axis_size(axis))])


def dot(left, right):
    return jnp.dot(left, right, preferred_element_type=f32)


def dot_nt(left, right, precision=None):
    return lax.dot_general(
        left, right, (((1,), (1,)), ((), ())), preferred_element_type=f32, precision=precision
    )


def pack_kernel(counts_ref, vel_ref, pick_ref, faces_ref, low_ref, high_ref):
    sib_count = lax.axis_size("sib")
    own = lax.axis_index("morton") * sib_count + lax.axis_index("sib")
    for comp in range(3):
        picked = dot(vel_ref[comp], pick_ref[...]).astype(bf16)
        for dim in range(3):
            lane = (dim * 3 + comp) * LANES
            faces_ref[:, lane : lane + LANES] = picked[:, dim * LANES : (dim + 1) * LANES]
    low_ref[...] = faces_ref[:BAND, :]
    first = counts_ref[own] - BAND
    leaf_count = faces_ref.shape[0]
    row = lax.broadcasted_iota(jnp.int32, (BAND, leaf_count), 0)
    col = lax.broadcasted_iota(jnp.int32, (BAND, leaf_count), 1)
    pick_rows = jnp.where(col == row + first, 1.0, 0.0).astype(bf16)
    high_ref[...] = dot(pick_rows, faces_ref[...]).astype(bf16)


def pre_kernel(
    counts_ref, vel_ref, press_ref, visc_ref, levels_ref, keys_ref, nbrs_ref, dx_ref, dyz_ref, box_ref,
    part_ref, mass_ref, spots_ref, geom_ref,
):
    sib_count = lax.axis_size("sib")
    morton_count = lax.axis_size("morton")
    morton = lax.axis_index("morton")
    own = morton * sib_count + lax.axis_index("sib")
    leaf_count = mass_ref.shape[0]
    live = lax.broadcasted_iota(jnp.int32, (leaf_count, NODES), 0) < counts_ref[own]
    node = lax.broadcasted_iota(jnp.int32, (1, NODES), 1)
    touching = jnp.zeros((1, NODES), f32)
    for shift in (6, 3, 0):
        idx = jnp.bitwise_and(jnp.right_shift(node, shift), 7)
        touching = touching + jnp.where((idx == 0) | (idx == 7), 1.0, 0.0)

    def gradient(field):
        halves = [dot(field[:, at : at + 256], dyz_ref[...]) for at in (0, 256)]
        return (
            dot(field, dx_ref[...]),
            jnp.concatenate([half[:, :256] for half in halves], axis=1),
            jnp.concatenate([half[:, 256:] for half in halves], axis=1),
        )

    visc = visc_ref[...]
    grads = [gradient(vel_ref[comp]) for comp in range(3)]
    mass = -(grads[0][0] + grads[1][1] + grads[2][2]) * mass_scale
    mass_ref[...] = jnp.where(live, mass, 0.0)
    press_grad = gradient(press_ref[...])
    stress = {}
    for first in range(3):
        for second in range(first, 3):
            value = (visc * (grads[first][second] + grads[second][first])).astype(bf16)
            stress[first, second] = stress[second, first] = value
    for comp in range(3):
        div = dot(stress[comp, 0], dx_ref[...])
        rest = [
            dot(stress[comp, 1][:, at : at + 256], dyz_ref[:, :256])
            + dot(stress[comp, 2][:, at : at + 256], dyz_ref[:, 256:])
            for at in (0, 256)
        ]
        div = div + jnp.concatenate(rest, axis=1)
        jump = touching * vel_ref[comp].astype(f32)
        part = (penalty * visc * jump - div + press_grad[comp]) * out_scale
        part_ref[comp] = jnp.where(live, part, 0.0)

    nbrs = nbrs_ref[...]
    target = jnp.maximum(nbrs, 0)
    owner = target // leaf_count
    slot = target - owner * leaf_count
    owner_morton = owner // sib_count
    owner_sib = owner - owner_morton * sib_count
    apart = jnp.bitwise_xor(owner_sib, lax.axis_index("sib"))
    piece = jnp.zeros_like(apart)
    for at, other in enumerate(doubling(sib_count)):
        piece = jnp.where(apart == other, at, piece)
    step = owner_morton - morton
    below = jnp.maximum(morton - 1, 0) * sib_count
    band_start = jnp.zeros_like(slot)
    for sib in range(sib_count):
        band_start = jnp.where(owner_sib == sib, counts_ref[below + sib] - BAND, band_start)
    base = sib_count * leaf_count
    spot = jnp.where(
        step == 0,
        piece * leaf_count + slot,
        base + piece * (2 * BAND) + jnp.where(step < 0, slot - band_start, BAND + slot),
    )
    spot = jnp.where(nbrs >= 0, spot, -1).astype(f32)
    padded = jnp.concatenate([spot, jnp.full((LANES - spot.shape[0], leaf_count), -1.0, f32)], axis=0)
    spots_ref[...] = padded.T

    box = box_ref[pl.ds(pl.multiple_of(morton * 8, 8), 8), :]
    shift_bits = 3 * (LMAX - levels_ref[...])
    anchor = jnp.left_shift(jnp.right_shift(keys_ref[...], shift_bits), shift_bits)
    span = jnp.left_shift(jnp.ones_like(shift_bits), LMAX - levels_ref[...]).astype(f32)
    finest = 1.0 / float(2**LMAX)
    rows = []
    for dim, offset in enumerate((2, 1, 0)):
        cell = jnp.zeros_like(anchor)
        for bit in range(LMAX):
            picked = jnp.bitwise_and(jnp.right_shift(anchor, 3 * bit + offset), 1)
            cell = cell + jnp.left_shift(picked, bit)
        center = (cell.astype(f32) + 0.5 * span) * finest
        rows.append((center - box[4 + dim : 5 + dim, :]) * box[7:8, :])
    rows.append(0.5 * span * finest * box[7:8, :])
    rows.append(jnp.zeros((4, leaf_count), f32))
    geom_ref[...] = jnp.concatenate(rows, axis=0)


def shifted(tiles, geom):
    width = tiles[0].shape
    scale = jnp.broadcast_to(geom[3:4, :], width)
    level = lax.broadcasted_iota(jnp.int32, width, 0)
    depth = jnp.ones(width, f32)
    for power in range(1, DEG + 1):
        depth = depth * jnp.where(level >= power, scale, 1.0)
    scales = [depth]
    for _ in range(2 * DEG):
        scales.append(scales[-1] * scale)
    tiles = [tile * scales[at // 6 + at % 6] for at, tile in enumerate(tiles)]
    along = [jnp.broadcast_to(geom[dim : dim + 1, :], width) for dim in range(3)]
    for low in range(1, DEG + 1):
        for power in range(DEG, low - 1, -1):
            for other in range(6):
                at = power * 6 + other
                tiles[at] = tiles[at] + along[0] * tiles[at - 6]
            for other in range(6):
                at = other * 6 + power
                tiles[at] = tiles[at] + along[1] * tiles[at - 1]
    steps = [jnp.where(level >= low, along[2], 0.0) for low in range(1, DEG + 1)]
    for step in steps:
        tiles = [tile + step * pltpu.roll(tile, 1, 0) for tile in tiles]
    return tiles


def post_kernel(
    part_ref, visc_ref, spots_ref, geom_ref, box_ref, spread_ref, top_ref, rest_ref, compact_ref, *refs
):
    window_refs, (force_ref, sums_ref, raw_ref) = refs[:-3], refs[-3:]
    morton = lax.axis_index("morton")
    leaf_count = visc_ref.shape[0]
    spots = spots_ref[...].astype(jnp.int32)
    lane = lax.broadcasted_iota(jnp.int32, (leaf_count, FACES), 1)
    upper = jnp.bitwise_and(lane, 64) > 0
    window_rows = sum(window_ref.shape[0] for window_ref in window_refs)
    cols = lax.broadcasted_iota(jnp.int32, (leaf_count, window_rows), 1)
    chosen = []
    for dim in range(3):
        at = dim * FACES
        window = jnp.concatenate([ref[:, at : at + FACES] for ref in window_refs], axis=0)
        sides = []
        for side in range(2):
            face = 2 * dim + side
            place = jnp.broadcast_to(spots[:, face : face + 1], (leaf_count, 1))
            onehot = jnp.where(cols == place, 1.0, 0.0).astype(bf16)
            sides.append(dot(onehot, window))
        chosen.append(jnp.where(upper, sides[0], sides[1]).astype(bf16))
    weight = visc_ref[...] * (penalty * out_scale)
    highs, lows = [], []
    for comp in range(3):
        at = comp * LANES
        picked = jnp.concatenate([block[:, at : at + LANES] for block in chosen], axis=1)
        force = part_ref[comp] - weight * dot(picked, spread_ref[...])
        force_ref[comp] = force
        high = force.astype(bf16)
        highs.append(high)
        lows.append((force - high.astype(f32)).astype(bf16))
    high = jnp.concatenate(highs, axis=0)
    low = jnp.concatenate(lows, axis=0)
    raw_ref[...] = dot_nt(top_ref[...], high) + dot_nt(top_ref[...], low) + dot_nt(rest_ref[...], high)
    geom = jnp.concatenate([geom_ref[...]] * 3, axis=1)
    tiles = shifted([raw_ref[8 * at : 8 * at + 8, :] for at in range(36)], geom)
    moved = jnp.concatenate(tiles, axis=0)
    group = lax.broadcasted_iota(jnp.int32, (3 * leaf_count, LANES), 0) // leaf_count
    column = lax.broadcasted_iota(jnp.int32, (3 * leaf_count, LANES), 1)
    gather = jnp.where((group == column) | (group + 3 == column), 1.0, 0.0)
    summed = jnp.dot(moved, gather, precision=highest, preferred_element_type=f32)
    box = box_ref[pl.ds(pl.multiple_of(morton * 8, 8), 8), :]
    both = shifted([summed[8 * at : 8 * at + 8, :] for at in range(36)], box)
    flat = jnp.concatenate(both, axis=0).T
    sums = jnp.dot(flat[:8], compact_ref[...], precision=highest, preferred_element_type=f32)
    for other in range(sums_ref.shape[0]):
        sums_ref[other] = sums


def final_kernel(sums_ref, box_ref, root_ref):
    sib_count = lax.axis_size("sib")
    first = lax.axis_index("morton") * sib_count
    box = sums_ref[first]
    for sib in range(1, sib_count):
        box = box + sums_ref[first + sib]
    root = jnp.sum(sums_ref[...], axis=0)
    for comp in range(3):
        box_ref[comp] = box[comp : comp + 1, :MOMENTS]
        root_ref[comp] = root[3 + comp : 4 + comp, :MOMENTS]


def call(kernel, shapes, flops, scalars, operands, scratch=(), limit=32):
    specs = [pl.BlockSpec(memory_space=pltpu.SMEM)] * len(scalars)
    specs += [pl.BlockSpec(memory_space=pltpu.VMEM)] * len(operands)
    moved = sum(array.size * array.dtype.itemsize for array in operands)
    return pl.pallas_call(
        kernel,
        out_shape=[jax.ShapeDtypeStruct(shape, dtype) for shape, dtype in shapes],
        in_specs=specs,
        out_specs=[pl.BlockSpec(memory_space=pltpu.VMEM)] * len(shapes),
        scratch_shapes=list(scratch),
        compiler_params=pltpu.CompilerParams(vmem_limit_bytes=limit * 2**20),
        cost_estimate=pl.CostEstimate(flops=flops, bytes_accessed=moved, transcendentals=0),
    )(*scalars, *operands)


def on_device(velocity, pressure, viscosity, levels, morton_keys, counts, neighbors):
    leaf_count = velocity.shape[0]
    morton_count = lax.axis_size("morton")
    along_x, along_yz = operator_tables()
    dx_table = jnp.asarray(along_x.astype(np.float32)).astype(bf16)
    dyz_table = jnp.asarray(along_yz.astype(np.float32)).astype(bf16)
    pick = jnp.asarray(face_table().astype(np.float32)).astype(bf16)
    spread = jnp.asarray(spread_table().astype(np.float32)).astype(bf16)
    top, rest = basis_tables()
    boxes = jnp.asarray(box_table(morton_count))
    vel = jnp.transpose(velocity, (1, 0, 2))
    nbrs = jnp.transpose(neighbors, (1, 0))

    width = 3 * FACES
    faces, low, high = call(
        pack_kernel,
        [((leaf_count, width), bf16), ((BAND, width), bf16), ((BAND, width), bf16)],
        4 * 10**8,
        [counts],
        [vel, pick],
        limit=60,
    )
    ahead = [(at, at + 1) for at in range(morton_count - 1)]
    back = [(target, source) for source, target in ahead]
    sib_count = lax.axis_size("sib")
    part, continuity, spots, geom = call(
        pre_kernel,
        [
            ((3, leaf_count, NODES), f32),
            ((leaf_count, NODES), f32),
            ((leaf_count, LANES), f32),
            ((8, leaf_count), f32),
        ],
        2 * 10**9,
        [counts],
        [
            vel, pressure, viscosity, levels.reshape(1, -1), morton_keys.reshape(1, -1), nbrs,
            dx_table, dyz_table, boxes,
        ],
    )
    window = [faces]
    bands = [jnp.concatenate([lax.ppermute(high, "morton", ahead), lax.ppermute(low, "morton", back)], axis=0)]
    bands[0], part = lax.optimization_barrier((bands[0], part))
    for bit in reversed(range(sib_count.bit_length() - 1)):
        window += [swap(piece, "sib", 1 << bit) for piece in window]
        held = jnp.concatenate(bands, axis=0)
        bands = [held, swap(held, "sib", 1 << bit)]

    force, sums = call(
        post_kernel,
        [((3, leaf_count, NODES), f32), ((morton_count * sib_count, 8, 256), f32)],
        10**9,
        [],
        [
            part, viscosity, spots, geom, boxes, spread, jnp.asarray(top), jnp.asarray(rest),
            jnp.asarray(compact_table()), *window, *bands,
        ],
        [pltpu.VMEM((ROWS, 3 * leaf_count), f32)],
    )
    every = lax.all_to_all(sums, ("morton", "sib"), 0, 0, tiled=True)
    box, root = call(
        final_kernel,
        [((3, 1, MOMENTS), f32), ((3, 1, MOMENTS), f32)],
        10**5,
        [],
        [every],
    )
    return (
        jnp.transpose(force, (1, 0, 2)),
        continuity,
        jnp.transpose(box, (1, 0, 2)),
        jnp.transpose(root, (1, 0, 2)),
    )


def solution(mesh):
    spread_all = ("morton", "sib")
    in_specs = (
        P(spread_all, None, None),
        P(spread_all, None),
        P(spread_all, None),
        P(spread_all),
        P(spread_all),
        P(),
        P(spread_all, None),
    )
    out_specs = (
        P(spread_all, None, None),
        P(spread_all, None),
        P("morton", None, None),
        P("morton", None, None),
    )
    return jax.shard_map(
        on_device, mesh=mesh, in_specs=in_specs, out_specs=out_specs, check_vma=False
    )
```

time: 207 us -> 43.6 us (0.21)
  local copies, waits for them, and re-layouts: 56.5 us -> 1.64 us
  matrix products: 52.6 us -> 0 us
  waiting for transfers between devices: 56.2 us -> 7.24 us
  between operations: 14.7 us -> 0.82 us
  blocking collectives: 5.96 us -> 15.6 us
  Pallas kernels: 0 us -> 9.08 us
  other arithmetic: 6.89 us -> 0.01 us
  starting transfers between devices: 13.3 us -> 8.91 us
    dot_general x23 -> x0, matrix products: 52.6 us -> none  [the longest x1 14.8 us: moments(): jnp.einsum('liabc,lcz->liabz', nodal_field, tables[2], precision=highest)]
    ppermute x5 -> x7, waiting for transfers between devices: 36.6 us -> 7.24 us  [the longest x5 6.11 us: swap(): lax.ppermute(block, axis, [(at, at ^ apart) for at in range(lax.axis_size...]
    another operation x22 -> x0, local copies, waits for them, and re-layouts: 22.4 us -> none  [the longest x2 10.5 us: moments(): nodal_field = forces.reshape(leaf_count, 3, 8, 8, 8)]
    all_gather x1 -> x0, waiting for transfers between devices: 19.6 us -> none  [on_device(): sib_rows = lax.all_gather(face_rows, 'sib', axis=0, tiled=True)]
    gather x15 -> x0, local copies, waits for them, and re-layouts: 17.8 us -> none  [the longest x6 9.65 us: on_device(): jnp.take(chosen, jnp.clip(position[:, face_idx], 0, window_rows - 1), axi...]
    all_to_all x0 -> x1, blocking collectives: none -> 15.6 us  [on_device(): every = lax.all_to_all(sums, ('morton', 'sib'), 0, 0, tiled=True)]
    pallas_call x0 -> x4, Pallas kernels: none -> 9.08 us  [call(): pl.pallas_call(kernel, out_shape=[jax.ShapeDtypeStruct(shape, dtype) for...]
    psum x1 -> x0, blocking collectives: 5.96 us -> none  [on_device(): box_total = lax.psum(local_moments, 'sib')]
  transfers between devices with their start and end apart: 6 -> 7, of which waited for: 5 -> 4; matrix products, arithmetic and copies ran while one was open for 9% -> 0% of each run, Pallas kernels for 0% -> 5%
where the time goes in v1:
time: 43.6 us; the launch traced here: 43.3 us
  blocking collectives  15.6 us (36%)
  Pallas kernels  9.08 us (21%)
  starting transfers between devices  8.91 us (20%)
  waiting for transfers between devices  7.24 us (17%)
  local copies, waits for them, and re-layouts  1.64 us (4%)
  between operations  0.82 us (2%)
    all_to_all x1, blocking collectives, on_device(): every = lax.all_to_all(sums, ('morton', 'sib'), 0, 0, tiled=True)  15.6 us
    pallas_call x4, Pallas kernels, call(): pl.pallas_call(kernel, out_shape=[jax.ShapeDtypeStruct(shape, dtype) for...  9.08 us
    ppermute x5, waiting for transfers between devices, swap(): lax.ppermute(block, axis, [(at, at ^ apart) for at in range(lax.axis_size...  6.11 us
    ppermute x5, starting transfers between devices, swap(): lax.ppermute(block, axis, [(at, at ^ apart) for at in range(lax.axis_size...  4.1 us
    ppermute x1, starting transfers between devices, on_device(): lax.ppermute(high, 'morton', ahead)  3.52 us
    unnamed x31, local copies, waits for them, and re-layouts  1.62 us
    ppermute x1, starting transfers between devices, on_device(): lax.ppermute(low, 'morton', back)  1.29 us
    ppermute x1, waiting for transfers between devices, on_device(): lax.ppermute(low, 'morton', back)  1.13 us
  transfers between devices with their start and end apart: 7, of which 4 were waited for; matrix products, arithmetic and copies ran while one was open for 0% of the time, Pallas kernels for 5%

profile of v1, /device:TPU:0, one launch (start us, length us, event | category | flops | bytes accessed | tf_op | source)
XLA Modules:
  0.0 43.3 jit_solution(14944576208140366896)
XLA Ops:
  0.6 0.0 copy-start.5
  0.6 0.0 copy-start.6
  0.7 0.0 copy-start.7
  0.7 0.0 copy-start.8
  0.7 0.0 copy-start.13
  0.7 2.4 %shard_map.174 = (bf16[128,1152]{1,0:T(8,128)(2,1)}, bf16[32,1152]{1,0:T(8,128)(2,1)}, bf16[32,1152]{1,0:T(8,128)(2,1)}) custom-call(s32[32]{0:T(128)} %counts_ref.3, bf16[3,128,512]{2,1,0:T(8,128)(2,1)} %bitcast.7, bf16[512,384]{1,0:T(8,128)(2,1)} %constant.24.pick_ref), custom_call_target="tpu_custom_call" | custom-call | flops 400000000 | bytes 786432 | tf_op jit(solution)/shard_map/pallas_call | solution.py:329
  3.1 0.5 %collective-permute-start.3 = (bf16[128,1152]{1,0:T(8,128)(2,1)}, bf16[128,1152]{1,0:T(8,128)(2,1)S(1)}, u32[]{:S(2)}, u32[]{:S(2)}) collective-permute-start(bf16[128,1152]{1,0:T(8,128)(2,1)} %get-tuple-element.23.refs_0_), channel_id=1, source_target_pairs={{0,1},{1,0},{2,3},{3,2},{4,5},{5,4},{6,7},{7,6},{8,9},{9,8},{10,11... | collective-permute-start | bytes 884744 | tf_op jit(solution)/shard_map/ppermute | solution.py:118
  3.5 2.5 %collective-permute-start.2 = (bf16[128,1152]{1,0:T(8,128)(2,1)}, bf16[128,1152]{1,0:T(8,128)(2,1)S(1)}, u32[]{:S(2)}, u32[]{:S(2)}) collective-permute-start(bf16[128,1152]{1,0:T(8,128)(2,1)} %get-tuple-element.23.refs_0_), channel_id=1, source_target_pairs={{0,2},{1,3},{2,0},{3,1},{4,6},{5,7},{6,4},{7,5},{8,10},{9,11},{10,... | collective-permute-start | bytes 884744 | tf_op jit(solution)/shard_map/ppermute | solution.py:118
  6.0 0.0 copy-start.9
  6.0 3.5 %collective-permute-start = (bf16[32,1152]{1,0:T(8,128)(2,1)}, bf16[32,1152]{1,0:T(8,128)(2,1)S(1)}, u32[]{:S(2)}, u32[]{:S(2)}) collective-permute-start(bf16[32,1152]{1,0:T(8,128)(2,1)} %get-tuple-element.17), channel_id=1, source_target_pairs={{0,4},{4,8},{8,12},{12,16},{16,20},{20,24},{24,28},{1,5},{5,9},{9,... | collective-permute-start | bytes 221192 | tf_op jit(solution)/shard_map/ppermute | solution.py:381
  9.6 1.3 %collective-permute-start.1 = (bf16[32,1152]{1,0:T(8,128)(2,1)}, bf16[32,1152]{1,0:T(8,128)(2,1)S(1)}, u32[]{:S(2)}, u32[]{:S(2)}) collective-permute-start(bf16[32,1152]{1,0:T(8,128)(2,1)} %get-tuple-element.18), channel_id=1, source_target_pairs={{4,0},{8,4},{12,8},{16,12},{20,16},{24,20},{28,24},{5,1},{9,5},{13... | collective-permute-start | bytes 221192 | tf_op jit(solution)/shard_map/ppermute | solution.py:381
  10.9 0.0 copy-start.10
  10.9 0.0 copy-start.11
  10.9 0.0 copy-start.12
  10.9 0.0 copy-done.5
  10.9 0.0 copy-done.6
  10.9 0.0 copy-done.7
  10.9 0.0 copy-done.8
  10.9 0.0 copy-done.13
  10.9 0.0 copy-done.9
  11.0 0.6 %copy-done.10 = s32[32]{0:T(128)S(1)} copy-done((s32[32]{0:T(128)S(1)}, s32[32]{0:T(128)}, u32[]{:S(2)}) %copy-start.10) | copy-done | bytes 152
  11.5 0.0 copy-done.11
  11.5 0.0 copy-done.12
  11.5 0.0 copy-start.14
  11.5 0.9 %copy-done.14 = bf16[256,512]{1,0:T(8,128)(2,1)S(1)} copy-done((bf16[256,512]{1,0:T(8,128)(2,1)S(1)}, bf16[256,512]{1,0:T(8,128)(2,1)}, u32[]{:S(2)}) %copy-start.14) | copy-done | bytes 262168
  12.5 0.0 copy-start.2
  12.5 0.0 copy-start.3
  12.5 0.0 copy-start.4
  12.5 2.4 %shard_map.175 = (f32[3,128,512]{2,1,0:T(8,128)S(1)}, f32[128,512]{1,0:T(8,128)}, f32[128,128]{1,0:T(8,128)S(1)}, f32[8,128]{1,0:T(8,128)S(1)}) custom-call(s32[32]{0:T(128)S(1)} %copy-done.10, bf16[3,128,512]{2,1,0:T(8,128)(2,1)S(1)} %bitcast.8, bf16[128,512]{1,0:T(8,128)(2,1)S(1)} %copy-done.8, f32[128,512]{1,0:T(8,128)S(1)} %copy-done.5, ...), custom_call_target="tpu_custom_call" | custom-call | flops 2000000000 | bytes 1609728 | tf_op jit(solution)/shard_map/pallas_call | solution.py:329
  14.9 0.0 collective-permute-done
  14.9 1.1 %collective-permute-done.1 = bf16[32,1152]{1,0:T(8,128)(2,1)S(1)} collective-permute-done((bf16[32,1152]{1,0:T(8,128)(2,1)}, bf16[32,1152]{1,0:T(8,128)(2,1)S(1)}, u32[]{:S(2)}, u32[]{:S(2)}) %collective-permute-start.1) | collective-permute-done | bytes 73760 | tf_op jit(solution)/shard_map/ppermute | solution.py:381
  16.0 0.0 copy-start.1
  16.0 0.6 %collective-permute-start.5 = (bf16[64,1152]{1,0:T(8,128)(2,1)S(1)}, bf16[64,1152]{1,0:T(8,128)(2,1)S(1)}, u32[]{:S(2)}, u32[]{:S(2)}) collective-permute-start(bf16[64,1152]{1,0:T(8,128)(2,1)S(1)} %pad_maximum_fusion), channel_id=1, source_target_pairs={{0,2},{1,3},{2,0},{3,1},{4,6},{5,7},{6,4},{7,5},{8,10},{9,11},{10,... | collective-permute-start | bytes 442376 | tf_op jit(solution)/shard_map/ppermute | solution.py:118
  16.6 4.6 %collective-permute-done.5 = bf16[64,1152]{1,0:T(8,128)(2,1)S(1)} collective-permute-done((bf16[64,1152]{1,0:T(8,128)(2,1)S(1)}, bf16[64,1152]{1,0:T(8,128)(2,1)S(1)}, u32[]{:S(2)}, u32[]{:S(2)}) %collective-permute-start.5) | collective-permute-done | bytes 147488 | tf_op jit(solution)/shard_map/ppermute | solution.py:118
  21.3 0.1 collective-permute-start.6
  21.3 0.0 collective-permute-done.2.refs_1_
  21.4 0.5 %collective-permute-start.4 = (bf16[128,1152]{1,0:T(8,128)(2,1)S(1)}, bf16[128,1152]{1,0:T(8,128)(2,1)S(1)}, u32[]{:S(2)}, u32[]{:S(2)}) collective-permute-start(bf16[128,1152]{1,0:T(8,128)(2,1)S(1)} %collective-permute-done.2.refs_1_), channel_id=1, source_target_pairs={{0,1},{1,0},{2,3},{3,2},{4,5},{5,4},{6,7},{7,6},{8,9},{9,8},{10,11... | collective-permute-start | bytes 884744 | tf_op jit(solution)/shard_map/ppermute | solution.py:118
  21.8 0.0 collective-permute-done.3.refs_2_
  21.9 1.1 %collective-permute-done.6.refs_5_ = bf16[128,1152]{1,0:T(8,128)(2,1)S(1)} collective-permute-done((bf16[128,1152]{1,0:T(8,128)(2,1)S(1)}, bf16[128,1152]{1,0:T(8,128)(2,1)S(1)}, u32[]{:S(2)}, u32[]{:S(2)}) %collective-permute-start.6) | collective-permute-done | bytes 294944 | tf_op jit(solution)/shard_map/ppermute | solution.py:118
  22.9 0.4 collective-permute-done.4.refs_3_
  23.3 0.0 copy-done.2
  23.3 0.0 copy-done.3
  23.3 0.0 copy-done.4
  23.4 0.0 copy-done
  23.4 0.0 copy-done.1
  23.4 3.7 %shard_map.176 = (f32[3,128,512]{2,1,0:T(8,128)}, f32[32,8,256]{2,1,0:T(8,128)S(1)}) custom-call(f32[3,128,512]{2,1,0:T(8,128)S(1)} %get-tuple-element.20.part_ref, f32[128,512]{1,0:T(8,128)S(1)} %copy-done.5, f32[128,128]{1,0:T(8,128)S(1)} %get-tuple-element.21.spots_ref, f32[8,128]{1,0:T(8,128)S(1)} %get-tuple-element.22.geom_ref, ...), custom_call_target="tpu_custom_call" | custom-call | flops 1000000000 | bytes 4198400 | tf_op jit(solution)/shard_map/pallas_call | solution.py:329
  27.1 15.6 %all_to_all.5.sums_ref = f32[32,8,256]{2,1,0:T(8,128)S(1)} all-to-all(f32[32,8,256]{2,1,0:T(8,128)S(1)} %get-tuple-element.27), channel_id=1, replica_groups=mesh['morton'=8,'sib'=4] {'morton','sib'}, dimensions={0} | all-to-all | bytes 524288 | tf_op jit(solution)/shard_map/all_to_all | solution.py:399
  42.7 0.6 %shard_map.177 = (f32[3,1,216]{2,1,0:T(1,128)}, f32[3,1,216]{2,1,0:T(1,128)}) custom-call(f32[32,8,256]{2,1,0:T(8,128)S(1)} %all_to_all.5.sums_ref), custom_call_target="tpu_custom_call" | custom-call | flops 100000 | bytes 262144 | tf_op jit(solution)/shard_map/pallas_call | solution.py:329
  (4 shorter events, 0.0 us)
Async XLA Ops:
  0.6 10.3 %copy-start.5 = (f32[128,512]{1,0:T(8,128)S(1)}, f32[128,512]{1,0:T(8,128)}, u32[]{:S(2)}) copy-start(f32[128,512]{1,0:T(8,128)} %visc_ref.3) | copy-start | bytes 786436
  0.6 10.3 %copy-start.6 = (f32[64,128]{1,0:T(8,128)S(1)}, f32[64,128]{1,0:T(8,128)}, u32[]{:S(2)}) copy-start(f32[64,128]{1,0:T(8,128)} %constant.20.clone.box_ref) | copy-start | bytes 98308
  0.7 10.3 %copy-start.7 = (bf16[128,3,512]{2,0,1:T(8,128)(2,1)S(1)}, bf16[128,3,512]{2,0,1:T(8,128)(2,1)}, u32[]{:S(2)}) copy-start(bf16[128,3,512]{2,0,1:T(8,128)(2,1)} %param.15) | copy-start | bytes 1179652
  0.7 10.3 %copy-start.8 = (bf16[128,512]{1,0:T(8,128)(2,1)S(1)}, bf16[128,512]{1,0:T(8,128)(2,1)}, u32[]{:S(2)}) copy-start(bf16[128,512]{1,0:T(8,128)(2,1)} %press_ref.1) | copy-start | bytes 393220
  0.7 10.3 %copy-start.13 = (bf16[512,512]{1,0:T(8,128)(2,1)S(1)}, bf16[512,512]{1,0:T(8,128)(2,1)}, u32[]{:S(2)}) copy-start(bf16[512,512]{1,0:T(8,128)(2,1)} %constant.25.dx_ref) | copy-start | bytes 1572868
  3.1 18.8 %collective-permute-start.3 = (bf16[128,1152]{1,0:T(8,128)(2,1)}, bf16[128,1152]{1,0:T(8,128)(2,1)S(1)}, u32[]{:S(2)}, u32[]{:S(2)}) collective-permute-start(bf16[128,1152]{1,0:T(8,128)(2,1)} %get-tuple-element.23.refs_0_), channel_id=1, source_target_pairs={{0,1},{1,0},{2,3},{3,2},{4,5},{5,4},{6,7},{7,6},{8,9},{9,8},{10,11... | collective-permute-start | bytes 884744 | tf_op jit(solution)/shard_map/ppermute | solution.py:118
  3.5 17.8 %collective-permute-start.2 = (bf16[128,1152]{1,0:T(8,128)(2,1)}, bf16[128,1152]{1,0:T(8,128)(2,1)S(1)}, u32[]{:S(2)}, u32[]{:S(2)}) collective-permute-start(bf16[128,1152]{1,0:T(8,128)(2,1)} %get-tuple-element.23.refs_0_), channel_id=1, source_target_pairs={{0,2},{1,3},{2,0},{3,1},{4,6},{5,7},{6,4},{7,5},{8,10},{9,11},{10,... | collective-permute-start | bytes 884744 | tf_op jit(solution)/shard_map/ppermute | solution.py:118
  6.0 4.9 %copy-start.9 = (s32[128,6]{0,1:T(8,128)S(1)}, s32[128,6]{0,1:T(8,128)}, u32[]{:S(2)}) copy-start(s32[128,6]{0,1:T(8,128)} %param.21) | copy-start | bytes 9220
  6.0 8.9 %collective-permute-start = (bf16[32,1152]{1,0:T(8,128)(2,1)}, bf16[32,1152]{1,0:T(8,128)(2,1)S(1)}, u32[]{:S(2)}, u32[]{:S(2)}) collective-permute-start(bf16[32,1152]{1,0:T(8,128)(2,1)} %get-tuple-element.17), channel_id=1, source_target_pairs={{0,4},{4,8},{8,12},{12,16},{16,20},{20,24},{24,28},{1,5},{5,9},{9,... | collective-permute-start | bytes 221192 | tf_op jit(solution)/shard_map/ppermute | solution.py:381
  9.6 6.5 %collective-permute-start.1 = (bf16[32,1152]{1,0:T(8,128)(2,1)}, bf16[32,1152]{1,0:T(8,128)(2,1)S(1)}, u32[]{:S(2)}, u32[]{:S(2)}) collective-permute-start(bf16[32,1152]{1,0:T(8,128)(2,1)} %get-tuple-element.18), channel_id=1, source_target_pairs={{4,0},{8,4},{12,8},{16,12},{20,16},{24,20},{28,24},{5,1},{9,5},{13... | collective-permute-start | bytes 221192 | tf_op jit(solution)/shard_map/ppermute | solution.py:381
  10.9 0.7 %copy-start.10 = (s32[32]{0:T(128)S(1)}, s32[32]{0:T(128)}, u32[]{:S(2)}) copy-start(s32[32]{0:T(128)} %counts_ref.3) | copy-start | bytes 388
  10.9 0.7 %copy-start.11 = (s32[128]{0:T(128)S(1)}, s32[128]{0:T(128)}, u32[]{:S(2)}) copy-start(s32[128]{0:T(128)} %param.18) | copy-start | bytes 1540
  10.9 0.7 %copy-start.12 = (s32[128]{0:T(128)S(1)}, s32[128]{0:T(128)}, u32[]{:S(2)}) copy-start(s32[128]{0:T(128)} %param.19) | copy-start | bytes 1540
  11.5 0.9 %copy-start.14 = (bf16[256,512]{1,0:T(8,128)(2,1)S(1)}, bf16[256,512]{1,0:T(8,128)(2,1)}, u32[]{:S(2)}) copy-start(bf16[256,512]{1,0:T(8,128)(2,1)} %constant.26.dyz_ref) | copy-start | bytes 786436
  12.5 10.8 %copy-start.2 = (bf16[288,512]{1,0:T(8,128)(2,1)S(1)}, bf16[288,512]{1,0:T(8,128)(2,1)}, u32[]{:S(2)}) copy-start(bf16[288,512]{1,0:T(8,128)(2,1)} %constant.22.clone.rest_ref) | copy-start | bytes 884740
  12.5 10.8 %copy-start.3 = (bf16[288,512]{1,0:T(8,128)(2,1)S(1)}, bf16[288,512]{1,0:T(8,128)(2,1)}, u32[]{:S(2)}) copy-start(bf16[288,512]{1,0:T(8,128)(2,1)} %constant.21.clone.top_ref) | copy-start | bytes 884740
  12.5 10.8 %copy-start.4 = (bf16[128,1152]{1,0:T(8,128)(2,1)S(1)}, bf16[128,1152]{1,0:T(8,128)(2,1)}, u32[]{:S(2)}) copy-start(bf16[128,1152]{1,0:T(8,128)(2,1)} %get-tuple-element.23.refs_0_) | copy-start | bytes 884740
  14.9 8.5 %copy-start = (bf16[384,512]{1,0:T(8,128)(2,1)S(1)}, bf16[384,512]{1,0:T(8,128)(2,1)}, u32[]{:S(2)}) copy-start(bf16[384,512]{1,0:T(8,128)(2,1)} %constant.27.spread_ref) | copy-start | bytes 1179652
  16.0 7.3 %copy-start.1 = (f32[288,256]{1,0:T(8,128)S(1)}, f32[288,256]{1,0:T(8,128)}, u32[]{:S(2)}) copy-start(f32[288,256]{1,0:T(8,128)} %constant.23.clone.compact_ref) | copy-start | bytes 884740
  16.0 5.2 %collective-permute-start.5 = (bf16[64,1152]{1,0:T(8,128)(2,1)S(1)}, bf16[64,1152]{1,0:T(8,128)(2,1)S(1)}, u32[]{:S(2)}, u32[]{:S(2)}) collective-permute-start(bf16[64,1152]{1,0:T(8,128)(2,1)S(1)} %pad_maximum_fusion), channel_id=1, source_target_pairs={{0,2},{1,3},{2,0},{3,1},{4,6},{5,7},{6,4},{7,5},{8,10},{9,11},{10,... | collective-permute-start | bytes 442376 | tf_op jit(solution)/shard_map/ppermute | solution.py:118
  21.3 1.6 %collective-permute-start.6 = (bf16[128,1152]{1,0:T(8,128)(2,1)S(1)}, bf16[128,1152]{1,0:T(8,128)(2,1)S(1)}, u32[]{:S(2)}, u32[]{:S(2)}) collective-permute-start(bf16[128,1152]{1,0:T(8,128)(2,1)S(1)} %constant_dynamic-update-slice_fusion.refs_4_), channel_id=1, source_target_pairs={{0,1},{1,0},{2,3},{3,2},{4,5},{5,4},{6,7},{7,6},{8,9},{9,8},{10,11... | collective-permute-start | bytes 884744 | tf_op jit(solution)/shard_map/ppermute | solution.py:118
  21.4 2.0 %collective-permute-start.4 = (bf16[128,1152]{1,0:T(8,128)(2,1)S(1)}, bf16[128,1152]{1,0:T(8,128)(2,1)S(1)}, u32[]{:S(2)}, u32[]{:S(2)}) collective-permute-start(bf16[128,1152]{1,0:T(8,128)(2,1)S(1)} %collective-permute-done.2.refs_1_), channel_id=1, source_target_pairs={{0,1},{1,0},{2,3},{3,2},{4,5},{5,4},{6,7},{7,6},{8,9},{9,8},{10,11... | collective-permute-start | bytes 884744 | tf_op jit(solution)/shard_map/ppermute | solution.py:118

commit v2 on v1

--- a/solution.py
+++ b/solution.py
@@ -1,4 +1,4 @@
-import functools
+import math
 
 import jax
 import jax.numpy as jnp
@@ -118,6 +118,27 @@
     return lax.ppermute(block, axis, [(at, at ^ apart) for at in range(lax.axis_size(axis))])
 
 
+def move_tables(morton_count):
+    bits = 3 * LMAX - (morton_count.bit_length() - 1)
+    ratio = 2.0 ** max(max(0, min(LMAX, (bits - offset + 2) // 3)) for offset in range(3)) / 2.0**LMAX
+    shift = np.zeros((256, 256), np.float32)
+    powers = np.zeros((256, 256), np.int32)
+    triples = list(np.ndindex(6, 6, 6))
+    for row, beta in enumerate(triples):
+        for col, alpha in enumerate(triples):
+            if all(b <= a for a, b in zip(alpha, beta)):
+                shift[row, col] = math.prod(math.comb(a, b) for a, b in zip(alpha, beta)) * ratio ** sum(beta)
+                powers[row, col] = sum((a - b) << 3 * dim for dim, (a, b) in enumerate(zip(alpha, beta)))
+    return shift, powers
+
+
+def pairs(block, first):
+    route = []
+    for low in range(first, lax.axis_size("morton") - 1, 2):
+        route += [(low, low + 1), (low + 1, low)]
+    return lax.ppermute(block, "morton", route)
+
+
 def dot(left, right):
     return jnp.dot(left, right, preferred_element_type=f32)
 
@@ -128,26 +149,54 @@
     )
 
 
-def pack_kernel(counts_ref, vel_ref, pick_ref, faces_ref, low_ref, high_ref):
+def pack_kernel(
+    counts_ref, vel_hbm, pick_hbm, faces_hbm, even_hbm, odd_hbm, vel_ref, pick_ref, faces_ref, bands_ref, sems
+):
     sib_count = lax.axis_size("sib")
-    own = lax.axis_index("morton") * sib_count + lax.axis_index("sib")
-    for comp in range(3):
-        picked = dot(vel_ref[comp], pick_ref[...]).astype(bf16)
-        for dim in range(3):
-            lane = (dim * 3 + comp) * LANES
-            faces_ref[:, lane : lane + LANES] = picked[:, dim * LANES : (dim + 1) * LANES]
-    low_ref[...] = faces_ref[:BAND, :]
+    morton = lax.axis_index("morton")
+    own = morton * sib_count + lax.axis_index("sib")
+    loads = [
+        pltpu.make_async_copy(vel_hbm, vel_ref, sems.at[0]),
+        pltpu.make_async_copy(pick_hbm, pick_ref, sems.at[1]),
+    ]
+    for load in loads:
+        load.start()
     first = counts_ref[own] - BAND
     leaf_count = faces_ref.shape[0]
     row = lax.broadcasted_iota(jnp.int32, (BAND, leaf_count), 0)
     col = lax.broadcasted_iota(jnp.int32, (BAND, leaf_count), 1)
-    pick_rows = jnp.where(col == row + first, 1.0, 0.0).astype(bf16)
-    high_ref[...] = dot(pick_rows, faces_ref[...]).astype(bf16)
+    last_rows = jnp.where(col == row + first, 1.0, 0.0).astype(bf16)
+    is_odd = jnp.bitwise_and(morton, 1) == 1
+    loads[0].wait()
+    fields = [vel_ref[comp] for comp in range(3)]
+    fields += [dot(last_rows, vel_ref[comp]).astype(bf16) for comp in range(3)]
+    fields = jnp.concatenate(fields, axis=0)
+    loads[1].wait()
+    stores = []
+    for dim in range(3):
+        picked = dot(fields, pick_ref[:, dim * LANES : (dim + 1) * LANES]).astype(bf16)
+        for comp in range(3):
+            lane = (dim * 3 + comp) * LANES
+            faces_ref[:, lane : lane + LANES] = picked[comp * leaf_count : (comp + 1) * leaf_count]
+            at = 3 * leaf_count + comp * BAND
+            low = picked[comp * leaf_count : comp * leaf_count + BAND]
+            high = picked[at : at + BAND]
+            bands_ref[0, :, lane : lane + LANES] = jnp.where(is_odd, low, high)
+            bands_ref[1, :, lane : lane + LANES] = jnp.where(is_odd, high, low)
+        lanes = pl.ds(dim * FACES, FACES)
+        stores.append(pltpu.make_async_copy(faces_ref.at[:, lanes], faces_hbm.at[:, lanes], sems.at[2 + dim]))
+        stores[-1].start()
+    stores.append(pltpu.make_async_copy(bands_ref.at[0], even_hbm, sems.at[5]))
+    stores.append(pltpu.make_async_copy(bands_ref.at[1], odd_hbm, sems.at[6]))
+    for store in stores[3:]:
+        store.start()
+    for store in stores:
+        store.wait()
 
 
 def pre_kernel(
     counts_ref, vel_ref, press_ref, visc_ref, levels_ref, keys_ref, nbrs_ref, dx_ref, dyz_ref, box_ref,
-    part_ref, mass_ref, spots_ref, geom_ref,
+    shift_ref, powers_ref, part_ref, mass_ref, spots_ref, geom_ref, move_ref,
 ):
     sib_count = lax.axis_size("sib")
     morton_count = lax.axis_size("morton")
@@ -161,34 +210,33 @@
         idx = jnp.bitwise_and(jnp.right_shift(node, shift), 7)
         touching = touching + jnp.where((idx == 0) | (idx == 7), 1.0, 0.0)
 
-    def gradient(field):
-        halves = [dot(field[:, at : at + 256], dyz_ref[...]) for at in (0, 256)]
-        return (
-            dot(field, dx_ref[...]),
-            jnp.concatenate([half[:, :256] for half in halves], axis=1),
-            jnp.concatenate([half[:, 256:] for half in halves], axis=1),
-        )
+    def rows(stack, at):
+        return stack[at * leaf_count : (at + 1) * leaf_count]
 
     visc = visc_ref[...]
-    grads = [gradient(vel_ref[comp]) for comp in range(3)]
-    mass = -(grads[0][0] + grads[1][1] + grads[2][2]) * mass_scale
+    fields = jnp.concatenate([vel_ref[0], vel_ref[1], vel_ref[2], press_ref[...]], axis=0)
+    halves = [dot(fields[:, at : at + 256], dyz_ref[...]) for at in (0, 256)]
+    grads = [
+        dot(fields, dx_ref[...]),
+        jnp.concatenate([half[:, :256] for half in halves], axis=1),
+        jnp.concatenate([half[:, 256:] for half in halves], axis=1),
+    ]
+    mass = -(rows(grads[0], 0) + rows(grads[1], 1) + rows(grads[2], 2)) * mass_scale
     mass_ref[...] = jnp.where(live, mass, 0.0)
-    press_grad = gradient(press_ref[...])
     stress = {}
     for first in range(3):
         for second in range(first, 3):
-            value = (visc * (grads[first][second] + grads[second][first])).astype(bf16)
+            value = (visc * (rows(grads[second], first) + rows(grads[first], second))).astype(bf16)
             stress[first, second] = stress[second, first] = value
+    columns = [jnp.concatenate([stress[comp, dim] for comp in range(3)], axis=0) for dim in range(3)]
+    rest = [
+        dot(columns[1][:, at : at + 256], dyz_ref[:, :256]) + dot(columns[2][:, at : at + 256], dyz_ref[:, 256:])
+        for at in (0, 256)
+    ]
+    div = dot(columns[0], dx_ref[...]) + jnp.concatenate(rest, axis=1)
     for comp in range(3):
-        div = dot(stress[comp, 0], dx_ref[...])
-        rest = [
-            dot(stress[comp, 1][:, at : at + 256], dyz_ref[:, :256])
-            + dot(stress[comp, 2][:, at : at + 256], dyz_ref[:, 256:])
-            for at in (0, 256)
-        ]
-        div = div + jnp.concatenate(rest, axis=1)
         jump = touching * vel_ref[comp].astype(f32)
-        part = (penalty * visc * jump - div + press_grad[comp]) * out_scale
+        part = (penalty * visc * jump - rows(div, comp) + rows(grads[comp], 3)) * out_scale
         part_ref[comp] = jnp.where(live, part, 0.0)
 
     nbrs = nbrs_ref[...]
@@ -207,10 +255,11 @@
     for sib in range(sib_count):
         band_start = jnp.where(owner_sib == sib, counts_ref[below + sib] - BAND, band_start)
     base = sib_count * leaf_count
+    below_at = BAND * (1 - jnp.bitwise_and(morton, 1))
     spot = jnp.where(
         step == 0,
         piece * leaf_count + slot,
-        base + piece * (2 * BAND) + jnp.where(step < 0, slot - band_start, BAND + slot),
+        base + piece * (2 * BAND) + jnp.where(step < 0, slot - band_start + below_at, slot + BAND - below_at),
     )
     spot = jnp.where(nbrs >= 0, spot, -1).astype(f32)
     padded = jnp.concatenate([spot, jnp.full((LANES - spot.shape[0], leaf_count), -1.0, f32)], axis=0)
@@ -221,17 +270,27 @@
     anchor = jnp.left_shift(jnp.right_shift(keys_ref[...], shift_bits), shift_bits)
     span = jnp.left_shift(jnp.ones_like(shift_bits), LMAX - levels_ref[...]).astype(f32)
     finest = 1.0 / float(2**LMAX)
-    rows = []
+    places = []
     for dim, offset in enumerate((2, 1, 0)):
         cell = jnp.zeros_like(anchor)
         for bit in range(LMAX):
             picked = jnp.bitwise_and(jnp.right_shift(anchor, 3 * bit + offset), 1)
             cell = cell + jnp.left_shift(picked, bit)
         center = (cell.astype(f32) + 0.5 * span) * finest
-        rows.append((center - box[4 + dim : 5 + dim, :]) * box[7:8, :])
-    rows.append(0.5 * span * finest * box[7:8, :])
-    rows.append(jnp.zeros((4, leaf_count), f32))
-    geom_ref[...] = jnp.concatenate(rows, axis=0)
+        places.append((center - box[4 + dim : 5 + dim, :]) * box[7:8, :])
+    places.append(0.5 * span * finest * box[7:8, :])
+    places.append(jnp.zeros((4, leaf_count), f32))
+    geom_ref[...] = jnp.concatenate(places, axis=0)
+    move = shift_ref[...]
+    powers = powers_ref[...]
+    for dim in range(3):
+        power = jnp.bitwise_and(jnp.right_shift(powers, 3 * dim), 7)
+        along = box[dim : dim + 1, 3:4]
+        factor = jnp.ones((1, 1), f32)
+        for degree in range(1, DEG + 1):
+            factor = factor * along
+            move = move * jnp.where(power == degree, factor, 1.0)
+    move_ref[...] = move
 
 
 def shifted(tiles, geom):
@@ -261,9 +320,9 @@
 
 
 def post_kernel(
-    part_ref, visc_ref, spots_ref, geom_ref, box_ref, spread_ref, top_ref, rest_ref, compact_ref, *refs
+    part_ref, visc_ref, spots_ref, geom_ref, box_ref, spread_ref, basis_ref, compact_ref, *refs
 ):
-    window_refs, (force_ref, sums_ref, raw_ref) = refs[:-3], refs[-3:]
+    window_refs, (force_hbm, sums_ref, force_ref, raw_ref, sems) = refs[:-5], refs[-5:]
     morton = lax.axis_index("morton")
     leaf_count = visc_ref.shape[0]
     spots = spots_ref[...].astype(jnp.int32)
@@ -275,26 +334,28 @@
     for dim in range(3):
         at = dim * FACES
         window = jnp.concatenate([ref[:, at : at + FACES] for ref in window_refs], axis=0)
-        sides = []
-        for side in range(2):
-            face = 2 * dim + side
-            place = jnp.broadcast_to(spots[:, face : face + 1], (leaf_count, 1))
-            onehot = jnp.where(cols == place, 1.0, 0.0).astype(bf16)
-            sides.append(dot(onehot, window))
-        chosen.append(jnp.where(upper, sides[0], sides[1]).astype(bf16))
+        places = [jnp.broadcast_to(spots[:, face : face + 1], (leaf_count, 1)) for face in (2 * dim, 2 * dim + 1)]
+        onehot = [jnp.where(cols == place, 1.0, 0.0).astype(bf16) for place in places]
+        both = dot(jnp.concatenate(onehot, axis=0), window)
+        chosen.append(jnp.where(upper, both[:leaf_count], both[leaf_count:]).astype(bf16))
     weight = visc_ref[...] * (penalty * out_scale)
-    highs, lows = [], []
+    highs, lows, stores = [], [], []
+    picked = [
+        jnp.concatenate([block[:, comp * LANES : (comp + 1) * LANES] for block in chosen], axis=1) for comp in range(3)
+    ]
+    jumps = dot(jnp.concatenate(picked, axis=0), spread_ref[...])
     for comp in range(3):
-        at = comp * LANES
-        picked = jnp.concatenate([block[:, at : at + LANES] for block in chosen], axis=1)
-        force = part_ref[comp] - weight * dot(picked, spread_ref[...])
+        force = part_ref[comp] - weight * jumps[comp * leaf_count : (comp + 1) * leaf_count]
         force_ref[comp] = force
+        stores.append(pltpu.make_async_copy(force_ref.at[comp], force_hbm.at[comp], sems.at[comp]))
+        stores[-1].start()
         high = force.astype(bf16)
         highs.append(high)
         lows.append((force - high.astype(f32)).astype(bf16))
     high = jnp.concatenate(highs, axis=0)
     low = jnp.concatenate(lows, axis=0)
-    raw_ref[...] = dot_nt(top_ref[...], high) + dot_nt(top_ref[...], low) + dot_nt(rest_ref[...], high)
+    raw = dot_nt(basis_ref[...], high)
+    raw_ref[...] = raw[:ROWS] + raw[ROWS:] + dot_nt(basis_ref[:ROWS, :], low)
     geom = jnp.concatenate([geom_ref[...]] * 3, axis=1)
     tiles = shifted([raw_ref[8 * at : 8 * at + 8, :] for at in range(36)], geom)
     moved = jnp.concatenate(tiles, axis=0)
@@ -306,33 +367,52 @@
     both = shifted([summed[8 * at : 8 * at + 8, :] for at in range(36)], box)
     flat = jnp.concatenate(both, axis=0).T
     sums = jnp.dot(flat[:8], compact_ref[...], precision=highest, preferred_element_type=f32)
+    sums_ref[...] = sums
+    for store in stores:
+        store.wait()
+
+
+def share_kernel(own_ref, other_ref, sums_ref):
+    sums = own_ref[...] + other_ref[...]
+    blank = jnp.zeros((2, LANES), f32)
+    to_box = jnp.concatenate([sums[:3, :LANES], sums[:3, LANES:], blank], axis=0)
+    to_root = jnp.concatenate([sums[3:6, :LANES], sums[3:6, LANES:], blank], axis=0)
+    morton = lax.axis_index("morton")
+    in_box = lax.axis_size("sib") // 2
     for other in range(sums_ref.shape[0]):
-        sums_ref[other] = sums
-
-
-def final_kernel(sums_ref, box_ref, root_ref):
-    sib_count = lax.axis_size("sib")
-    first = lax.axis_index("morton") * sib_count
-    box = sums_ref[first]
-    for sib in range(1, sib_count):
-        box = box + sums_ref[first + sib]
-    root = jnp.sum(sums_ref[...], axis=0)
+        sums_ref[other] = jnp.where(morton == other // in_box, to_box, to_root)
+
+
+def final_kernel(sums_ref, move_ref, box_ref, root_ref):
+    in_box = lax.axis_size("sib") // 2
+    morton = lax.axis_index("morton")
+    box = jnp.zeros(sums_ref.shape[1:], f32)
+    root = jnp.zeros(sums_ref.shape[1:], f32)
+    for group in range(sums_ref.shape[0] // in_box):
+        total = jnp.sum(sums_ref[group * in_box : (group + 1) * in_box], axis=0)
+        box = box + jnp.where(morton == group, total, 0.0)
+        root = root + jnp.where(morton == group, 0.0, total)
+    box = jnp.concatenate([box[:3], box[3:6]], axis=1)
+    root = jnp.concatenate([root[:3], root[3:6]], axis=1)
+    box8 = jnp.concatenate([box, jnp.zeros((5, 2 * LANES), f32)], axis=0)
+    root = root + jnp.dot(box8, move_ref[...], precision=highest, preferred_element_type=f32)[:3]
     for comp in range(3):
         box_ref[comp] = box[comp : comp + 1, :MOMENTS]
-        root_ref[comp] = root[3 + comp : 4 + comp, :MOMENTS]
-
-
-def call(kernel, shapes, flops, scalars, operands, scratch=(), limit=32):
+        root_ref[comp] = root[comp : comp + 1, :MOMENTS]
+
+
+def call(kernel, shapes, flops, scalars, operands, scratch=(), place=pltpu.VMEM, outs=None, grant=32):
     specs = [pl.BlockSpec(memory_space=pltpu.SMEM)] * len(scalars)
-    specs += [pl.BlockSpec(memory_space=pltpu.VMEM)] * len(operands)
+    specs += [pl.BlockSpec(memory_space=place)] * len(operands)
+    outs = outs or [pltpu.VMEM] * len(shapes)
     moved = sum(array.size * array.dtype.itemsize for array in operands)
     return pl.pallas_call(
         kernel,
         out_shape=[jax.ShapeDtypeStruct(shape, dtype) for shape, dtype in shapes],
         in_specs=specs,
-        out_specs=[pl.BlockSpec(memory_space=pltpu.VMEM)] * len(shapes),
+        out_specs=[pl.BlockSpec(memory_space=out) for out in outs],
         scratch_shapes=list(scratch),
-        compiler_params=pltpu.CompilerParams(vmem_limit_bytes=limit * 2**20),
+        compiler_params=pltpu.CompilerParams(vmem_limit_bytes=grant * 2**20),
         cost_estimate=pl.CostEstimate(flops=flops, bytes_accessed=moved, transcendentals=0),
     )(*scalars, *operands)
 
@@ -345,64 +425,88 @@
     dyz_table = jnp.asarray(along_yz.astype(np.float32)).astype(bf16)
     pick = jnp.asarray(face_table().astype(np.float32)).astype(bf16)
     spread = jnp.asarray(spread_table().astype(np.float32)).astype(bf16)
-    top, rest = basis_tables()
+    basis = jnp.asarray(np.concatenate(basis_tables(), axis=0))
     boxes = jnp.asarray(box_table(morton_count))
     vel = jnp.transpose(velocity, (1, 0, 2))
     nbrs = jnp.transpose(neighbors, (1, 0))
 
     width = 3 * FACES
-    faces, low, high = call(
+    faces, even, odd = call(
         pack_kernel,
         [((leaf_count, width), bf16), ((BAND, width), bf16), ((BAND, width), bf16)],
         4 * 10**8,
         [counts],
         [vel, pick],
-        limit=60,
-    )
-    ahead = [(at, at + 1) for at in range(morton_count - 1)]
-    back = [(target, source) for source, target in ahead]
+        [
+            pltpu.VMEM(vel.shape, bf16),
+            pltpu.VMEM(pick.shape, bf16),
+            pltpu.VMEM((leaf_count, width), bf16),
+            pltpu.VMEM((2, BAND, width), bf16),
+            pltpu.SemaphoreType.DMA((7,)),
+        ],
+        place=pltpu.HBM,
+        outs=[pltpu.HBM] * 3,
+        grant=60,
+    )
     sib_count = lax.axis_size("sib")
-    part, continuity, spots, geom = call(
+    shift, powers = move_tables(morton_count)
+    part, continuity, spots, geom, move = call(
         pre_kernel,
         [
             ((3, leaf_count, NODES), f32),
             ((leaf_count, NODES), f32),
             ((leaf_count, LANES), f32),
             ((8, leaf_count), f32),
+            ((256, 256), f32),
         ],
         2 * 10**9,
         [counts],
         [
             vel, pressure, viscosity, levels.reshape(1, -1), morton_keys.reshape(1, -1), nbrs,
-            dx_table, dyz_table, boxes,
+            dx_table, dyz_table, boxes, jnp.asarray(shift), jnp.asarray(powers),
         ],
     )
     window = [faces]
-    bands = [jnp.concatenate([lax.ppermute(high, "morton", ahead), lax.ppermute(low, "morton", back)], axis=0)]
-    bands[0], part = lax.optimization_barrier((bands[0], part))
+    bands = [jnp.concatenate([pairs(even, 0), pairs(odd, 1)], axis=0)]
     for bit in reversed(range(sib_count.bit_length() - 1)):
         window += [swap(piece, "sib", 1 << bit) for piece in window]
         held = jnp.concatenate(bands, axis=0)
+        if bit == 0:
+            held, part = lax.optimization_barrier((held, part))
         bands = [held, swap(held, "sib", 1 << bit)]
 
     force, sums = call(
         post_kernel,
-        [((3, leaf_count, NODES), f32), ((morton_count * sib_count, 8, 256), f32)],
+        [((3, leaf_count, NODES), f32), ((8, 2 * LANES), f32)],
         10**9,
         [],
         [
-            part, viscosity, spots, geom, boxes, spread, jnp.asarray(top), jnp.asarray(rest),
+            part, viscosity, spots, geom, boxes, spread, basis,
             jnp.asarray(compact_table()), *window, *bands,
         ],
-        [pltpu.VMEM((ROWS, 3 * leaf_count), f32)],
-    )
-    every = lax.all_to_all(sums, ("morton", "sib"), 0, 0, tiled=True)
+        [
+            pltpu.VMEM((3, leaf_count, NODES), f32),
+            pltpu.VMEM((ROWS, 3 * leaf_count), f32),
+            pltpu.SemaphoreType.DMA((3,)),
+        ],
+        outs=[pltpu.HBM, pltpu.VMEM],
+    )
+    total = morton_count * sib_count
+    (shared,) = call(
+        share_kernel,
+        [((total // 2, 8, LANES), f32)],
+        10**5,
+        [],
+        [sums, swap(sums, "sib", 1)],
+    )
+    halves = [list(range(side, total, 2)) for side in range(2)]
+    every = lax.all_to_all(shared, ("morton", "sib"), 0, 0, axis_index_groups=halves, tiled=True)
     box, root = call(
         final_kernel,
         [((3, 1, MOMENTS), f32), ((3, 1, MOMENTS), f32)],
         10**5,
         [],
-        [every],
+        [every, move],
     )
     return (
         jnp.transpose(force, (1, 0, 2)),

time: 43.6 us -> 44 us (level)
  waiting for transfers between devices: 7.24 us -> 6.27 us
  local copies, waits for them, and re-layouts: 1.64 us -> 2.57 us
  Pallas kernels: 9.08 us -> 9.85 us
  starting transfers between devices: 8.91 us -> 8.18 us
    ppermute x2, starting transfers between devices: 4.81 us -> 3.66 us  [pairs(): return lax.ppermute(block, 'morton', route)]
    unnamed x31 -> x32, local copies, waits for them, and re-layouts: 1.62 us -> 2.57 us
    ppermute x2, waiting for transfers between devices: 1.13 us -> 0.21 us  [pairs(): return lax.ppermute(block, 'morton', route)]
    pallas_call x4 -> x5, Pallas kernels: 9.08 us -> 9.85 us  [call(): pl.pallas_call(kernel, out_shape=[jax.ShapeDtypeStruct(shape, dtype) for...]
    ppermute x5 -> x6, starting transfers between devices: 4.1 us -> 4.52 us  [swap(): lax.ppermute(block, axis, [(at, at ^ apart) for at in range(lax.axis_size...]
    ppermute x5 -> x6, waiting for transfers between devices: 6.11 us -> 6.06 us  [swap(): lax.ppermute(block, axis, [(at, at ^ apart) for at in range(lax.axis_size...]
  transfers between devices with their start and end apart: 7 -> 8, of which waited for: 4 -> 5; matrix products, arithmetic and copies ran while one was open for 0% -> 0% of each run, Pallas kernels for 5% -> 6%
where the time goes in v2:
time: 44 us; the launch traced here: 43.7 us
  blocking collectives  16 us (36%)
  Pallas kernels  9.85 us (22%)
  starting transfers between devices  8.18 us (19%)
  waiting for transfers between devices  6.27 us (14%)
  local copies, waits for them, and re-layouts  2.57 us (6%)
  between operations  0.82 us (2%)
    all_to_all x1, blocking collectives, on_device(): lax.all_to_all(shared, ('morton', 'sib'), 0, 0, axis_index_groups=halves,...  16 us
    pallas_call x5, Pallas kernels, call(): pl.pallas_call(kernel, out_shape=[jax.ShapeDtypeStruct(shape, dtype) for...  9.85 us
    ppermute x6, waiting for transfers between devices, swap(): lax.ppermute(block, axis, [(at, at ^ apart) for at in range(lax.axis_size...  6.06 us
    ppermute x6, starting transfers between devices, swap(): lax.ppermute(block, axis, [(at, at ^ apart) for at in range(lax.axis_size...  4.52 us
    ppermute x2, starting transfers between devices, pairs(): return lax.ppermute(block, 'morton', route)  3.66 us
    unnamed x32, local copies, waits for them, and re-layouts  2.57 us
  transfers between devices with their start and end apart: 8, of which 5 were waited for; matrix products, arithmetic and copies ran while one was open for 0% of the time, Pallas kernels for 6%

profile of v2, /device:TPU:0, one launch (start us, length us, event | category | flops | bytes accessed | tf_op | source)
XLA Modules:
  0.0 43.7 jit_solution(11034328292630640244)
XLA Ops:
  0.6 0.0 copy-start.6
  0.6 0.0 copy-start.7
  0.7 0.0 copy-start.12
  0.7 0.0 copy-start.13
  0.7 3.3 %shard_map.183 = (bf16[128,1152]{1,0:T(8,128)(2,1)}, bf16[32,1152]{1,0:T(8,128)(2,1)}, bf16[32,1152]{1,0:T(8,128)(2,1)}) custom-call(s32[32]{0:T(128)} %counts_ref.3, bf16[3,128,512]{2,1,0:T(8,128)(2,1)} %bitcast.7, bf16[512,384]{1,0:T(8,128)(2,1)} %constant.27.pick_hbm), custom_call_target="tpu_custom_call" | custom-call | flops 400000000 | bytes 786432 | tf_op jit(solution)/shard_map/pallas_call | solution.py:409
  4.0 0.0 copy-start.4
  4.0 3.0 %collective-permute-start = (bf16[32,1152]{1,0:T(8,128)(2,1)}, bf16[32,1152]{1,0:T(8,128)(2,1)S(1)}, u32[]{:S(2)}, u32[]{:S(2)}) collective-permute-start(bf16[32,1152]{1,0:T(8,128)(2,1)} %get-tuple-element.18), channel_id=1, source_target_pairs={{0,4},{4,0},{8,12},{12,8},{16,20},{20,16},{24,28},{28,24},{1,5},{5... | collective-permute-start | bytes 221192 | tf_op jit(solution)/shard_map/ppermute | solution.py:139
  7.0 0.7 %collective-permute-start.1 = (bf16[32,1152]{1,0:T(8,128)(2,1)}, bf16[32,1152]{1,0:T(8,128)(2,1)S(1)}, u32[]{:S(2)}, u32[]{:S(2)}) collective-permute-start(bf16[32,1152]{1,0:T(8,128)(2,1)} %get-tuple-element.19), channel_id=1, source_target_pairs={{4,8},{8,4},{12,16},{16,12},{20,24},{24,20},{5,9},{9,5},{13,17},{1... | collective-permute-start | bytes 221192 | tf_op jit(solution)/shard_map/ppermute | solution.py:139
  7.6 0.0 copy-start.5
  7.6 0.1 collective-permute-start.4
  7.7 1.6 %collective-permute-start.3 = (bf16[128,1152]{1,0:T(8,128)(2,1)}, bf16[128,1152]{1,0:T(8,128)(2,1)S(1)}, u32[]{:S(2)}, u32[]{:S(2)}) collective-permute-start(bf16[128,1152]{1,0:T(8,128)(2,1)} %get-tuple-element.24.refs_0_), channel_id=1, source_target_pairs={{0,2},{1,3},{2,0},{3,1},{4,6},{5,7},{6,4},{7,5},{8,10},{9,11},{10,... | collective-permute-start | bytes 884744 | tf_op jit(solution)/shard_map/ppermute | solution.py:118
  9.3 0.2 collective-permute-done
  9.5 0.0 collective-permute-done.1
  9.5 0.0 copy-start.8
  9.5 2.1 %collective-permute-start.2 = (bf16[64,1152]{1,0:T(8,128)(2,1)S(1)}, bf16[64,1152]{1,0:T(8,128)(2,1)S(1)}, u32[]{:S(2)}, u32[]{:S(2)}) collective-permute-start(bf16[64,1152]{1,0:T(8,128)(2,1)S(1)} %pad_maximum_fusion.1), channel_id=1, source_target_pairs={{0,2},{1,3},{2,0},{3,1},{4,6},{5,7},{6,4},{7,5},{8,10},{9,11},{10,... | collective-permute-start | bytes 442376 | tf_op jit(solution)/shard_map/ppermute | solution.py:118
  11.7 0.0 copy-start.9
  11.7 0.0 copy-start.10
  11.7 0.0 copy-done.6
  11.7 0.0 copy-done.7
  11.7 0.0 copy-done.12
  11.7 0.0 copy-done.13
  11.7 0.0 copy-done.4
  11.7 0.0 copy-done.5
  11.7 0.0 copy-done.8
  11.7 0.6 %copy-done.9 = s32[32]{0:T(128)S(1)} copy-done((s32[32]{0:T(128)S(1)}, s32[32]{0:T(128)}, u32[]{:S(2)}) %copy-start.9) | copy-done | bytes 152
  12.3 0.0 copy-done.10
  12.3 0.0 copy-done.11
  12.3 0.0 copy-start.14
  12.3 0.9 %copy-done.14 = s32[256,256]{1,0:T(8,128)S(1)} copy-done((s32[256,256]{1,0:T(8,128)S(1)}, s32[256,256]{1,0:T(8,128)}, u32[]{:S(2)}) %copy-start.14) | copy-done | bytes 262168
  13.3 0.0 copy-start.15
  13.3 0.9 %copy-done.15 = f32[256,256]{1,0:T(8,128)S(1)} copy-done((f32[256,256]{1,0:T(8,128)S(1)}, f32[256,256]{1,0:T(8,128)}, u32[]{:S(2)}) %copy-start.15) | copy-done | bytes 262168
  14.3 2.7 %shard_map.184 = (f32[3,128,512]{2,1,0:T(8,128)S(1)}, f32[128,512]{1,0:T(8,128)}, f32[128,128]{1,0:T(8,128)S(1)}, f32[8,128]{1,0:T(8,128)S(1)}, f32[256,256]{1,0:T(8,128)S(1)}) custom-call(s32[32]{0:T(128)S(1)} %copy-done.9, bf16[3,128,512]{2,1,0:T(8,128)(2,1)S(1)} %bitcast.8, bf16[128,512]{1,0:T(8,128)(2,1)S(1)} %copy-done.7, f32[128,512]{1,0:T(8,128)S(1)} %copy-done.4, ...), custom_call_target="tpu_custom_call" | custom-call | flops 2000000000 | bytes 2134016 | tf_op jit(solution)/shard_map/pallas_call | solution.py:409
  17.0 3.5 %collective-permute-done.2 = bf16[64,1152]{1,0:T(8,128)(2,1)S(1)} collective-permute-done((bf16[64,1152]{1,0:T(8,128)(2,1)S(1)}, bf16[64,1152]{1,0:T(8,128)(2,1)S(1)}, u32[]{:S(2)}, u32[]{:S(2)}) %collective-permute-start.2) | collective-permute-done | bytes 147488 | tf_op jit(solution)/shard_map/ppermute | solution.py:118
  20.5 0.1 collective-permute-start.6
  20.6 0.0 collective-permute-done.3.refs_1_
  20.6 0.5 %collective-permute-start.5 = (bf16[128,1152]{1,0:T(8,128)(2,1)S(1)}, bf16[128,1152]{1,0:T(8,128)(2,1)S(1)}, u32[]{:S(2)}, u32[]{:S(2)}) collective-permute-start(bf16[128,1152]{1,0:T(8,128)(2,1)S(1)} %collective-permute-done.3.refs_1_), channel_id=1, source_target_pairs={{0,1},{1,0},{2,3},{3,2},{4,5},{5,4},{6,7},{7,6},{8,9},{9,8},{10,11... | collective-permute-start | bytes 884744 | tf_op jit(solution)/shard_map/ppermute | solution.py:118
  21.1 0.0 collective-permute-done.4.refs_2_
  21.1 1.1 %collective-permute-done.6.refs_5_ = bf16[128,1152]{1,0:T(8,128)(2,1)S(1)} collective-permute-done((bf16[128,1152]{1,0:T(8,128)(2,1)S(1)}, bf16[128,1152]{1,0:T(8,128)(2,1)S(1)}, u32[]{:S(2)}, u32[]{:S(2)}) %collective-permute-start.6) | collective-permute-done | bytes 294944 | tf_op jit(solution)/shard_map/ppermute | solution.py:118
  22.2 0.4 collective-permute-done.5.refs_3_
  22.6 0.0 copy-done.1
  22.6 0.0 copy-done.2
  22.6 0.0 copy-done.3
  22.6 0.0 copy-done
  22.6 3.0 %shard_map.185 = (f32[3,128,512]{2,1,0:T(8,128)}, f32[8,256]{1,0:T(8,128)S(1)}) custom-call(f32[3,128,512]{2,1,0:T(8,128)S(1)} %get-tuple-element.21.part_ref, f32[128,512]{1,0:T(8,128)S(1)} %copy-done.4, f32[128,128]{1,0:T(8,128)S(1)} %get-tuple-element.22.spots_ref, f32[8,128]{1,0:T(8,128)S(1)} %get-tuple-element.23.geom_ref, f32[64,128]{1,0:T(8,128)S(1)} %copy-done.5, ...), custom_call_target="tpu_custom_call" | custom-call | flops 1000000000 | bytes 4198400 | tf_op jit(solution)/shard_map/pallas_call | solution.py:409
  25.7 0.2 collective-permute-start.7
  25.9 1.0 %collective-permute-done.7.other_ref = f32[8,256]{1,0:T(8,128)S(1)} collective-permute-done((f32[8,256]{1,0:T(8,128)S(1)}, f32[8,256]{1,0:T(8,128)S(1)}, u32[]{:S(2)}, u32[]{:S(2)}) %collective-permute-start.7) | collective-permute-done | bytes 8224 | tf_op jit(solution)/shard_map/ppermute | solution.py:118
  26.9 16.0 %all_to_all.5.sums_ref = f32[16,8,128]{2,1,0:T(8,128)S(1)} all-to-all(f32[16,8,128]{2,1,0:T(8,128)S(1)} %shard_map.186), channel_id=1, replica_groups={{0,2,4,6,8,10,12,14,16,18,20,22,24,26,28,30},{1,3,5,7,9,11,13,15,17,19,..., dimensions={0} | all-to-all | bytes 131072 | tf_op jit(solution)/shard_map/all_to_all | solution.py:503
  42.9 0.8 %shard_map.187 = (f32[3,1,216]{2,1,0:T(1,128)}, f32[3,1,216]{2,1,0:T(1,128)}) custom-call(f32[16,8,128]{2,1,0:T(8,128)S(1)} %all_to_all.5.sums_ref, f32[256,256]{1,0:T(8,128)S(1)} %get-tuple-element.29.move_ref), custom_call_target="tpu_custom_call" | custom-call | flops 100000 | bytes 327680 | tf_op jit(solution)/shard_map/pallas_call | solution.py:409
  (8 shorter events, 0.1 us)
Async XLA Ops:
  0.6 11.0 %copy-start.6 = (bf16[128,3,512]{2,0,1:T(8,128)(2,1)S(1)}, bf16[128,3,512]{2,0,1:T(8,128)(2,1)}, u32[]{:S(2)}) copy-start(bf16[128,3,512]{2,0,1:T(8,128)(2,1)} %param.16) | copy-start | bytes 1179652
  0.6 11.0 %copy-start.7 = (bf16[128,512]{1,0:T(8,128)(2,1)S(1)}, bf16[128,512]{1,0:T(8,128)(2,1)}, u32[]{:S(2)}) copy-start(bf16[128,512]{1,0:T(8,128)(2,1)} %press_ref.1) | copy-start | bytes 393220
  0.7 11.0 %copy-start.12 = (bf16[512,512]{1,0:T(8,128)(2,1)S(1)}, bf16[512,512]{1,0:T(8,128)(2,1)}, u32[]{:S(2)}) copy-start(bf16[512,512]{1,0:T(8,128)(2,1)} %constant.28.dx_ref) | copy-start | bytes 1572868
  0.7 11.0 %copy-start.13 = (bf16[256,512]{1,0:T(8,128)(2,1)S(1)}, bf16[256,512]{1,0:T(8,128)(2,1)}, u32[]{:S(2)}) copy-start(bf16[256,512]{1,0:T(8,128)(2,1)} %constant.29.dyz_ref) | copy-start | bytes 786436
  4.0 7.8 %copy-start.4 = (f32[128,512]{1,0:T(8,128)S(1)}, f32[128,512]{1,0:T(8,128)}, u32[]{:S(2)}) copy-start(f32[128,512]{1,0:T(8,128)} %visc_ref.3) | copy-start | bytes 786436
  4.0 5.5 %collective-permute-start = (bf16[32,1152]{1,0:T(8,128)(2,1)}, bf16[32,1152]{1,0:T(8,128)(2,1)S(1)}, u32[]{:S(2)}, u32[]{:S(2)}) collective-permute-start(bf16[32,1152]{1,0:T(8,128)(2,1)} %get-tuple-element.18), channel_id=1, source_target_pairs={{0,4},{4,0},{8,12},{12,8},{16,20},{20,16},{24,28},{28,24},{1,5},{5... | collective-permute-start | bytes 221192 | tf_op jit(solution)/shard_map/ppermute | solution.py:139
  7.0 2.5 %collective-permute-start.1 = (bf16[32,1152]{1,0:T(8,128)(2,1)}, bf16[32,1152]{1,0:T(8,128)(2,1)S(1)}, u32[]{:S(2)}, u32[]{:S(2)}) collective-permute-start(bf16[32,1152]{1,0:T(8,128)(2,1)} %get-tuple-element.19), channel_id=1, source_target_pairs={{4,8},{8,4},{12,16},{16,12},{20,24},{24,20},{5,9},{9,5},{13,17},{1... | collective-permute-start | bytes 221192 | tf_op jit(solution)/shard_map/ppermute | solution.py:139
  7.6 4.1 %copy-start.5 = (f32[64,128]{1,0:T(8,128)S(1)}, f32[64,128]{1,0:T(8,128)}, u32[]{:S(2)}) copy-start(f32[64,128]{1,0:T(8,128)} %constant.23.clone.box_ref) | copy-start | bytes 98308
  7.6 13.5 %collective-permute-start.4 = (bf16[128,1152]{1,0:T(8,128)(2,1)}, bf16[128,1152]{1,0:T(8,128)(2,1)S(1)}, u32[]{:S(2)}, u32[]{:S(2)}) collective-permute-start(bf16[128,1152]{1,0:T(8,128)(2,1)} %get-tuple-element.24.refs_0_), channel_id=1, source_target_pairs={{0,1},{1,0},{2,3},{3,2},{4,5},{5,4},{6,7},{7,6},{8,9},{9,8},{10,11... | collective-permute-start | bytes 884744 | tf_op jit(solution)/shard_map/ppermute | solution.py:118
  7.7 12.9 %collective-permute-start.3 = (bf16[128,1152]{1,0:T(8,128)(2,1)}, bf16[128,1152]{1,0:T(8,128)(2,1)S(1)}, u32[]{:S(2)}, u32[]{:S(2)}) collective-permute-start(bf16[128,1152]{1,0:T(8,128)(2,1)} %get-tuple-element.24.refs_0_), channel_id=1, source_target_pairs={{0,2},{1,3},{2,0},{3,1},{4,6},{5,7},{6,4},{7,5},{8,10},{9,11},{10,... | collective-permute-start | bytes 884744 | tf_op jit(solution)/shard_map/ppermute | solution.py:118
  9.5 2.2 %copy-start.8 = (s32[128,6]{0,1:T(8,128)S(1)}, s32[128,6]{0,1:T(8,128)}, u32[]{:S(2)}) copy-start(s32[128,6]{0,1:T(8,128)} %param.22) | copy-start | bytes 9220
  9.5 11.0 %collective-permute-start.2 = (bf16[64,1152]{1,0:T(8,128)(2,1)S(1)}, bf16[64,1152]{1,0:T(8,128)(2,1)S(1)}, u32[]{:S(2)}, u32[]{:S(2)}) collective-permute-start(bf16[64,1152]{1,0:T(8,128)(2,1)S(1)} %pad_maximum_fusion.1), channel_id=1, source_target_pairs={{0,2},{1,3},{2,0},{3,1},{4,6},{5,7},{6,4},{7,5},{8,10},{9,11},{10,... | collective-permute-start | bytes 442376 | tf_op jit(solution)/shard_map/ppermute | solution.py:118
  11.7 0.7 %copy-start.9 = (s32[32]{0:T(128)S(1)}, s32[32]{0:T(128)}, u32[]{:S(2)}) copy-start(s32[32]{0:T(128)} %counts_ref.3) | copy-start | bytes 388
  11.7 0.7 %copy-start.10 = (s32[128]{0:T(128)S(1)}, s32[128]{0:T(128)}, u32[]{:S(2)}) copy-start(s32[128]{0:T(128)} %param.19) | copy-start | bytes 1540
  11.7 0.7 %copy-start.11 = (s32[128]{0:T(128)S(1)}, s32[128]{0:T(128)}, u32[]{:S(2)}) copy-start(s32[128]{0:T(128)} %param.20) | copy-start | bytes 1540
  12.3 0.9 %copy-start.14 = (s32[256,256]{1,0:T(8,128)S(1)}, s32[256,256]{1,0:T(8,128)}, u32[]{:S(2)}) copy-start(s32[256,256]{1,0:T(8,128)} %constant.25.clone.powers_ref) | copy-start | bytes 786436
  13.3 0.9 %copy-start.15 = (f32[256,256]{1,0:T(8,128)S(1)}, f32[256,256]{1,0:T(8,128)}, u32[]{:S(2)}) copy-start(f32[256,256]{1,0:T(8,128)} %constant.24.clone.shift_ref) | copy-start | bytes 786436
  14.2 8.4 %copy-start.1 = (bf16[384,512]{1,0:T(8,128)(2,1)S(1)}, bf16[384,512]{1,0:T(8,128)(2,1)}, u32[]{:S(2)}) copy-start(bf16[384,512]{1,0:T(8,128)(2,1)} %constant.30.spread_ref) | copy-start | bytes 1179652
  14.2 8.4 %copy-start.2 = (f32[288,256]{1,0:T(8,128)S(1)}, f32[288,256]{1,0:T(8,128)}, u32[]{:S(2)}) copy-start(f32[288,256]{1,0:T(8,128)} %constant.26.clone.compact_ref) | copy-start | bytes 884740
  14.2 8.4 %copy-start.3 = (bf16[128,1152]{1,0:T(8,128)(2,1)S(1)}, bf16[128,1152]{1,0:T(8,128)(2,1)}, u32[]{:S(2)}) copy-start(bf16[128,1152]{1,0:T(8,128)(2,1)} %get-tuple-element.24.refs_0_) | copy-start | bytes 884740
  17.0 5.6 %copy-start = (bf16[576,512]{1,0:T(8,128)(2,1)S(1)}, bf16[576,512]{1,0:T(8,128)(2,1)}, u32[]{:S(2)}) copy-start(bf16[576,512]{1,0:T(8,128)(2,1)} %constant.22.clone.basis_ref) | copy-start | bytes 1769476
  20.5 1.6 %collective-permute-start.6 = (bf16[128,1152]{1,0:T(8,128)(2,1)S(1)}, bf16[128,1152]{1,0:T(8,128)(2,1)S(1)}, u32[]{:S(2)}, u32[]{:S(2)}) collective-permute-start(bf16[128,1152]{1,0:T(8,128)(2,1)S(1)} %pad_maximum_fusion.refs_4_), channel_id=1, source_target_pairs={{0,1},{1,0},{2,3},{3,2},{4,5},{5,4},{6,7},{7,6},{8,9},{9,8},{10,11... | collective-permute-start | bytes 884744 | tf_op jit(solution)/shard_map/ppermute | solution.py:118
  20.6 2.0 %collective-permute-start.5 = (bf16[128,1152]{1,0:T(8,128)(2,1)S(1)}, bf16[128,1152]{1,0:T(8,128)(2,1)S(1)}, u32[]{:S(2)}, u32[]{:S(2)}) collective-permute-start(bf16[128,1152]{1,0:T(8,128)(2,1)S(1)} %collective-permute-done.3.refs_1_), channel_id=1, source_target_pairs={{0,1},{1,0},{2,3},{3,2},{4,5},{5,4},{6,7},{7,6},{8,9},{9,8},{10,11... | collective-permute-start | bytes 884744 | tf_op jit(solution)/shard_map/ppermute | solution.py:118
  25.7 1.2 %collective-permute-start.7 = (f32[8,256]{1,0:T(8,128)S(1)}, f32[8,256]{1,0:T(8,128)S(1)}, u32[]{:S(2)}, u32[]{:S(2)}) collective-permute-start(f32[8,256]{1,0:T(8,128)S(1)} %get-tuple-element.28.own_ref), channel_id=1, source_target_pairs={{0,1},{1,0},{2,3},{3,2},{4,5},{5,4},{6,7},{7,6},{8,9},{9,8},{10,11... | collective-permute-start | bytes 24584 | tf_op jit(solution)/shard_map/ppermute | solution.py:118

commit v3 on v2

--- a/solution.py
+++ b/solution.py
@@ -1,5 +1,3 @@
-import math
-
 import jax
 import jax.numpy as jnp
 import numpy as np
@@ -118,18 +116,9 @@
     return lax.ppermute(block, axis, [(at, at ^ apart) for at in range(lax.axis_size(axis))])
 
 
-def move_tables(morton_count):
-    bits = 3 * LMAX - (morton_count.bit_length() - 1)
-    ratio = 2.0 ** max(max(0, min(LMAX, (bits - offset + 2) // 3)) for offset in range(3)) / 2.0**LMAX
-    shift = np.zeros((256, 256), np.float32)
-    powers = np.zeros((256, 256), np.int32)
-    triples = list(np.ndindex(6, 6, 6))
-    for row, beta in enumerate(triples):
-        for col, alpha in enumerate(triples):
-            if all(b <= a for a, b in zip(alpha, beta)):
-                shift[row, col] = math.prod(math.comb(a, b) for a, b in zip(alpha, beta)) * ratio ** sum(beta)
-                powers[row, col] = sum((a - b) << 3 * dim for dim, (a, b) in enumerate(zip(alpha, beta)))
-    return shift, powers
+def exchange(block, mask):
+    total = lax.axis_size("morton") * lax.axis_size("sib")
+    return lax.ppermute(block, ("morton", "sib"), [(at, at ^ mask) for at in range(total)])
 
 
 def pairs(block, first):
@@ -149,54 +138,31 @@
     )
 
 
-def pack_kernel(
-    counts_ref, vel_hbm, pick_hbm, faces_hbm, even_hbm, odd_hbm, vel_ref, pick_ref, faces_ref, bands_ref, sems
-):
+def pack_kernel(counts_ref, vel_ref, pick_ref, faces_ref, even_ref, odd_ref):
     sib_count = lax.axis_size("sib")
     morton = lax.axis_index("morton")
     own = morton * sib_count + lax.axis_index("sib")
-    loads = [
-        pltpu.make_async_copy(vel_hbm, vel_ref, sems.at[0]),
-        pltpu.make_async_copy(pick_hbm, pick_ref, sems.at[1]),
-    ]
-    for load in loads:
-        load.start()
+    leaf_count = faces_ref.shape[0]
+    picked = dot(vel_ref[...].reshape(3 * leaf_count, NODES), pick_ref[...]).astype(bf16)
+    for comp in range(3):
+        for dim in range(3):
+            lane = (dim * 3 + comp) * LANES
+            rows = picked[comp * leaf_count : (comp + 1) * leaf_count]
+            faces_ref[:, lane : lane + LANES] = rows[:, dim * LANES : (dim + 1) * LANES]
     first = counts_ref[own] - BAND
-    leaf_count = faces_ref.shape[0]
     row = lax.broadcasted_iota(jnp.int32, (BAND, leaf_count), 0)
     col = lax.broadcasted_iota(jnp.int32, (BAND, leaf_count), 1)
     last_rows = jnp.where(col == row + first, 1.0, 0.0).astype(bf16)
+    high = dot(last_rows, faces_ref[...]).astype(bf16)
+    low = faces_ref[:BAND, :]
     is_odd = jnp.bitwise_and(morton, 1) == 1
-    loads[0].wait()
-    fields = [vel_ref[comp] for comp in range(3)]
-    fields += [dot(last_rows, vel_ref[comp]).astype(bf16) for comp in range(3)]
-    fields = jnp.concatenate(fields, axis=0)
-    loads[1].wait()
-    stores = []
-    for dim in range(3):
-        picked = dot(fields, pick_ref[:, dim * LANES : (dim + 1) * LANES]).astype(bf16)
-        for comp in range(3):
-            lane = (dim * 3 + comp) * LANES
-            faces_ref[:, lane : lane + LANES] = picked[comp * leaf_count : (comp + 1) * leaf_count]
-            at = 3 * leaf_count + comp * BAND
-            low = picked[comp * leaf_count : comp * leaf_count + BAND]
-            high = picked[at : at + BAND]
-            bands_ref[0, :, lane : lane + LANES] = jnp.where(is_odd, low, high)
-            bands_ref[1, :, lane : lane + LANES] = jnp.where(is_odd, high, low)
-        lanes = pl.ds(dim * FACES, FACES)
-        stores.append(pltpu.make_async_copy(faces_ref.at[:, lanes], faces_hbm.at[:, lanes], sems.at[2 + dim]))
-        stores[-1].start()
-    stores.append(pltpu.make_async_copy(bands_ref.at[0], even_hbm, sems.at[5]))
-    stores.append(pltpu.make_async_copy(bands_ref.at[1], odd_hbm, sems.at[6]))
-    for store in stores[3:]:
-        store.start()
-    for store in stores:
-        store.wait()
+    even_ref[...] = jnp.where(is_odd, low, high)
+    odd_ref[...] = jnp.where(is_odd, high, low)
 
 
 def pre_kernel(
     counts_ref, vel_ref, press_ref, visc_ref, levels_ref, keys_ref, nbrs_ref, dx_ref, dyz_ref, box_ref,
-    shift_ref, powers_ref, part_ref, mass_ref, spots_ref, geom_ref, move_ref,
+    part_ref, mass_ref, spots_ref, geom_ref,
 ):
     sib_count = lax.axis_size("sib")
     morton_count = lax.axis_size("morton")
@@ -281,16 +247,6 @@
     places.append(0.5 * span * finest * box[7:8, :])
     places.append(jnp.zeros((4, leaf_count), f32))
     geom_ref[...] = jnp.concatenate(places, axis=0)
-    move = shift_ref[...]
-    powers = powers_ref[...]
-    for dim in range(3):
-        power = jnp.bitwise_and(jnp.right_shift(powers, 3 * dim), 7)
-        along = box[dim : dim + 1, 3:4]
-        factor = jnp.ones((1, 1), f32)
-        for degree in range(1, DEG + 1):
-            factor = factor * along
-            move = move * jnp.where(power == degree, factor, 1.0)
-    move_ref[...] = move
 
 
 def shifted(tiles, geom):
@@ -372,32 +328,13 @@
         store.wait()
 
 
-def share_kernel(own_ref, other_ref, sums_ref):
-    sums = own_ref[...] + other_ref[...]
-    blank = jnp.zeros((2, LANES), f32)
-    to_box = jnp.concatenate([sums[:3, :LANES], sums[:3, LANES:], blank], axis=0)
-    to_root = jnp.concatenate([sums[3:6, :LANES], sums[3:6, LANES:], blank], axis=0)
-    morton = lax.axis_index("morton")
-    in_box = lax.axis_size("sib") // 2
-    for other in range(sums_ref.shape[0]):
-        sums_ref[other] = jnp.where(morton == other // in_box, to_box, to_root)
-
-
-def final_kernel(sums_ref, move_ref, box_ref, root_ref):
-    in_box = lax.axis_size("sib") // 2
-    morton = lax.axis_index("morton")
-    box = jnp.zeros(sums_ref.shape[1:], f32)
-    root = jnp.zeros(sums_ref.shape[1:], f32)
-    for group in range(sums_ref.shape[0] // in_box):
-        total = jnp.sum(sums_ref[group * in_box : (group + 1) * in_box], axis=0)
-        box = box + jnp.where(morton == group, total, 0.0)
-        root = root + jnp.where(morton == group, 0.0, total)
-    box = jnp.concatenate([box[:3], box[3:6]], axis=1)
-    root = jnp.concatenate([root[:3], root[3:6]], axis=1)
-    box8 = jnp.concatenate([box, jnp.zeros((5, 2 * LANES), f32)], axis=0)
-    root = root + jnp.dot(box8, move_ref[...], precision=highest, preferred_element_type=f32)[:3]
+def final_kernel(sums_ref, *refs):
+    others, (box_ref, root_ref) = refs[:-2], refs[-2:]
+    root = sums_ref[3:6, :] + others[0][3:6, :]
+    if len(others) > 1:
+        root = root + (others[1][3:6, :] + others[2][3:6, :])
     for comp in range(3):
-        box_ref[comp] = box[comp : comp + 1, :MOMENTS]
+        box_ref[comp] = sums_ref[comp : comp + 1, :MOMENTS]
         root_ref[comp] = root[comp : comp + 1, :MOMENTS]
 
 
@@ -437,33 +374,22 @@
         4 * 10**8,
         [counts],
         [vel, pick],
-        [
-            pltpu.VMEM(vel.shape, bf16),
-            pltpu.VMEM(pick.shape, bf16),
-            pltpu.VMEM((leaf_count, width), bf16),
-            pltpu.VMEM((2, BAND, width), bf16),
-            pltpu.SemaphoreType.DMA((7,)),
-        ],
-        place=pltpu.HBM,
-        outs=[pltpu.HBM] * 3,
         grant=60,
     )
     sib_count = lax.axis_size("sib")
-    shift, powers = move_tables(morton_count)
-    part, continuity, spots, geom, move = call(
+    part, continuity, spots, geom = call(
         pre_kernel,
         [
             ((3, leaf_count, NODES), f32),
             ((leaf_count, NODES), f32),
             ((leaf_count, LANES), f32),
             ((8, leaf_count), f32),
-            ((256, 256), f32),
         ],
         2 * 10**9,
         [counts],
         [
             vel, pressure, viscosity, levels.reshape(1, -1), morton_keys.reshape(1, -1), nbrs,
-            dx_table, dyz_table, boxes, jnp.asarray(shift), jnp.asarray(powers),
+            dx_table, dyz_table, boxes,
         ],
     )
     window = [faces]
@@ -491,22 +417,23 @@
         ],
         outs=[pltpu.HBM, pltpu.VMEM],
     )
-    total = morton_count * sib_count
-    (shared,) = call(
-        share_kernel,
-        [((total // 2, 8, LANES), f32)],
-        10**5,
-        [],
-        [sums, swap(sums, "sib", 1)],
-    )
-    halves = [list(range(side, total, 2)) for side in range(2)]
-    every = lax.all_to_all(shared, ("morton", "sib"), 0, 0, axis_index_groups=halves, tiled=True)
+    bits = (morton_count * sib_count).bit_length() - 1
+    rounds = [[1]]
+    for bit in range(1, bits, 2):
+        rounds.append([part << bit for part in ((1, 2, 3) if bit + 1 < bits else (1,))])
+    is_box = jnp.arange(8)[:, None] < 3
+    for masks in rounds[:-1]:
+        got = [exchange(sums, mask) for mask in masks]
+        pair = sums + got[0]
+        every = pair + (got[1] + got[2]) if len(got) > 1 else pair
+        inside = [sums, pair, every][sum(mask < sib_count for mask in masks[:2])]
+        sums = jnp.where(is_box, inside, every)
     box, root = call(
         final_kernel,
         [((3, 1, MOMENTS), f32), ((3, 1, MOMENTS), f32)],
         10**5,
         [],
-        [every, move],
+        [sums] + [exchange(sums, mask) for mask in rounds[-1]],
     )
     return (
         jnp.transpose(force, (1, 0, 2)),

time: 44 us -> 43.1 us (0.980)
  blocking collectives: 16 us -> 0 us
  starting transfers between devices: 8.18 us -> 18 us
  waiting for transfers between devices: 6.27 us -> 15 us
  local copies, waits for them, and re-layouts: 2.57 us -> 0.67 us
  Pallas kernels: 9.85 us -> 8.36 us
    all_to_all x1 -> x0, blocking collectives: 16 us -> none  [on_device(): lax.all_to_all(shared, ('morton', 'sib'), 0, 0, axis_index_groups=halves,...]
    ppermute x0 -> x7, starting transfers between devices: none -> 10.1 us  [exchange(): lax.ppermute(block, ('morton', 'sib'), [(at, at ^ mask) for at in range(t...]
    ppermute x0 -> x7, waiting for transfers between devices: none -> 8.36 us  [exchange(): lax.ppermute(block, ('morton', 'sib'), [(at, at ^ mask) for at in range(t...]
    unnamed x32 -> x28, local copies, waits for them, and re-layouts: 2.57 us -> 0.67 us
    pallas_call x5 -> x4, Pallas kernels: 9.85 us -> 8.36 us  [call(): pl.pallas_call(kernel, out_shape=[jax.ShapeDtypeStruct(shape, dtype) for...]
    ppermute x6 -> x5, waiting for transfers between devices: 6.06 us -> 6.38 us  [swap(): lax.ppermute(block, axis, [(at, at ^ apart) for at in range(lax.axis_size...]
    ppermute x6 -> x5, starting transfers between devices: 4.52 us -> 4.27 us  [swap(): lax.ppermute(block, axis, [(at, at ^ apart) for at in range(lax.axis_size...]
  transfers between devices with their start and end apart: 8 -> 14, of which waited for: 5 -> 10; matrix products, arithmetic and copies ran while one was open for 0% -> 0% of each run, Pallas kernels for 6% -> 5%
where the time goes in v3:
time: 43.1 us; the launch traced here: 42.9 us
  starting transfers between devices  18 us (42%)
  waiting for transfers between devices  15 us (35%)
  Pallas kernels  8.36 us (19%)
  between operations  0.8 us (2%)
  local copies, waits for them, and re-layouts  0.67 us (2%)
    ppermute x7, starting transfers between devices, exchange(): lax.ppermute(block, ('morton', 'sib'), [(at, at ^ mask) for at in range(t...  10.1 us
    ppermute x7, waiting for transfers between devices, exchange(): lax.ppermute(block, ('morton', 'sib'), [(at, at ^ mask) for at in range(t...  8.36 us
    pallas_call x4, Pallas kernels, call(): pl.pallas_call(kernel, out_shape=[jax.ShapeDtypeStruct(shape, dtype) for...  8.36 us
    ppermute x5, waiting for transfers between devices, swap(): lax.ppermute(block, axis, [(at, at ^ apart) for at in range(lax.axis_size...  6.38 us
    ppermute x5, starting transfers between devices, swap(): lax.ppermute(block, axis, [(at, at ^ apart) for at in range(lax.axis_size...  4.27 us
    ppermute x2, starting transfers between devices, pairs(): return lax.ppermute(block, 'morton', route)  3.59 us
  transfers between devices with their start and end apart: 14, of which 10 were waited for; matrix products, arithmetic and copies ran while one was open for 0% of the time, Pallas kernels for 5%

profile of v3, /device:TPU:0, one launch (start us, length us, event | category | flops | bytes accessed | tf_op | source)
XLA Modules:
  0.0 42.9 jit_solution(3722490426076433619)
XLA Ops:
  0.6 0.0 copy-start.6
  0.6 0.0 copy-start.7
  0.7 0.0 copy-start.12
  0.7 0.0 copy-start.13
  0.7 2.4 %shard_map.165 = (bf16[128,1152]{1,0:T(8,128)(2,1)}, bf16[32,1152]{1,0:T(8,128)(2,1)}, bf16[32,1152]{1,0:T(8,128)(2,1)}) custom-call(s32[32]{0:T(128)} %counts_ref.3, bf16[3,128,512]{2,1,0:T(8,128)(2,1)} %bitcast.7, bf16[512,384]{1,0:T(8,128)(2,1)} %constant.23.pick_ref), custom_call_target="tpu_custom_call" | custom-call | flops 400000000 | bytes 786432 | tf_op jit(solution)/shard_map/pallas_call | solution.py:346
  3.1 2.9 %collective-permute-start = (bf16[32,1152]{1,0:T(8,128)(2,1)}, bf16[32,1152]{1,0:T(8,128)(2,1)S(1)}, u32[]{:S(2)}, u32[]{:S(2)}) collective-permute-start(bf16[32,1152]{1,0:T(8,128)(2,1)} %get-tuple-element.17), channel_id=1, source_target_pairs={{0,4},{4,0},{8,12},{12,8},{16,20},{20,16},{24,28},{28,24},{1,5},{5... | collective-permute-start | bytes 221192 | tf_op jit(solution)/shard_map/ppermute | solution.py:128
  6.0 0.7 %collective-permute-start.1 = (bf16[32,1152]{1,0:T(8,128)(2,1)}, bf16[32,1152]{1,0:T(8,128)(2,1)S(1)}, u32[]{:S(2)}, u32[]{:S(2)}) collective-permute-start(bf16[32,1152]{1,0:T(8,128)(2,1)} %get-tuple-element.18), channel_id=1, source_target_pairs={{4,8},{8,4},{12,16},{16,12},{20,24},{24,20},{5,9},{9,5},{13,17},{1... | collective-permute-start | bytes 221192 | tf_op jit(solution)/shard_map/ppermute | solution.py:128
  6.7 0.0 copy-start.5
  6.7 1.6 %collective-permute-start.3 = (bf16[128,1152]{1,0:T(8,128)(2,1)}, bf16[128,1152]{1,0:T(8,128)(2,1)S(1)}, u32[]{:S(2)}, u32[]{:S(2)}) collective-permute-start(bf16[128,1152]{1,0:T(8,128)(2,1)} %get-tuple-element.23.refs_0_), channel_id=1, source_target_pairs={{0,2},{1,3},{2,0},{3,1},{4,6},{5,7},{6,4},{7,5},{8,10},{9,11},{10,... | collective-permute-start | bytes 884744 | tf_op jit(solution)/shard_map/ppermute | solution.py:116
  8.3 0.0 collective-permute-start.4
  8.3 0.3 collective-permute-done
  8.6 0.0 collective-permute-done.1
  8.6 0.0 copy-start.8
  8.6 2.1 %collective-permute-start.2 = (bf16[64,1152]{1,0:T(8,128)(2,1)S(1)}, bf16[64,1152]{1,0:T(8,128)(2,1)S(1)}, u32[]{:S(2)}, u32[]{:S(2)}) collective-permute-start(bf16[64,1152]{1,0:T(8,128)(2,1)S(1)} %pad_maximum_fusion.1), channel_id=1, source_target_pairs={{0,2},{1,3},{2,0},{3,1},{4,6},{5,7},{6,4},{7,5},{8,10},{9,11},{10,... | collective-permute-start | bytes 442376 | tf_op jit(solution)/shard_map/ppermute | solution.py:116
  10.7 0.0 copy-done.6
  10.8 0.0 copy-done.7
  10.8 0.0 copy-done.12
  10.8 0.0 copy-done.13
  10.8 0.6 %copy-done.9 = s32[32]{0:T(128)S(1)} copy-done((s32[32]{0:T(128)S(1)}, s32[32]{0:T(128)}, u32[]{:S(2)}) %copy-start.9) | copy-done | bytes 152
  11.4 0.0 copy-done.10
  11.4 0.0 copy-done.11
  11.4 2.3 %shard_map.166 = (f32[3,128,512]{2,1,0:T(8,128)S(1)}, f32[128,512]{1,0:T(8,128)}, f32[128,128]{1,0:T(8,128)S(1)}, f32[8,128]{1,0:T(8,128)S(1)}) custom-call(s32[32]{0:T(128)S(1)} %copy-done.9, bf16[3,128,512]{2,1,0:T(8,128)(2,1)S(1)} %bitcast.8, bf16[128,512]{1,0:T(8,128)(2,1)S(1)} %copy-done.7, f32[128,512]{1,0:T(8,128)S(1)} %copy-done.4, ...), custom_call_target="tpu_custom_call" | custom-call | flops 2000000000 | bytes 1609728 | tf_op jit(solution)/shard_map/pallas_call | solution.py:346
  13.7 4.9 %collective-permute-done.2 = bf16[64,1152]{1,0:T(8,128)(2,1)S(1)} collective-permute-done((bf16[64,1152]{1,0:T(8,128)(2,1)S(1)}, bf16[64,1152]{1,0:T(8,128)(2,1)S(1)}, u32[]{:S(2)}, u32[]{:S(2)}) %collective-permute-start.2) | collective-permute-done | bytes 147488 | tf_op jit(solution)/shard_map/ppermute | solution.py:116
  18.7 0.1 collective-permute-start.6
  18.7 0.0 collective-permute-done.3.refs_1_
  18.7 0.5 %collective-permute-start.5 = (bf16[128,1152]{1,0:T(8,128)(2,1)S(1)}, bf16[128,1152]{1,0:T(8,128)(2,1)S(1)}, u32[]{:S(2)}, u32[]{:S(2)}) collective-permute-start(bf16[128,1152]{1,0:T(8,128)(2,1)S(1)} %collective-permute-done.3.refs_1_), channel_id=1, source_target_pairs={{0,1},{1,0},{2,3},{3,2},{4,5},{5,4},{6,7},{7,6},{8,9},{9,8},{10,11... | collective-permute-start | bytes 884744 | tf_op jit(solution)/shard_map/ppermute | solution.py:116
  19.2 0.0 collective-permute-done.4.refs_2_
  19.2 1.1 %collective-permute-done.6.refs_5_ = bf16[128,1152]{1,0:T(8,128)(2,1)S(1)} collective-permute-done((bf16[128,1152]{1,0:T(8,128)(2,1)S(1)}, bf16[128,1152]{1,0:T(8,128)(2,1)S(1)}, u32[]{:S(2)}, u32[]{:S(2)}) %collective-permute-start.6) | collective-permute-done | bytes 294944 | tf_op jit(solution)/shard_map/ppermute | solution.py:116
  20.3 0.4 collective-permute-done.5.refs_3_
  20.7 0.0 copy-done.3
  20.7 0.0 copy-done
  20.7 3.0 %shard_map.167 = (f32[3,128,512]{2,1,0:T(8,128)}, f32[8,256]{1,0:T(8,128)S(1)}) custom-call(f32[3,128,512]{2,1,0:T(8,128)S(1)} %get-tuple-element.20.part_ref, f32[128,512]{1,0:T(8,128)S(1)} %copy-done.4, f32[128,128]{1,0:T(8,128)S(1)} %get-tuple-element.21.spots_ref, f32[8,128]{1,0:T(8,128)S(1)} %get-tuple-element.22.geom_ref, f32[64,128]{1,0:T(8,128)S(1)} %copy-done.5, ...), custom_call_target="tpu_custom_call" | custom-call | flops 1000000000 | bytes 4198400 | tf_op jit(solution)/shard_map/pallas_call | solution.py:346
  23.8 0.2 collective-permute-start.7
  24.0 1.0 %collective-permute-done.7 = f32[8,256]{1,0:T(8,128)S(1)} collective-permute-done((f32[8,256]{1,0:T(8,128)S(1)}, f32[8,256]{1,0:T(8,128)S(1)}, u32[]{:S(2)}, u32[]{:S(2)}) %collective-permute-start.7) | collective-permute-done | bytes 8224 | tf_op jit(solution)/shard_map/ppermute | solution.py:121
  25.0 5.0 %collective-permute-start.10 = (f32[8,256]{1,0:T(8,128)S(1)}, f32[8,256]{1,0:T(8,128)S(1)}, u32[]{:S(2)}, u32[]{:S(2)}) collective-permute-start(f32[8,256]{1,0:T(8,128)S(1)} %add.12), channel_id=1, source_target_pairs={{0,6},{1,7},{2,4},{3,5},{4,2},{5,3},{6,0},{7,1},{8,14},{9,15},{10,... | collective-permute-start | bytes 24584 | tf_op jit(solution)/shard_map/ppermute | solution.py:121
  30.0 0.5 %collective-permute-start.8 = (f32[8,256]{1,0:T(8,128)S(1)}, f32[8,256]{1,0:T(8,128)S(1)}, u32[]{:S(2)}, u32[]{:S(2)}) collective-permute-start(f32[8,256]{1,0:T(8,128)S(1)} %add.12), channel_id=1, source_target_pairs={{0,2},{1,3},{2,0},{3,1},{4,6},{5,7},{6,4},{7,5},{8,10},{9,11},{10,... | collective-permute-start | bytes 24584 | tf_op jit(solution)/shard_map/ppermute | solution.py:121
  30.5 0.1 collective-permute-start.9
  30.6 1.1 %collective-permute-done.10 = f32[8,256]{1,0:T(8,128)S(1)} collective-permute-done((f32[8,256]{1,0:T(8,128)S(1)}, f32[8,256]{1,0:T(8,128)S(1)}, u32[]{:S(2)}, u32[]{:S(2)}) %collective-permute-start.10) | collective-permute-done | bytes 8224 | tf_op jit(solution)/shard_map/ppermute | solution.py:121
  31.6 2.0 %collective-permute-done.8 = f32[8,256]{1,0:T(8,128)S(1)} collective-permute-done((f32[8,256]{1,0:T(8,128)S(1)}, f32[8,256]{1,0:T(8,128)S(1)}, u32[]{:S(2)}, u32[]{:S(2)}) %collective-permute-start.8) | collective-permute-done | bytes 8224 | tf_op jit(solution)/shard_map/ppermute | solution.py:121
  33.6 0.5 %collective-permute-done.9 = f32[8,256]{1,0:T(8,128)S(1)} collective-permute-done((f32[8,256]{1,0:T(8,128)S(1)}, f32[8,256]{1,0:T(8,128)S(1)}, u32[]{:S(2)}, u32[]{:S(2)}) %collective-permute-start.9) | collective-permute-done | bytes 8224 | tf_op jit(solution)/shard_map/ppermute | solution.py:121
  34.1 0.1 add_select_fusion.sums_ref
  34.2 1.6 %collective-permute-start.11 = (f32[8,256]{1,0:T(8,128)S(1)}, f32[8,256]{1,0:T(8,128)S(1)}, u32[]{:S(2)}, u32[]{:S(2)}) collective-permute-start(f32[8,256]{1,0:T(8,128)S(1)} %add_select_fusion.sums_ref), channel_id=1, source_target_pairs={{0,8},{1,9},{2,10},{3,11},{4,12},{5,13},{6,14},{7,15},{8,0},{9,1},... | collective-permute-start | bytes 24584 | tf_op jit(solution)/shard_map/ppermute | solution.py:121
  35.8 1.1 %collective-permute-start.12 = (f32[8,256]{1,0:T(8,128)S(1)}, f32[8,256]{1,0:T(8,128)S(1)}, u32[]{:S(2)}, u32[]{:S(2)}) collective-permute-start(f32[8,256]{1,0:T(8,128)S(1)} %add_select_fusion.sums_ref), channel_id=1, source_target_pairs={{0,16},{1,17},{2,18},{3,19},{4,20},{5,21},{6,22},{7,23},{8,24},{9,... | collective-permute-start | bytes 24584 | tf_op jit(solution)/shard_map/ppermute | solution.py:121
  36.9 1.7 %collective-permute-start.13 = (f32[8,256]{1,0:T(8,128)S(1)}, f32[8,256]{1,0:T(8,128)S(1)}, u32[]{:S(2)}, u32[]{:S(2)}) collective-permute-start(f32[8,256]{1,0:T(8,128)S(1)} %add_select_fusion.sums_ref), channel_id=1, source_target_pairs={{0,24},{1,25},{2,26},{3,27},{4,28},{5,29},{6,30},{7,31},{8,16},{9,... | collective-permute-start | bytes 24584 | tf_op jit(solution)/shard_map/ppermute | solution.py:121
  38.6 0.0 collective-permute-done.11.refs_0_
  38.6 1.7 %collective-permute-done.12.refs_1_ = f32[8,256]{1,0:T(8,128)S(1)} collective-permute-done((f32[8,256]{1,0:T(8,128)S(1)}, f32[8,256]{1,0:T(8,128)S(1)}, u32[]{:S(2)}, u32[]{:S(2)}) %collective-permute-start.12) | collective-permute-done | bytes 8224 | tf_op jit(solution)/shard_map/ppermute | solution.py:121
  40.4 2.0 %collective-permute-done.13.refs_2_ = f32[8,256]{1,0:T(8,128)S(1)} collective-permute-done((f32[8,256]{1,0:T(8,128)S(1)}, f32[8,256]{1,0:T(8,128)S(1)}, u32[]{:S(2)}, u32[]{:S(2)}) %collective-permute-start.13) | collective-permute-done | bytes 8224 | tf_op jit(solution)/shard_map/ppermute | solution.py:121
  42.3 0.6 %shard_map.168 = (f32[3,1,216]{2,1,0:T(1,128)}, f32[3,1,216]{2,1,0:T(1,128)}) custom-call(f32[8,256]{1,0:T(8,128)S(1)} %add_select_fusion.sums_ref, f32[8,256]{1,0:T(8,128)S(1)} %collective-permute-done.11.refs_0_, f32[8,256]{1,0:T(8,128)S(1)} %collective-permute-done.12.refs_1_, f32[8,256]{1,0:T(8,128)S(1)} %collective-permute-done.13.refs_2_), custom_call_target="tpu_custom_call" | custom-call | flops 100000 | bytes 32768 | tf_op jit(solution)/shard_map/pallas_call | solution.py:346
  (17 shorter events, 0.1 us)
Async XLA Ops:
  0.6 10.1 %copy-start.6 = (bf16[128,3,512]{2,0,1:T(8,128)(2,1)S(1)}, bf16[128,3,512]{2,0,1:T(8,128)(2,1)}, u32[]{:S(2)}) copy-start(bf16[128,3,512]{2,0,1:T(8,128)(2,1)} %param.14) | copy-start | bytes 1179652
  0.6 10.1 %copy-start.7 = (bf16[128,512]{1,0:T(8,128)(2,1)S(1)}, bf16[128,512]{1,0:T(8,128)(2,1)}, u32[]{:S(2)}) copy-start(bf16[128,512]{1,0:T(8,128)(2,1)} %press_ref.1) | copy-start | bytes 393220
  0.7 10.1 %copy-start.12 = (bf16[512,512]{1,0:T(8,128)(2,1)S(1)}, bf16[512,512]{1,0:T(8,128)(2,1)}, u32[]{:S(2)}) copy-start(bf16[512,512]{1,0:T(8,128)(2,1)} %constant.24.dx_ref) | copy-start | bytes 1572868
  0.7 10.1 %copy-start.13 = (bf16[256,512]{1,0:T(8,128)(2,1)S(1)}, bf16[256,512]{1,0:T(8,128)(2,1)}, u32[]{:S(2)}) copy-start(bf16[256,512]{1,0:T(8,128)(2,1)} %constant.25.dyz_ref) | copy-start | bytes 786436
  3.1 7.7 %copy-start.4 = (f32[128,512]{1,0:T(8,128)S(1)}, f32[128,512]{1,0:T(8,128)}, u32[]{:S(2)}) copy-start(f32[128,512]{1,0:T(8,128)} %visc_ref.3) | copy-start | bytes 786436
  3.1 5.5 %collective-permute-start = (bf16[32,1152]{1,0:T(8,128)(2,1)}, bf16[32,1152]{1,0:T(8,128)(2,1)S(1)}, u32[]{:S(2)}, u32[]{:S(2)}) collective-permute-start(bf16[32,1152]{1,0:T(8,128)(2,1)} %get-tuple-element.17), channel_id=1, source_target_pairs={{0,4},{4,0},{8,12},{12,8},{16,20},{20,16},{24,28},{28,24},{1,5},{5... | collective-permute-start | bytes 221192 | tf_op jit(solution)/shard_map/ppermute | solution.py:128
  6.0 2.5 %collective-permute-start.1 = (bf16[32,1152]{1,0:T(8,128)(2,1)}, bf16[32,1152]{1,0:T(8,128)(2,1)S(1)}, u32[]{:S(2)}, u32[]{:S(2)}) collective-permute-start(bf16[32,1152]{1,0:T(8,128)(2,1)} %get-tuple-element.18), channel_id=1, source_target_pairs={{4,8},{8,4},{12,16},{16,12},{20,24},{24,20},{5,9},{9,5},{13,17},{1... | collective-permute-start | bytes 221192 | tf_op jit(solution)/shard_map/ppermute | solution.py:128
  6.7 4.1 %copy-start.5 = (f32[64,128]{1,0:T(8,128)S(1)}, f32[64,128]{1,0:T(8,128)}, u32[]{:S(2)}) copy-start(f32[64,128]{1,0:T(8,128)} %constant.21.clone.box_ref) | copy-start | bytes 98308
  6.7 12.0 %collective-permute-start.3 = (bf16[128,1152]{1,0:T(8,128)(2,1)}, bf16[128,1152]{1,0:T(8,128)(2,1)S(1)}, u32[]{:S(2)}, u32[]{:S(2)}) collective-permute-start(bf16[128,1152]{1,0:T(8,128)(2,1)} %get-tuple-element.23.refs_0_), channel_id=1, source_target_pairs={{0,2},{1,3},{2,0},{3,1},{4,6},{5,7},{6,4},{7,5},{8,10},{9,11},{10,... | collective-permute-start | bytes 884744 | tf_op jit(solution)/shard_map/ppermute | solution.py:116
  8.3 10.9 %collective-permute-start.4 = (bf16[128,1152]{1,0:T(8,128)(2,1)}, bf16[128,1152]{1,0:T(8,128)(2,1)S(1)}, u32[]{:S(2)}, u32[]{:S(2)}) collective-permute-start(bf16[128,1152]{1,0:T(8,128)(2,1)} %get-tuple-element.23.refs_0_), channel_id=1, source_target_pairs={{0,1},{1,0},{2,3},{3,2},{4,5},{5,4},{6,7},{7,6},{8,9},{9,8},{10,11... | collective-permute-start | bytes 884744 | tf_op jit(solution)/shard_map/ppermute | solution.py:116
  8.6 2.2 %copy-start.8 = (s32[128,6]{0,1:T(8,128)S(1)}, s32[128,6]{0,1:T(8,128)}, u32[]{:S(2)}) copy-start(s32[128,6]{0,1:T(8,128)} %param.20) | copy-start | bytes 9220
  8.6 10.0 %collective-permute-start.2 = (bf16[64,1152]{1,0:T(8,128)(2,1)S(1)}, bf16[64,1152]{1,0:T(8,128)(2,1)S(1)}, u32[]{:S(2)}, u32[]{:S(2)}) collective-permute-start(bf16[64,1152]{1,0:T(8,128)(2,1)S(1)} %pad_maximum_fusion.1), channel_id=1, source_target_pairs={{0,2},{1,3},{2,0},{3,1},{4,6},{5,7},{6,4},{7,5},{8,10},{9,11},{10,... | collective-permute-start | bytes 442376 | tf_op jit(solution)/shard_map/ppermute | solution.py:116
  10.7 0.7 %copy-start.9 = (s32[32]{0:T(128)S(1)}, s32[32]{0:T(128)}, u32[]{:S(2)}) copy-start(s32[32]{0:T(128)} %counts_ref.3) | copy-start | bytes 388
  10.7 0.7 %copy-start.10 = (s32[128]{0:T(128)S(1)}, s32[128]{0:T(128)}, u32[]{:S(2)}) copy-start(s32[128]{0:T(128)} %param.17) | copy-start | bytes 1540
  10.7 0.7 %copy-start.11 = (s32[128]{0:T(128)S(1)}, s32[128]{0:T(128)}, u32[]{:S(2)}) copy-start(s32[128]{0:T(128)} %param.18) | copy-start | bytes 1540
  11.4 9.3 %copy-start.1 = (bf16[384,512]{1,0:T(8,128)(2,1)S(1)}, bf16[384,512]{1,0:T(8,128)(2,1)}, u32[]{:S(2)}) copy-start(bf16[384,512]{1,0:T(8,128)(2,1)} %constant.26.spread_ref) | copy-start | bytes 1179652
  11.4 9.3 %copy-start.2 = (f32[288,256]{1,0:T(8,128)S(1)}, f32[288,256]{1,0:T(8,128)}, u32[]{:S(2)}) copy-start(f32[288,256]{1,0:T(8,128)} %constant.22.clone.compact_ref) | copy-start | bytes 884740
  11.4 9.3 %copy-start.3 = (bf16[128,1152]{1,0:T(8,128)(2,1)S(1)}, bf16[128,1152]{1,0:T(8,128)(2,1)}, u32[]{:S(2)}) copy-start(bf16[128,1152]{1,0:T(8,128)(2,1)} %get-tuple-element.23.refs_0_) | copy-start | bytes 884740
  13.7 7.0 %copy-start = (bf16[576,512]{1,0:T(8,128)(2,1)S(1)}, bf16[576,512]{1,0:T(8,128)(2,1)}, u32[]{:S(2)}) copy-start(bf16[576,512]{1,0:T(8,128)(2,1)} %constant.20.clone.basis_ref) | copy-start | bytes 1769476
  18.7 1.6 %collective-permute-start.6 = (bf16[128,1152]{1,0:T(8,128)(2,1)S(1)}, bf16[128,1152]{1,0:T(8,128)(2,1)S(1)}, u32[]{:S(2)}, u32[]{:S(2)}) collective-permute-start(bf16[128,1152]{1,0:T(8,128)(2,1)S(1)} %pad_maximum_fusion.refs_4_), channel_id=1, source_target_pairs={{0,1},{1,0},{2,3},{3,2},{4,5},{5,4},{6,7},{7,6},{8,9},{9,8},{10,11... | collective-permute-start | bytes 884744 | tf_op jit(solution)/shard_map/ppermute | solution.py:116
  18.7 2.0 %collective-permute-start.5 = (bf16[128,1152]{1,0:T(8,128)(2,1)S(1)}, bf16[128,1152]{1,0:T(8,128)(2,1)S(1)}, u32[]{:S(2)}, u32[]{:S(2)}) collective-permute-start(bf16[128,1152]{1,0:T(8,128)(2,1)S(1)} %collective-permute-done.3.refs_1_), channel_id=1, source_target_pairs={{0,1},{1,0},{2,3},{3,2},{4,5},{5,4},{6,7},{7,6},{8,9},{9,8},{10,11... | collective-permute-start | bytes 884744 | tf_op jit(solution)/shard_map/ppermute | solution.py:116
  23.8 1.2 %collective-permute-start.7 = (f32[8,256]{1,0:T(8,128)S(1)}, f32[8,256]{1,0:T(8,128)S(1)}, u32[]{:S(2)}, u32[]{:S(2)}) collective-permute-start(f32[8,256]{1,0:T(8,128)S(1)} %get-tuple-element.27), channel_id=1, source_target_pairs={{0,1},{1,0},{2,3},{3,2},{4,5},{5,4},{6,7},{7,6},{8,9},{9,8},{10,11... | collective-permute-start | bytes 24584 | tf_op jit(solution)/shard_map/ppermute | solution.py:121
  25.0 6.6 %collective-permute-start.10 = (f32[8,256]{1,0:T(8,128)S(1)}, f32[8,256]{1,0:T(8,128)S(1)}, u32[]{:S(2)}, u32[]{:S(2)}) collective-permute-start(f32[8,256]{1,0:T(8,128)S(1)} %add.12), channel_id=1, source_target_pairs={{0,6},{1,7},{2,4},{3,5},{4,2},{5,3},{6,0},{7,1},{8,14},{9,15},{10,... | collective-permute-start | bytes 24584 | tf_op jit(solution)/shard_map/ppermute | solution.py:121
  30.0 3.7 %collective-permute-start.8 = (f32[8,256]{1,0:T(8,128)S(1)}, f32[8,256]{1,0:T(8,128)S(1)}, u32[]{:S(2)}, u32[]{:S(2)}) collective-permute-start(f32[8,256]{1,0:T(8,128)S(1)} %add.12), channel_id=1, source_target_pairs={{0,2},{1,3},{2,0},{3,1},{4,6},{5,7},{6,4},{7,5},{8,10},{9,11},{10,... | collective-permute-start | bytes 24584 | tf_op jit(solution)/shard_map/ppermute | solution.py:121
  30.5 3.7 %collective-permute-start.9 = (f32[8,256]{1,0:T(8,128)S(1)}, f32[8,256]{1,0:T(8,128)S(1)}, u32[]{:S(2)}, u32[]{:S(2)}) collective-permute-start(f32[8,256]{1,0:T(8,128)S(1)} %add.12), channel_id=1, source_target_pairs={{0,4},{1,5},{2,6},{3,7},{4,0},{5,1},{6,2},{7,3},{8,12},{9,13},{10,... | collective-permute-start | bytes 24584 | tf_op jit(solution)/shard_map/ppermute | solution.py:121
  34.2 4.4 %collective-permute-start.11 = (f32[8,256]{1,0:T(8,128)S(1)}, f32[8,256]{1,0:T(8,128)S(1)}, u32[]{:S(2)}, u32[]{:S(2)}) collective-permute-start(f32[8,256]{1,0:T(8,128)S(1)} %add_select_fusion.sums_ref), channel_id=1, source_target_pairs={{0,8},{1,9},{2,10},{3,11},{4,12},{5,13},{6,14},{7,15},{8,0},{9,1},... | collective-permute-start | bytes 24584 | tf_op jit(solution)/shard_map/ppermute | solution.py:121
  35.8 4.5 %collective-permute-start.12 = (f32[8,256]{1,0:T(8,128)S(1)}, f32[8,256]{1,0:T(8,128)S(1)}, u32[]{:S(2)}, u32[]{:S(2)}) collective-permute-start(f32[8,256]{1,0:T(8,128)S(1)} %add_select_fusion.sums_ref), channel_id=1, source_target_pairs={{0,16},{1,17},{2,18},{3,19},{4,20},{5,21},{6,22},{7,23},{8,24},{9,... | collective-permute-start | bytes 24584 | tf_op jit(solution)/shard_map/ppermute | solution.py:121
  36.9 5.4 %collective-permute-start.13 = (f32[8,256]{1,0:T(8,128)S(1)}, f32[8,256]{1,0:T(8,128)S(1)}, u32[]{:S(2)}, u32[]{:S(2)}) collective-permute-start(f32[8,256]{1,0:T(8,128)S(1)} %add_select_fusion.sums_ref), channel_id=1, source_target_pairs={{0,24},{1,25},{2,26},{3,27},{4,28},{5,29},{6,30},{7,31},{8,16},{9,... | collective-permute-start | bytes 24584 | tf_op jit(solution)/shard_map/ppermute | solution.py:121

commit v4 on v3

--- a/solution.py
+++ b/solution.py
@@ -1,3 +1,5 @@
+import math
+
 import jax
 import jax.numpy as jnp
 import numpy as np
@@ -105,20 +107,22 @@
     return table.reshape(morton_count * 8, LANES)
 
 
-def doubling(count):
-    order = [0]
-    for bit in reversed(range(count.bit_length() - 1)):
-        order += [other ^ 1 << bit for other in order]
-    return order
-
-
 def swap(block, axis, apart):
     return lax.ppermute(block, axis, [(at, at ^ apart) for at in range(lax.axis_size(axis))])
 
 
-def exchange(block, mask):
-    total = lax.axis_size("morton") * lax.axis_size("sib")
-    return lax.ppermute(block, ("morton", "sib"), [(at, at ^ mask) for at in range(total)])
+def move_tables(morton_count):
+    bits = 3 * LMAX - (morton_count.bit_length() - 1)
+    ratio = 2.0 ** max(max(0, min(LMAX, (bits - offset + 2) // 3)) for offset in range(3)) / 2.0**LMAX
+    shift = np.zeros((256, 256), np.float32)
+    powers = np.zeros((256, 256), np.int32)
+    triples = list(np.ndindex(6, 6, 6))
+    for row, beta in enumerate(triples):
+        for col, alpha in enumerate(triples):
+            if all(b <= a for a, b in zip(alpha, beta)):
+                shift[row, col] = math.prod(math.comb(a, b) for a, b in zip(alpha, beta)) * ratio ** sum(beta)
+                powers[row, col] = sum((a - b) << 3 * dim for dim, (a, b) in enumerate(zip(alpha, beta)))
+    return shift, powers
 
 
 def pairs(block, first):
@@ -138,10 +142,11 @@
     )
 
 
-def pack_kernel(counts_ref, vel_ref, pick_ref, faces_ref, even_ref, odd_ref):
+def pack_kernel(counts_ref, vel_ref, nbrs_ref, pick_ref, faces_ref, even_ref, odd_ref, *spots_refs):
     sib_count = lax.axis_size("sib")
     morton = lax.axis_index("morton")
-    own = morton * sib_count + lax.axis_index("sib")
+    sib = lax.axis_index("sib")
+    own = morton * sib_count + sib
     leaf_count = faces_ref.shape[0]
     picked = dot(vel_ref[...].reshape(3 * leaf_count, NODES), pick_ref[...]).astype(bf16)
     for comp in range(3):
@@ -159,11 +164,62 @@
     even_ref[...] = jnp.where(is_odd, low, high)
     odd_ref[...] = jnp.where(is_odd, high, low)
 
+    nbrs = nbrs_ref[...]
+    target = jnp.maximum(nbrs, 0)
+    owner = target // leaf_count
+    slot = target - owner * leaf_count
+    owner_morton = owner // sib_count
+    owner_sib = owner - owner_morton * sib_count
+    step = owner_morton - morton
+    below = jnp.maximum(morton - 1, 0) * sib_count
+    band_start = jnp.zeros_like(slot)
+    for other in range(sib_count):
+        band_start = jnp.where(owner_sib == other, counts_ref[below + other] - BAND, band_start)
+    below_at = BAND * (1 - jnp.bitwise_and(morton, 1))
+    in_band = jnp.where(step < 0, slot - band_start + below_at, slot + BAND - below_at)
+    for side, spots_ref in enumerate(spots_refs):
+        piece = jnp.bitwise_xor(owner_sib, jnp.bitwise_xor(sib, 2 * side))
+        spot = jnp.where(step == 0, piece * leaf_count + slot, 2 * leaf_count + piece * (2 * BAND) + in_band)
+        spot = jnp.where((nbrs >= 0) & (piece < 2), spot, -1).astype(f32)
+        spots_ref[...] = jnp.concatenate([spot, jnp.full((2, leaf_count), -1.0, f32)], axis=0)
+
+
+def gathered(spots, window_refs):
+    leaf_count = spots.shape[1]
+    rows = sum(ref.shape[0] for ref in window_refs)
+    filled = jnp.concatenate([spots, jnp.full((LANES - spots.shape[0], leaf_count), -1.0, f32)], axis=0)
+    places = filled.T.astype(jnp.int32)
+    cols = lax.broadcasted_iota(jnp.int32, (leaf_count, rows), 1)
+    upper = jnp.bitwise_and(lax.broadcasted_iota(jnp.int32, (leaf_count, FACES), 1), 64) > 0
+    chosen = []
+    for dim in range(3):
+        at = dim * FACES
+        window = jnp.concatenate([ref[:, at : at + FACES] for ref in window_refs], axis=0)
+        faces = (2 * dim, 2 * dim + 1)
+        onehot = [jnp.where(cols == places[:, face : face + 1], 1.0, 0.0).astype(bf16) for face in faces]
+        both = dot(jnp.concatenate(onehot, axis=0), window)
+        chosen.append(jnp.where(upper, both[:leaf_count], both[leaf_count:]).astype(bf16))
+    return chosen
+
+
+def spread_out(chosen, spread):
+    comps = [
+        jnp.concatenate([block[:, comp * LANES : (comp + 1) * LANES] for block in chosen], axis=1) for comp in range(3)
+    ]
+    return dot(jnp.concatenate(comps, axis=0), spread)
+
+
+def serve_kernel(spots_ref, *refs):
+    window_refs, out_ref = refs[:-1], refs[-1]
+    for dim, block in enumerate(gathered(spots_ref[...], window_refs)):
+        out_ref[:, dim * FACES : (dim + 1) * FACES] = block
+
 
 def pre_kernel(
-    counts_ref, vel_ref, press_ref, visc_ref, levels_ref, keys_ref, nbrs_ref, dx_ref, dyz_ref, box_ref,
-    part_ref, mass_ref, spots_ref, geom_ref,
+    counts_ref, vel_ref, press_ref, visc_ref, levels_ref, keys_ref, spots_ref, dx_ref, dyz_ref, box_ref,
+    shift_ref, powers_ref, spread_ref, *refs,
 ):
+    window_refs, (part_ref, mass_ref, geom_ref, move_ref) = refs[:-4], refs[-4:]
     sib_count = lax.axis_size("sib")
     morton_count = lax.axis_size("morton")
     morton = lax.axis_index("morton")
@@ -200,36 +256,11 @@
         for at in (0, 256)
     ]
     div = dot(columns[0], dx_ref[...]) + jnp.concatenate(rest, axis=1)
+    nearby = spread_out(gathered(spots_ref[...], window_refs), spread_ref[...])
     for comp in range(3):
-        jump = touching * vel_ref[comp].astype(f32)
+        jump = touching * vel_ref[comp].astype(f32) - rows(nearby, comp)
         part = (penalty * visc * jump - rows(div, comp) + rows(grads[comp], 3)) * out_scale
         part_ref[comp] = jnp.where(live, part, 0.0)
-
-    nbrs = nbrs_ref[...]
-    target = jnp.maximum(nbrs, 0)
-    owner = target // leaf_count
-    slot = target - owner * leaf_count
-    owner_morton = owner // sib_count
-    owner_sib = owner - owner_morton * sib_count
-    apart = jnp.bitwise_xor(owner_sib, lax.axis_index("sib"))
-    piece = jnp.zeros_like(apart)
-    for at, other in enumerate(doubling(sib_count)):
-        piece = jnp.where(apart == other, at, piece)
-    step = owner_morton - morton
-    below = jnp.maximum(morton - 1, 0) * sib_count
-    band_start = jnp.zeros_like(slot)
-    for sib in range(sib_count):
-        band_start = jnp.where(owner_sib == sib, counts_ref[below + sib] - BAND, band_start)
-    base = sib_count * leaf_count
-    below_at = BAND * (1 - jnp.bitwise_and(morton, 1))
-    spot = jnp.where(
-        step == 0,
-        piece * leaf_count + slot,
-        base + piece * (2 * BAND) + jnp.where(step < 0, slot - band_start + below_at, slot + BAND - below_at),
-    )
-    spot = jnp.where(nbrs >= 0, spot, -1).astype(f32)
-    padded = jnp.concatenate([spot, jnp.full((LANES - spot.shape[0], leaf_count), -1.0, f32)], axis=0)
-    spots_ref[...] = padded.T
 
     box = box_ref[pl.ds(pl.multiple_of(morton * 8, 8), 8), :]
     shift_bits = 3 * (LMAX - levels_ref[...])
@@ -247,6 +278,16 @@
     places.append(0.5 * span * finest * box[7:8, :])
     places.append(jnp.zeros((4, leaf_count), f32))
     geom_ref[...] = jnp.concatenate(places, axis=0)
+    move = shift_ref[...]
+    powers = powers_ref[...]
+    for dim in range(3):
+        power = jnp.bitwise_and(jnp.right_shift(powers, 3 * dim), 7)
+        along = box[dim : dim + 1, 3:4]
+        factor = jnp.ones((1, 1), f32)
+        for degree in range(1, DEG + 1):
+            factor = factor * along
+            move = move * jnp.where(power == degree, factor, 1.0)
+    move_ref[...] = move
 
 
 def shifted(tiles, geom):
@@ -276,30 +317,20 @@
 
 
 def post_kernel(
-    part_ref, visc_ref, spots_ref, geom_ref, box_ref, spread_ref, basis_ref, compact_ref, *refs
+    part_ref, visc_ref, geom_ref, box_ref, spread_ref, basis_ref, compact_ref, *refs
 ):
-    window_refs, (force_hbm, sums_ref, force_ref, raw_ref, sems) = refs[:-5], refs[-5:]
+    got_refs, (force_hbm, sums_ref, force_ref, raw_ref, sems) = refs[:-5], refs[-5:]
     morton = lax.axis_index("morton")
     leaf_count = visc_ref.shape[0]
-    spots = spots_ref[...].astype(jnp.int32)
-    lane = lax.broadcasted_iota(jnp.int32, (leaf_count, FACES), 1)
-    upper = jnp.bitwise_and(lane, 64) > 0
-    window_rows = sum(window_ref.shape[0] for window_ref in window_refs)
-    cols = lax.broadcasted_iota(jnp.int32, (leaf_count, window_rows), 1)
     chosen = []
     for dim in range(3):
-        at = dim * FACES
-        window = jnp.concatenate([ref[:, at : at + FACES] for ref in window_refs], axis=0)
-        places = [jnp.broadcast_to(spots[:, face : face + 1], (leaf_count, 1)) for face in (2 * dim, 2 * dim + 1)]
-        onehot = [jnp.where(cols == place, 1.0, 0.0).astype(bf16) for place in places]
-        both = dot(jnp.concatenate(onehot, axis=0), window)
-        chosen.append(jnp.where(upper, both[:leaf_count], both[leaf_count:]).astype(bf16))
+        lanes = slice(dim * FACES, (dim + 1) * FACES)
+        chosen.append(got_refs[0][:, lanes])
+        for got_ref in got_refs[1:]:
+            chosen[dim] = chosen[dim] + got_ref[:, lanes]
+    jumps = spread_out(chosen, spread_ref[...])
     weight = visc_ref[...] * (penalty * out_scale)
     highs, lows, stores = [], [], []
-    picked = [
-        jnp.concatenate([block[:, comp * LANES : (comp + 1) * LANES] for block in chosen], axis=1) for comp in range(3)
-    ]
-    jumps = dot(jnp.concatenate(picked, axis=0), spread_ref[...])
     for comp in range(3):
         force = part_ref[comp] - weight * jumps[comp * leaf_count : (comp + 1) * leaf_count]
         force_ref[comp] = force
@@ -323,18 +354,31 @@
     both = shifted([summed[8 * at : 8 * at + 8, :] for at in range(36)], box)
     flat = jnp.concatenate(both, axis=0).T
     sums = jnp.dot(flat[:8], compact_ref[...], precision=highest, preferred_element_type=f32)
-    sums_ref[...] = sums
+    blank = jnp.zeros((2, LANES), f32)
+    to_box = jnp.concatenate([sums[:3, :LANES], sums[:3, LANES:], blank], axis=0)
+    to_root = jnp.concatenate([sums[3:6, :LANES], sums[3:6, LANES:], blank], axis=0)
+    sib_count = lax.axis_size("sib")
+    for other in range(sums_ref.shape[0]):
+        sums_ref[other] = jnp.where(morton == other // sib_count, to_box, to_root)
     for store in stores:
         store.wait()
 
 
-def final_kernel(sums_ref, *refs):
-    others, (box_ref, root_ref) = refs[:-2], refs[-2:]
-    root = sums_ref[3:6, :] + others[0][3:6, :]
-    if len(others) > 1:
-        root = root + (others[1][3:6, :] + others[2][3:6, :])
+def final_kernel(sums_ref, move_ref, box_ref, root_ref):
+    sib_count = lax.axis_size("sib")
+    morton = lax.axis_index("morton")
+    box = jnp.zeros(sums_ref.shape[1:], f32)
+    root = jnp.zeros(sums_ref.shape[1:], f32)
+    for group in range(sums_ref.shape[0] // sib_count):
+        total = jnp.sum(sums_ref[group * sib_count : (group + 1) * sib_count], axis=0)
+        box = box + jnp.where(morton == group, total, 0.0)
+        root = root + jnp.where(morton == group, 0.0, total)
+    box = jnp.concatenate([box[:3], box[3:6]], axis=1)
+    root = jnp.concatenate([root[:3], root[3:6]], axis=1)
+    box8 = jnp.concatenate([box, jnp.zeros((5, 2 * LANES), f32)], axis=0)
+    root = root + jnp.dot(box8, move_ref[...], precision=highest, preferred_element_type=f32)[:3]
     for comp in range(3):
-        box_ref[comp] = sums_ref[comp : comp + 1, :MOMENTS]
+        box_ref[comp] = box[comp : comp + 1, :MOMENTS]
         root_ref[comp] = root[comp : comp + 1, :MOMENTS]
 
 
@@ -368,48 +412,54 @@
     nbrs = jnp.transpose(neighbors, (1, 0))
 
     width = 3 * FACES
-    faces, even, odd = call(
+    sib_count = lax.axis_size("sib")
+    sides = sib_count // 2
+    faces, even, odd, *spots = call(
         pack_kernel,
-        [((leaf_count, width), bf16), ((BAND, width), bf16), ((BAND, width), bf16)],
+        [
+            ((leaf_count, width), bf16),
+            ((BAND, width), bf16),
+            ((BAND, width), bf16),
+        ]
+        + [((8, leaf_count), f32)] * sides,
         4 * 10**8,
         [counts],
-        [vel, pick],
+        [vel, nbrs, pick],
         grant=60,
     )
-    sib_count = lax.axis_size("sib")
-    part, continuity, spots, geom = call(
+    asked = [swap(spots[side], "sib", 2 * side) for side in range(1, sides)]
+    bands = jnp.concatenate([pairs(even, 0), pairs(odd, 1)], axis=0)
+    bands, *asked = lax.optimization_barrier((bands, *asked))
+    window = [faces, swap(faces, "sib", 1), bands, swap(bands, "sib", 1)]
+    got = []
+    for side in range(1, sides):
+        (served,) = call(
+            serve_kernel, [((leaf_count, width), bf16)], 4 * 10**8, [], [asked[side - 1], *window]
+        )
+        got.append(swap(served, "sib", 2 * side))
+
+    shift, powers = move_tables(morton_count)
+    part, continuity, geom, move = call(
         pre_kernel,
         [
             ((3, leaf_count, NODES), f32),
             ((leaf_count, NODES), f32),
-            ((leaf_count, LANES), f32),
             ((8, leaf_count), f32),
+            ((256, 256), f32),
         ],
         2 * 10**9,
         [counts],
         [
-            vel, pressure, viscosity, levels.reshape(1, -1), morton_keys.reshape(1, -1), nbrs,
-            dx_table, dyz_table, boxes,
+            vel, pressure, viscosity, levels.reshape(1, -1), morton_keys.reshape(1, -1), spots[0],
+            dx_table, dyz_table, boxes, jnp.asarray(shift), jnp.asarray(powers), spread, *window,
         ],
     )
-    window = [faces]
-    bands = [jnp.concatenate([pairs(even, 0), pairs(odd, 1)], axis=0)]
-    for bit in reversed(range(sib_count.bit_length() - 1)):
-        window += [swap(piece, "sib", 1 << bit) for piece in window]
-        held = jnp.concatenate(bands, axis=0)
-        if bit == 0:
-            held, part = lax.optimization_barrier((held, part))
-        bands = [held, swap(held, "sib", 1 << bit)]
-
     force, sums = call(
         post_kernel,
-        [((3, leaf_count, NODES), f32), ((8, 2 * LANES), f32)],
+        [((3, leaf_count, NODES), f32), ((morton_count * sib_count, 8, LANES), f32)],
         10**9,
         [],
-        [
-            part, viscosity, spots, geom, boxes, spread, basis,
-            jnp.asarray(compact_table()), *window, *bands,
-        ],
+        [part, viscosity, geom, boxes, spread, basis, jnp.asarray(compact_table()), *got],
         [
             pltpu.VMEM((3, leaf_count, NODES), f32),
             pltpu.VMEM((ROWS, 3 * leaf_count), f32),
@@ -417,23 +467,13 @@
         ],
         outs=[pltpu.HBM, pltpu.VMEM],
     )
-    bits = (morton_count * sib_count).bit_length() - 1
-    rounds = [[1]]
-    for bit in range(1, bits, 2):
-        rounds.append([part << bit for part in ((1, 2, 3) if bit + 1 < bits else (1,))])
-    is_box = jnp.arange(8)[:, None] < 3
-    for masks in rounds[:-1]:
-        got = [exchange(sums, mask) for mask in masks]
-        pair = sums + got[0]
-        every = pair + (got[1] + got[2]) if len(got) > 1 else pair
-        inside = [sums, pair, every][sum(mask < sib_count for mask in masks[:2])]
-        sums = jnp.where(is_box, inside, every)
+    every = lax.all_to_all(sums, ("morton", "sib"), 0, 0, tiled=True)
     box, root = call(
         final_kernel,
         [((3, 1, MOMENTS), f32), ((3, 1, MOMENTS), f32)],
         10**5,
         [],
-        [sums] + [exchange(sums, mask) for mask in rounds[-1]],
+        [every, move],
     )
     return (
         jnp.transpose(force, (1, 0, 2)),

time: 43.1 us -> 41 us (0.951)
  blocking collectives: 0 us -> 15.9 us
  starting transfers between devices: 18 us -> 6.77 us
  waiting for transfers between devices: 15 us -> 7 us
  Pallas kernels: 8.36 us -> 9.66 us
    all_to_all x0 -> x1, blocking collectives: none -> 15.9 us  [on_device(): every = lax.all_to_all(sums, ('morton', 'sib'), 0, 0, tiled=True)]
    ppermute x7 -> x0, starting transfers between devices: 10.1 us -> none  [exchange(): lax.ppermute(block, ('morton', 'sib'), [(at, at ^ mask) for at in range(t...]
    ppermute x7 -> x0, waiting for transfers between devices: 8.36 us -> none  [exchange(): lax.ppermute(block, ('morton', 'sib'), [(at, at ^ mask) for at in range(t...]
    pallas_call x4 -> x5, Pallas kernels: 8.36 us -> 9.66 us  [call(): pl.pallas_call(kernel, out_shape=[jax.ShapeDtypeStruct(shape, dtype) for...]
    ppermute x5 -> x4, starting transfers between devices: 4.27 us -> 3.17 us  [swap(): lax.ppermute(block, axis, [(at, at ^ apart) for at in range(lax.axis_size...]
    ppermute x5 -> x4, waiting for transfers between devices: 6.38 us -> 6.7 us  [swap(): lax.ppermute(block, axis, [(at, at ^ apart) for at in range(lax.axis_size...]
  transfers between devices with their start and end apart: 14 -> 6, of which waited for: 10 -> 4; matrix products, arithmetic and copies ran while one was open for 0% -> 0% of each run, Pallas kernels for 5% -> 8%
where the time goes in v4:
time: 41 us; the launch traced here: 40.8 us
  blocking collectives  15.9 us (39%)
  Pallas kernels  9.66 us (24%)
  waiting for transfers between devices  7 us (17%)
  starting transfers between devices  6.77 us (17%)
  between operations  0.82 us (2%)
  local copies, waits for them, and re-layouts  0.66 us (2%)
    all_to_all x1, blocking collectives, on_device(): every = lax.all_to_all(sums, ('morton', 'sib'), 0, 0, tiled=True)  15.9 us
    pallas_call x5, Pallas kernels, call(): pl.pallas_call(kernel, out_shape=[jax.ShapeDtypeStruct(shape, dtype) for...  9.66 us
    ppermute x4, waiting for transfers between devices, swap(): lax.ppermute(block, axis, [(at, at ^ apart) for at in range(lax.axis_size...  6.7 us
    ppermute x2, starting transfers between devices, pairs(): return lax.ppermute(block, 'morton', route)  3.59 us
    ppermute x4, starting transfers between devices, swap(): lax.ppermute(block, axis, [(at, at ^ apart) for at in range(lax.axis_size...  3.17 us
  transfers between devices with their start and end apart: 6, of which 4 were waited for; matrix products, arithmetic and copies ran while one was open for 0% of the time, Pallas kernels for 8%

profile of v4, /device:TPU:0, one launch (start us, length us, event | category | flops | bytes accessed | tf_op | source)
XLA Modules:
  0.0 40.8 jit_solution(2274566431315887702)
XLA Ops:
  0.6 0.0 copy-start.9
  0.6 0.0 copy-start.11
  0.7 0.0 copy-start.12
  0.7 0.0 copy-start.13
  0.7 2.4 %shard_map.183 = (bf16[128,1152]{1,0:T(8,128)(2,1)}, bf16[32,1152]{1,0:T(8,128)(2,1)}, bf16[32,1152]{1,0:T(8,128)(2,1)}, f32[8,128]{1,0:T(8,128)}, f32[8,128]{1,0:T(8,128)}) custom-call(s32[32]{0:T(128)} %counts_ref.3, bf16[3,128,512]{2,1,0:T(8,128)(2,1)} %bitcast.7, s32[6,128]{1,0:T(8,128)} %bitcast.11, bf16[512,384]{1,0:T(8,128)(2,1)} %constant.27.pick_ref), custom_call_target="tpu_custom_call" | custom-call | flops 400000000 | bytes 789504 | tf_op jit(solution)/shard_map/pallas_call | solution.py:390
  3.1 0.0 copy-start.1
  3.1 2.9 %collective-permute-start.1 = (bf16[32,1152]{1,0:T(8,128)(2,1)}, bf16[32,1152]{1,0:T(8,128)(2,1)S(1)}, u32[]{:S(2)}, u32[]{:S(2)}) collective-permute-start(bf16[32,1152]{1,0:T(8,128)(2,1)} %get-tuple-element.21), channel_id=1, source_target_pairs={{0,4},{4,0},{8,12},{12,8},{16,20},{20,16},{24,28},{28,24},{1,5},{5... | collective-permute-start | bytes 221192 | tf_op jit(solution)/shard_map/ppermute | solution.py:132
  6.0 0.7 %collective-permute-start.2 = (bf16[32,1152]{1,0:T(8,128)(2,1)}, bf16[32,1152]{1,0:T(8,128)(2,1)S(1)}, u32[]{:S(2)}, u32[]{:S(2)}) collective-permute-start(bf16[32,1152]{1,0:T(8,128)(2,1)} %get-tuple-element.22), channel_id=1, source_target_pairs={{4,8},{8,4},{12,16},{16,12},{20,24},{24,20},{5,9},{9,5},{13,17},{1... | collective-permute-start | bytes 221192 | tf_op jit(solution)/shard_map/ppermute | solution.py:132
  6.7 1.6 %collective-permute-start.3 = (f32[8,128]{1,0:T(8,128)}, f32[8,128]{1,0:T(8,128)S(1)}, u32[]{:S(2)}, u32[]{:S(2)}) collective-permute-start(f32[8,128]{1,0:T(8,128)} %get-tuple-element.23), channel_id=1, source_target_pairs={{0,2},{1,3},{2,0},{3,1},{4,6},{5,7},{6,4},{7,5},{8,10},{9,11},{10,... | collective-permute-start | bytes 12296 | tf_op jit(solution)/shard_map/ppermute | solution.py:111
  8.3 0.0 collective-permute-start
  8.3 0.3 collective-permute-done.1
  8.6 0.0 collective-permute-done.2
  8.6 0.0 copy-start
  8.6 0.0 copy-start.2
  8.6 0.0 copy-start.3
  8.6 0.0 copy-start.8
  8.7 0.0 copy-start.14
  8.7 1.9 %collective-permute-done.3.spots_ref = f32[8,128]{1,0:T(8,128)S(1)} collective-permute-done((f32[8,128]{1,0:T(8,128)}, f32[8,128]{1,0:T(8,128)S(1)}, u32[]{:S(2)}, u32[]{:S(2)}) %collective-permute-start.3) | collective-permute-done | bytes 4128 | tf_op jit(solution)/shard_map/ppermute | solution.py:111
  10.6 0.0 collective-permute-start.4
  10.6 1.4 %collective-permute-done.4.refs_3_ = bf16[64,1152]{1,0:T(8,128)(2,1)S(1)} collective-permute-done((bf16[64,1152]{1,0:T(8,128)(2,1)S(1)}, bf16[64,1152]{1,0:T(8,128)(2,1)S(1)}, u32[]{:S(2)}, u32[]{:S(2)}) %collective-permute-start.4) | collective-permute-done | bytes 147488 | tf_op jit(solution)/shard_map/ppermute | solution.py:111
  12.0 0.0 collective-permute-done.refs_1_
  12.0 0.0 copy-done.1
  12.0 0.7 %shard_map.185 = bf16[128,1152]{1,0:T(8,128)(2,1)S(1)} custom-call(f32[8,128]{1,0:T(8,128)S(1)} %collective-permute-done.3.spots_ref, bf16[128,1152]{1,0:T(8,128)(2,1)S(1)} %copy-done.1, bf16[128,1152]{1,0:T(8,128)(2,1)S(1)} %collective-permute-done.refs_1_, bf16[64,1152]{1,0:T(8,128)(2,1)S(1)} %pad_maximum_fusion.refs_2_, ...), custom_call_target="tpu_custom_call" | custom-call | flops 400000000 | bytes 888832 | tf_op jit(solution)/shard_map/pallas_call | solution.py:390
  12.6 0.0 copy-start.15
  12.6 1.6 %collective-permute-start.5 = (bf16[128,1152]{1,0:T(8,128)(2,1)S(1)}, bf16[128,1152]{1,0:T(8,128)(2,1)S(1)}, u32[]{:S(2)}, u32[]{:S(2)}) collective-permute-start(bf16[128,1152]{1,0:T(8,128)(2,1)S(1)} %shard_map.185), channel_id=1, source_target_pairs={{0,2},{1,3},{2,0},{3,1},{4,6},{5,7},{6,4},{7,5},{8,10},{9,11},{10,... | collective-permute-start | bytes 884744 | tf_op jit(solution)/shard_map/ppermute | solution.py:111
  14.2 0.0 copy-start.4
  14.2 0.0 copy-start.5
  14.2 0.0 copy-start.6
  14.2 0.0 copy-done.9
  14.2 0.0 copy-done.11
  14.3 0.0 copy-done.12
  14.3 0.0 copy-done.13
  14.3 0.0 copy-done
  14.3 0.0 copy-done.2
  14.3 0.0 copy-done.3
  14.3 0.0 copy-done.8
  14.3 0.0 copy-done.14
  14.3 0.0 copy-done.15
  14.3 0.6 %copy-done.4 = s32[32]{0:T(128)S(1)} copy-done((s32[32]{0:T(128)S(1)}, s32[32]{0:T(128)}, u32[]{:S(2)}) %copy-start.4) | copy-done | bytes 152
  14.9 0.0 copy-done.5
  14.9 0.0 copy-done.6
  14.9 3.4 %shard_map.184 = (f32[3,128,512]{2,1,0:T(8,128)S(1)}, f32[128,512]{1,0:T(8,128)}, f32[8,128]{1,0:T(8,128)S(1)}, f32[256,256]{1,0:T(8,128)S(1)}) custom-call(s32[32]{0:T(128)S(1)} %copy-done.4, bf16[3,128,512]{2,1,0:T(8,128)(2,1)S(1)} %bitcast.8, bf16[128,512]{1,0:T(8,128)(2,1)S(1)} %copy-done.3, f32[128,512]{1,0:T(8,128)S(1)} %copy-done.2, ...), custom_call_target="tpu_custom_call" | custom-call | flops 2000000000 | bytes 3412992 | tf_op jit(solution)/shard_map/pallas_call | solution.py:390
  18.4 3.4 %collective-permute-done.5.refs_0_ = bf16[128,1152]{1,0:T(8,128)(2,1)S(1)} collective-permute-done((bf16[128,1152]{1,0:T(8,128)(2,1)S(1)}, bf16[128,1152]{1,0:T(8,128)(2,1)S(1)}, u32[]{:S(2)}, u32[]{:S(2)}) %collective-permute-start.5) | collective-permute-done | bytes 294944 | tf_op jit(solution)/shard_map/ppermute | solution.py:111
  21.8 0.0 copy-done.7
  21.8 0.0 copy-done.10
  21.8 2.3 %shard_map.186 = (f32[3,128,512]{2,1,0:T(8,128)}, f32[32,8,128]{2,1,0:T(8,128)S(1)}) custom-call(f32[3,128,512]{2,1,0:T(8,128)S(1)} %get-tuple-element.25.part_ref, f32[128,512]{1,0:T(8,128)S(1)} %copy-done.2, f32[8,128]{1,0:T(8,128)S(1)} %get-tuple-element.26.geom_ref, f32[64,128]{1,0:T(8,128)S(1)} %copy-done.14, bf16[384,512]{1,0:T(8,128)(2,1)S(1)} %copy-done.9, ...), custom_call_target="tpu_custom_call" | custom-call | flops 1000000000 | bytes 2658304 | tf_op jit(solution)/shard_map/pallas_call | solution.py:390
  24.1 15.9 %all_to_all.5.sums_ref = f32[32,8,128]{2,1,0:T(8,128)S(1)} all-to-all(f32[32,8,128]{2,1,0:T(8,128)S(1)} %get-tuple-element.30), channel_id=1, replica_groups=mesh['morton'=8,'sib'=4] {'morton','sib'}, dimensions={0} | all-to-all | bytes 262144 | tf_op jit(solution)/shard_map/all_to_all | solution.py:470
  40.0 0.8 %shard_map.187 = (f32[3,1,216]{2,1,0:T(1,128)}, f32[3,1,216]{2,1,0:T(1,128)}) custom-call(f32[32,8,128]{2,1,0:T(8,128)S(1)} %all_to_all.5.sums_ref, f32[256,256]{1,0:T(8,128)S(1)} %get-tuple-element.31.move_ref), custom_call_target="tpu_custom_call" | custom-call | flops 100000 | bytes 393216 | tf_op jit(solution)/shard_map/pallas_call | solution.py:390
  (3 shorter events, 0.0 us)
Async XLA Ops:
  0.6 13.6 %copy-start.9 = (bf16[384,512]{1,0:T(8,128)(2,1)S(1)}, bf16[384,512]{1,0:T(8,128)(2,1)}, u32[]{:S(2)}) copy-start(bf16[384,512]{1,0:T(8,128)(2,1)} %constant.30.spread_ref) | copy-start | bytes 1179652
  0.6 13.6 %copy-start.11 = (bf16[256,512]{1,0:T(8,128)(2,1)S(1)}, bf16[256,512]{1,0:T(8,128)(2,1)}, u32[]{:S(2)}) copy-start(bf16[256,512]{1,0:T(8,128)(2,1)} %constant.29.dyz_ref) | copy-start | bytes 786436
  0.7 13.6 %copy-start.12 = (s32[256,256]{1,0:T(8,128)S(1)}, s32[256,256]{1,0:T(8,128)}, u32[]{:S(2)}) copy-start(s32[256,256]{1,0:T(8,128)} %constant.25.clone.powers_ref) | copy-start | bytes 786436
  0.7 13.6 %copy-start.13 = (f32[256,256]{1,0:T(8,128)S(1)}, f32[256,256]{1,0:T(8,128)}, u32[]{:S(2)}) copy-start(f32[256,256]{1,0:T(8,128)} %constant.24.clone.shift_ref) | copy-start | bytes 786436
  3.1 8.9 %copy-start.1 = (bf16[128,1152]{1,0:T(8,128)(2,1)S(1)}, bf16[128,1152]{1,0:T(8,128)(2,1)}, u32[]{:S(2)}) copy-start(bf16[128,1152]{1,0:T(8,128)(2,1)} %get-tuple-element.20.refs_0_) | copy-start | bytes 884740
  3.1 5.5 %collective-permute-start.1 = (bf16[32,1152]{1,0:T(8,128)(2,1)}, bf16[32,1152]{1,0:T(8,128)(2,1)S(1)}, u32[]{:S(2)}, u32[]{:S(2)}) collective-permute-start(bf16[32,1152]{1,0:T(8,128)(2,1)} %get-tuple-element.21), channel_id=1, source_target_pairs={{0,4},{4,0},{8,12},{12,8},{16,20},{20,16},{24,28},{28,24},{1,5},{5... | collective-permute-start | bytes 221192 | tf_op jit(solution)/shard_map/ppermute | solution.py:132
  6.0 2.5 %collective-permute-start.2 = (bf16[32,1152]{1,0:T(8,128)(2,1)}, bf16[32,1152]{1,0:T(8,128)(2,1)S(1)}, u32[]{:S(2)}, u32[]{:S(2)}) collective-permute-start(bf16[32,1152]{1,0:T(8,128)(2,1)} %get-tuple-element.22), channel_id=1, source_target_pairs={{4,8},{8,4},{12,16},{16,12},{20,24},{24,20},{5,9},{9,5},{13,17},{1... | collective-permute-start | bytes 221192 | tf_op jit(solution)/shard_map/ppermute | solution.py:132
  6.7 3.9 %collective-permute-start.3 = (f32[8,128]{1,0:T(8,128)}, f32[8,128]{1,0:T(8,128)S(1)}, u32[]{:S(2)}, u32[]{:S(2)}) collective-permute-start(f32[8,128]{1,0:T(8,128)} %get-tuple-element.23), channel_id=1, source_target_pairs={{0,2},{1,3},{2,0},{3,1},{4,6},{5,7},{6,4},{7,5},{8,10},{9,11},{10,... | collective-permute-start | bytes 12296 | tf_op jit(solution)/shard_map/ppermute | solution.py:111
  8.3 3.7 %collective-permute-start = (bf16[128,1152]{1,0:T(8,128)(2,1)}, bf16[128,1152]{1,0:T(8,128)(2,1)S(1)}, u32[]{:S(2)}, u32[]{:S(2)}) collective-permute-start(bf16[128,1152]{1,0:T(8,128)(2,1)} %get-tuple-element.20.refs_0_), channel_id=1, source_target_pairs={{0,1},{1,0},{2,3},{3,2},{4,5},{5,4},{6,7},{7,6},{8,9},{9,8},{10,11... | collective-permute-start | bytes 884744 | tf_op jit(solution)/shard_map/ppermute | solution.py:111
  8.6 5.7 %copy-start = (bf16[128,3,512]{2,0,1:T(8,128)(2,1)S(1)}, bf16[128,3,512]{2,0,1:T(8,128)(2,1)}, u32[]{:S(2)}) copy-start(bf16[128,3,512]{2,0,1:T(8,128)(2,1)} %param.16) | copy-start | bytes 1179652
  8.6 5.7 %copy-start.2 = (f32[128,512]{1,0:T(8,128)S(1)}, f32[128,512]{1,0:T(8,128)}, u32[]{:S(2)}) copy-start(f32[128,512]{1,0:T(8,128)} %visc_ref.3) | copy-start | bytes 786436
  8.6 5.7 %copy-start.3 = (bf16[128,512]{1,0:T(8,128)(2,1)S(1)}, bf16[128,512]{1,0:T(8,128)(2,1)}, u32[]{:S(2)}) copy-start(bf16[128,512]{1,0:T(8,128)(2,1)} %press_ref.1) | copy-start | bytes 393220
  8.6 5.7 %copy-start.8 = (bf16[512,512]{1,0:T(8,128)(2,1)S(1)}, bf16[512,512]{1,0:T(8,128)(2,1)}, u32[]{:S(2)}) copy-start(bf16[512,512]{1,0:T(8,128)(2,1)} %constant.28.dx_ref) | copy-start | bytes 1572868
  8.7 5.7 %copy-start.14 = (f32[64,128]{1,0:T(8,128)S(1)}, f32[64,128]{1,0:T(8,128)}, u32[]{:S(2)}) copy-start(f32[64,128]{1,0:T(8,128)} %constant.23.clone.box_ref) | copy-start | bytes 98308
  10.6 1.4 %collective-permute-start.4 = (bf16[64,1152]{1,0:T(8,128)(2,1)S(1)}, bf16[64,1152]{1,0:T(8,128)(2,1)S(1)}, u32[]{:S(2)}, u32[]{:S(2)}) collective-permute-start(bf16[64,1152]{1,0:T(8,128)(2,1)S(1)} %pad_maximum_fusion.refs_2_), channel_id=1, source_target_pairs={{0,1},{1,0},{2,3},{3,2},{4,5},{5,4},{6,7},{7,6},{8,9},{9,8},{10,11... | collective-permute-start | bytes 442376 | tf_op jit(solution)/shard_map/ppermute | solution.py:111
  12.6 1.7 %copy-start.15 = (f32[8,128]{1,0:T(8,128)S(1)}, f32[8,128]{1,0:T(8,128)}, u32[]{:S(2)}) copy-start(f32[8,128]{1,0:T(8,128)} %get-tuple-element.19.spots_ref) | copy-start | bytes 12292
  12.6 9.1 %collective-permute-start.5 = (bf16[128,1152]{1,0:T(8,128)(2,1)S(1)}, bf16[128,1152]{1,0:T(8,128)(2,1)S(1)}, u32[]{:S(2)}, u32[]{:S(2)}) collective-permute-start(bf16[128,1152]{1,0:T(8,128)(2,1)S(1)} %shard_map.185), channel_id=1, source_target_pairs={{0,2},{1,3},{2,0},{3,1},{4,6},{5,7},{6,4},{7,5},{8,10},{9,11},{10,... | collective-permute-start | bytes 884744 | tf_op jit(solution)/shard_map/ppermute | solution.py:111
  14.2 0.7 %copy-start.4 = (s32[32]{0:T(128)S(1)}, s32[32]{0:T(128)}, u32[]{:S(2)}) copy-start(s32[32]{0:T(128)} %counts_ref.3) | copy-start | bytes 388
  14.2 0.7 %copy-start.5 = (s32[128]{0:T(128)S(1)}, s32[128]{0:T(128)}, u32[]{:S(2)}) copy-start(s32[128]{0:T(128)} %param.19) | copy-start | bytes 1540
  14.2 0.7 %copy-start.6 = (s32[128]{0:T(128)S(1)}, s32[128]{0:T(128)}, u32[]{:S(2)}) copy-start(s32[128]{0:T(128)} %param.20) | copy-start | bytes 1540
  14.9 6.9 %copy-start.7 = (bf16[576,512]{1,0:T(8,128)(2,1)S(1)}, bf16[576,512]{1,0:T(8,128)(2,1)}, u32[]{:S(2)}) copy-start(bf16[576,512]{1,0:T(8,128)(2,1)} %constant.22.clone.basis_ref) | copy-start | bytes 1769476
  14.9 6.9 %copy-start.10 = (f32[288,256]{1,0:T(8,128)S(1)}, f32[288,256]{1,0:T(8,128)}, u32[]{:S(2)}) copy-start(f32[288,256]{1,0:T(8,128)} %constant.26.clone.compact_ref) | copy-start | bytes 884740

commit v5 on v4

--- a/solution.py
+++ b/solution.py
@@ -142,7 +142,9 @@
     )
 
 
-def pack_kernel(counts_ref, vel_ref, nbrs_ref, pick_ref, faces_ref, even_ref, odd_ref, *spots_refs):
+def pack_kernel(
+    counts_ref, vel_ref, nbrs_ref, levels_ref, keys_ref, box_ref, pick_ref, faces_ref, even_ref, odd_ref, *spots_refs
+):
     sib_count = lax.axis_size("sib")
     morton = lax.axis_index("morton")
     sib = lax.axis_index("sib")
@@ -177,49 +179,60 @@
         band_start = jnp.where(owner_sib == other, counts_ref[below + other] - BAND, band_start)
     below_at = BAND * (1 - jnp.bitwise_and(morton, 1))
     in_band = jnp.where(step < 0, slot - band_start + below_at, slot + BAND - below_at)
+    box = box_ref[pl.ds(pl.multiple_of(morton * 8, 8), 8), :]
+    shift_bits = 3 * (LMAX - levels_ref[...])
+    anchor = jnp.left_shift(jnp.right_shift(keys_ref[...], shift_bits), shift_bits)
+    span = jnp.left_shift(jnp.ones_like(shift_bits), LMAX - levels_ref[...]).astype(f32)
+    finest = 1.0 / float(2**LMAX)
+    places = []
+    for dim, offset in enumerate((2, 1, 0)):
+        cell = jnp.zeros_like(anchor)
+        for bit in range(LMAX):
+            picked = jnp.bitwise_and(jnp.right_shift(anchor, 3 * bit + offset), 1)
+            cell = cell + jnp.left_shift(picked, bit)
+        center = (cell.astype(f32) + 0.5 * span) * finest
+        places.append((center - box[4 + dim : 5 + dim, :]) * box[7:8, :])
+    places.append(0.5 * span * finest * box[7:8, :])
+    places.append(jnp.zeros((4, leaf_count), f32))
+    geom = jnp.concatenate(places, axis=0)
     for side, spots_ref in enumerate(spots_refs):
         piece = jnp.bitwise_xor(owner_sib, jnp.bitwise_xor(sib, 2 * side))
         spot = jnp.where(step == 0, piece * leaf_count + slot, 2 * leaf_count + piece * (2 * BAND) + in_band)
         spot = jnp.where((nbrs >= 0) & (piece < 2), spot, -1).astype(f32)
-        spots_ref[...] = jnp.concatenate([spot, jnp.full((2, leaf_count), -1.0, f32)], axis=0)
-
-
-def gathered(spots, window_refs):
-    leaf_count = spots.shape[1]
+        spots_ref[...] = jnp.concatenate([spot, jnp.full((2, leaf_count), -1.0, f32), geom], axis=0)
+
+
+def gathered(asked, window_refs):
+    leaf_count = asked[0].shape[1]
     rows = sum(ref.shape[0] for ref in window_refs)
-    filled = jnp.concatenate([spots, jnp.full((LANES - spots.shape[0], leaf_count), -1.0, f32)], axis=0)
-    places = filled.T.astype(jnp.int32)
+    blank = jnp.full((LANES - 8 * len(asked), leaf_count), -1.0, f32)
+    places = jnp.concatenate([spots[:8] for spots in asked] + [blank], axis=0).T.astype(jnp.int32)
     cols = lax.broadcasted_iota(jnp.int32, (leaf_count, rows), 1)
     upper = jnp.bitwise_and(lax.broadcasted_iota(jnp.int32, (leaf_count, FACES), 1), 64) > 0
-    chosen = []
+    chosen = [[] for _ in asked]
     for dim in range(3):
         at = dim * FACES
         window = jnp.concatenate([ref[:, at : at + FACES] for ref in window_refs], axis=0)
-        faces = (2 * dim, 2 * dim + 1)
+        faces = [8 * who + face for who in range(len(asked)) for face in (2 * dim, 2 * dim + 1)]
         onehot = [jnp.where(cols == places[:, face : face + 1], 1.0, 0.0).astype(bf16) for face in faces]
-        both = dot(jnp.concatenate(onehot, axis=0), window)
-        chosen.append(jnp.where(upper, both[:leaf_count], both[leaf_count:]).astype(bf16))
+        found = dot(jnp.concatenate(onehot, axis=0), window)
+        for who in range(len(asked)):
+            first, second = (found[(2 * who + side) * leaf_count : (2 * who + side + 1) * leaf_count] for side in (0, 1))
+            chosen[who].append(jnp.where(upper, first, second).astype(bf16))
     return chosen
 
 
-def spread_out(chosen, spread):
+def by_comp(chosen):
     comps = [
         jnp.concatenate([block[:, comp * LANES : (comp + 1) * LANES] for block in chosen], axis=1) for comp in range(3)
     ]
-    return dot(jnp.concatenate(comps, axis=0), spread)
-
-
-def serve_kernel(spots_ref, *refs):
-    window_refs, out_ref = refs[:-1], refs[-1]
-    for dim, block in enumerate(gathered(spots_ref[...], window_refs)):
-        out_ref[:, dim * FACES : (dim + 1) * FACES] = block
+    return jnp.concatenate(comps, axis=0)
 
 
 def pre_kernel(
-    counts_ref, vel_ref, press_ref, visc_ref, levels_ref, keys_ref, spots_ref, dx_ref, dyz_ref, box_ref,
-    shift_ref, powers_ref, spread_ref, *refs,
+    counts_ref, vel_ref, press_ref, visc_ref, dx_ref, dyz_ref, box_ref, shift_ref, powers_ref,
+    part_ref, mass_ref, move_ref,
 ):
-    window_refs, (part_ref, mass_ref, geom_ref, move_ref) = refs[:-4], refs[-4:]
     sib_count = lax.axis_size("sib")
     morton_count = lax.axis_size("morton")
     morton = lax.axis_index("morton")
@@ -256,28 +269,12 @@
         for at in (0, 256)
     ]
     div = dot(columns[0], dx_ref[...]) + jnp.concatenate(rest, axis=1)
-    nearby = spread_out(gathered(spots_ref[...], window_refs), spread_ref[...])
     for comp in range(3):
-        jump = touching * vel_ref[comp].astype(f32) - rows(nearby, comp)
+        jump = touching * vel_ref[comp].astype(f32)
         part = (penalty * visc * jump - rows(div, comp) + rows(grads[comp], 3)) * out_scale
         part_ref[comp] = jnp.where(live, part, 0.0)
 
     box = box_ref[pl.ds(pl.multiple_of(morton * 8, 8), 8), :]
-    shift_bits = 3 * (LMAX - levels_ref[...])
-    anchor = jnp.left_shift(jnp.right_shift(keys_ref[...], shift_bits), shift_bits)
-    span = jnp.left_shift(jnp.ones_like(shift_bits), LMAX - levels_ref[...]).astype(f32)
-    finest = 1.0 / float(2**LMAX)
-    places = []
-    for dim, offset in enumerate((2, 1, 0)):
-        cell = jnp.zeros_like(anchor)
-        for bit in range(LMAX):
-            picked = jnp.bitwise_and(jnp.right_shift(anchor, 3 * bit + offset), 1)
-            cell = cell + jnp.left_shift(picked, bit)
-        center = (cell.astype(f32) + 0.5 * span) * finest
-        places.append((center - box[4 + dim : 5 + dim, :]) * box[7:8, :])
-    places.append(0.5 * span * finest * box[7:8, :])
-    places.append(jnp.zeros((4, leaf_count), f32))
-    geom_ref[...] = jnp.concatenate(places, axis=0)
     move = shift_ref[...]
     powers = powers_ref[...]
     for dim in range(3):
@@ -316,38 +313,41 @@
     return tiles
 
 
-def post_kernel(
-    part_ref, visc_ref, geom_ref, box_ref, spread_ref, basis_ref, compact_ref, *refs
+def moment_kernel(
+    part_ref, visc_ref, box_ref, spread_ref, basis_ref, compact_ref, spots_ref, *refs
 ):
-    got_refs, (force_hbm, sums_ref, force_ref, raw_ref, sems) = refs[:-5], refs[-5:]
+    sides = lax.axis_size("sib") // 2
+    window_refs = refs[:4]
+    asked_refs, their_visc_refs = refs[4 : 3 + sides], refs[3 + sides : 2 + 2 * sides]
+    near_ref, served_refs, sums_ref, raw_ref = refs[2 + 2 * sides], refs[3 + 2 * sides : -2], refs[-2], refs[-1]
     morton = lax.axis_index("morton")
     leaf_count = visc_ref.shape[0]
-    chosen = []
-    for dim in range(3):
-        lanes = slice(dim * FACES, (dim + 1) * FACES)
-        chosen.append(got_refs[0][:, lanes])
-        for got_ref in got_refs[1:]:
-            chosen[dim] = chosen[dim] + got_ref[:, lanes]
-    jumps = spread_out(chosen, spread_ref[...])
-    weight = visc_ref[...] * (penalty * out_scale)
-    highs, lows, stores = [], [], []
-    for comp in range(3):
-        force = part_ref[comp] - weight * jumps[comp * leaf_count : (comp + 1) * leaf_count]
-        force_ref[comp] = force
-        stores.append(pltpu.make_async_copy(force_ref.at[comp], force_hbm.at[comp], sems.at[comp]))
-        stores[-1].start()
-        high = force.astype(bf16)
-        highs.append(high)
-        lows.append((force - high.astype(f32)).astype(bf16))
+    asked = [spots_ref[...]] + [ref[...] for ref in asked_refs]
+    chosen = gathered(asked, window_refs)
+    for blocks, out_ref in zip(chosen, (near_ref, *served_refs)):
+        for dim, block in enumerate(blocks):
+            out_ref[:, dim * FACES : (dim + 1) * FACES] = block
+    jumps = dot(jnp.concatenate([by_comp(blocks) for blocks in chosen], axis=0), spread_ref[...])
+    highs, lows = [], []
+    for who, ref in enumerate((visc_ref, *their_visc_refs)):
+        weight = ref[...] * (penalty * out_scale)
+        for comp in range(3):
+            at = (3 * who + comp) * leaf_count
+            force = -weight * jumps[at : at + leaf_count]
+            if who == 0:
+                force = force + part_ref[comp]
+            high = force.astype(bf16)
+            highs.append(high)
+            lows.append((force - high.astype(f32)).astype(bf16))
     high = jnp.concatenate(highs, axis=0)
     low = jnp.concatenate(lows, axis=0)
     raw = dot_nt(basis_ref[...], high)
     raw_ref[...] = raw[:ROWS] + raw[ROWS:] + dot_nt(basis_ref[:ROWS, :], low)
-    geom = jnp.concatenate([geom_ref[...]] * 3, axis=1)
+    geom = jnp.concatenate([spots[8:] for spots in asked for _ in range(3)], axis=1)
     tiles = shifted([raw_ref[8 * at : 8 * at + 8, :] for at in range(36)], geom)
     moved = jnp.concatenate(tiles, axis=0)
-    group = lax.broadcasted_iota(jnp.int32, (3 * leaf_count, LANES), 0) // leaf_count
-    column = lax.broadcasted_iota(jnp.int32, (3 * leaf_count, LANES), 1)
+    group = lax.broadcasted_iota(jnp.int32, (raw_ref.shape[1], LANES), 0) // leaf_count % 3
+    column = lax.broadcasted_iota(jnp.int32, (raw_ref.shape[1], LANES), 1)
     gather = jnp.where((group == column) | (group + 3 == column), 1.0, 0.0)
     summed = jnp.dot(moved, gather, precision=highest, preferred_element_type=f32)
     box = box_ref[pl.ds(pl.multiple_of(morton * 8, 8), 8), :]
@@ -360,6 +360,21 @@
     sib_count = lax.axis_size("sib")
     for other in range(sums_ref.shape[0]):
         sums_ref[other] = jnp.where(morton == other // sib_count, to_box, to_root)
+
+
+def force_kernel(part_ref, visc_ref, spread_ref, near_ref, *refs):
+    got_refs, (force_hbm, force_ref, sems) = refs[:-3], refs[-3:]
+    faces = near_ref[...]
+    for got_ref in got_refs:
+        faces = faces + got_ref[...]
+    weight = visc_ref[...] * (penalty * out_scale)
+    stores = []
+    for comp in range(3):
+        lanes = [(dim * 3 + comp) * LANES for dim in range(3)]
+        jump = dot(jnp.concatenate([faces[:, at : at + LANES] for at in lanes], axis=1), spread_ref[...])
+        force_ref[comp] = part_ref[comp] - weight * jump
+        stores.append(pltpu.make_async_copy(force_ref.at[comp], force_hbm.at[comp], sems.at[comp]))
+        stores[-1].start()
     for store in stores:
         store.wait()
 
@@ -414,6 +429,8 @@
     width = 3 * FACES
     sib_count = lax.axis_size("sib")
     sides = sib_count // 2
+    other_sides = [2 * side for side in range(1, sides)]
+    their_visc = [swap(viscosity, "sib", apart) for apart in other_sides]
     faces, even, odd, *spots = call(
         pack_kernel,
         [
@@ -421,53 +438,50 @@
             ((BAND, width), bf16),
             ((BAND, width), bf16),
         ]
-        + [((8, leaf_count), f32)] * sides,
+        + [((16, leaf_count), f32)] * sides,
         4 * 10**8,
         [counts],
-        [vel, nbrs, pick],
+        [vel, nbrs, levels.reshape(1, -1), morton_keys.reshape(1, -1), boxes, pick],
         grant=60,
     )
-    asked = [swap(spots[side], "sib", 2 * side) for side in range(1, sides)]
+    asked = [swap(block, "sib", apart) for block, apart in zip(spots[1:], other_sides)]
     bands = jnp.concatenate([pairs(even, 0), pairs(odd, 1)], axis=0)
-    bands, *asked = lax.optimization_barrier((bands, *asked))
     window = [faces, swap(faces, "sib", 1), bands, swap(bands, "sib", 1)]
-    got = []
-    for side in range(1, sides):
-        (served,) = call(
-            serve_kernel, [((leaf_count, width), bf16)], 4 * 10**8, [], [asked[side - 1], *window]
-        )
-        got.append(swap(served, "sib", 2 * side))
-
     shift, powers = move_tables(morton_count)
-    part, continuity, geom, move = call(
+    part, continuity, move = call(
         pre_kernel,
         [
             ((3, leaf_count, NODES), f32),
             ((leaf_count, NODES), f32),
-            ((8, leaf_count), f32),
             ((256, 256), f32),
         ],
         2 * 10**9,
         [counts],
+        [vel, pressure, viscosity, dx_table, dyz_table, boxes, jnp.asarray(shift), jnp.asarray(powers)],
+    )
+    near, *served, sums = call(
+        moment_kernel,
+        [((leaf_count, width), bf16)] * sides + [((morton_count * sib_count, 8, LANES), f32)],
+        2 * 10**9,
+        [],
         [
-            vel, pressure, viscosity, levels.reshape(1, -1), morton_keys.reshape(1, -1), spots[0],
-            dx_table, dyz_table, boxes, jnp.asarray(shift), jnp.asarray(powers), spread, *window,
+            part, viscosity, boxes, spread, basis, jnp.asarray(compact_table()), spots[0],
+            *window, *asked, *their_visc,
         ],
-    )
-    force, sums = call(
-        post_kernel,
-        [((3, leaf_count, NODES), f32), ((morton_count * sib_count, 8, LANES), f32)],
-        10**9,
+        [pltpu.VMEM((ROWS, 3 * sides * leaf_count), f32)],
+    )
+    got = [swap(block, "sib", apart) for block, apart in zip(served, other_sides)]
+    every = lax.all_to_all(sums, ("morton", "sib"), 0, 0, tiled=True)
+    every, *got = lax.optimization_barrier((every, *got))
+    (force,) = call(
+        force_kernel,
+        [((3, leaf_count, NODES), f32)],
+        2 * 10**8,
         [],
-        [part, viscosity, geom, boxes, spread, basis, jnp.asarray(compact_table()), *got],
-        [
-            pltpu.VMEM((3, leaf_count, NODES), f32),
-            pltpu.VMEM((ROWS, 3 * leaf_count), f32),
-            pltpu.SemaphoreType.DMA((3,)),
-        ],
-        outs=[pltpu.HBM, pltpu.VMEM],
-    )
-    every = lax.all_to_all(sums, ("morton", "sib"), 0, 0, tiled=True)
+        [part, viscosity, spread, near, *got],
+        [pltpu.VMEM((3, leaf_count, NODES), f32), pltpu.SemaphoreType.DMA((3,))],
+        outs=[pltpu.HBM],
+    )
     box, root = call(
         final_kernel,
         [((3, 1, MOMENTS), f32), ((3, 1, MOMENTS), f32)],

time: 41 us -> 41 us (level)
  waiting for transfers between devices: 7 us -> 0.02 us
  Pallas kernels: 9.66 us -> 11.9 us
  blocking collectives: 15.9 us -> 17.8 us
  local copies, waits for them, and re-layouts: 0.66 us -> 2.12 us
  starting transfers between devices: 6.77 us -> 8.09 us
    ppermute x4 -> x5, waiting for transfers between devices: 6.7 us -> 0.01 us  [swap(): lax.ppermute(block, axis, [(at, at ^ apart) for at in range(lax.axis_size...]
    pallas_call x5, Pallas kernels: 9.66 us -> 11.9 us  [call(): pl.pallas_call(kernel, out_shape=[jax.ShapeDtypeStruct(shape, dtype) for...]
    all_to_all x1, blocking collectives: 15.9 us -> 17.8 us  [on_device(): every = lax.all_to_all(sums, ('morton', 'sib'), 0, 0, tiled=True)]
    unnamed x32 -> x29, local copies, waits for them, and re-layouts: 0.66 us -> 2.11 us
    ppermute x4 -> x5, starting transfers between devices: 3.17 us -> 4.5 us  [swap(): lax.ppermute(block, axis, [(at, at ^ apart) for at in range(lax.axis_size...]
  transfers between devices with their start and end apart: 6 -> 7, of which waited for: 4 -> 0; matrix products, arithmetic and copies ran while one was open for 0% -> 0% of each run, Pallas kernels for 8% -> 7%
where the time goes in v5:
time: 41 us; the launch traced here: 40.7 us
  blocking collectives  17.8 us (43%)
  Pallas kernels  11.9 us (29%)
  starting transfers between devices  8.09 us (20%)
  local copies, waits for them, and re-layouts  2.12 us (5%)
  between operations  0.83 us (2%)
    all_to_all x1, blocking collectives, on_device(): every = lax.all_to_all(sums, ('morton', 'sib'), 0, 0, tiled=True)  17.8 us
    pallas_call x5, Pallas kernels, call(): pl.pallas_call(kernel, out_shape=[jax.ShapeDtypeStruct(shape, dtype) for...  11.9 us
    ppermute x5, starting transfers between devices, swap(): lax.ppermute(block, axis, [(at, at ^ apart) for at in range(lax.axis_size...  4.5 us
    ppermute x2, starting transfers between devices, pairs(): return lax.ppermute(block, 'morton', route)  3.59 us
    unnamed x29, local copies, waits for them, and re-layouts  2.11 us
  transfers between devices with their start and end apart: 7, of which 0 were waited for; matrix products, arithmetic and copies ran while one was open for 0% of the time, Pallas kernels for 7%

profile of v5, /device:TPU:0, one launch (start us, length us, event | category | flops | bytes accessed | tf_op | source)
XLA Modules:
  0.0 40.7 jit_solution(12417681918950876587)
XLA Ops:
  0.6 0.0 copy-start.1
  0.6 0.0 copy-start.2
  0.7 0.0 copy-start.7
  0.7 0.0 copy-start.9
  0.7 2.5 %shard_map.184 = (bf16[128,1152]{1,0:T(8,128)(2,1)}, bf16[32,1152]{1,0:T(8,128)(2,1)}, bf16[32,1152]{1,0:T(8,128)(2,1)}, f32[16,128]{1,0:T(8,128)}, f32[16,128]{1,0:T(8,128)}) custom-call(s32[32]{0:T(128)} %counts_ref.3, bf16[3,128,512]{2,1,0:T(8,128)(2,1)} %bitcast.7, s32[6,128]{1,0:T(8,128)} %bitcast.10, s32[1,128]{1,0:T(1,128)} %bitcast.13, ...), custom_call_target="tpu_custom_call" | custom-call | flops 400000000 | bytes 823296 | tf_op jit(solution)/shard_map/pallas_call | solution.py:405
  3.2 2.9 %collective-permute-start.1 = (bf16[32,1152]{1,0:T(8,128)(2,1)}, bf16[32,1152]{1,0:T(8,128)(2,1)S(1)}, u32[]{:S(2)}, u32[]{:S(2)}) collective-permute-start(bf16[32,1152]{1,0:T(8,128)(2,1)} %get-tuple-element.22), channel_id=1, source_target_pairs={{0,4},{4,0},{8,12},{12,8},{16,20},{20,16},{24,28},{28,24},{1,5},{5... | collective-permute-start | bytes 221192 | tf_op jit(solution)/shard_map/ppermute | solution.py:132
  6.1 0.0 copy-done.1
  6.1 1.5 %collective-permute-start.5 = (f32[128,512]{1,0:T(8,128)S(1)}, f32[128,512]{1,0:T(8,128)S(1)}, u32[]{:S(2)}, u32[]{:S(2)}) collective-permute-start(f32[128,512]{1,0:T(8,128)S(1)} %copy-done.1), channel_id=1, source_target_pairs={{0,2},{1,3},{2,0},{3,1},{4,6},{5,7},{6,4},{7,5},{8,10},{9,11},{10,... | collective-permute-start | bytes 786440 | tf_op jit(solution)/shard_map/ppermute | solution.py:111
  7.6 0.5 %collective-permute-start.4 = (f32[16,128]{1,0:T(8,128)}, f32[16,128]{1,0:T(8,128)S(1)}, u32[]{:S(2)}, u32[]{:S(2)}) collective-permute-start(f32[16,128]{1,0:T(8,128)} %get-tuple-element.24), channel_id=1, source_target_pairs={{0,2},{1,3},{2,0},{3,1},{4,6},{5,7},{6,4},{7,5},{8,10},{9,11},{10,... | collective-permute-start | bytes 24584 | tf_op jit(solution)/shard_map/ppermute | solution.py:111
  8.1 0.7 %collective-permute-start.2 = (bf16[32,1152]{1,0:T(8,128)(2,1)}, bf16[32,1152]{1,0:T(8,128)(2,1)S(1)}, u32[]{:S(2)}, u32[]{:S(2)}) collective-permute-start(bf16[32,1152]{1,0:T(8,128)(2,1)} %get-tuple-element.23), channel_id=1, source_target_pairs={{4,8},{8,4},{12,16},{16,12},{20,24},{24,20},{5,9},{9,5},{13,17},{1... | collective-permute-start | bytes 221192 | tf_op jit(solution)/shard_map/ppermute | solution.py:132
  8.8 0.0 copy-start.4
  8.8 0.1 collective-permute-start
  8.9 0.0 collective-permute-done.1
  8.9 0.0 copy-start.5
  8.9 0.0 copy-start.12
  8.9 0.0 collective-permute-done.2
  9.0 0.0 copy-start
  9.0 0.0 copy-start.3
  9.0 0.0 copy-start.6
  9.0 0.0 copy-start.8
  9.0 0.5 %collective-permute-start.3 = (bf16[64,1152]{1,0:T(8,128)(2,1)S(1)}, bf16[64,1152]{1,0:T(8,128)(2,1)S(1)}, u32[]{:S(2)}, u32[]{:S(2)}) collective-permute-start(bf16[64,1152]{1,0:T(8,128)(2,1)S(1)} %constant_dynamic-update-slice_fusion.refs_2_), channel_id=1, source_target_pairs={{0,1},{1,0},{2,3},{3,2},{4,5},{5,4},{6,7},{7,6},{8,9},{9,8},{10,11... | collective-permute-start | bytes 442376 | tf_op jit(solution)/shard_map/ppermute | solution.py:111
  9.6 0.0 copy-done.2
  9.6 0.0 copy-done.7
  9.6 0.0 copy-done.9
  9.6 0.1 copy-done.4
  9.7 0.0 copy-done.5
  9.7 0.0 copy-done.12
  9.7 0.0 copy-start.10
  9.7 0.9 %copy-done.10 = s32[256,256]{1,0:T(8,128)S(1)} copy-done((s32[256,256]{1,0:T(8,128)S(1)}, s32[256,256]{1,0:T(8,128)}, u32[]{:S(2)}) %copy-start.10) | copy-done | bytes 262168
  10.7 0.0 copy-start.11
  10.7 0.9 %copy-done.11 = f32[256,256]{1,0:T(8,128)S(1)} copy-done((f32[256,256]{1,0:T(8,128)S(1)}, f32[256,256]{1,0:T(8,128)}, u32[]{:S(2)}) %copy-start.11) | copy-done | bytes 262168
  11.6 0.0 copy-start.13
  11.6 2.7 %shard_map.183 = (f32[3,128,512]{2,1,0:T(8,128)S(1)}, f32[128,512]{1,0:T(8,128)}, f32[256,256]{1,0:T(8,128)S(1)}) custom-call(s32[32]{0:T(128)S(1)} %copy-done.5, bf16[3,128,512]{2,1,0:T(8,128)(2,1)S(1)} %bitcast.8, bf16[128,512]{1,0:T(8,128)(2,1)S(1)} %copy-done.4, f32[128,512]{1,0:T(8,128)S(1)} %copy-done.1, bf16[512,512]{1,0:T(8,128)(2,1)S(1)} %copy-done.7, ...), custom_call_target="tpu_custom_call" | custom-call | flops 2000000000 | bytes 2129920 | tf_op jit(solution)/shard_map/pallas_call | solution.py:405
  14.3 0.0 collective-permute-done.4.refs_4_
  14.3 0.0 collective-permute-done.3.refs_3_
  14.4 0.0 collective-permute-done.5.refs_5_
  14.4 0.0 collective-permute-done.refs_1_
  14.4 0.0 copy-done
  14.4 0.0 copy-done.3
  14.4 0.0 copy-done.6
  14.4 0.0 copy-done.8
  14.4 0.0 copy-done.13
  14.4 4.7 %shard_map.185 = (bf16[128,1152]{1,0:T(8,128)(2,1)S(1)}, bf16[128,1152]{1,0:T(8,128)(2,1)S(1)}, f32[32,8,128]{2,1,0:T(8,128)S(1)}) custom-call(f32[3,128,512]{2,1,0:T(8,128)S(1)} %get-tuple-element.19.part_ref, f32[128,512]{1,0:T(8,128)S(1)} %copy-done.1, f32[64,128]{1,0:T(8,128)S(1)} %copy-done.12, bf16[384,512]{1,0:T(8,128)(2,1)S(1)} %copy-done, ...), custom_call_target="tpu_custom_call" | custom-call | flops 2000000000 | bytes 3522560 | tf_op jit(solution)/shard_map/pallas_call | solution.py:405
  19.1 1.9 %collective-permute-start.6 = (bf16[128,1152]{1,0:T(8,128)(2,1)S(1)}, bf16[128,1152]{1,0:T(8,128)(2,1)S(1)}, u32[]{:S(2)}, u32[]{:S(2)}) collective-permute-start(bf16[128,1152]{1,0:T(8,128)(2,1)S(1)} %get-tuple-element.27), channel_id=1, source_target_pairs={{0,2},{1,3},{2,0},{3,1},{4,6},{5,7},{6,4},{7,5},{8,10},{9,11},{10,... | collective-permute-start | bytes 884744 | tf_op jit(solution)/shard_map/ppermute | solution.py:111
  21.0 17.8 %all_to_all.5.sums_ref = f32[32,8,128]{2,1,0:T(8,128)S(1)} all-to-all(f32[32,8,128]{2,1,0:T(8,128)S(1)} %get-tuple-element.26), channel_id=1, replica_groups=mesh['morton'=8,'sib'=4] {'morton','sib'}, dimensions={0} | all-to-all | bytes 262144 | tf_op jit(solution)/shard_map/all_to_all | solution.py:474
  38.8 0.0 collective-permute-done.6.refs_0_
  38.8 0.8 %shard_map.187 = (f32[3,1,216]{2,1,0:T(1,128)}, f32[3,1,216]{2,1,0:T(1,128)}) custom-call(f32[32,8,128]{2,1,0:T(8,128)S(1)} %all_to_all.5.sums_ref, f32[256,256]{1,0:T(8,128)S(1)} %get-tuple-element.31.move_ref), custom_call_target="tpu_custom_call" | custom-call | flops 100000 | bytes 393216 | tf_op jit(solution)/shard_map/pallas_call | solution.py:405
  39.6 1.1 %shard_map.186 = f32[3,128,512]{2,1,0:T(8,128)} custom-call(f32[3,128,512]{2,1,0:T(8,128)S(1)} %get-tuple-element.19.part_ref, f32[128,512]{1,0:T(8,128)S(1)} %copy-done.1, bf16[384,512]{1,0:T(8,128)(2,1)S(1)} %copy-done, bf16[128,1152]{1,0:T(8,128)(2,1)S(1)} %get-tuple-element.25.near_ref, bf16[128,1152]{1,0:T(8,128)(2,1)S(1)} %collective-permute-done.6.refs_0_), custom_call_target="tpu_custom_call" | custom-call | flops 200000000 | bytes 2031616 | tf_op jit(solution)/shard_map/pallas_call | solution.py:405
  (2 shorter events, 0.0 us)
Async XLA Ops:
  0.6 5.5 %copy-start.1 = (f32[128,512]{1,0:T(8,128)S(1)}, f32[128,512]{1,0:T(8,128)}, u32[]{:S(2)}) copy-start(f32[128,512]{1,0:T(8,128)} %visc_ref.5) | copy-start | bytes 786436
  0.6 8.9 %copy-start.2 = (bf16[128,3,512]{2,0,1:T(8,128)(2,1)S(1)}, bf16[128,3,512]{2,0,1:T(8,128)(2,1)}, u32[]{:S(2)}) copy-start(bf16[128,3,512]{2,0,1:T(8,128)(2,1)} %param.16) | copy-start | bytes 1179652
  0.7 8.9 %copy-start.7 = (bf16[512,512]{1,0:T(8,128)(2,1)S(1)}, bf16[512,512]{1,0:T(8,128)(2,1)}, u32[]{:S(2)}) copy-start(bf16[512,512]{1,0:T(8,128)(2,1)} %constant.27.dx_ref) | copy-start | bytes 1572868
  0.7 8.9 %copy-start.9 = (bf16[256,512]{1,0:T(8,128)(2,1)S(1)}, bf16[256,512]{1,0:T(8,128)(2,1)}, u32[]{:S(2)}) copy-start(bf16[256,512]{1,0:T(8,128)(2,1)} %constant.28.dyz_ref) | copy-start | bytes 786436
  3.2 5.7 %collective-permute-start.1 = (bf16[32,1152]{1,0:T(8,128)(2,1)}, bf16[32,1152]{1,0:T(8,128)(2,1)S(1)}, u32[]{:S(2)}, u32[]{:S(2)}) collective-permute-start(bf16[32,1152]{1,0:T(8,128)(2,1)} %get-tuple-element.22), channel_id=1, source_target_pairs={{0,4},{4,0},{8,12},{12,8},{16,20},{20,16},{24,28},{28,24},{1,5},{5... | collective-permute-start | bytes 221192 | tf_op jit(solution)/shard_map/ppermute | solution.py:132
  6.1 8.2 %collective-permute-start.5 = (f32[128,512]{1,0:T(8,128)S(1)}, f32[128,512]{1,0:T(8,128)S(1)}, u32[]{:S(2)}, u32[]{:S(2)}) collective-permute-start(f32[128,512]{1,0:T(8,128)S(1)} %copy-done.1), channel_id=1, source_target_pairs={{0,2},{1,3},{2,0},{3,1},{4,6},{5,7},{6,4},{7,5},{8,10},{9,11},{10,... | collective-permute-start | bytes 786440 | tf_op jit(solution)/shard_map/ppermute | solution.py:111
  7.6 6.7 %collective-permute-start.4 = (f32[16,128]{1,0:T(8,128)}, f32[16,128]{1,0:T(8,128)S(1)}, u32[]{:S(2)}, u32[]{:S(2)}) collective-permute-start(f32[16,128]{1,0:T(8,128)} %get-tuple-element.24), channel_id=1, source_target_pairs={{0,2},{1,3},{2,0},{3,1},{4,6},{5,7},{6,4},{7,5},{8,10},{9,11},{10,... | collective-permute-start | bytes 24584 | tf_op jit(solution)/shard_map/ppermute | solution.py:111
  8.1 0.8 %collective-permute-start.2 = (bf16[32,1152]{1,0:T(8,128)(2,1)}, bf16[32,1152]{1,0:T(8,128)(2,1)S(1)}, u32[]{:S(2)}, u32[]{:S(2)}) collective-permute-start(bf16[32,1152]{1,0:T(8,128)(2,1)} %get-tuple-element.23), channel_id=1, source_target_pairs={{4,8},{8,4},{12,16},{16,12},{20,24},{24,20},{5,9},{9,5},{13,17},{1... | collective-permute-start | bytes 221192 | tf_op jit(solution)/shard_map/ppermute | solution.py:132
  8.8 0.9 %copy-start.4 = (bf16[128,512]{1,0:T(8,128)(2,1)S(1)}, bf16[128,512]{1,0:T(8,128)(2,1)}, u32[]{:S(2)}) copy-start(bf16[128,512]{1,0:T(8,128)(2,1)} %press_ref.1) | copy-start | bytes 393220
  8.8 5.5 %collective-permute-start = (bf16[128,1152]{1,0:T(8,128)(2,1)}, bf16[128,1152]{1,0:T(8,128)(2,1)S(1)}, u32[]{:S(2)}, u32[]{:S(2)}) collective-permute-start(bf16[128,1152]{1,0:T(8,128)(2,1)} %get-tuple-element.21.refs_0_), channel_id=1, source_target_pairs={{0,1},{1,0},{2,3},{3,2},{4,5},{5,4},{6,7},{7,6},{8,9},{9,8},{10,11... | collective-permute-start | bytes 884744 | tf_op jit(solution)/shard_map/ppermute | solution.py:111
  8.9 0.8 %copy-start.5 = (s32[32]{0:T(128)S(1)}, s32[32]{0:T(128)}, u32[]{:S(2)}) copy-start(s32[32]{0:T(128)} %counts_ref.3) | copy-start | bytes 388
  8.9 0.8 %copy-start.12 = (f32[64,128]{1,0:T(8,128)S(1)}, f32[64,128]{1,0:T(8,128)}, u32[]{:S(2)}) copy-start(f32[64,128]{1,0:T(8,128)} %constant.23.clone.box_ref) | copy-start | bytes 98308
  9.0 5.4 %copy-start = (bf16[384,512]{1,0:T(8,128)(2,1)S(1)}, bf16[384,512]{1,0:T(8,128)(2,1)}, u32[]{:S(2)}) copy-start(bf16[384,512]{1,0:T(8,128)(2,1)} %constant.29.spread_ref) | copy-start | bytes 1179652
  9.0 5.4 %copy-start.3 = (bf16[128,1152]{1,0:T(8,128)(2,1)S(1)}, bf16[128,1152]{1,0:T(8,128)(2,1)}, u32[]{:S(2)}) copy-start(bf16[128,1152]{1,0:T(8,128)(2,1)} %get-tuple-element.21.refs_0_) | copy-start | bytes 884740
  9.0 5.4 %copy-start.6 = (bf16[576,512]{1,0:T(8,128)(2,1)S(1)}, bf16[576,512]{1,0:T(8,128)(2,1)}, u32[]{:S(2)}) copy-start(bf16[576,512]{1,0:T(8,128)(2,1)} %constant.22.clone.basis_ref) | copy-start | bytes 1769476
  9.0 5.4 %copy-start.8 = (f32[288,256]{1,0:T(8,128)S(1)}, f32[288,256]{1,0:T(8,128)}, u32[]{:S(2)}) copy-start(f32[288,256]{1,0:T(8,128)} %constant.26.clone.compact_ref) | copy-start | bytes 884740
  9.0 5.3 %collective-permute-start.3 = (bf16[64,1152]{1,0:T(8,128)(2,1)S(1)}, bf16[64,1152]{1,0:T(8,128)(2,1)S(1)}, u32[]{:S(2)}, u32[]{:S(2)}) collective-permute-start(bf16[64,1152]{1,0:T(8,128)(2,1)S(1)} %constant_dynamic-update-slice_fusion.refs_2_), channel_id=1, source_target_pairs={{0,1},{1,0},{2,3},{3,2},{4,5},{5,4},{6,7},{7,6},{8,9},{9,8},{10,11... | collective-permute-start | bytes 442376 | tf_op jit(solution)/shard_map/ppermute | solution.py:111
  9.7 1.0 %copy-start.10 = (s32[256,256]{1,0:T(8,128)S(1)}, s32[256,256]{1,0:T(8,128)}, u32[]{:S(2)}) copy-start(s32[256,256]{1,0:T(8,128)} %constant.25.clone.powers_ref) | copy-start | bytes 786436
  10.7 0.9 %copy-start.11 = (f32[256,256]{1,0:T(8,128)S(1)}, f32[256,256]{1,0:T(8,128)}, u32[]{:S(2)}) copy-start(f32[256,256]{1,0:T(8,128)} %constant.24.clone.shift_ref) | copy-start | bytes 786436
  11.6 2.8 %copy-start.13 = (f32[16,128]{1,0:T(8,128)S(1)}, f32[16,128]{1,0:T(8,128)}, u32[]{:S(2)}) copy-start(f32[16,128]{1,0:T(8,128)} %get-tuple-element.20.spots_ref) | copy-start | bytes 24580
  19.1 19.7 %collective-permute-start.6 = (bf16[128,1152]{1,0:T(8,128)(2,1)S(1)}, bf16[128,1152]{1,0:T(8,128)(2,1)S(1)}, u32[]{:S(2)}, u32[]{:S(2)}) collective-permute-start(bf16[128,1152]{1,0:T(8,128)(2,1)S(1)} %get-tuple-element.27), channel_id=1, source_target_pairs={{0,2},{1,3},{2,0},{3,1},{4,6},{5,7},{6,4},{7,5},{8,10},{9,11},{10,... | collective-permute-start | bytes 884744 | tf_op jit(solution)/shard_map/ppermute | solution.py:111

commit v6 on v5

--- a/solution.py
+++ b/solution.py
@@ -73,7 +73,7 @@
     basis = basis.reshape(ROWS, NODES).astype(np.float32)
     top = np.asarray(basis.astype(jnp.bfloat16))
     rest = np.asarray((basis - top.astype(np.float32)).astype(jnp.bfloat16))
-    return top, rest
+    return np.concatenate([top, rest], axis=0)
 
 
 def compact_table():
@@ -111,18 +111,16 @@
     return lax.ppermute(block, axis, [(at, at ^ apart) for at in range(lax.axis_size(axis))])
 
 
-def move_tables(morton_count):
+def move_table(morton_count):
     bits = 3 * LMAX - (morton_count.bit_length() - 1)
     ratio = 2.0 ** max(max(0, min(LMAX, (bits - offset + 2) // 3)) for offset in range(3)) / 2.0**LMAX
-    shift = np.zeros((256, 256), np.float32)
-    powers = np.zeros((256, 256), np.int32)
+    table = np.zeros((256, 256), np.float32)
     triples = list(np.ndindex(6, 6, 6))
     for row, beta in enumerate(triples):
         for col, alpha in enumerate(triples):
             if all(b <= a for a, b in zip(alpha, beta)):
-                shift[row, col] = math.prod(math.comb(a, b) for a, b in zip(alpha, beta)) * ratio ** sum(beta)
-                powers[row, col] = sum((a - b) << 3 * dim for dim, (a, b) in enumerate(zip(alpha, beta)))
-    return shift, powers
+                table[row, col] = math.prod(math.comb(a, b) for a, b in zip(alpha, beta)) * ratio ** sum(beta)
+    return table
 
 
 def pairs(block, first):
@@ -143,14 +141,20 @@
 
 
 def pack_kernel(
-    counts_ref, vel_ref, nbrs_ref, levels_ref, keys_ref, box_ref, pick_ref, faces_ref, even_ref, odd_ref, *spots_refs
+    counts_ref, vel_ref, visc_ref, nbrs_ref, levels_ref, keys_ref, box_ref, pick_ref,
+    faces_ref, even_ref, odd_ref, weight_ref, *spots_refs,
 ):
     sib_count = lax.axis_size("sib")
     morton = lax.axis_index("morton")
     sib = lax.axis_index("sib")
     own = morton * sib_count + sib
     leaf_count = faces_ref.shape[0]
-    picked = dot(vel_ref[...].reshape(3 * leaf_count, NODES), pick_ref[...]).astype(bf16)
+    fields = jnp.concatenate([vel_ref[0], vel_ref[1], vel_ref[2], visc_ref[...].astype(bf16)], axis=0)
+    picked = dot(fields, pick_ref[...])
+    for dim in range(3):
+        block = picked[3 * leaf_count :, dim * LANES : (dim + 1) * LANES]
+        weight_ref[:, dim * LANES : (dim + 1) * LANES] = pltpu.roll(block, LANES // 2, 1).astype(bf16)
+    picked = picked[: 3 * leaf_count].astype(bf16)
     for comp in range(3):
         for dim in range(3):
             lane = (dim * 3 + comp) * LANES
@@ -230,7 +234,7 @@
 
 
 def pre_kernel(
-    counts_ref, vel_ref, press_ref, visc_ref, dx_ref, dyz_ref, box_ref, shift_ref, powers_ref,
+    counts_ref, vel_ref, press_ref, visc_ref, dx_ref, dyz_ref, box_ref, binomial_ref,
     part_ref, mass_ref, move_ref,
 ):
     sib_count = lax.axis_size("sib")
@@ -275,15 +279,18 @@
         part_ref[comp] = jnp.where(live, part, 0.0)
 
     box = box_ref[pl.ds(pl.multiple_of(morton * 8, 8), 8), :]
-    move = shift_ref[...]
-    powers = powers_ref[...]
-    for dim in range(3):
-        power = jnp.bitwise_and(jnp.right_shift(powers, 3 * dim), 7)
+    move = binomial_ref[...]
+    for dim, stride in enumerate((36, 6, 1)):
+        col = lax.broadcasted_iota(jnp.int32, (1, 256), 1) // stride % 6
+        row = lax.broadcasted_iota(jnp.int32, (256, 1), 0) // stride % 6
+        power = col - row
         along = box[dim : dim + 1, 3:4]
         factor = jnp.ones((1, 1), f32)
+        raised = jnp.ones((256, 256), f32)
         for degree in range(1, DEG + 1):
             factor = factor * along
-            move = move * jnp.where(power == degree, factor, 1.0)
+            raised = jnp.where(power == degree, factor, raised)
+        move = move * raised
     move_ref[...] = move
 
 
@@ -313,12 +320,20 @@
     return tiles
 
 
+def split(values, parts):
+    pieces = []
+    for _ in range(parts):
+        pieces.append(values.astype(bf16))
+        values = values - pieces[-1].astype(f32)
+    return pieces
+
+
 def moment_kernel(
-    part_ref, visc_ref, box_ref, spread_ref, basis_ref, compact_ref, spots_ref, *refs
+    part_ref, visc_ref, box_ref, spread_ref, basis_ref, face_basis_ref, compact_ref, spots_ref, *refs
 ):
     sides = lax.axis_size("sib") // 2
     window_refs = refs[:4]
-    asked_refs, their_visc_refs = refs[4 : 3 + sides], refs[3 + sides : 2 + 2 * sides]
+    asked_refs, their_weight_refs = refs[4 : 3 + sides], refs[3 + sides : 2 + 2 * sides]
     near_ref, served_refs, sums_ref, raw_ref = refs[2 + 2 * sides], refs[3 + 2 * sides : -2], refs[-2], refs[-1]
     morton = lax.axis_index("morton")
     leaf_count = visc_ref.shape[0]
@@ -327,29 +342,31 @@
     for blocks, out_ref in zip(chosen, (near_ref, *served_refs)):
         for dim, block in enumerate(blocks):
             out_ref[:, dim * FACES : (dim + 1) * FACES] = block
-    jumps = dot(jnp.concatenate([by_comp(blocks) for blocks in chosen], axis=0), spread_ref[...])
-    highs, lows = [], []
-    for who, ref in enumerate((visc_ref, *their_visc_refs)):
-        weight = ref[...] * (penalty * out_scale)
-        for comp in range(3):
-            at = (3 * who + comp) * leaf_count
-            force = -weight * jumps[at : at + leaf_count]
-            if who == 0:
-                force = force + part_ref[comp]
-            high = force.astype(bf16)
-            highs.append(high)
-            lows.append((force - high.astype(f32)).astype(bf16))
-    high = jnp.concatenate(highs, axis=0)
-    low = jnp.concatenate(lows, axis=0)
-    raw = dot_nt(basis_ref[...], high)
-    raw_ref[...] = raw[:ROWS] + raw[ROWS:] + dot_nt(basis_ref[:ROWS, :], low)
+
+    def add_moments(who, values, table_ref):
+        high, low = split(values, 2)
+        raw = dot_nt(table_ref[...], high)
+        lanes = slice(3 * who * leaf_count, 3 * (who + 1) * leaf_count)
+        raw_ref[:, lanes] = raw[:ROWS] + raw[ROWS:] + dot_nt(table_ref[:ROWS, :], low)
+
+    for who, ref in enumerate(their_weight_refs, 1):
+        weight = ref[...].astype(f32) * (-penalty * out_scale)
+        weight = jnp.concatenate([weight] * 3, axis=0)
+        add_moments(who, weight * by_comp(chosen[who]).astype(f32), face_basis_ref)
+    jumps = dot(by_comp(chosen[0]), spread_ref[...])
+    weight = visc_ref[...] * (penalty * out_scale)
+    force = [
+        part_ref[comp] - weight * jumps[comp * leaf_count : (comp + 1) * leaf_count] for comp in range(3)
+    ]
+    add_moments(0, jnp.concatenate(force, axis=0), basis_ref)
     geom = jnp.concatenate([spots[8:] for spots in asked for _ in range(3)], axis=1)
     tiles = shifted([raw_ref[8 * at : 8 * at + 8, :] for at in range(36)], geom)
-    moved = jnp.concatenate(tiles, axis=0)
-    group = lax.broadcasted_iota(jnp.int32, (raw_ref.shape[1], LANES), 0) // leaf_count % 3
-    column = lax.broadcasted_iota(jnp.int32, (raw_ref.shape[1], LANES), 1)
-    gather = jnp.where((group == column) | (group + 3 == column), 1.0, 0.0)
-    summed = jnp.dot(moved, gather, precision=highest, preferred_element_type=f32)
+    span = 3 * leaf_count
+    tiles = [sum(tile[:, span * who : span * (who + 1)] for who in range(sides)) for tile in tiles]
+    group = lax.broadcasted_iota(jnp.int32, (span, LANES), 0) // leaf_count
+    column = lax.broadcasted_iota(jnp.int32, (span, LANES), 1)
+    gather = jnp.where((group == column) | (group + 3 == column), 1.0, 0.0).astype(bf16)
+    summed = sum(dot(piece, gather) for piece in split(jnp.concatenate(tiles, axis=0), 3))
     box = box_ref[pl.ds(pl.multiple_of(morton * 8, 8), 8), :]
     both = shifted([summed[8 * at : 8 * at + 8, :] for at in range(36)], box)
     flat = jnp.concatenate(both, axis=0).T
@@ -421,7 +438,9 @@
     dyz_table = jnp.asarray(along_yz.astype(np.float32)).astype(bf16)
     pick = jnp.asarray(face_table().astype(np.float32)).astype(bf16)
     spread = jnp.asarray(spread_table().astype(np.float32)).astype(bf16)
-    basis = jnp.asarray(np.concatenate(basis_tables(), axis=0))
+    basis = basis_tables()
+    face_basis = (basis.astype(np.float32) @ spread_table().T.astype(np.float32)).astype(jnp.bfloat16)
+    basis, face_basis = jnp.asarray(basis), jnp.asarray(face_basis)
     boxes = jnp.asarray(box_table(morton_count))
     vel = jnp.transpose(velocity, (1, 0, 2))
     nbrs = jnp.transpose(neighbors, (1, 0))
@@ -430,24 +449,24 @@
     sib_count = lax.axis_size("sib")
     sides = sib_count // 2
     other_sides = [2 * side for side in range(1, sides)]
-    their_visc = [swap(viscosity, "sib", apart) for apart in other_sides]
-    faces, even, odd, *spots = call(
+    faces, even, odd, weights, *spots = call(
         pack_kernel,
         [
             ((leaf_count, width), bf16),
             ((BAND, width), bf16),
             ((BAND, width), bf16),
+            ((leaf_count, FACES), bf16),
         ]
         + [((16, leaf_count), f32)] * sides,
         4 * 10**8,
         [counts],
-        [vel, nbrs, levels.reshape(1, -1), morton_keys.reshape(1, -1), boxes, pick],
+        [vel, viscosity, nbrs, levels.reshape(1, -1), morton_keys.reshape(1, -1), boxes, pick],
         grant=60,
     )
+    odd, even = pairs(odd, 1), pairs(even, 0)
     asked = [swap(block, "sib", apart) for block, apart in zip(spots[1:], other_sides)]
-    bands = jnp.concatenate([pairs(even, 0), pairs(odd, 1)], axis=0)
-    window = [faces, swap(faces, "sib", 1), bands, swap(bands, "sib", 1)]
-    shift, powers = move_tables(morton_count)
+    their_weights = [swap(weights, "sib", apart) for apart in other_sides]
+    bands = jnp.concatenate([even, odd], axis=0)
     part, continuity, move = call(
         pre_kernel,
         [
@@ -457,16 +476,18 @@
         ],
         2 * 10**9,
         [counts],
-        [vel, pressure, viscosity, dx_table, dyz_table, boxes, jnp.asarray(shift), jnp.asarray(powers)],
-    )
+        [vel, pressure, viscosity, dx_table, dyz_table, boxes, jnp.asarray(move_table(morton_count))],
+    )
+    bands, part, asked, their_weights = lax.optimization_barrier((bands, part, asked, their_weights))
+    window = [faces, swap(faces, "sib", 1), bands, swap(bands, "sib", 1)]
     near, *served, sums = call(
         moment_kernel,
         [((leaf_count, width), bf16)] * sides + [((morton_count * sib_count, 8, LANES), f32)],
         2 * 10**9,
         [],
         [
-            part, viscosity, boxes, spread, basis, jnp.asarray(compact_table()), spots[0],
-            *window, *asked, *their_visc,
+            part, viscosity, boxes, spread, basis, face_basis, jnp.asarray(compact_table()), spots[0],
+            *window, *asked, *their_weights,
         ],
         [pltpu.VMEM((ROWS, 3 * sides * leaf_count), f32)],
     )

time: 41 us -> 36.8 us (0.90)
  blocking collectives: 17.8 us -> 14.7 us
  Pallas kernels: 11.9 us -> 10.2 us
  waiting for transfers between devices: 0.02 us -> 1.02 us
    all_to_all x1, blocking collectives: 17.8 us -> 14.7 us  [on_device(): every = lax.all_to_all(sums, ('morton', 'sib'), 0, 0, tiled=True)]
    pallas_call x5, Pallas kernels: 11.9 us -> 10.2 us  [call(): pl.pallas_call(kernel, out_shape=[jax.ShapeDtypeStruct(shape, dtype) for...]
    ppermute x2, starting transfers between devices: 3.59 us -> 2.14 us  [pairs(): return lax.ppermute(block, 'morton', route)]
    ppermute x5, starting transfers between devices: 4.5 us -> 5.58 us  [swap(): lax.ppermute(block, axis, [(at, at ^ apart) for at in range(lax.axis_size...]
    ppermute x5, waiting for transfers between devices: 0.01 us -> 1.02 us  [swap(): lax.ppermute(block, axis, [(at, at ^ apart) for at in range(lax.axis_size...]
    unnamed x29 -> x28, local copies, waits for them, and re-layouts: 2.11 us -> 2.06 us
  transfers between devices with their start and end apart: 7 -> 7, of which waited for: 0 -> 1; matrix products, arithmetic and copies ran while one was open for 0% -> 0% of each run, Pallas kernels for 7% -> 6%
where the time goes in v6:
time: 36.8 us; the launch traced here: 36.6 us
  blocking collectives  14.7 us (40%)
  Pallas kernels  10.2 us (28%)
  starting transfers between devices  7.73 us (21%)
  local copies, waits for them, and re-layouts  2.06 us (6%)
  waiting for transfers between devices  1.02 us (3%)
  between operations  0.84 us (2%)
    all_to_all x1, blocking collectives, on_device(): every = lax.all_to_all(sums, ('morton', 'sib'), 0, 0, tiled=True)  14.7 us
    pallas_call x5, Pallas kernels, call(): pl.pallas_call(kernel, out_shape=[jax.ShapeDtypeStruct(shape, dtype) for...  10.2 us
    ppermute x5, starting transfers between devices, swap(): lax.ppermute(block, axis, [(at, at ^ apart) for at in range(lax.axis_size...  5.58 us
    ppermute x2, starting transfers between devices, pairs(): return lax.ppermute(block, 'morton', route)  2.14 us
    unnamed x28, local copies, waits for them, and re-layouts  2.06 us
    ppermute x5, waiting for transfers between devices, swap(): lax.ppermute(block, axis, [(at, at ^ apart) for at in range(lax.axis_size...  1.02 us
  transfers between devices with their start and end apart: 7, of which 1 were waited for; matrix products, arithmetic and copies ran while one was open for 0% of the time, Pallas kernels for 6%

profile of v6, /device:TPU:0, one launch (start us, length us, event | category | flops | bytes accessed | tf_op | source)
XLA Modules:
  0.0 36.6 jit_solution(1557134174650975085)
XLA Ops:
  0.6 0.0 copy-start.1
  0.6 0.0 copy-start.2
  0.7 0.0 copy-start.4
  0.7 0.0 copy-start.7
  0.7 0.0 copy-start.12
  0.7 2.6 %shard_map.183 = (bf16[128,1152]{1,0:T(8,128)(2,1)}, bf16[32,1152]{1,0:T(8,128)(2,1)}, bf16[32,1152]{1,0:T(8,128)(2,1)}, bf16[128,384]{1,0:T(8,128)(2,1)}, f32[16,128]{1,0:T(8,128)}, /*index=5*/f32[16,128]{1,0:T(8,128)}) custom-call(s32[32]{0:T(128)} %counts_ref.3, bf16[3,128,512]{2,1,0:T(8,128)(2,1)} %bitcast.7, f32[128,512]{1,0:T(8,128)} %visc_ref.7, ...), custom_call_target="tpu_custom_call" | custom-call | flops 400000000 | bytes 1085440 | tf_op jit(solution)/shard_map/pallas_call | solution.py:422
  3.3 3.0 %collective-permute-start.2 = (f32[16,128]{1,0:T(8,128)}, f32[16,128]{1,0:T(8,128)S(1)}, u32[]{:S(2)}, u32[]{:S(2)}) collective-permute-start(f32[16,128]{1,0:T(8,128)} %get-tuple-element.27), channel_id=1, source_target_pairs={{0,2},{1,3},{2,0},{3,1},{4,6},{5,7},{6,4},{7,5},{8,10},{9,11},{10,... | collective-permute-start | bytes 24584 | tf_op jit(solution)/shard_map/ppermute | solution.py:111
  6.3 1.5 %collective-permute-start = (bf16[32,1152]{1,0:T(8,128)(2,1)}, bf16[32,1152]{1,0:T(8,128)(2,1)S(1)}, u32[]{:S(2)}, u32[]{:S(2)}) collective-permute-start(bf16[32,1152]{1,0:T(8,128)(2,1)} %get-tuple-element.24), channel_id=1, source_target_pairs={{0,4},{4,0},{8,12},{12,8},{16,20},{20,16},{24,28},{28,24},{1,5},{5... | collective-permute-start | bytes 221192 | tf_op jit(solution)/shard_map/ppermute | solution.py:130
  7.7 0.7 %collective-permute-start.1 = (bf16[32,1152]{1,0:T(8,128)(2,1)}, bf16[32,1152]{1,0:T(8,128)(2,1)S(1)}, u32[]{:S(2)}, u32[]{:S(2)}) collective-permute-start(bf16[32,1152]{1,0:T(8,128)(2,1)} %get-tuple-element.25), channel_id=1, source_target_pairs={{4,8},{8,4},{12,16},{16,12},{20,24},{24,20},{5,9},{9,5},{13,17},{1... | collective-permute-start | bytes 221192 | tf_op jit(solution)/shard_map/ppermute | solution.py:130
  8.4 0.0 copy-start.5
  8.4 0.6 %collective-permute-start.3 = (bf16[128,384]{1,0:T(8,128)(2,1)}, bf16[128,384]{1,0:T(8,128)(2,1)S(1)}, u32[]{:S(2)}, u32[]{:S(2)}) collective-permute-start(bf16[128,384]{1,0:T(8,128)(2,1)} %get-tuple-element.28), channel_id=1, source_target_pairs={{0,2},{1,3},{2,0},{3,1},{4,6},{5,7},{6,4},{7,5},{8,10},{9,11},{10,... | collective-permute-start | bytes 294920 | tf_op jit(solution)/shard_map/ppermute | solution.py:111
  9.0 0.0 copy-start
  9.0 0.0 copy-start.6
  9.0 0.0 copy-start.8
  9.0 0.0 collective-permute-start.4
  9.0 0.0 copy-done.1
  9.0 0.0 copy-done.2
  9.0 0.0 copy-done.4
  9.0 0.0 copy-done.7
  9.0 0.0 copy-done.12
  9.1 0.0 copy-done.5
  9.1 0.0 copy-start.10
  9.1 1.0 %copy-done.10 = bf16[256,512]{1,0:T(8,128)(2,1)S(1)} copy-done((bf16[256,512]{1,0:T(8,128)(2,1)S(1)}, bf16[256,512]{1,0:T(8,128)(2,1)}, u32[]{:S(2)}) %copy-start.10) | copy-done | bytes 262168
  10.1 0.0 copy-start.11
  10.1 0.9 %copy-done.11 = f32[256,256]{1,0:T(8,128)S(1)} copy-done((f32[256,256]{1,0:T(8,128)S(1)}, f32[256,256]{1,0:T(8,128)}, u32[]{:S(2)}) %copy-start.11) | copy-done | bytes 262168
  11.1 0.0 copy-start.9
  11.1 0.0 copy-start.13
  11.1 2.3 %shard_map.184 = (f32[3,128,512]{2,1,0:T(8,128)S(1)}, f32[128,512]{1,0:T(8,128)}, f32[256,256]{1,0:T(8,128)S(1)}) custom-call(s32[32]{0:T(128)S(1)} %copy-done.5, bf16[3,128,512]{2,1,0:T(8,128)(2,1)S(1)} %bitcast.8, bf16[128,512]{1,0:T(8,128)(2,1)S(1)} %copy-done.4, f32[128,512]{1,0:T(8,128)S(1)} %copy-done.1, bf16[512,512]{1,0:T(8,128)(2,1)S(1)} %copy-done.7, ...), custom_call_target="tpu_custom_call" | custom-call | flops 2000000000 | bytes 1867776 | tf_op jit(solution)/shard_map/pallas_call | solution.py:422
  13.4 0.0 copy-start.3
  13.4 0.0 collective-permute-done
  13.4 0.0 collective-permute-done.1
  13.4 0.0 collective-permute-done.2.refs_4_
  13.4 0.0 collective-permute-done.3.refs_5_
  13.4 0.4 %collective-permute-start.5 = (bf16[64,1152]{1,0:T(8,128)(2,1)S(1)}, bf16[64,1152]{1,0:T(8,128)(2,1)S(1)}, u32[]{:S(2)}, u32[]{:S(2)}) collective-permute-start(bf16[64,1152]{1,0:T(8,128)(2,1)S(1)} %pad_maximum_fusion.refs_2_), channel_id=1, source_target_pairs={{0,1},{1,0},{2,3},{3,2},{4,5},{5,4},{6,7},{7,6},{8,9},{9,8},{10,11... | collective-permute-start | bytes 442376 | tf_op jit(solution)/shard_map/ppermute | solution.py:111
  13.9 1.0 %collective-permute-done.5.refs_3_ = bf16[64,1152]{1,0:T(8,128)(2,1)S(1)} collective-permute-done((bf16[64,1152]{1,0:T(8,128)(2,1)S(1)}, bf16[64,1152]{1,0:T(8,128)(2,1)S(1)}, u32[]{:S(2)}, u32[]{:S(2)}) %collective-permute-start.5) | collective-permute-done | bytes 147488 | tf_op jit(solution)/shard_map/ppermute | solution.py:111
  14.9 0.0 collective-permute-done.4.refs_1_
  14.9 0.0 copy-done
  14.9 0.0 copy-done.6
  14.9 0.0 copy-done.8
  14.9 0.0 copy-done.9
  14.9 0.0 copy-done.13
  14.9 0.0 copy-done.3
  14.9 3.4 %shard_map.185 = (bf16[128,1152]{1,0:T(8,128)(2,1)S(1)}, bf16[128,1152]{1,0:T(8,128)(2,1)S(1)}, f32[32,8,128]{2,1,0:T(8,128)S(1)}) custom-call(f32[3,128,512]{2,1,0:T(8,128)S(1)} %get-tuple-element.29.part_ref, f32[128,512]{1,0:T(8,128)S(1)} %copy-done.1, f32[64,128]{1,0:T(8,128)S(1)} %copy-done.12, bf16[384,512]{1,0:T(8,128)(2,1)S(1)} %copy-done, ...), custom_call_target="tpu_custom_call" | custom-call | flops 2000000000 | bytes 3801088 | tf_op jit(solution)/shard_map/pallas_call | solution.py:422
  18.3 1.6 %collective-permute-start.6 = (bf16[128,1152]{1,0:T(8,128)(2,1)S(1)}, bf16[128,1152]{1,0:T(8,128)(2,1)S(1)}, u32[]{:S(2)}, u32[]{:S(2)}) collective-permute-start(bf16[128,1152]{1,0:T(8,128)(2,1)S(1)} %get-tuple-element.37), channel_id=1, source_target_pairs={{0,2},{1,3},{2,0},{3,1},{4,6},{5,7},{6,4},{7,5},{8,10},{9,11},{10,... | collective-permute-start | bytes 884744 | tf_op jit(solution)/shard_map/ppermute | solution.py:111
  19.9 14.7 %all_to_all.5.sums_ref = f32[32,8,128]{2,1,0:T(8,128)S(1)} all-to-all(f32[32,8,128]{2,1,0:T(8,128)S(1)} %get-tuple-element.36), channel_id=1, replica_groups=mesh['morton'=8,'sib'=4] {'morton','sib'}, dimensions={0} | all-to-all | bytes 262144 | tf_op jit(solution)/shard_map/all_to_all | solution.py:495
  34.6 0.0 collective-permute-done.6.refs_0_
  34.6 0.8 %shard_map.187 = (f32[3,1,216]{2,1,0:T(1,128)}, f32[3,1,216]{2,1,0:T(1,128)}) custom-call(f32[32,8,128]{2,1,0:T(8,128)S(1)} %all_to_all.5.sums_ref, f32[256,256]{1,0:T(8,128)S(1)} %get-tuple-element.41.move_ref), custom_call_target="tpu_custom_call" | custom-call | flops 100000 | bytes 393216 | tf_op jit(solution)/shard_map/pallas_call | solution.py:422
  35.4 1.1 %shard_map.186 = f32[3,128,512]{2,1,0:T(8,128)} custom-call(f32[3,128,512]{2,1,0:T(8,128)S(1)} %get-tuple-element.29.part_ref, f32[128,512]{1,0:T(8,128)S(1)} %copy-done.1, bf16[384,512]{1,0:T(8,128)(2,1)S(1)} %copy-done, bf16[128,1152]{1,0:T(8,128)(2,1)S(1)} %get-tuple-element.35.near_ref, bf16[128,1152]{1,0:T(8,128)(2,1)S(1)} %collective-permute-done.6.refs_0_), custom_call_target="tpu_custom_call" | custom-call | flops 200000000 | bytes 2031616 | tf_op jit(solution)/shard_map/pallas_call | solution.py:422
  (1 shorter events, 0.0 us)
Async XLA Ops:
  0.6 8.4 %copy-start.1 = (f32[128,512]{1,0:T(8,128)S(1)}, f32[128,512]{1,0:T(8,128)}, u32[]{:S(2)}) copy-start(f32[128,512]{1,0:T(8,128)} %visc_ref.7) | copy-start | bytes 786436
  0.6 8.4 %copy-start.2 = (bf16[128,3,512]{2,0,1:T(8,128)(2,1)S(1)}, bf16[128,3,512]{2,0,1:T(8,128)(2,1)}, u32[]{:S(2)}) copy-start(bf16[128,3,512]{2,0,1:T(8,128)(2,1)} %param.16) | copy-start | bytes 1179652
  0.7 8.4 %copy-start.4 = (bf16[128,512]{1,0:T(8,128)(2,1)S(1)}, bf16[128,512]{1,0:T(8,128)(2,1)}, u32[]{:S(2)}) copy-start(bf16[128,512]{1,0:T(8,128)(2,1)} %press_ref.1) | copy-start | bytes 393220
  0.7 8.4 %copy-start.7 = (bf16[512,512]{1,0:T(8,128)(2,1)S(1)}, bf16[512,512]{1,0:T(8,128)(2,1)}, u32[]{:S(2)}) copy-start(bf16[512,512]{1,0:T(8,128)(2,1)} %constant.28.dx_ref) | copy-start | bytes 1572868
  0.7 8.4 %copy-start.12 = (f32[64,128]{1,0:T(8,128)S(1)}, f32[64,128]{1,0:T(8,128)}, u32[]{:S(2)}) copy-start(f32[64,128]{1,0:T(8,128)} %constant.24.clone.box_ref) | copy-start | bytes 98308
  3.3 10.1 %collective-permute-start.2 = (f32[16,128]{1,0:T(8,128)}, f32[16,128]{1,0:T(8,128)S(1)}, u32[]{:S(2)}, u32[]{:S(2)}) collective-permute-start(f32[16,128]{1,0:T(8,128)} %get-tuple-element.27), channel_id=1, source_target_pairs={{0,2},{1,3},{2,0},{3,1},{4,6},{5,7},{6,4},{7,5},{8,10},{9,11},{10,... | collective-permute-start | bytes 24584 | tf_op jit(solution)/shard_map/ppermute | solution.py:111
  6.3 7.1 %collective-permute-start = (bf16[32,1152]{1,0:T(8,128)(2,1)}, bf16[32,1152]{1,0:T(8,128)(2,1)S(1)}, u32[]{:S(2)}, u32[]{:S(2)}) collective-permute-start(bf16[32,1152]{1,0:T(8,128)(2,1)} %get-tuple-element.24), channel_id=1, source_target_pairs={{0,4},{4,0},{8,12},{12,8},{16,20},{20,16},{24,28},{28,24},{1,5},{5... | collective-permute-start | bytes 221192 | tf_op jit(solution)/shard_map/ppermute | solution.py:130
  7.7 5.6 %collective-permute-start.1 = (bf16[32,1152]{1,0:T(8,128)(2,1)}, bf16[32,1152]{1,0:T(8,128)(2,1)S(1)}, u32[]{:S(2)}, u32[]{:S(2)}) collective-permute-start(bf16[32,1152]{1,0:T(8,128)(2,1)} %get-tuple-element.25), channel_id=1, source_target_pairs={{4,8},{8,4},{12,16},{16,12},{20,24},{24,20},{5,9},{9,5},{13,17},{1... | collective-permute-start | bytes 221192 | tf_op jit(solution)/shard_map/ppermute | solution.py:130
  8.4 0.7 %copy-start.5 = (s32[32]{0:T(128)S(1)}, s32[32]{0:T(128)}, u32[]{:S(2)}) copy-start(s32[32]{0:T(128)} %counts_ref.3) | copy-start | bytes 388
  8.4 5.0 %collective-permute-start.3 = (bf16[128,384]{1,0:T(8,128)(2,1)}, bf16[128,384]{1,0:T(8,128)(2,1)S(1)}, u32[]{:S(2)}, u32[]{:S(2)}) collective-permute-start(bf16[128,384]{1,0:T(8,128)(2,1)} %get-tuple-element.28), channel_id=1, source_target_pairs={{0,2},{1,3},{2,0},{3,1},{4,6},{5,7},{6,4},{7,5},{8,10},{9,11},{10,... | collective-permute-start | bytes 294920 | tf_op jit(solution)/shard_map/ppermute | solution.py:111
  9.0 5.9 %copy-start = (bf16[384,512]{1,0:T(8,128)(2,1)S(1)}, bf16[384,512]{1,0:T(8,128)(2,1)}, u32[]{:S(2)}) copy-start(bf16[384,512]{1,0:T(8,128)(2,1)} %constant.30.spread_ref) | copy-start | bytes 1179652
  9.0 5.9 %copy-start.6 = (bf16[576,512]{1,0:T(8,128)(2,1)S(1)}, bf16[576,512]{1,0:T(8,128)(2,1)}, u32[]{:S(2)}) copy-start(bf16[576,512]{1,0:T(8,128)(2,1)} %constant.22.clone.basis_ref) | copy-start | bytes 1769476
  9.0 5.9 %copy-start.8 = (bf16[576,384]{1,0:T(8,128)(2,1)S(1)}, bf16[576,384]{1,0:T(8,128)(2,1)}, u32[]{:S(2)}) copy-start(bf16[576,384]{1,0:T(8,128)(2,1)} %constant.23.clone.face_basis_ref) | copy-start | bytes 1327108
  9.0 5.9 %collective-permute-start.4 = (bf16[128,1152]{1,0:T(8,128)(2,1)}, bf16[128,1152]{1,0:T(8,128)(2,1)S(1)}, u32[]{:S(2)}, u32[]{:S(2)}) collective-permute-start(bf16[128,1152]{1,0:T(8,128)(2,1)} %get-tuple-element.31.refs_0_), channel_id=1, source_target_pairs={{0,1},{1,0},{2,3},{3,2},{4,5},{5,4},{6,7},{7,6},{8,9},{9,8},{10,11... | collective-permute-start | bytes 884744 | tf_op jit(solution)/shard_map/ppermute | solution.py:111
  9.1 1.0 %copy-start.10 = (bf16[256,512]{1,0:T(8,128)(2,1)S(1)}, bf16[256,512]{1,0:T(8,128)(2,1)}, u32[]{:S(2)}) copy-start(bf16[256,512]{1,0:T(8,128)(2,1)} %constant.29.dyz_ref) | copy-start | bytes 786436
  10.1 0.9 %copy-start.11 = (f32[256,256]{1,0:T(8,128)S(1)}, f32[256,256]{1,0:T(8,128)}, u32[]{:S(2)}) copy-start(f32[256,256]{1,0:T(8,128)} %constant.25.clone.binomial_ref) | copy-start | bytes 786436
  11.1 3.8 %copy-start.9 = (f32[288,256]{1,0:T(8,128)S(1)}, f32[288,256]{1,0:T(8,128)}, u32[]{:S(2)}) copy-start(f32[288,256]{1,0:T(8,128)} %constant.26.clone.compact_ref) | copy-start | bytes 884740
  11.1 3.8 %copy-start.13 = (f32[16,128]{1,0:T(8,128)S(1)}, f32[16,128]{1,0:T(8,128)}, u32[]{:S(2)}) copy-start(f32[16,128]{1,0:T(8,128)} %get-tuple-element.30.spots_ref) | copy-start | bytes 24580
  13.4 1.6 %copy-start.3 = (bf16[128,1152]{1,0:T(8,128)(2,1)S(1)}, bf16[128,1152]{1,0:T(8,128)(2,1)}, u32[]{:S(2)}) copy-start(bf16[128,1152]{1,0:T(8,128)(2,1)} %get-tuple-element.31.refs_0_) | copy-start | bytes 884740
  13.4 1.4 %collective-permute-start.5 = (bf16[64,1152]{1,0:T(8,128)(2,1)S(1)}, bf16[64,1152]{1,0:T(8,128)(2,1)S(1)}, u32[]{:S(2)}, u32[]{:S(2)}) collective-permute-start(bf16[64,1152]{1,0:T(8,128)(2,1)S(1)} %pad_maximum_fusion.refs_2_), channel_id=1, source_target_pairs={{0,1},{1,0},{2,3},{3,2},{4,5},{5,4},{6,7},{7,6},{8,9},{9,8},{10,11... | collective-permute-start | bytes 442376 | tf_op jit(solution)/shard_map/ppermute | solution.py:111
  18.3 16.3 %collective-permute-start.6 = (bf16[128,1152]{1,0:T(8,128)(2,1)S(1)}, bf16[128,1152]{1,0:T(8,128)(2,1)S(1)}, u32[]{:S(2)}, u32[]{:S(2)}) collective-permute-start(bf16[128,1152]{1,0:T(8,128)(2,1)S(1)} %get-tuple-element.37), channel_id=1, source_target_pairs={{0,2},{1,3},{2,0},{3,1},{4,6},{5,7},{6,4},{7,5},{8,10},{9,11},{10,... | collective-permute-start | bytes 884744 | tf_op jit(solution)/shard_map/ppermute | solution.py:111

commit v7 on v6

--- a/solution.py
+++ b/solution.py
@@ -44,7 +44,7 @@
     along_x = np.kron(derivative, np.eye(64)).T
     along_y = np.kron(np.eye(4), np.kron(derivative, np.eye(8))).T
     along_z = np.kron(np.eye(32), derivative).T
-    return along_x, np.concatenate([along_y, along_z], axis=1)
+    return np.concatenate([along_x, np.concatenate([along_y, along_z], axis=1)], axis=0)
 
 
 def face_table():
@@ -111,18 +111,6 @@
     return lax.ppermute(block, axis, [(at, at ^ apart) for at in range(lax.axis_size(axis))])
 
 
-def move_table(morton_count):
-    bits = 3 * LMAX - (morton_count.bit_length() - 1)
-    ratio = 2.0 ** max(max(0, min(LMAX, (bits - offset + 2) // 3)) for offset in range(3)) / 2.0**LMAX
-    table = np.zeros((256, 256), np.float32)
-    triples = list(np.ndindex(6, 6, 6))
-    for row, beta in enumerate(triples):
-        for col, alpha in enumerate(triples):
-            if all(b <= a for a, b in zip(alpha, beta)):
-                table[row, col] = math.prod(math.comb(a, b) for a, b in zip(alpha, beta)) * ratio ** sum(beta)
-    return table
-
-
 def pairs(block, first):
     route = []
     for low in range(first, lax.axis_size("morton") - 1, 2):
@@ -142,7 +130,7 @@
 
 def pack_kernel(
     counts_ref, vel_ref, visc_ref, nbrs_ref, levels_ref, keys_ref, box_ref, pick_ref,
-    faces_ref, even_ref, odd_ref, weight_ref, *spots_refs,
+    faces_ref, even_ref, odd_ref, spots_ref, *request_refs,
 ):
     sib_count = lax.axis_size("sib")
     morton = lax.axis_index("morton")
@@ -153,7 +141,9 @@
     picked = dot(fields, pick_ref[...])
     for dim in range(3):
         block = picked[3 * leaf_count :, dim * LANES : (dim + 1) * LANES]
-        weight_ref[:, dim * LANES : (dim + 1) * LANES] = pltpu.roll(block, LANES // 2, 1).astype(bf16)
+        block = pltpu.roll(block, LANES // 2, 1).astype(bf16)
+        for request_ref in request_refs:
+            request_ref[:leaf_count, dim * LANES : (dim + 1) * LANES] = block
     picked = picked[: 3 * leaf_count].astype(bf16)
     for comp in range(3):
         for dim in range(3):
@@ -199,11 +189,18 @@
     places.append(0.5 * span * finest * box[7:8, :])
     places.append(jnp.zeros((4, leaf_count), f32))
     geom = jnp.concatenate(places, axis=0)
-    for side, spots_ref in enumerate(spots_refs):
+    for side in range(sib_count // 2):
         piece = jnp.bitwise_xor(owner_sib, jnp.bitwise_xor(sib, 2 * side))
         spot = jnp.where(step == 0, piece * leaf_count + slot, 2 * leaf_count + piece * (2 * BAND) + in_band)
-        spot = jnp.where((nbrs >= 0) & (piece < 2), spot, -1).astype(f32)
-        spots_ref[...] = jnp.concatenate([spot, jnp.full((2, leaf_count), -1.0, f32), geom], axis=0)
+        spot = jnp.where((nbrs >= 0) & (piece < 2), spot, -1)
+        if side == 0:
+            spots_ref[...] = jnp.concatenate([spot.astype(f32), jnp.zeros((2, leaf_count), f32), geom], axis=0)
+            continue
+        whole = jnp.right_shift(spot, 4)
+        parts = [whole.astype(f32), (spot - 16 * whole).astype(f32), geom[:4]]
+        request_ref = request_refs[side - 1]
+        request_ref[leaf_count:, :LANES] = jnp.concatenate(parts, axis=0).astype(bf16)
+        request_ref[leaf_count:, LANES:] = jnp.zeros((16, FACES - LANES), bf16)
 
 
 def gathered(asked, window_refs):
@@ -234,7 +231,7 @@
 
 
 def pre_kernel(
-    counts_ref, vel_ref, press_ref, visc_ref, dx_ref, dyz_ref, box_ref, binomial_ref,
+    counts_ref, vel_ref, press_ref, visc_ref, table_ref, box_ref,
     part_ref, mass_ref, move_ref,
 ):
     sib_count = lax.axis_size("sib")
@@ -254,9 +251,9 @@
 
     visc = visc_ref[...]
     fields = jnp.concatenate([vel_ref[0], vel_ref[1], vel_ref[2], press_ref[...]], axis=0)
-    halves = [dot(fields[:, at : at + 256], dyz_ref[...]) for at in (0, 256)]
+    halves = [dot(fields[:, at : at + 256], table_ref[NODES:, :]) for at in (0, 256)]
     grads = [
-        dot(fields, dx_ref[...]),
+        dot(fields, table_ref[:NODES, :]),
         jnp.concatenate([half[:, :256] for half in halves], axis=1),
         jnp.concatenate([half[:, 256:] for half in halves], axis=1),
     ]
@@ -269,28 +266,33 @@
             stress[first, second] = stress[second, first] = value
     columns = [jnp.concatenate([stress[comp, dim] for comp in range(3)], axis=0) for dim in range(3)]
     rest = [
-        dot(columns[1][:, at : at + 256], dyz_ref[:, :256]) + dot(columns[2][:, at : at + 256], dyz_ref[:, 256:])
+        dot(columns[1][:, at : at + 256], table_ref[NODES:, :256]) + dot(columns[2][:, at : at + 256], table_ref[NODES:, 256:])
         for at in (0, 256)
     ]
-    div = dot(columns[0], dx_ref[...]) + jnp.concatenate(rest, axis=1)
+    div = dot(columns[0], table_ref[:NODES, :]) + jnp.concatenate(rest, axis=1)
     for comp in range(3):
         jump = touching * vel_ref[comp].astype(f32)
         part = (penalty * visc * jump - rows(div, comp) + rows(grads[comp], 3)) * out_scale
         part_ref[comp] = jnp.where(live, part, 0.0)
 
     box = box_ref[pl.ds(pl.multiple_of(morton * 8, 8), 8), :]
-    move = binomial_ref[...]
+    move = jnp.ones((256, 256), f32)
     for dim, stride in enumerate((36, 6, 1)):
         col = lax.broadcasted_iota(jnp.int32, (1, 256), 1) // stride % 6
         row = lax.broadcasted_iota(jnp.int32, (256, 1), 0) // stride % 6
-        power = col - row
-        along = box[dim : dim + 1, 3:4]
-        factor = jnp.ones((1, 1), f32)
-        raised = jnp.ones((256, 256), f32)
-        for degree in range(1, DEG + 1):
-            factor = factor * along
-            raised = jnp.where(power == degree, factor, raised)
-        move = move * raised
+        along, scale = box[dim : dim + 1, 3:4], box[3:4, 3:4]
+        powers = [jnp.ones((1, 1), f32)]
+        for _ in range(DEG):
+            powers.append(powers[-1] * along)
+        factor = jnp.zeros((256, 256), f32)
+        below = jnp.ones((1, 1), f32)
+        for low in range(DEG + 1):
+            line = jnp.zeros((1, 256), f32)
+            for high in range(low, DEG + 1):
+                line = jnp.where(col == high, powers[high - low] * below * float(math.comb(high, low)), line)
+            factor = jnp.where(row == low, line, factor)
+            below = below * scale
+        move = move * factor
     move_ref[...] = move
 
 
@@ -333,11 +335,17 @@
 ):
     sides = lax.axis_size("sib") // 2
     window_refs = refs[:4]
-    asked_refs, their_weight_refs = refs[4 : 3 + sides], refs[3 + sides : 2 + 2 * sides]
-    near_ref, served_refs, sums_ref, raw_ref = refs[2 + 2 * sides], refs[3 + 2 * sides : -2], refs[-2], refs[-1]
+    request_refs = refs[4 : 3 + sides]
+    near_ref, served_refs, sums_ref, raw_ref = refs[3 + sides], refs[4 + sides : -2], refs[-2], refs[-1]
     morton = lax.axis_index("morton")
     leaf_count = visc_ref.shape[0]
-    asked = [spots_ref[...]] + [ref[...] for ref in asked_refs]
+    asked = [spots_ref[...]]
+    for ref in request_refs:
+        parts = ref[leaf_count:, :LANES].astype(f32)
+        blank = jnp.zeros((2, leaf_count), f32)
+        asked.append(
+            jnp.concatenate([parts[:6] * 16.0 + parts[6:12], blank, parts[12:], jnp.zeros((4, leaf_count), f32)], axis=0)
+        )
     chosen = gathered(asked, window_refs)
     for blocks, out_ref in zip(chosen, (near_ref, *served_refs)):
         for dim, block in enumerate(blocks):
@@ -349,8 +357,8 @@
         lanes = slice(3 * who * leaf_count, 3 * (who + 1) * leaf_count)
         raw_ref[:, lanes] = raw[:ROWS] + raw[ROWS:] + dot_nt(table_ref[:ROWS, :], low)
 
-    for who, ref in enumerate(their_weight_refs, 1):
-        weight = ref[...].astype(f32) * (-penalty * out_scale)
+    for who, ref in enumerate(request_refs, 1):
+        weight = ref[:leaf_count].astype(f32) * (-penalty * out_scale)
         weight = jnp.concatenate([weight] * 3, axis=0)
         add_moments(who, weight * by_comp(chosen[who]).astype(f32), face_basis_ref)
     jumps = dot(by_comp(chosen[0]), spread_ref[...])
@@ -379,8 +387,8 @@
         sums_ref[other] = jnp.where(morton == other // sib_count, to_box, to_root)
 
 
-def force_kernel(part_ref, visc_ref, spread_ref, near_ref, *refs):
-    got_refs, (force_hbm, force_ref, sems) = refs[:-3], refs[-3:]
+def last_kernel(part_ref, visc_ref, spread_ref, sums_ref, move_ref, near_ref, *refs):
+    got_refs, (force_hbm, box_ref, root_ref, force_ref, sems) = refs[:-5], refs[-5:]
     faces = near_ref[...]
     for got_ref in got_refs:
         faces = faces + got_ref[...]
@@ -392,11 +400,6 @@
         force_ref[comp] = part_ref[comp] - weight * jump
         stores.append(pltpu.make_async_copy(force_ref.at[comp], force_hbm.at[comp], sems.at[comp]))
         stores[-1].start()
-    for store in stores:
-        store.wait()
-
-
-def final_kernel(sums_ref, move_ref, box_ref, root_ref):
     sib_count = lax.axis_size("sib")
     morton = lax.axis_index("morton")
     box = jnp.zeros(sums_ref.shape[1:], f32)
@@ -412,6 +415,8 @@
     for comp in range(3):
         box_ref[comp] = box[comp : comp + 1, :MOMENTS]
         root_ref[comp] = root[comp : comp + 1, :MOMENTS]
+    for store in stores:
+        store.wait()
 
 
 def call(kernel, shapes, flops, scalars, operands, scratch=(), place=pltpu.VMEM, outs=None, grant=32):
@@ -433,9 +438,7 @@
 def on_device(velocity, pressure, viscosity, levels, morton_keys, counts, neighbors):
     leaf_count = velocity.shape[0]
     morton_count = lax.axis_size("morton")
-    along_x, along_yz = operator_tables()
-    dx_table = jnp.asarray(along_x.astype(np.float32)).astype(bf16)
-    dyz_table = jnp.asarray(along_yz.astype(np.float32)).astype(bf16)
+    tables = jnp.asarray(operator_tables().astype(np.float32)).astype(bf16)
     pick = jnp.asarray(face_table().astype(np.float32)).astype(bf16)
     spread = jnp.asarray(spread_table().astype(np.float32)).astype(bf16)
     basis = basis_tables()
@@ -449,23 +452,23 @@
     sib_count = lax.axis_size("sib")
     sides = sib_count // 2
     other_sides = [2 * side for side in range(1, sides)]
-    faces, even, odd, weights, *spots = call(
+    faces, even, odd, spots, *requests = call(
         pack_kernel,
         [
             ((leaf_count, width), bf16),
             ((BAND, width), bf16),
             ((BAND, width), bf16),
-            ((leaf_count, FACES), bf16),
+            ((16, leaf_count), f32),
         ]
-        + [((16, leaf_count), f32)] * sides,
+        + [((leaf_count + 16, FACES), bf16)] * (sides - 1),
         4 * 10**8,
         [counts],
         [vel, viscosity, nbrs, levels.reshape(1, -1), morton_keys.reshape(1, -1), boxes, pick],
         grant=60,
     )
     odd, even = pairs(odd, 1), pairs(even, 0)
-    asked = [swap(block, "sib", apart) for block, apart in zip(spots[1:], other_sides)]
-    their_weights = [swap(weights, "sib", apart) for apart in other_sides]
+    even, requests, pressure = lax.optimization_barrier((even, requests, pressure))
+    requests = [swap(block, "sib", apart) for block, apart in zip(requests, other_sides)]
     bands = jnp.concatenate([even, odd], axis=0)
     part, continuity, move = call(
         pre_kernel,
@@ -476,9 +479,9 @@
         ],
         2 * 10**9,
         [counts],
-        [vel, pressure, viscosity, dx_table, dyz_table, boxes, jnp.asarray(move_table(morton_count))],
-    )
-    bands, part, asked, their_weights = lax.optimization_barrier((bands, part, asked, their_weights))
+        [vel, pressure, viscosity, tables, boxes],
+    )
+    bands, part, requests = lax.optimization_barrier((bands, part, requests))
     window = [faces, swap(faces, "sib", 1), bands, swap(bands, "sib", 1)]
     near, *served, sums = call(
         moment_kernel,
@@ -486,29 +489,22 @@
         2 * 10**9,
         [],
         [
-            part, viscosity, boxes, spread, basis, face_basis, jnp.asarray(compact_table()), spots[0],
-            *window, *asked, *their_weights,
+            part, viscosity, boxes, spread, basis, face_basis, jnp.asarray(compact_table()), spots,
+            *window, *requests,
         ],
         [pltpu.VMEM((ROWS, 3 * sides * leaf_count), f32)],
     )
     got = [swap(block, "sib", apart) for block, apart in zip(served, other_sides)]
     every = lax.all_to_all(sums, ("morton", "sib"), 0, 0, tiled=True)
     every, *got = lax.optimization_barrier((every, *got))
-    (force,) = call(
-        force_kernel,
-        [((3, leaf_count, NODES), f32)],
+    force, box, root = call(
+        last_kernel,
+        [((3, leaf_count, NODES), f32), ((3, 1, MOMENTS), f32), ((3, 1, MOMENTS), f32)],
         2 * 10**8,
         [],
-        [part, viscosity, spread, near, *got],
+        [part, viscosity, spread, every, move, near, *got],
         [pltpu.VMEM((3, leaf_count, NODES), f32), pltpu.SemaphoreType.DMA((3,))],
-        outs=[pltpu.HBM],
-    )
-    box, root = call(
-        final_kernel,
-        [((3, 1, MOMENTS), f32), ((3, 1, MOMENTS), f32)],
-        10**5,
-        [],
-        [every, move],
+        outs=[pltpu.HBM, pltpu.VMEM, pltpu.VMEM],
     )
     return (
         jnp.transpose(force, (1, 0, 2)),

time: 36.8 us -> 36.8 us (level)
  waiting for transfers between devices: 1.02 us -> 3.45 us
  local copies, waits for them, and re-layouts: 2.06 us -> 0.06 us
  blocking collectives: 14.7 us -> 14 us
    unnamed x28 -> x24, local copies, waits for them, and re-layouts: 2.06 us -> 0.06 us
    ppermute x2, waiting for transfers between devices: 0.01 us -> 1.81 us  [pairs(): return lax.ppermute(block, 'morton', route)]
    ppermute x2, starting transfers between devices: 2.14 us -> 3.62 us  [pairs(): return lax.ppermute(block, 'morton', route)]
    ppermute x5 -> x4, starting transfers between devices: 5.58 us -> 4.21 us  [swap(): lax.ppermute(block, axis, [(at, at ^ apart) for at in range(lax.axis_size...]
    all_to_all x1, blocking collectives: 14.7 us -> 14 us  [on_device(): every = lax.all_to_all(sums, ('morton', 'sib'), 0, 0, tiled=True)]
    ppermute x5 -> x4, waiting for transfers between devices: 1.02 us -> 1.64 us  [swap(): lax.ppermute(block, axis, [(at, at ^ apart) for at in range(lax.axis_size...]
    pallas_call x5 -> x4, Pallas kernels: 10.2 us -> 10.4 us  [call(): pl.pallas_call(kernel, out_shape=[jax.ShapeDtypeStruct(shape, dtype) for...]
  transfers between devices with their start and end apart: 7 -> 6, of which waited for: 1 -> 3; matrix products, arithmetic and copies ran while one was open for 0% -> 0% of each run, Pallas kernels for 6% -> 7%
where the time goes in v7:
time: 36.8 us; the launch traced here: 36.6 us
  blocking collectives  14 us (38%)
  Pallas kernels  10.4 us (28%)
  starting transfers between devices  7.82 us (21%)
  waiting for transfers between devices  3.45 us (9%)
  between operations  0.82 us (2%)
    all_to_all x1, blocking collectives, on_device(): every = lax.all_to_all(sums, ('morton', 'sib'), 0, 0, tiled=True)  14 us
    pallas_call x4, Pallas kernels, call(): pl.pallas_call(kernel, out_shape=[jax.ShapeDtypeStruct(shape, dtype) for...  10.4 us
    ppermute x4, starting transfers between devices, swap(): lax.ppermute(block, axis, [(at, at ^ apart) for at in range(lax.axis_size...  4.21 us
    ppermute x2, starting transfers between devices, pairs(): return lax.ppermute(block, 'morton', route)  3.62 us
    ppermute x2, waiting for transfers between devices, pairs(): return lax.ppermute(block, 'morton', route)  1.81 us
    ppermute x4, waiting for transfers between devices, swap(): lax.ppermute(block, axis, [(at, at ^ apart) for at in range(lax.axis_size...  1.64 us
  transfers between devices with their start and end apart: 6, of which 3 were waited for; matrix products, arithmetic and copies ran while one was open for 0% of the time, Pallas kernels for 7%

profile of v7, /device:TPU:0, one launch (start us, length us, event | category | flops | bytes accessed | tf_op | source)
XLA Modules:
  0.0 36.6 jit_solution(11833229136355328898)
XLA Ops:
  0.6 0.0 copy-start.2
  0.6 0.0 copy-start.4
  0.7 0.0 copy-start.6
  0.7 2.6 %shard_map.165 = (bf16[128,1152]{1,0:T(8,128)(2,1)}, bf16[32,1152]{1,0:T(8,128)(2,1)}, bf16[32,1152]{1,0:T(8,128)(2,1)}, f32[16,128]{1,0:T(8,128)}, bf16[144,384]{1,0:T(8,128)(2,1)}) custom-call(s32[32]{0:T(128)} %counts_ref.3, bf16[3,128,512]{2,1,0:T(8,128)(2,1)} %bitcast.7, f32[128,512]{1,0:T(8,128)} %visc_ref.7, s32[6,128]{1,0:T(8,128)} %bitcast.10, ...), custom_call_target="tpu_custom_call" | custom-call | flops 400000000 | bytes 1085440 | tf_op jit(solution)/shard_map/pallas_call | solution.py:427
  3.3 0.0 copy-start.1
  3.3 3.0 %collective-permute-start = (bf16[32,1152]{1,0:T(8,128)(2,1)}, bf16[32,1152]{1,0:T(8,128)(2,1)S(1)}, u32[]{:S(2)}, u32[]{:S(2)}) collective-permute-start(bf16[32,1152]{1,0:T(8,128)(2,1)} %get-tuple-element.26), channel_id=1, source_target_pairs={{0,4},{4,0},{8,12},{12,8},{16,20},{20,16},{24,28},{28,24},{1,5},{5... | collective-permute-start | bytes 221192 | tf_op jit(solution)/shard_map/ppermute | solution.py:118
  6.2 0.7 %collective-permute-start.1 = (bf16[32,1152]{1,0:T(8,128)(2,1)}, bf16[32,1152]{1,0:T(8,128)(2,1)S(1)}, u32[]{:S(2)}, u32[]{:S(2)}) collective-permute-start(bf16[32,1152]{1,0:T(8,128)(2,1)} %get-tuple-element.29), channel_id=1, source_target_pairs={{4,8},{8,4},{12,16},{16,12},{20,24},{24,20},{5,9},{9,5},{13,17},{1... | collective-permute-start | bytes 221192 | tf_op jit(solution)/shard_map/ppermute | solution.py:118
  6.9 0.1 collective-permute-start.3
  7.0 1.8 %collective-permute-done = bf16[32,1152]{1,0:T(8,128)(2,1)S(1)} collective-permute-done((bf16[32,1152]{1,0:T(8,128)(2,1)}, bf16[32,1152]{1,0:T(8,128)(2,1)S(1)}, u32[]{:S(2)}, u32[]{:S(2)}) %collective-permute-start) | collective-permute-done | bytes 73760 | tf_op jit(solution)/shard_map/ppermute | solution.py:118
  8.8 0.0 copy-start.5
  8.8 0.0 copy-start.10
  8.8 2.0 %collective-permute-start.2 = (bf16[144,384]{1,0:T(8,128)(2,1)}, bf16[144,384]{1,0:T(8,128)(2,1)S(1)}, u32[]{:S(2)}, u32[]{:S(2)}) collective-permute-start(bf16[144,384]{1,0:T(8,128)(2,1)} %get-tuple-element.32), channel_id=1, source_target_pairs={{0,2},{1,3},{2,0},{3,1},{4,6},{5,7},{6,4},{7,5},{8,10},{9,11},{10,... | collective-permute-start | bytes 331784 | tf_op jit(solution)/shard_map/ppermute | solution.py:111
  10.8 0.0 collective-permute-done.1
  10.9 0.0 copy-done.2
  10.9 0.0 copy-done.4
  10.9 0.0 copy-done.6
  10.9 0.0 copy-done.1
  10.9 0.0 copy-done.5
  10.9 0.0 copy-done.10
  10.9 0.0 copy-start
  10.9 0.0 copy-start.3
  10.9 0.0 copy-start.7
  11.0 0.0 copy-start.8
  11.0 0.0 copy-start.9
  11.0 0.0 copy-start.11
  11.0 2.5 %shard_map.166 = (f32[3,128,512]{2,1,0:T(8,128)S(1)}, f32[128,512]{1,0:T(8,128)}, f32[256,256]{1,0:T(8,128)S(1)}) custom-call(s32[32]{0:T(128)S(1)} %copy-done.5, bf16[3,128,512]{2,1,0:T(8,128)(2,1)S(1)} %bitcast.8, bf16[128,512]{1,0:T(8,128)(2,1)S(1)} %copy-done.4, f32[128,512]{1,0:T(8,128)S(1)} %copy-done.1, bf16[768,512]{1,0:T(8,128)(2,1)S(1)} %copy-done.6, ...), custom_call_target="tpu_custom_call" | custom-call | flops 2000000000 | bytes 1605632 | tf_op jit(solution)/shard_map/pallas_call | solution.py:427
  13.5 0.3 collective-permute-done.2.refs_4_
  13.8 0.0 collective-permute-start.4
  13.8 0.0 collective-permute-done.3.refs_1_
  13.8 1.4 %collective-permute-done.4.refs_3_ = bf16[64,1152]{1,0:T(8,128)(2,1)S(1)} collective-permute-done((bf16[64,1152]{1,0:T(8,128)(2,1)S(1)}, bf16[64,1152]{1,0:T(8,128)(2,1)S(1)}, u32[]{:S(2)}, u32[]{:S(2)}) %collective-permute-start.4) | collective-permute-done | bytes 147488 | tf_op jit(solution)/shard_map/ppermute | solution.py:111
  15.2 0.0 copy-done
  15.2 0.0 copy-done.3
  15.2 0.0 copy-done.7
  15.2 0.0 copy-done.8
  15.2 0.0 copy-done.9
  15.2 0.0 copy-done.11
  15.2 3.4 %shard_map.167 = (bf16[128,1152]{1,0:T(8,128)(2,1)S(1)}, bf16[128,1152]{1,0:T(8,128)(2,1)S(1)}, f32[32,8,128]{2,1,0:T(8,128)S(1)}) custom-call(f32[3,128,512]{2,1,0:T(8,128)S(1)} %get-tuple-element.33.part_ref, f32[128,512]{1,0:T(8,128)S(1)} %copy-done.1, f32[64,128]{1,0:T(8,128)S(1)} %copy-done.10, bf16[384,512]{1,0:T(8,128)(2,1)S(1)} %copy-done, ...), custom_call_target="tpu_custom_call" | custom-call | flops 2000000000 | bytes 3805184 | tf_op jit(solution)/shard_map/pallas_call | solution.py:427
  18.6 2.1 %collective-permute-start.5 = (bf16[128,1152]{1,0:T(8,128)(2,1)S(1)}, bf16[128,1152]{1,0:T(8,128)(2,1)S(1)}, u32[]{:S(2)}, u32[]{:S(2)}) collective-permute-start(bf16[128,1152]{1,0:T(8,128)(2,1)S(1)} %get-tuple-element.39), channel_id=1, source_target_pairs={{0,2},{1,3},{2,0},{3,1},{4,6},{5,7},{6,4},{7,5},{8,10},{9,11},{10,... | collective-permute-start | bytes 884744 | tf_op jit(solution)/shard_map/ppermute | solution.py:111
  20.7 14.0 %all_to_all.5.sums_ref = f32[32,8,128]{2,1,0:T(8,128)S(1)} all-to-all(f32[32,8,128]{2,1,0:T(8,128)S(1)} %get-tuple-element.38), channel_id=1, replica_groups=mesh['morton'=8,'sib'=4] {'morton','sib'}, dimensions={0} | all-to-all | bytes 262144 | tf_op jit(solution)/shard_map/all_to_all | solution.py:498
  34.7 0.0 collective-permute-done.5.refs_0_
  34.7 1.8 %shard_map.168 = (f32[3,128,512]{2,1,0:T(8,128)}, f32[3,1,216]{2,1,0:T(1,128)}, f32[3,1,216]{2,1,0:T(1,128)}) custom-call(f32[3,128,512]{2,1,0:T(8,128)S(1)} %get-tuple-element.33.part_ref, f32[128,512]{1,0:T(8,128)S(1)} %copy-done.1, bf16[384,512]{1,0:T(8,128)(2,1)S(1)} %copy-done, f32[32,8,128]{2,1,0:T(8,128)S(1)} %all_to_all.5.sums_ref, ...), custom_call_target="tpu_custom_call" | custom-call | flops 200000000 | bytes 2424832 | tf_op jit(solution)/shard_map/pallas_call | solution.py:427
  (1 shorter events, 0.0 us)
Async XLA Ops:
  0.6 10.2 %copy-start.2 = (bf16[128,3,512]{2,0,1:T(8,128)(2,1)S(1)}, bf16[128,3,512]{2,0,1:T(8,128)(2,1)}, u32[]{:S(2)}) copy-start(bf16[128,3,512]{2,0,1:T(8,128)(2,1)} %param.14) | copy-start | bytes 1179652
  0.6 10.2 %copy-start.4 = (bf16[128,512]{1,0:T(8,128)(2,1)S(1)}, bf16[128,512]{1,0:T(8,128)(2,1)}, u32[]{:S(2)}) copy-start(bf16[128,512]{1,0:T(8,128)(2,1)} %press_ref) | copy-start | bytes 393220
  0.7 10.2 %copy-start.6 = (bf16[768,512]{1,0:T(8,128)(2,1)S(1)}, bf16[768,512]{1,0:T(8,128)(2,1)}, u32[]{:S(2)}) copy-start(bf16[768,512]{1,0:T(8,128)(2,1)} %constant.22.table_ref) | copy-start | bytes 2359300
  3.3 7.6 %copy-start.1 = (f32[128,512]{1,0:T(8,128)S(1)}, f32[128,512]{1,0:T(8,128)}, u32[]{:S(2)}) copy-start(f32[128,512]{1,0:T(8,128)} %visc_ref.7) | copy-start | bytes 786436
  3.3 5.5 %collective-permute-start = (bf16[32,1152]{1,0:T(8,128)(2,1)}, bf16[32,1152]{1,0:T(8,128)(2,1)S(1)}, u32[]{:S(2)}, u32[]{:S(2)}) collective-permute-start(bf16[32,1152]{1,0:T(8,128)(2,1)} %get-tuple-element.26), channel_id=1, source_target_pairs={{0,4},{4,0},{8,12},{12,8},{16,20},{20,16},{24,28},{28,24},{1,5},{5... | collective-permute-start | bytes 221192 | tf_op jit(solution)/shard_map/ppermute | solution.py:118
  6.2 4.6 %collective-permute-start.1 = (bf16[32,1152]{1,0:T(8,128)(2,1)}, bf16[32,1152]{1,0:T(8,128)(2,1)S(1)}, u32[]{:S(2)}, u32[]{:S(2)}) collective-permute-start(bf16[32,1152]{1,0:T(8,128)(2,1)} %get-tuple-element.29), channel_id=1, source_target_pairs={{4,8},{8,4},{12,16},{16,12},{20,24},{24,20},{5,9},{9,5},{13,17},{1... | collective-permute-start | bytes 221192 | tf_op jit(solution)/shard_map/ppermute | solution.py:118
  6.9 6.9 %collective-permute-start.3 = (bf16[128,1152]{1,0:T(8,128)(2,1)}, bf16[128,1152]{1,0:T(8,128)(2,1)S(1)}, u32[]{:S(2)}, u32[]{:S(2)}) collective-permute-start(bf16[128,1152]{1,0:T(8,128)(2,1)} %get-tuple-element.35.refs_0_), channel_id=1, source_target_pairs={{0,1},{1,0},{2,3},{3,2},{4,5},{5,4},{6,7},{7,6},{8,9},{9,8},{10,11... | collective-permute-start | bytes 884744 | tf_op jit(solution)/shard_map/ppermute | solution.py:111
  8.8 2.1 %copy-start.5 = (s32[32]{0:T(128)S(1)}, s32[32]{0:T(128)}, u32[]{:S(2)}) copy-start(s32[32]{0:T(128)} %counts_ref.3) | copy-start | bytes 388
  8.8 2.1 %copy-start.10 = (f32[64,128]{1,0:T(8,128)S(1)}, f32[64,128]{1,0:T(8,128)}, u32[]{:S(2)}) copy-start(f32[64,128]{1,0:T(8,128)} %constant.19.clone.box_ref) | copy-start | bytes 98308
  8.8 5.0 %collective-permute-start.2 = (bf16[144,384]{1,0:T(8,128)(2,1)}, bf16[144,384]{1,0:T(8,128)(2,1)S(1)}, u32[]{:S(2)}, u32[]{:S(2)}) collective-permute-start(bf16[144,384]{1,0:T(8,128)(2,1)} %get-tuple-element.32), channel_id=1, source_target_pairs={{0,2},{1,3},{2,0},{3,1},{4,6},{5,7},{6,4},{7,5},{8,10},{9,11},{10,... | collective-permute-start | bytes 331784 | tf_op jit(solution)/shard_map/ppermute | solution.py:111
  10.9 4.2 %copy-start = (bf16[384,512]{1,0:T(8,128)(2,1)S(1)}, bf16[384,512]{1,0:T(8,128)(2,1)}, u32[]{:S(2)}) copy-start(bf16[384,512]{1,0:T(8,128)(2,1)} %constant.23.spread_ref) | copy-start | bytes 1179652
  10.9 4.2 %copy-start.3 = (bf16[128,1152]{1,0:T(8,128)(2,1)S(1)}, bf16[128,1152]{1,0:T(8,128)(2,1)}, u32[]{:S(2)}) copy-start(bf16[128,1152]{1,0:T(8,128)(2,1)} %get-tuple-element.35.refs_0_) | copy-start | bytes 884740
  10.9 4.2 %copy-start.7 = (bf16[576,512]{1,0:T(8,128)(2,1)S(1)}, bf16[576,512]{1,0:T(8,128)(2,1)}, u32[]{:S(2)}) copy-start(bf16[576,512]{1,0:T(8,128)(2,1)} %constant.17.clone.basis_ref) | copy-start | bytes 1769476
  11.0 4.2 %copy-start.8 = (bf16[576,384]{1,0:T(8,128)(2,1)S(1)}, bf16[576,384]{1,0:T(8,128)(2,1)}, u32[]{:S(2)}) copy-start(bf16[576,384]{1,0:T(8,128)(2,1)} %constant.18.clone.face_basis_ref) | copy-start | bytes 1327108
  11.0 4.2 %copy-start.9 = (f32[288,256]{1,0:T(8,128)S(1)}, f32[288,256]{1,0:T(8,128)}, u32[]{:S(2)}) copy-start(f32[288,256]{1,0:T(8,128)} %constant.20.clone.compact_ref) | copy-start | bytes 884740
  11.0 4.2 %copy-start.11 = (f32[16,128]{1,0:T(8,128)S(1)}, f32[16,128]{1,0:T(8,128)}, u32[]{:S(2)}) copy-start(f32[16,128]{1,0:T(8,128)} %get-tuple-element.34.spots_ref) | copy-start | bytes 24580
  13.8 1.4 %collective-permute-start.4 = (bf16[64,1152]{1,0:T(8,128)(2,1)S(1)}, bf16[64,1152]{1,0:T(8,128)(2,1)S(1)}, u32[]{:S(2)}, u32[]{:S(2)}) collective-permute-start(bf16[64,1152]{1,0:T(8,128)(2,1)S(1)} %pad_maximum_fusion.refs_2_), channel_id=1, source_target_pairs={{0,1},{1,0},{2,3},{3,2},{4,5},{5,4},{6,7},{7,6},{8,9},{9,8},{10,11... | collective-permute-start | bytes 442376 | tf_op jit(solution)/shard_map/ppermute | solution.py:111
  18.6 16.1 %collective-permute-start.5 = (bf16[128,1152]{1,0:T(8,128)(2,1)S(1)}, bf16[128,1152]{1,0:T(8,128)(2,1)S(1)}, u32[]{:S(2)}, u32[]{:S(2)}) collective-permute-start(bf16[128,1152]{1,0:T(8,128)(2,1)S(1)} %get-tuple-element.39), channel_id=1, source_target_pairs={{0,2},{1,3},{2,0},{3,1},{4,6},{5,7},{6,4},{7,5},{8,10},{9,11},{10,... | collective-permute-start | bytes 884744 | tf_op jit(solution)/shard_map/ppermute | solution.py:111

commit v8 on v7

--- a/solution.py
+++ b/solution.py
@@ -171,7 +171,7 @@
     band_start = jnp.zeros_like(slot)
     for other in range(sib_count):
         band_start = jnp.where(owner_sib == other, counts_ref[below + other] - BAND, band_start)
-    below_at = BAND * (1 - jnp.bitwise_and(morton, 1))
+    below_at = BAND * jnp.bitwise_and(morton, 1)
     in_band = jnp.where(step < 0, slot - band_start + below_at, slot + BAND - below_at)
     box = box_ref[pl.ds(pl.multiple_of(morton * 8, 8), 8), :]
     shift_bits = 3 * (LMAX - levels_ref[...])
@@ -467,9 +467,9 @@
         grant=60,
     )
     odd, even = pairs(odd, 1), pairs(even, 0)
-    even, requests, pressure = lax.optimization_barrier((even, requests, pressure))
+    across = swap(faces, "sib", 1)
+    across, requests, pressure = lax.optimization_barrier((across, requests, pressure))
     requests = [swap(block, "sib", apart) for block, apart in zip(requests, other_sides)]
-    bands = jnp.concatenate([even, odd], axis=0)
     part, continuity, move = call(
         pre_kernel,
         [
@@ -481,8 +481,9 @@
         [counts],
         [vel, pressure, viscosity, tables, boxes],
     )
-    bands, part, requests = lax.optimization_barrier((bands, part, requests))
-    window = [faces, swap(faces, "sib", 1), bands, swap(bands, "sib", 1)]
+    odd, even, part, requests = lax.optimization_barrier((odd, even, part, requests))
+    bands = jnp.concatenate([odd, even], axis=0)
+    window = [faces, across, bands, swap(bands, "sib", 1)]
     near, *served, sums = call(
         moment_kernel,
         [((leaf_count, width), bf16)] * sides + [((morton_count * sib_count, 8, LANES), f32)],

time: 36.8 us -> 35.3 us (0.959)
  blocking collectives: 14 us -> 11.9 us
  waiting for transfers between devices: 3.45 us -> 1.37 us
  starting transfers between devices: 7.82 us -> 9.48 us
  local copies, waits for them, and re-layouts: 0.06 us -> 1.2 us
    ppermute x2, starting transfers between devices: 3.62 us -> 6 us  [pairs(): return lax.ppermute(block, 'morton', route)]
    all_to_all x1, blocking collectives: 14 us -> 11.9 us  [on_device(): every = lax.all_to_all(sums, ('morton', 'sib'), 0, 0, tiled=True)]
    ppermute x2, waiting for transfers between devices: 1.81 us -> 0.01 us  [pairs(): return lax.ppermute(block, 'morton', route)]
    unnamed x24 -> x25, local copies, waits for them, and re-layouts: 0.06 us -> 1.19 us
    ppermute x4, starting transfers between devices: 4.21 us -> 3.48 us  [swap(): lax.ppermute(block, axis, [(at, at ^ apart) for at in range(lax.axis_size...]
  transfers between devices with their start and end apart: 6 -> 6, of which waited for: 3 -> 1; matrix products, arithmetic and copies ran while one was open for 0% -> 0% of each run, Pallas kernels for 7% -> 7%
where the time goes in v8:
time: 35.3 us; the launch traced here: 35.1 us
  blocking collectives  11.9 us (34%)
  Pallas kernels  10.3 us (29%)
  starting transfers between devices  9.48 us (27%)
  waiting for transfers between devices  1.37 us (4%)
  local copies, waits for them, and re-layouts  1.2 us (3%)
  between operations  0.81 us (2%)
    all_to_all x1, blocking collectives, on_device(): every = lax.all_to_all(sums, ('morton', 'sib'), 0, 0, tiled=True)  11.9 us
    pallas_call x4, Pallas kernels, call(): pl.pallas_call(kernel, out_shape=[jax.ShapeDtypeStruct(shape, dtype) for...  10.3 us
    ppermute x2, starting transfers between devices, pairs(): return lax.ppermute(block, 'morton', route)  6 us
    ppermute x4, starting transfers between devices, swap(): lax.ppermute(block, axis, [(at, at ^ apart) for at in range(lax.axis_size...  3.48 us
    ppermute x4, waiting for transfers between devices, swap(): lax.ppermute(block, axis, [(at, at ^ apart) for at in range(lax.axis_size...  1.37 us
    unnamed x25, local copies, waits for them, and re-layouts  1.19 us
  transfers between devices with their start and end apart: 6, of which 1 were waited for; matrix products, arithmetic and copies ran while one was open for 0% of the time, Pallas kernels for 7%

profile of v8, /device:TPU:0, one launch (start us, length us, event | category | flops | bytes accessed | tf_op | source)
XLA Modules:
  0.0 35.1 jit_solution(15223187848410568428)
XLA Ops:
  0.6 0.0 copy-start.1
  0.6 0.0 copy-start.2
  0.7 0.0 copy-start.4
  0.7 0.0 copy-start.10
  0.7 2.6 %shard_map.165 = (bf16[128,1152]{1,0:T(8,128)(2,1)}, bf16[32,1152]{1,0:T(8,128)(2,1)}, bf16[32,1152]{1,0:T(8,128)(2,1)}, f32[16,128]{1,0:T(8,128)}, bf16[144,384]{1,0:T(8,128)(2,1)}) custom-call(s32[32]{0:T(128)} %counts_ref.3, bf16[3,128,512]{2,1,0:T(8,128)(2,1)} %bitcast.7, f32[128,512]{1,0:T(8,128)} %visc_ref.7, s32[6,128]{1,0:T(8,128)} %bitcast.10, ...), custom_call_target="tpu_custom_call" | custom-call | flops 400000000 | bytes 1085440 | tf_op jit(solution)/shard_map/pallas_call | solution.py:427
  3.2 0.5 %collective-permute-start.2 = (bf16[128,1152]{1,0:T(8,128)(2,1)}, bf16[128,1152]{1,0:T(8,128)(2,1)S(1)}, u32[]{:S(2)}, u32[]{:S(2)}) collective-permute-start(bf16[128,1152]{1,0:T(8,128)(2,1)} %get-tuple-element.29.refs_0_), channel_id=1, source_target_pairs={{0,1},{1,0},{2,3},{3,2},{4,5},{5,4},{6,7},{7,6},{8,9},{9,8},{10,11... | collective-permute-start | bytes 884744 | tf_op jit(solution)/shard_map/ppermute | solution.py:111
  3.7 0.7 %collective-permute-start = (bf16[32,1152]{1,0:T(8,128)(2,1)}, bf16[32,1152]{1,0:T(8,128)(2,1)S(1)}, u32[]{:S(2)}, u32[]{:S(2)}) collective-permute-start(bf16[32,1152]{1,0:T(8,128)(2,1)} %get-tuple-element.27), channel_id=1, source_target_pairs={{4,8},{8,4},{12,16},{16,12},{20,24},{24,20},{5,9},{9,5},{13,17},{1... | collective-permute-start | bytes 221192 | tf_op jit(solution)/shard_map/ppermute | solution.py:118
  4.4 0.0 copy-start.5
  4.4 5.4 %collective-permute-start.1 = (bf16[32,1152]{1,0:T(8,128)(2,1)}, bf16[32,1152]{1,0:T(8,128)(2,1)S(1)}, u32[]{:S(2)}, u32[]{:S(2)}) collective-permute-start(bf16[32,1152]{1,0:T(8,128)(2,1)} %get-tuple-element.28), channel_id=1, source_target_pairs={{0,4},{4,0},{8,12},{12,8},{16,20},{20,16},{24,28},{28,24},{1,5},{5... | collective-permute-start | bytes 221192 | tf_op jit(solution)/shard_map/ppermute | solution.py:118
  9.7 0.0 collective-permute-done.2.refs_1_
  9.7 0.0 copy-start
  9.7 1.5 %collective-permute-start.3 = (bf16[144,384]{1,0:T(8,128)(2,1)}, bf16[144,384]{1,0:T(8,128)(2,1)S(1)}, u32[]{:S(2)}, u32[]{:S(2)}) collective-permute-start(bf16[144,384]{1,0:T(8,128)(2,1)} %get-tuple-element.33), channel_id=1, source_target_pairs={{0,2},{1,3},{2,0},{3,1},{4,6},{5,7},{6,4},{7,5},{8,10},{9,11},{10,... | collective-permute-start | bytes 331784 | tf_op jit(solution)/shard_map/ppermute | solution.py:111
  11.3 0.0 copy-done.1
  11.3 0.0 copy-done.2
  11.3 0.0 copy-done.4
  11.3 0.0 copy-done.10
  11.3 0.0 copy-done.5
  11.3 0.0 copy-start.6
  11.3 1.1 %copy-done.6 = bf16[768,512]{1,0:T(8,128)(2,1)S(1)} copy-done((bf16[768,512]{1,0:T(8,128)(2,1)S(1)}, bf16[768,512]{1,0:T(8,128)(2,1)}, u32[]{:S(2)}) %copy-start.6) | copy-done | bytes 786456
  12.4 0.0 copy-start.7
  12.4 0.0 copy-start.8
  12.4 0.0 copy-start.9
  12.4 0.0 copy-start.11
  12.4 2.5 %shard_map.166 = (f32[3,128,512]{2,1,0:T(8,128)S(1)}, f32[128,512]{1,0:T(8,128)}, f32[256,256]{1,0:T(8,128)S(1)}) custom-call(s32[32]{0:T(128)S(1)} %copy-done.5, bf16[3,128,512]{2,1,0:T(8,128)(2,1)S(1)} %bitcast.8, bf16[128,512]{1,0:T(8,128)(2,1)S(1)} %copy-done.4, f32[128,512]{1,0:T(8,128)S(1)} %copy-done.1, bf16[768,512]{1,0:T(8,128)(2,1)S(1)} %copy-done.6, ...), custom_call_target="tpu_custom_call" | custom-call | flops 2000000000 | bytes 1605632 | tf_op jit(solution)/shard_map/pallas_call | solution.py:427
  14.9 0.0 copy-start.3
  14.9 0.0 collective-permute-done
  15.0 0.0 collective-permute-done.1
  15.0 0.0 collective-permute-done.3.refs_4_
  15.0 0.1 collective-permute-start.4
  15.1 1.4 %collective-permute-done.4.refs_3_ = bf16[64,1152]{1,0:T(8,128)(2,1)S(1)} collective-permute-done((bf16[64,1152]{1,0:T(8,128)(2,1)S(1)}, bf16[64,1152]{1,0:T(8,128)(2,1)S(1)}, u32[]{:S(2)}, u32[]{:S(2)}) %collective-permute-start.4) | collective-permute-done | bytes 147488 | tf_op jit(solution)/shard_map/ppermute | solution.py:111
  16.4 0.0 copy-done
  16.5 0.0 copy-done.7
  16.5 0.0 copy-done.8
  16.5 0.0 copy-done.9
  16.5 0.0 copy-done.11
  16.5 0.0 copy-done.3
  16.5 3.4 %shard_map.167 = (bf16[128,1152]{1,0:T(8,128)(2,1)S(1)}, bf16[128,1152]{1,0:T(8,128)(2,1)S(1)}, f32[32,8,128]{2,1,0:T(8,128)S(1)}) custom-call(f32[3,128,512]{2,1,0:T(8,128)S(1)} %get-tuple-element.34.part_ref, f32[128,512]{1,0:T(8,128)S(1)} %copy-done.1, f32[64,128]{1,0:T(8,128)S(1)} %copy-done.10, bf16[384,512]{1,0:T(8,128)(2,1)S(1)} %copy-done, ...), custom_call_target="tpu_custom_call" | custom-call | flops 2000000000 | bytes 3805184 | tf_op jit(solution)/shard_map/pallas_call | solution.py:427
  19.9 1.4 %collective-permute-start.5 = (bf16[128,1152]{1,0:T(8,128)(2,1)S(1)}, bf16[128,1152]{1,0:T(8,128)(2,1)S(1)}, u32[]{:S(2)}, u32[]{:S(2)}) collective-permute-start(bf16[128,1152]{1,0:T(8,128)(2,1)S(1)} %get-tuple-element.41), channel_id=1, source_target_pairs={{0,2},{1,3},{2,0},{3,1},{4,6},{5,7},{6,4},{7,5},{8,10},{9,11},{10,... | collective-permute-start | bytes 884744 | tf_op jit(solution)/shard_map/ppermute | solution.py:111
  21.3 11.9 %all_to_all.5.sums_ref = f32[32,8,128]{2,1,0:T(8,128)S(1)} all-to-all(f32[32,8,128]{2,1,0:T(8,128)S(1)} %get-tuple-element.40), channel_id=1, replica_groups=mesh['morton'=8,'sib'=4] {'morton','sib'}, dimensions={0} | all-to-all | bytes 262144 | tf_op jit(solution)/shard_map/all_to_all | solution.py:499
  33.2 0.0 collective-permute-done.5.refs_0_
  33.2 1.8 %shard_map.168 = (f32[3,128,512]{2,1,0:T(8,128)}, f32[3,1,216]{2,1,0:T(1,128)}, f32[3,1,216]{2,1,0:T(1,128)}) custom-call(f32[3,128,512]{2,1,0:T(8,128)S(1)} %get-tuple-element.34.part_ref, f32[128,512]{1,0:T(8,128)S(1)} %copy-done.1, bf16[384,512]{1,0:T(8,128)(2,1)S(1)} %copy-done, f32[32,8,128]{2,1,0:T(8,128)S(1)} %all_to_all.5.sums_ref, ...), custom_call_target="tpu_custom_call" | custom-call | flops 200000000 | bytes 2424832 | tf_op jit(solution)/shard_map/pallas_call | solution.py:427
  (2 shorter events, 0.0 us)
Async XLA Ops:
  0.6 10.6 %copy-start.1 = (f32[128,512]{1,0:T(8,128)S(1)}, f32[128,512]{1,0:T(8,128)}, u32[]{:S(2)}) copy-start(f32[128,512]{1,0:T(8,128)} %visc_ref.7) | copy-start | bytes 786436
  0.6 10.6 %copy-start.2 = (bf16[128,3,512]{2,0,1:T(8,128)(2,1)S(1)}, bf16[128,3,512]{2,0,1:T(8,128)(2,1)}, u32[]{:S(2)}) copy-start(bf16[128,3,512]{2,0,1:T(8,128)(2,1)} %param.14) | copy-start | bytes 1179652
  0.7 10.6 %copy-start.4 = (bf16[128,512]{1,0:T(8,128)(2,1)S(1)}, bf16[128,512]{1,0:T(8,128)(2,1)}, u32[]{:S(2)}) copy-start(bf16[128,512]{1,0:T(8,128)(2,1)} %press_ref) | copy-start | bytes 393220
  0.7 10.6 %copy-start.10 = (f32[64,128]{1,0:T(8,128)S(1)}, f32[64,128]{1,0:T(8,128)}, u32[]{:S(2)}) copy-start(f32[64,128]{1,0:T(8,128)} %constant.19.clone.box_ref) | copy-start | bytes 98308
  3.2 6.5 %collective-permute-start.2 = (bf16[128,1152]{1,0:T(8,128)(2,1)}, bf16[128,1152]{1,0:T(8,128)(2,1)S(1)}, u32[]{:S(2)}, u32[]{:S(2)}) collective-permute-start(bf16[128,1152]{1,0:T(8,128)(2,1)} %get-tuple-element.29.refs_0_), channel_id=1, source_target_pairs={{0,1},{1,0},{2,3},{3,2},{4,5},{5,4},{6,7},{7,6},{8,9},{9,8},{10,11... | collective-permute-start | bytes 884744 | tf_op jit(solution)/shard_map/ppermute | solution.py:111
  3.7 11.2 %collective-permute-start = (bf16[32,1152]{1,0:T(8,128)(2,1)}, bf16[32,1152]{1,0:T(8,128)(2,1)S(1)}, u32[]{:S(2)}, u32[]{:S(2)}) collective-permute-start(bf16[32,1152]{1,0:T(8,128)(2,1)} %get-tuple-element.27), channel_id=1, source_target_pairs={{4,8},{8,4},{12,16},{16,12},{20,24},{24,20},{5,9},{9,5},{13,17},{1... | collective-permute-start | bytes 221192 | tf_op jit(solution)/shard_map/ppermute | solution.py:118
  4.4 6.9 %copy-start.5 = (s32[32]{0:T(128)S(1)}, s32[32]{0:T(128)}, u32[]{:S(2)}) copy-start(s32[32]{0:T(128)} %counts_ref.3) | copy-start | bytes 388
  4.4 10.6 %collective-permute-start.1 = (bf16[32,1152]{1,0:T(8,128)(2,1)}, bf16[32,1152]{1,0:T(8,128)(2,1)S(1)}, u32[]{:S(2)}, u32[]{:S(2)}) collective-permute-start(bf16[32,1152]{1,0:T(8,128)(2,1)} %get-tuple-element.28), channel_id=1, source_target_pairs={{0,4},{4,0},{8,12},{12,8},{16,20},{20,16},{24,28},{28,24},{1,5},{5... | collective-permute-start | bytes 221192 | tf_op jit(solution)/shard_map/ppermute | solution.py:118
  9.7 6.7 %copy-start = (bf16[384,512]{1,0:T(8,128)(2,1)S(1)}, bf16[384,512]{1,0:T(8,128)(2,1)}, u32[]{:S(2)}) copy-start(bf16[384,512]{1,0:T(8,128)(2,1)} %constant.23.spread_ref) | copy-start | bytes 1179652
  9.7 5.2 %collective-permute-start.3 = (bf16[144,384]{1,0:T(8,128)(2,1)}, bf16[144,384]{1,0:T(8,128)(2,1)S(1)}, u32[]{:S(2)}, u32[]{:S(2)}) collective-permute-start(bf16[144,384]{1,0:T(8,128)(2,1)} %get-tuple-element.33), channel_id=1, source_target_pairs={{0,2},{1,3},{2,0},{3,1},{4,6},{5,7},{6,4},{7,5},{8,10},{9,11},{10,... | collective-permute-start | bytes 331784 | tf_op jit(solution)/shard_map/ppermute | solution.py:111
  11.3 1.1 %copy-start.6 = (bf16[768,512]{1,0:T(8,128)(2,1)S(1)}, bf16[768,512]{1,0:T(8,128)(2,1)}, u32[]{:S(2)}) copy-start(bf16[768,512]{1,0:T(8,128)(2,1)} %constant.22.table_ref) | copy-start | bytes 2359300
  12.4 4.0 %copy-start.7 = (bf16[576,512]{1,0:T(8,128)(2,1)S(1)}, bf16[576,512]{1,0:T(8,128)(2,1)}, u32[]{:S(2)}) copy-start(bf16[576,512]{1,0:T(8,128)(2,1)} %constant.17.clone.basis_ref) | copy-start | bytes 1769476
  12.4 4.0 %copy-start.8 = (bf16[576,384]{1,0:T(8,128)(2,1)S(1)}, bf16[576,384]{1,0:T(8,128)(2,1)}, u32[]{:S(2)}) copy-start(bf16[576,384]{1,0:T(8,128)(2,1)} %constant.18.clone.face_basis_ref) | copy-start | bytes 1327108
  12.4 4.0 %copy-start.9 = (f32[288,256]{1,0:T(8,128)S(1)}, f32[288,256]{1,0:T(8,128)}, u32[]{:S(2)}) copy-start(f32[288,256]{1,0:T(8,128)} %constant.20.clone.compact_ref) | copy-start | bytes 884740
  12.4 4.1 %copy-start.11 = (f32[16,128]{1,0:T(8,128)S(1)}, f32[16,128]{1,0:T(8,128)}, u32[]{:S(2)}) copy-start(f32[16,128]{1,0:T(8,128)} %get-tuple-element.35.spots_ref) | copy-start | bytes 24580
  14.9 1.5 %copy-start.3 = (bf16[128,1152]{1,0:T(8,128)(2,1)S(1)}, bf16[128,1152]{1,0:T(8,128)(2,1)}, u32[]{:S(2)}) copy-start(bf16[128,1152]{1,0:T(8,128)(2,1)} %get-tuple-element.29.refs_0_) | copy-start | bytes 884740
  15.0 1.4 %collective-permute-start.4 = (bf16[64,1152]{1,0:T(8,128)(2,1)S(1)}, bf16[64,1152]{1,0:T(8,128)(2,1)S(1)}, u32[]{:S(2)}, u32[]{:S(2)}) collective-permute-start(bf16[64,1152]{1,0:T(8,128)(2,1)S(1)} %constant_dynamic-update-slice_fusion.refs_2_), channel_id=1, source_target_pairs={{0,1},{1,0},{2,3},{3,2},{4,5},{5,4},{6,7},{7,6},{8,9},{9,8},{10,11... | collective-permute-start | bytes 442376 | tf_op jit(solution)/shard_map/ppermute | solution.py:111
  19.9 13.3 %collective-permute-start.5 = (bf16[128,1152]{1,0:T(8,128)(2,1)S(1)}, bf16[128,1152]{1,0:T(8,128)(2,1)S(1)}, u32[]{:S(2)}, u32[]{:S(2)}) collective-permute-start(bf16[128,1152]{1,0:T(8,128)(2,1)S(1)} %get-tuple-element.41), channel_id=1, source_target_pairs={{0,2},{1,3},{2,0},{3,1},{4,6},{5,7},{6,4},{7,5},{8,10},{9,11},{10,... | collective-permute-start | bytes 884744 | tf_op jit(solution)/shard_map/ppermute | solution.py:111

commit v9 on v8

--- a/solution.py
+++ b/solution.py
@@ -39,12 +39,10 @@
     return points, derivative
 
 
-def operator_tables():
+def derivative_rows():
     _, derivative = cheb_matrix()
-    along_x = np.kron(derivative, np.eye(64)).T
-    along_y = np.kron(np.eye(4), np.kron(derivative, np.eye(8))).T
-    along_z = np.kron(np.eye(32), derivative).T
-    return np.concatenate([along_x, np.concatenate([along_y, along_z], axis=1)], axis=0)
+    lane = np.arange(NODES)
+    return np.concatenate([derivative[lane // 64 % 8].T, derivative[lane // 8 % 8].T, derivative[lane % 8].T], axis=0)
 
 
 def face_table():
@@ -77,7 +75,7 @@
 
 
 def compact_table():
-    table = np.zeros((ROWS, 256), np.float32)
+    table = np.zeros((ROWS, 256), jnp.bfloat16)
     for group in range(36):
         for power in range(6):
             table[group * 8 + power, group * 6 + power] = 1.0 / 512.0
@@ -230,14 +228,32 @@
     return jnp.concatenate(comps, axis=0)
 
 
-def pre_kernel(
-    counts_ref, vel_ref, press_ref, visc_ref, table_ref, box_ref,
-    part_ref, mass_ref, move_ref,
+def fill_tables(rows_ref, dx_ref, dyz_ref):
+    row = lax.broadcasted_iota(jnp.int32, (64, NODES), 0)
+    col = lax.broadcasted_iota(jnp.int32, (64, NODES), 1)
+    same = row == jnp.bitwise_and(col, 63)
+    for at in range(8):
+        dx_ref[64 * at : 64 * at + 64, :] = jnp.where(same, rows_ref[at : at + 1, :], 0.0).astype(bf16)
+    row = lax.broadcasted_iota(jnp.int32, (8, 256), 0)
+    col = lax.broadcasted_iota(jnp.int32, (8, 256), 1)
+    same = row == jnp.bitwise_and(col, 7)
+    group = jnp.right_shift(col, 3)
+    for pair in range(16):
+        blocks = []
+        for at in (2 * pair, 2 * pair + 1):
+            here = same & (jnp.right_shift(group, 3) == at // 8)
+            along_y = jnp.where(here, rows_ref[8 + at % 8 : 9 + at % 8, :256], 0.0)
+            along_z = jnp.where(group == at, rows_ref[16:24, :256], 0.0)
+            blocks.append(jnp.concatenate([along_y, along_z], axis=1))
+        dyz_ref[16 * pair : 16 * pair + 16, :] = jnp.concatenate(blocks, axis=0).astype(bf16)
+
+
+def stress_kernel(
+    counts_ref, vel_ref, press_ref, visc_ref, rows_ref,
+    part_ref, mass_ref, stress_ref, dx_ref, dyz_ref,
 ):
     sib_count = lax.axis_size("sib")
-    morton_count = lax.axis_size("morton")
-    morton = lax.axis_index("morton")
-    own = morton * sib_count + lax.axis_index("sib")
+    own = lax.axis_index("morton") * sib_count + lax.axis_index("sib")
     leaf_count = mass_ref.shape[0]
     live = lax.broadcasted_iota(jnp.int32, (leaf_count, NODES), 0) < counts_ref[own]
     node = lax.broadcasted_iota(jnp.int32, (1, NODES), 1)
@@ -245,36 +261,47 @@
     for shift in (6, 3, 0):
         idx = jnp.bitwise_and(jnp.right_shift(node, shift), 7)
         touching = touching + jnp.where((idx == 0) | (idx == 7), 1.0, 0.0)
+    fill_tables(rows_ref, dx_ref, dyz_ref)
 
     def rows(stack, at):
         return stack[at * leaf_count : (at + 1) * leaf_count]
 
     visc = visc_ref[...]
     fields = jnp.concatenate([vel_ref[0], vel_ref[1], vel_ref[2], press_ref[...]], axis=0)
-    halves = [dot(fields[:, at : at + 256], table_ref[NODES:, :]) for at in (0, 256)]
+    halves = [dot(fields[:, at : at + 256], dyz_ref[...]) for at in (0, 256)]
     grads = [
-        dot(fields, table_ref[:NODES, :]),
+        dot(fields, dx_ref[...]),
         jnp.concatenate([half[:, :256] for half in halves], axis=1),
         jnp.concatenate([half[:, 256:] for half in halves], axis=1),
     ]
     mass = -(rows(grads[0], 0) + rows(grads[1], 1) + rows(grads[2], 2)) * mass_scale
     mass_ref[...] = jnp.where(live, mass, 0.0)
-    stress = {}
-    for first in range(3):
-        for second in range(first, 3):
-            value = (visc * (rows(grads[second], first) + rows(grads[first], second))).astype(bf16)
-            stress[first, second] = stress[second, first] = value
-    columns = [jnp.concatenate([stress[comp, dim] for comp in range(3)], axis=0) for dim in range(3)]
+    pairs_at = [(first, second) for first in range(3) for second in range(first, 3)]
+    for at, (first, second) in enumerate(pairs_at):
+        stress_ref[at] = (visc * (rows(grads[second], first) + rows(grads[first], second))).astype(bf16)
+    for comp in range(3):
+        jump = touching * vel_ref[comp].astype(f32)
+        part_ref[comp] = (penalty * visc * jump + rows(grads[comp], 3)) * out_scale
+
+
+def divergence_kernel(counts_ref, part_ref, stress_ref, dx_ref, dyz_ref, box_ref, full_ref, move_ref):
+    sib_count = lax.axis_size("sib")
+    morton = lax.axis_index("morton")
+    leaf_count = part_ref.shape[1]
+    live = lax.broadcasted_iota(jnp.int32, (leaf_count, NODES), 0) < counts_ref[morton * sib_count + lax.axis_index("sib")]
+    at_pair = {(0, 0): 0, (0, 1): 1, (0, 2): 2, (1, 1): 3, (1, 2): 4, (2, 2): 5}
+    columns = [
+        jnp.concatenate([stress_ref[at_pair[min(comp, dim), max(comp, dim)]] for comp in range(3)], axis=0)
+        for dim in range(3)
+    ]
     rest = [
-        dot(columns[1][:, at : at + 256], table_ref[NODES:, :256]) + dot(columns[2][:, at : at + 256], table_ref[NODES:, 256:])
+        dot(columns[1][:, at : at + 256], dyz_ref[:, :256]) + dot(columns[2][:, at : at + 256], dyz_ref[:, 256:])
         for at in (0, 256)
     ]
-    div = dot(columns[0], table_ref[:NODES, :]) + jnp.concatenate(rest, axis=1)
+    div = dot(columns[0], dx_ref[...]) + jnp.concatenate(rest, axis=1)
     for comp in range(3):
-        jump = touching * vel_ref[comp].astype(f32)
-        part = (penalty * visc * jump - rows(div, comp) + rows(grads[comp], 3)) * out_scale
-        part_ref[comp] = jnp.where(live, part, 0.0)
-
+        part = part_ref[comp] - div[comp * leaf_count : (comp + 1) * leaf_count] * out_scale
+        full_ref[comp] = jnp.where(live, part, 0.0)
     box = box_ref[pl.ds(pl.multiple_of(morton * 8, 8), 8), :]
     move = jnp.ones((256, 256), f32)
     for dim, stride in enumerate((36, 6, 1)):
@@ -378,7 +405,7 @@
     box = box_ref[pl.ds(pl.multiple_of(morton * 8, 8), 8), :]
     both = shifted([summed[8 * at : 8 * at + 8, :] for at in range(36)], box)
     flat = jnp.concatenate(both, axis=0).T
-    sums = jnp.dot(flat[:8], compact_ref[...], precision=highest, preferred_element_type=f32)
+    sums = sum(dot(piece, compact_ref[...]) for piece in split(flat[:8], 3))
     blank = jnp.zeros((2, LANES), f32)
     to_box = jnp.concatenate([sums[:3, :LANES], sums[:3, LANES:], blank], axis=0)
     to_root = jnp.concatenate([sums[3:6, :LANES], sums[3:6, LANES:], blank], axis=0)
@@ -388,18 +415,7 @@
 
 
 def last_kernel(part_ref, visc_ref, spread_ref, sums_ref, move_ref, near_ref, *refs):
-    got_refs, (force_hbm, box_ref, root_ref, force_ref, sems) = refs[:-5], refs[-5:]
-    faces = near_ref[...]
-    for got_ref in got_refs:
-        faces = faces + got_ref[...]
-    weight = visc_ref[...] * (penalty * out_scale)
-    stores = []
-    for comp in range(3):
-        lanes = [(dim * 3 + comp) * LANES for dim in range(3)]
-        jump = dot(jnp.concatenate([faces[:, at : at + LANES] for at in lanes], axis=1), spread_ref[...])
-        force_ref[comp] = part_ref[comp] - weight * jump
-        stores.append(pltpu.make_async_copy(force_ref.at[comp], force_hbm.at[comp], sems.at[comp]))
-        stores[-1].start()
+    got_refs, (force_hbm, box_hbm, root_hbm, force_ref, box_ref, root_ref, sems) = refs[:-7], refs[-7:]
     sib_count = lax.axis_size("sib")
     morton = lax.axis_index("morton")
     box = jnp.zeros(sums_ref.shape[1:], f32)
@@ -415,6 +431,22 @@
     for comp in range(3):
         box_ref[comp] = box[comp : comp + 1, :MOMENTS]
         root_ref[comp] = root[comp : comp + 1, :MOMENTS]
+    stores = [
+        pltpu.make_async_copy(box_ref, box_hbm, sems.at[3]),
+        pltpu.make_async_copy(root_ref, root_hbm, sems.at[4]),
+    ]
+    for store in stores:
+        store.start()
+    faces = near_ref[...]
+    for got_ref in got_refs:
+        faces = faces + got_ref[...]
+    weight = visc_ref[...] * (penalty * out_scale)
+    for comp in range(3):
+        lanes = [(dim * 3 + comp) * LANES for dim in range(3)]
+        jump = dot(jnp.concatenate([faces[:, at : at + LANES] for at in lanes], axis=1), spread_ref[...])
+        force_ref[comp] = part_ref[comp] - weight * jump
+        stores.append(pltpu.make_async_copy(force_ref.at[comp], force_hbm.at[comp], sems.at[comp]))
+        stores[-1].start()
     for store in stores:
         store.wait()
 
@@ -438,7 +470,7 @@
 def on_device(velocity, pressure, viscosity, levels, morton_keys, counts, neighbors):
     leaf_count = velocity.shape[0]
     morton_count = lax.axis_size("morton")
-    tables = jnp.asarray(operator_tables().astype(np.float32)).astype(bf16)
+    rows = jnp.asarray(derivative_rows().astype(np.float32))
     pick = jnp.asarray(face_table().astype(np.float32)).astype(bf16)
     spread = jnp.asarray(spread_table().astype(np.float32)).astype(bf16)
     basis = basis_tables()
@@ -470,20 +502,29 @@
     across = swap(faces, "sib", 1)
     across, requests, pressure = lax.optimization_barrier((across, requests, pressure))
     requests = [swap(block, "sib", apart) for block, apart in zip(requests, other_sides)]
-    part, continuity, move = call(
-        pre_kernel,
+    part, continuity, stress, along_x, along_yz = call(
+        stress_kernel,
         [
             ((3, leaf_count, NODES), f32),
             ((leaf_count, NODES), f32),
-            ((256, 256), f32),
+            ((6, leaf_count, NODES), bf16),
+            ((NODES, NODES), bf16),
+            ((256, NODES), bf16),
         ],
         2 * 10**9,
         [counts],
-        [vel, pressure, viscosity, tables, boxes],
+        [vel, pressure, viscosity, rows],
     )
     odd, even, part, requests = lax.optimization_barrier((odd, even, part, requests))
     bands = jnp.concatenate([odd, even], axis=0)
     window = [faces, across, bands, swap(bands, "sib", 1)]
+    part, move = call(
+        divergence_kernel,
+        [((3, leaf_count, NODES), f32), ((256, 256), f32)],
+        10**9,
+        [counts],
+        [part, stress, along_x, along_yz, boxes],
+    )
     near, *served, sums = call(
         moment_kernel,
         [((leaf_count, width), bf16)] * sides + [((morton_count * sib_count, 8, LANES), f32)],
@@ -504,8 +545,13 @@
         2 * 10**8,
         [],
         [part, viscosity, spread, every, move, near, *got],
-        [pltpu.VMEM((3, leaf_count, NODES), f32), pltpu.SemaphoreType.DMA((3,))],
-        outs=[pltpu.HBM, pltpu.VMEM, pltpu.VMEM],
+        [
+            pltpu.VMEM((3, leaf_count, NODES), f32),
+            pltpu.VMEM((3, 1, MOMENTS), f32),
+            pltpu.VMEM((3, 1, MOMENTS), f32),
+            pltpu.SemaphoreType.DMA((5,)),
+        ],
+        outs=[pltpu.HBM] * 3,
     )
     return (
         jnp.transpose(force, (1, 0, 2)),

time: 35.3 us -> 35.7 us (1.011)
  Pallas kernels: 10.3 us -> 10.9 us
  local copies, waits for them, and re-layouts: 1.2 us -> 0.73 us
    pallas_call x4 -> x5, Pallas kernels: 10.3 us -> 10.9 us  [call(): pl.pallas_call(kernel, out_shape=[jax.ShapeDtypeStruct(shape, dtype) for...]
    unnamed x25, local copies, waits for them, and re-layouts: 1.19 us -> 0.71 us
  transfers between devices with their start and end apart: 6 -> 6, of which waited for: 1 -> 1; matrix products, arithmetic and copies ran while one was open for 0% -> 0% of each run, Pallas kernels for 7% -> 11%
where the time goes in v9:
time: 35.7 us; the launch traced here: 35.5 us
  blocking collectives  11.8 us (33%)
  Pallas kernels  10.9 us (31%)
  starting transfers between devices  9.63 us (27%)
  waiting for transfers between devices  1.61 us (5%)
  between operations  0.81 us (2%)
  local copies, waits for them, and re-layouts  0.73 us (2%)
    all_to_all x1, blocking collectives, on_device(): every = lax.all_to_all(sums, ('morton', 'sib'), 0, 0, tiled=True)  11.8 us
    pallas_call x5, Pallas kernels, call(): pl.pallas_call(kernel, out_shape=[jax.ShapeDtypeStruct(shape, dtype) for...  10.9 us
    ppermute x2, starting transfers between devices, pairs(): return lax.ppermute(block, 'morton', route)  6 us
    ppermute x4, starting transfers between devices, swap(): lax.ppermute(block, axis, [(at, at ^ apart) for at in range(lax.axis_size...  3.63 us
    ppermute x4, waiting for transfers between devices, swap(): lax.ppermute(block, axis, [(at, at ^ apart) for at in range(lax.axis_size...  1.61 us
  transfers between devices with their start and end apart: 6, of which 1 were waited for; matrix products, arithmetic and copies ran while one was open for 0% of the time, Pallas kernels for 11%

profile of v9, /device:TPU:0, one launch (start us, length us, event | category | flops | bytes accessed | tf_op | source)
XLA Modules:
  0.0 35.5 jit_solution(1629712489226718297)
XLA Ops:
  0.6 0.0 copy-start.1
  0.6 0.0 copy-start.2
  0.7 0.0 copy-start.4
  0.7 0.0 copy-start.9
  0.7 2.6 %shard_map.165 = (bf16[128,1152]{1,0:T(8,128)(2,1)}, bf16[32,1152]{1,0:T(8,128)(2,1)}, bf16[32,1152]{1,0:T(8,128)(2,1)}, f32[16,128]{1,0:T(8,128)}, bf16[144,384]{1,0:T(8,128)(2,1)}) custom-call(s32[32]{0:T(128)} %counts_ref.5, bf16[3,128,512]{2,1,0:T(8,128)(2,1)} %bitcast.7, f32[128,512]{1,0:T(8,128)} %visc_ref.7, s32[6,128]{1,0:T(8,128)} %bitcast.10, ...), custom_call_target="tpu_custom_call" | custom-call | flops 400000000 | bytes 1085440 | tf_op jit(solution)/shard_map/pallas_call | solution.py:459
  3.2 0.5 %collective-permute-start.2 = (bf16[128,1152]{1,0:T(8,128)(2,1)}, bf16[128,1152]{1,0:T(8,128)(2,1)S(1)}, u32[]{:S(2)}, u32[]{:S(2)}) collective-permute-start(bf16[128,1152]{1,0:T(8,128)(2,1)} %get-tuple-element.33.refs_0_), channel_id=1, source_target_pairs={{0,1},{1,0},{2,3},{3,2},{4,5},{5,4},{6,7},{7,6},{8,9},{9,8},{10,11... | collective-permute-start | bytes 884744 | tf_op jit(solution)/shard_map/ppermute | solution.py:109
  3.7 0.7 %collective-permute-start = (bf16[32,1152]{1,0:T(8,128)(2,1)}, bf16[32,1152]{1,0:T(8,128)(2,1)S(1)}, u32[]{:S(2)}, u32[]{:S(2)}) collective-permute-start(bf16[32,1152]{1,0:T(8,128)(2,1)} %get-tuple-element.31), channel_id=1, source_target_pairs={{4,8},{8,4},{12,16},{16,12},{20,24},{24,20},{5,9},{9,5},{13,17},{1... | collective-permute-start | bytes 221192 | tf_op jit(solution)/shard_map/ppermute | solution.py:116
  4.4 0.0 copy-start.5
  4.4 5.4 %collective-permute-start.1 = (bf16[32,1152]{1,0:T(8,128)(2,1)}, bf16[32,1152]{1,0:T(8,128)(2,1)S(1)}, u32[]{:S(2)}, u32[]{:S(2)}) collective-permute-start(bf16[32,1152]{1,0:T(8,128)(2,1)} %get-tuple-element.32), channel_id=1, source_target_pairs={{0,4},{4,0},{8,12},{12,8},{16,20},{20,16},{24,28},{28,24},{1,5},{5... | collective-permute-start | bytes 221192 | tf_op jit(solution)/shard_map/ppermute | solution.py:116
  9.7 0.0 collective-permute-done.2.refs_1_
  9.7 1.5 %collective-permute-start.3 = (bf16[144,384]{1,0:T(8,128)(2,1)}, bf16[144,384]{1,0:T(8,128)(2,1)S(1)}, u32[]{:S(2)}, u32[]{:S(2)}) collective-permute-start(bf16[144,384]{1,0:T(8,128)(2,1)} %get-tuple-element.37), channel_id=1, source_target_pairs={{0,2},{1,3},{2,0},{3,1},{4,6},{5,7},{6,4},{7,5},{8,10},{9,11},{10,... | collective-permute-start | bytes 331784 | tf_op jit(solution)/shard_map/ppermute | solution.py:109
  11.3 0.0 copy-done.1
  11.3 0.0 copy-done.2
  11.3 0.0 copy-done.4
  11.3 0.0 copy-done.9
  11.3 0.0 copy-done.5
  11.3 2.0 %shard_map.166 = (f32[3,128,512]{2,1,0:T(8,128)S(1)}, f32[128,512]{1,0:T(8,128)}, bf16[6,128,512]{2,1,0:T(8,128)(2,1)S(1)}, bf16[512,512]{1,0:T(8,128)(2,1)S(1)}, bf16[256,512]{1,0:T(8,128)(2,1)S(1)}) custom-call(s32[32]{0:T(128)S(1)} %copy-done.5, bf16[3,128,512]{2,1,0:T(8,128)(2,1)S(1)} %bitcast.8, bf16[128,512]{1,0:T(8,128)(2,1)S(1)} %copy-done.4, ...), custom_call_target="tpu_custom_call" | custom-call | flops 2000000000 | bytes 835584 | tf_op jit(solution)/shard_map/pallas_call | solution.py:459
  13.2 0.0 collective-permute-done
  13.2 0.0 collective-permute-done.1
  13.2 1.6 %collective-permute-done.3.refs_4_ = bf16[144,384]{1,0:T(8,128)(2,1)S(1)} collective-permute-done((bf16[144,384]{1,0:T(8,128)(2,1)}, bf16[144,384]{1,0:T(8,128)(2,1)S(1)}, u32[]{:S(2)}, u32[]{:S(2)}) %collective-permute-start.3) | collective-permute-done | bytes 110624 | tf_op jit(solution)/shard_map/ppermute | solution.py:109
  14.9 0.0 copy-start.10
  14.9 0.1 collective-permute-start.4
  15.0 0.7 %copy-done.10 = f32[64,128]{1,0:T(8,128)S(1)} copy-done((f32[64,128]{1,0:T(8,128)S(1)}, f32[64,128]{1,0:T(8,128)}, u32[]{:S(2)}) %copy-start.10) | copy-done | bytes 32792
  15.6 0.0 copy-start
  15.6 0.0 copy-start.3
  15.6 0.0 copy-start.6
  15.6 0.0 copy-start.7
  15.6 0.0 copy-start.8
  15.6 0.0 copy-start.11
  15.6 1.8 %shard_map.167 = (f32[3,128,512]{2,1,0:T(8,128)S(1)}, f32[256,256]{1,0:T(8,128)S(1)}) custom-call(s32[32]{0:T(128)S(1)} %copy-done.5, f32[3,128,512]{2,1,0:T(8,128)S(1)} %get-tuple-element.38.part_ref, bf16[6,128,512]{2,1,0:T(8,128)(2,1)S(1)} %get-tuple-element.39.stress_ref, bf16[512,512]{1,0:T(8,128)(2,1)S(1)} %get-tuple-element.40.dx_ref, ...), custom_call_target="tpu_custom_call" | custom-call | flops 1000000000 | bytes 2392064 | tf_op jit(solution)/shard_map/pallas_call | solution.py:459
  17.4 0.0 collective-permute-done.4.refs_3_
  17.4 0.0 copy-done
  17.4 0.0 copy-done.3
  17.5 0.0 copy-done.6
  17.5 0.0 copy-done.7
  17.5 0.0 copy-done.8
  17.5 0.0 copy-done.11
  17.5 3.3 %shard_map.168 = (bf16[128,1152]{1,0:T(8,128)(2,1)S(1)}, bf16[128,1152]{1,0:T(8,128)(2,1)S(1)}, f32[32,8,128]{2,1,0:T(8,128)S(1)}) custom-call(f32[3,128,512]{2,1,0:T(8,128)S(1)} %get-tuple-element.42.part_ref, f32[128,512]{1,0:T(8,128)S(1)} %copy-done.1, f32[64,128]{1,0:T(8,128)S(1)} %copy-done.10, bf16[384,512]{1,0:T(8,128)(2,1)S(1)} %copy-done, ...), custom_call_target="tpu_custom_call" | custom-call | flops 2000000000 | bytes 3657728 | tf_op jit(solution)/shard_map/pallas_call | solution.py:459
  20.8 1.6 %collective-permute-start.5 = (bf16[128,1152]{1,0:T(8,128)(2,1)S(1)}, bf16[128,1152]{1,0:T(8,128)(2,1)S(1)}, u32[]{:S(2)}, u32[]{:S(2)}) collective-permute-start(bf16[128,1152]{1,0:T(8,128)(2,1)S(1)} %get-tuple-element.49), channel_id=1, source_target_pairs={{0,2},{1,3},{2,0},{3,1},{4,6},{5,7},{6,4},{7,5},{8,10},{9,11},{10,... | collective-permute-start | bytes 884744 | tf_op jit(solution)/shard_map/ppermute | solution.py:109
  22.4 11.8 %all_to_all.5.sums_ref = f32[32,8,128]{2,1,0:T(8,128)S(1)} all-to-all(f32[32,8,128]{2,1,0:T(8,128)S(1)} %get-tuple-element.48), channel_id=1, replica_groups=mesh['morton'=8,'sib'=4] {'morton','sib'}, dimensions={0} | all-to-all | bytes 262144 | tf_op jit(solution)/shard_map/all_to_all | solution.py:540
  34.2 0.0 collective-permute-done.5.refs_0_
  34.2 1.3 %shard_map.169 = (f32[3,128,512]{2,1,0:T(8,128)}, f32[3,1,216]{2,1,0:T(1,128)}, f32[3,1,216]{2,1,0:T(1,128)}) custom-call(f32[3,128,512]{2,1,0:T(8,128)S(1)} %get-tuple-element.42.part_ref, f32[128,512]{1,0:T(8,128)S(1)} %copy-done.1, bf16[384,512]{1,0:T(8,128)(2,1)S(1)} %copy-done, f32[32,8,128]{2,1,0:T(8,128)S(1)} %all_to_all.5.sums_ref, ...), custom_call_target="tpu_custom_call" | custom-call | flops 200000000 | bytes 2424832 | tf_op jit(solution)/shard_map/pallas_call | solution.py:459
  (2 shorter events, 0.0 us)
Async XLA Ops:
  0.6 10.6 %copy-start.1 = (f32[128,512]{1,0:T(8,128)S(1)}, f32[128,512]{1,0:T(8,128)}, u32[]{:S(2)}) copy-start(f32[128,512]{1,0:T(8,128)} %visc_ref.7) | copy-start | bytes 786436
  0.6 10.6 %copy-start.2 = (bf16[128,3,512]{2,0,1:T(8,128)(2,1)S(1)}, bf16[128,3,512]{2,0,1:T(8,128)(2,1)}, u32[]{:S(2)}) copy-start(bf16[128,3,512]{2,0,1:T(8,128)(2,1)} %param.14) | copy-start | bytes 1179652
  0.7 10.6 %copy-start.4 = (bf16[128,512]{1,0:T(8,128)(2,1)S(1)}, bf16[128,512]{1,0:T(8,128)(2,1)}, u32[]{:S(2)}) copy-start(bf16[128,512]{1,0:T(8,128)(2,1)} %press_ref) | copy-start | bytes 393220
  0.7 10.6 %copy-start.9 = (f32[24,512]{1,0:T(8,128)S(1)}, f32[24,512]{1,0:T(8,128)}, u32[]{:S(2)}) copy-start(f32[24,512]{1,0:T(8,128)} %constant.14.clone.rows_ref) | copy-start | bytes 147460
  3.2 6.5 %collective-permute-start.2 = (bf16[128,1152]{1,0:T(8,128)(2,1)}, bf16[128,1152]{1,0:T(8,128)(2,1)S(1)}, u32[]{:S(2)}, u32[]{:S(2)}) collective-permute-start(bf16[128,1152]{1,0:T(8,128)(2,1)} %get-tuple-element.33.refs_0_), channel_id=1, source_target_pairs={{0,1},{1,0},{2,3},{3,2},{4,5},{5,4},{6,7},{7,6},{8,9},{9,8},{10,11... | collective-permute-start | bytes 884744 | tf_op jit(solution)/shard_map/ppermute | solution.py:109
  3.7 9.5 %collective-permute-start = (bf16[32,1152]{1,0:T(8,128)(2,1)}, bf16[32,1152]{1,0:T(8,128)(2,1)S(1)}, u32[]{:S(2)}, u32[]{:S(2)}) collective-permute-start(bf16[32,1152]{1,0:T(8,128)(2,1)} %get-tuple-element.31), channel_id=1, source_target_pairs={{4,8},{8,4},{12,16},{16,12},{20,24},{24,20},{5,9},{9,5},{13,17},{1... | collective-permute-start | bytes 221192 | tf_op jit(solution)/shard_map/ppermute | solution.py:116
  4.4 6.9 %copy-start.5 = (s32[32]{0:T(128)S(1)}, s32[32]{0:T(128)}, u32[]{:S(2)}) copy-start(s32[32]{0:T(128)} %counts_ref.5) | copy-start | bytes 388
  4.4 8.9 %collective-permute-start.1 = (bf16[32,1152]{1,0:T(8,128)(2,1)}, bf16[32,1152]{1,0:T(8,128)(2,1)S(1)}, u32[]{:S(2)}, u32[]{:S(2)}) collective-permute-start(bf16[32,1152]{1,0:T(8,128)(2,1)} %get-tuple-element.32), channel_id=1, source_target_pairs={{0,4},{4,0},{8,12},{12,8},{16,20},{20,16},{24,28},{28,24},{1,5},{5... | collective-permute-start | bytes 221192 | tf_op jit(solution)/shard_map/ppermute | solution.py:116
  9.7 5.1 %collective-permute-start.3 = (bf16[144,384]{1,0:T(8,128)(2,1)}, bf16[144,384]{1,0:T(8,128)(2,1)S(1)}, u32[]{:S(2)}, u32[]{:S(2)}) collective-permute-start(bf16[144,384]{1,0:T(8,128)(2,1)} %get-tuple-element.37), channel_id=1, source_target_pairs={{0,2},{1,3},{2,0},{3,1},{4,6},{5,7},{6,4},{7,5},{8,10},{9,11},{10,... | collective-permute-start | bytes 331784 | tf_op jit(solution)/shard_map/ppermute | solution.py:109
  14.9 0.8 %copy-start.10 = (f32[64,128]{1,0:T(8,128)S(1)}, f32[64,128]{1,0:T(8,128)}, u32[]{:S(2)}) copy-start(f32[64,128]{1,0:T(8,128)} %constant.19.clone.box_ref) | copy-start | bytes 98308
  14.9 2.5 %collective-permute-start.4 = (bf16[64,1152]{1,0:T(8,128)(2,1)S(1)}, bf16[64,1152]{1,0:T(8,128)(2,1)S(1)}, u32[]{:S(2)}, u32[]{:S(2)}) collective-permute-start(bf16[64,1152]{1,0:T(8,128)(2,1)S(1)} %constant_dynamic-update-slice_fusion.refs_2_), channel_id=1, source_target_pairs={{0,1},{1,0},{2,3},{3,2},{4,5},{5,4},{6,7},{7,6},{8,9},{9,8},{10,11... | collective-permute-start | bytes 442376 | tf_op jit(solution)/shard_map/ppermute | solution.py:109
  15.6 1.8 %copy-start = (bf16[384,512]{1,0:T(8,128)(2,1)S(1)}, bf16[384,512]{1,0:T(8,128)(2,1)}, u32[]{:S(2)}) copy-start(bf16[384,512]{1,0:T(8,128)(2,1)} %constant.22.spread_ref) | copy-start | bytes 1179652
  15.6 1.8 %copy-start.3 = (bf16[128,1152]{1,0:T(8,128)(2,1)S(1)}, bf16[128,1152]{1,0:T(8,128)(2,1)}, u32[]{:S(2)}) copy-start(bf16[128,1152]{1,0:T(8,128)(2,1)} %get-tuple-element.33.refs_0_) | copy-start | bytes 884740
  15.6 1.8 %copy-start.6 = (bf16[576,512]{1,0:T(8,128)(2,1)S(1)}, bf16[576,512]{1,0:T(8,128)(2,1)}, u32[]{:S(2)}) copy-start(bf16[576,512]{1,0:T(8,128)(2,1)} %constant.17.clone.basis_ref) | copy-start | bytes 1769476
  15.6 1.8 %copy-start.7 = (bf16[576,384]{1,0:T(8,128)(2,1)S(1)}, bf16[576,384]{1,0:T(8,128)(2,1)}, u32[]{:S(2)}) copy-start(bf16[576,384]{1,0:T(8,128)(2,1)} %constant.18.clone.face_basis_ref) | copy-start | bytes 1327108
  15.6 1.9 %copy-start.8 = (bf16[288,256]{1,0:T(8,128)(2,1)S(1)}, bf16[288,256]{1,0:T(8,128)(2,1)}, u32[]{:S(2)}) copy-start(bf16[288,256]{1,0:T(8,128)(2,1)} %constant.20.clone.compact_ref) | copy-start | bytes 442372
  15.6 1.8 %copy-start.11 = (f32[16,128]{1,0:T(8,128)S(1)}, f32[16,128]{1,0:T(8,128)}, u32[]{:S(2)}) copy-start(f32[16,128]{1,0:T(8,128)} %get-tuple-element.43.spots_ref) | copy-start | bytes 24580
  20.8 13.4 %collective-permute-start.5 = (bf16[128,1152]{1,0:T(8,128)(2,1)S(1)}, bf16[128,1152]{1,0:T(8,128)(2,1)S(1)}, u32[]{:S(2)}, u32[]{:S(2)}) collective-permute-start(bf16[128,1152]{1,0:T(8,128)(2,1)S(1)} %get-tuple-element.49), channel_id=1, source_target_pairs={{0,2},{1,3},{2,0},{3,1},{4,6},{5,7},{6,4},{7,5},{8,10},{9,11},{10,... | collective-permute-start | bytes 884744 | tf_op jit(solution)/shard_map/ppermute | solution.py:109

commit v10 on v9

--- a/solution.py
+++ b/solution.py
@@ -201,12 +201,12 @@
         request_ref[leaf_count:, LANES:] = jnp.zeros((16, FACES - LANES), bf16)
 
 
-def gathered(asked, window_refs):
+def gathered(asked, window_refs, start):
     leaf_count = asked[0].shape[1]
     rows = sum(ref.shape[0] for ref in window_refs)
     blank = jnp.full((LANES - 8 * len(asked), leaf_count), -1.0, f32)
     places = jnp.concatenate([spots[:8] for spots in asked] + [blank], axis=0).T.astype(jnp.int32)
-    cols = lax.broadcasted_iota(jnp.int32, (leaf_count, rows), 1)
+    cols = lax.broadcasted_iota(jnp.int32, (leaf_count, rows), 1) + start
     upper = jnp.bitwise_and(lax.broadcasted_iota(jnp.int32, (leaf_count, FACES), 1), 64) > 0
     chosen = [[] for _ in asked]
     for dim in range(3):
@@ -219,6 +219,14 @@
             first, second = (found[(2 * who + side) * leaf_count : (2 * who + side + 1) * leaf_count] for side in (0, 1))
             chosen[who].append(jnp.where(upper, first, second).astype(bf16))
     return chosen
+
+
+def requested(ref):
+    leaf_count = ref.shape[0] - 16
+    parts = ref[leaf_count:, :LANES].astype(f32)
+    blank = jnp.zeros((2, leaf_count), f32)
+    rows = [parts[:6] * 16.0 + parts[6:12], blank, parts[12:], jnp.zeros((4, leaf_count), f32)]
+    return jnp.concatenate(rows, axis=0)
 
 
 def by_comp(chosen):
@@ -248,9 +256,9 @@
         dyz_ref[16 * pair : 16 * pair + 16, :] = jnp.concatenate(blocks, axis=0).astype(bf16)
 
 
-def stress_kernel(
+def operator_kernel(
     counts_ref, vel_ref, press_ref, visc_ref, rows_ref,
-    part_ref, mass_ref, stress_ref, dx_ref, dyz_ref,
+    part_ref, mass_ref, dx_ref, dyz_ref,
 ):
     sib_count = lax.axis_size("sib")
     own = lax.axis_index("morton") * sib_count + lax.axis_index("sib")
@@ -276,32 +284,31 @@
     ]
     mass = -(rows(grads[0], 0) + rows(grads[1], 1) + rows(grads[2], 2)) * mass_scale
     mass_ref[...] = jnp.where(live, mass, 0.0)
-    pairs_at = [(first, second) for first in range(3) for second in range(first, 3)]
-    for at, (first, second) in enumerate(pairs_at):
-        stress_ref[at] = (visc * (rows(grads[second], first) + rows(grads[first], second))).astype(bf16)
-    for comp in range(3):
-        jump = touching * vel_ref[comp].astype(f32)
-        part_ref[comp] = (penalty * visc * jump + rows(grads[comp], 3)) * out_scale
-
-
-def divergence_kernel(counts_ref, part_ref, stress_ref, dx_ref, dyz_ref, box_ref, full_ref, move_ref):
-    sib_count = lax.axis_size("sib")
-    morton = lax.axis_index("morton")
-    leaf_count = part_ref.shape[1]
-    live = lax.broadcasted_iota(jnp.int32, (leaf_count, NODES), 0) < counts_ref[morton * sib_count + lax.axis_index("sib")]
-    at_pair = {(0, 0): 0, (0, 1): 1, (0, 2): 2, (1, 1): 3, (1, 2): 4, (2, 2): 5}
-    columns = [
-        jnp.concatenate([stress_ref[at_pair[min(comp, dim), max(comp, dim)]] for comp in range(3)], axis=0)
-        for dim in range(3)
-    ]
+    stress = {}
+    for first in range(3):
+        for second in range(first, 3):
+            value = (visc * (rows(grads[second], first) + rows(grads[first], second))).astype(bf16)
+            stress[first, second] = stress[second, first] = value
+    columns = [jnp.concatenate([stress[comp, dim] for comp in range(3)], axis=0) for dim in range(3)]
     rest = [
         dot(columns[1][:, at : at + 256], dyz_ref[:, :256]) + dot(columns[2][:, at : at + 256], dyz_ref[:, 256:])
         for at in (0, 256)
     ]
     div = dot(columns[0], dx_ref[...]) + jnp.concatenate(rest, axis=1)
     for comp in range(3):
-        part = part_ref[comp] - div[comp * leaf_count : (comp + 1) * leaf_count] * out_scale
-        full_ref[comp] = jnp.where(live, part, 0.0)
+        jump = touching * vel_ref[comp].astype(f32)
+        part = (penalty * visc * jump - rows(div, comp) + rows(grads[comp], 3)) * out_scale
+        part_ref[comp] = jnp.where(live, part, 0.0)
+
+
+def group_kernel(box_ref, spots_ref, *refs):
+    sides = lax.axis_size("sib") // 2
+    request_refs, window_refs, move_ref, out_refs = refs[: sides - 1], refs[sides - 1 : sides + 1], refs[sides + 1], refs[sides + 2 :]
+    chosen = gathered([spots_ref[...]] + [requested(ref) for ref in request_refs], window_refs, 0)
+    for blocks, out_ref in zip(chosen, out_refs):
+        for dim, block in enumerate(blocks):
+            out_ref[:, dim * FACES : (dim + 1) * FACES] = block
+    morton = lax.axis_index("morton")
     box = box_ref[pl.ds(pl.multiple_of(morton * 8, 8), 8), :]
     move = jnp.ones((256, 256), f32)
     for dim, stride in enumerate((36, 6, 1)):
@@ -361,22 +368,17 @@
     part_ref, visc_ref, box_ref, spread_ref, basis_ref, face_basis_ref, compact_ref, spots_ref, *refs
 ):
     sides = lax.axis_size("sib") // 2
-    window_refs = refs[:4]
-    request_refs = refs[4 : 3 + sides]
-    near_ref, served_refs, sums_ref, raw_ref = refs[3 + sides], refs[4 + sides : -2], refs[-2], refs[-1]
+    window_refs, request_refs, group_refs = refs[:2], refs[2 : 1 + sides], refs[1 + sides : 1 + 2 * sides]
+    near_ref, served_refs, sums_ref, raw_ref = refs[1 + 2 * sides], refs[2 + 2 * sides : -2], refs[-2], refs[-1]
     morton = lax.axis_index("morton")
     leaf_count = visc_ref.shape[0]
-    asked = [spots_ref[...]]
-    for ref in request_refs:
-        parts = ref[leaf_count:, :LANES].astype(f32)
-        blank = jnp.zeros((2, leaf_count), f32)
-        asked.append(
-            jnp.concatenate([parts[:6] * 16.0 + parts[6:12], blank, parts[12:], jnp.zeros((4, leaf_count), f32)], axis=0)
-        )
-    chosen = gathered(asked, window_refs)
-    for blocks, out_ref in zip(chosen, (near_ref, *served_refs)):
-        for dim, block in enumerate(blocks):
-            out_ref[:, dim * FACES : (dim + 1) * FACES] = block
+    asked = [spots_ref[...]] + [requested(ref) for ref in request_refs]
+    chosen = gathered(asked, window_refs, 2 * leaf_count)
+    for blocks, group_ref, out_ref in zip(chosen, group_refs, (near_ref, *served_refs)):
+        for dim in range(3):
+            lanes = slice(dim * FACES, (dim + 1) * FACES)
+            blocks[dim] = blocks[dim] + group_ref[:, lanes]
+            out_ref[:, lanes] = blocks[dim]
 
     def add_moments(who, values, table_ref):
         high, low = split(values, 2)
@@ -498,32 +500,27 @@
         [vel, viscosity, nbrs, levels.reshape(1, -1), morton_keys.reshape(1, -1), boxes, pick],
         grant=60,
     )
-    odd, even = pairs(odd, 1), pairs(even, 0)
+    odd = pairs(odd, 1)
     across = swap(faces, "sib", 1)
-    across, requests, pressure = lax.optimization_barrier((across, requests, pressure))
+    across, requests, even, pressure = lax.optimization_barrier((across, requests, even, pressure))
     requests = [swap(block, "sib", apart) for block, apart in zip(requests, other_sides)]
-    part, continuity, stress, along_x, along_yz = call(
-        stress_kernel,
-        [
-            ((3, leaf_count, NODES), f32),
-            ((leaf_count, NODES), f32),
-            ((6, leaf_count, NODES), bf16),
-            ((NODES, NODES), bf16),
-            ((256, NODES), bf16),
-        ],
+    even = pairs(even, 0)
+    part, continuity = call(
+        operator_kernel,
+        [((3, leaf_count, NODES), f32), ((leaf_count, NODES), f32)],
         2 * 10**9,
         [counts],
         [vel, pressure, viscosity, rows],
+        [pltpu.VMEM((NODES, NODES), bf16), pltpu.VMEM((256, NODES), bf16)],
     )
     odd, even, part, requests = lax.optimization_barrier((odd, even, part, requests))
     bands = jnp.concatenate([odd, even], axis=0)
-    window = [faces, across, bands, swap(bands, "sib", 1)]
-    part, move = call(
-        divergence_kernel,
-        [((3, leaf_count, NODES), f32), ((256, 256), f32)],
+    move, *group = call(
+        group_kernel,
+        [((256, 256), f32)] + [((leaf_count, width), bf16)] * sides,
         10**9,
-        [counts],
-        [part, stress, along_x, along_yz, boxes],
+        [],
+        [boxes, spots, *requests, faces, across],
     )
     near, *served, sums = call(
         moment_kernel,
@@ -532,7 +529,7 @@
         [],
         [
             part, viscosity, boxes, spread, basis, face_basis, jnp.asarray(compact_table()), spots,
-            *window, *requests,
+            bands, swap(bands, "sib", 1), *requests, *group,
         ],
         [pltpu.VMEM((ROWS, 3 * sides * leaf_count), f32)],
     )

time: 35.7 us -> 34.1 us (0.955)
  Pallas kernels: 10.9 us -> 9.93 us
  waiting for transfers between devices: 1.61 us -> 2.41 us
  starting transfers between devices: 9.63 us -> 8.89 us
  local copies, waits for them, and re-layouts: 0.73 us -> 0.08 us
    pallas_call x5, Pallas kernels: 10.9 us -> 9.93 us  [call(): pl.pallas_call(kernel, out_shape=[jax.ShapeDtypeStruct(shape, dtype) for...]
    ppermute x4, waiting for transfers between devices: 1.61 us -> 2.4 us  [swap(): lax.ppermute(block, axis, [(at, at ^ apart) for at in range(lax.axis_size...]
    ppermute x2, starting transfers between devices: 6 us -> 5.27 us  [pairs(): return lax.ppermute(block, 'morton', route)]
    unnamed x25, local copies, waits for them, and re-layouts: 0.71 us -> 0.07 us
  transfers between devices with their start and end apart: 6 -> 6, of which waited for: 1 -> 2; matrix products, arithmetic and copies ran while one was open for 0% -> 0% of each run, Pallas kernels for 11% -> 9%
where the time goes in v10:
time: 34.1 us; the launch traced here: 33.9 us
  blocking collectives  11.8 us (35%)
  Pallas kernels  9.93 us (29%)
  starting transfers between devices  8.89 us (26%)
  waiting for transfers between devices  2.41 us (7%)
  between operations  0.83 us (2%)
    all_to_all x1, blocking collectives, on_device(): every = lax.all_to_all(sums, ('morton', 'sib'), 0, 0, tiled=True)  11.8 us
    pallas_call x5, Pallas kernels, call(): pl.pallas_call(kernel, out_shape=[jax.ShapeDtypeStruct(shape, dtype) for...  9.93 us
    ppermute x2, starting transfers between devices, pairs(): return lax.ppermute(block, 'morton', route)  5.27 us
    ppermute x4, starting transfers between devices, swap(): lax.ppermute(block, axis, [(at, at ^ apart) for at in range(lax.axis_size...  3.63 us
    ppermute x4, waiting for transfers between devices, swap(): lax.ppermute(block, axis, [(at, at ^ apart) for at in range(lax.axis_size...  2.4 us
  transfers between devices with their start and end apart: 6, of which 2 were waited for; matrix products, arithmetic and copies ran while one was open for 0% of the time, Pallas kernels for 9%

profile of v10, /device:TPU:0, one launch (start us, length us, event | category | flops | bytes accessed | tf_op | source)
XLA Modules:
  0.0 33.9 jit_solution(17649279739734210541)
XLA Ops:
  0.6 0.0 copy-start.1
  0.6 0.0 copy-start.2
  0.7 0.0 copy-start.4
  0.7 0.0 copy-start.9
  0.7 2.6 %shard_map.165 = (bf16[128,1152]{1,0:T(8,128)(2,1)}, bf16[32,1152]{1,0:T(8,128)(2,1)}, bf16[32,1152]{1,0:T(8,128)(2,1)}, f32[16,128]{1,0:T(8,128)}, bf16[144,384]{1,0:T(8,128)(2,1)}) custom-call(s32[32]{0:T(128)} %counts_ref.3, bf16[3,128,512]{2,1,0:T(8,128)(2,1)} %bitcast.7, f32[128,512]{1,0:T(8,128)} %visc_ref.7, s32[6,128]{1,0:T(8,128)} %bitcast.10, ...), custom_call_target="tpu_custom_call" | custom-call | flops 400000000 | bytes 1085440 | tf_op jit(solution)/shard_map/pallas_call | solution.py:461
  3.2 0.5 %collective-permute-start.1 = (bf16[128,1152]{1,0:T(8,128)(2,1)}, bf16[128,1152]{1,0:T(8,128)(2,1)S(1)}, u32[]{:S(2)}, u32[]{:S(2)}) collective-permute-start(bf16[128,1152]{1,0:T(8,128)(2,1)} %get-tuple-element.31.refs_1_), channel_id=1, source_target_pairs={{0,1},{1,0},{2,3},{3,2},{4,5},{5,4},{6,7},{7,6},{8,9},{9,8},{10,11... | collective-permute-start | bytes 884744 | tf_op jit(solution)/shard_map/ppermute | solution.py:109
  3.7 0.7 %collective-permute-start = (bf16[32,1152]{1,0:T(8,128)(2,1)}, bf16[32,1152]{1,0:T(8,128)(2,1)S(1)}, u32[]{:S(2)}, u32[]{:S(2)}) collective-permute-start(bf16[32,1152]{1,0:T(8,128)(2,1)} %get-tuple-element.30), channel_id=1, source_target_pairs={{4,8},{8,4},{12,16},{16,12},{20,24},{24,20},{5,9},{9,5},{13,17},{1... | collective-permute-start | bytes 221192 | tf_op jit(solution)/shard_map/ppermute | solution.py:116
  4.4 0.8 %collective-permute-done.1.refs_2_ = bf16[128,1152]{1,0:T(8,128)(2,1)S(1)} collective-permute-done((bf16[128,1152]{1,0:T(8,128)(2,1)}, bf16[128,1152]{1,0:T(8,128)(2,1)S(1)}, u32[]{:S(2)}, u32[]{:S(2)}) %collective-permute-start.1) | collective-permute-done | bytes 294944 | tf_op jit(solution)/shard_map/ppermute | solution.py:109
  5.1 0.0 copy-start.5
  5.1 4.6 %collective-permute-start.2 = (bf16[32,1152]{1,0:T(8,128)(2,1)}, bf16[32,1152]{1,0:T(8,128)(2,1)S(1)}, u32[]{:S(2)}, u32[]{:S(2)}) collective-permute-start(bf16[32,1152]{1,0:T(8,128)(2,1)} %get-tuple-element.34), channel_id=1, source_target_pairs={{0,4},{4,0},{8,12},{12,8},{16,20},{20,16},{24,28},{28,24},{1,5},{5... | collective-permute-start | bytes 221192 | tf_op jit(solution)/shard_map/ppermute | solution.py:116
  9.7 1.5 %collective-permute-start.3 = (bf16[144,384]{1,0:T(8,128)(2,1)}, bf16[144,384]{1,0:T(8,128)(2,1)S(1)}, u32[]{:S(2)}, u32[]{:S(2)}) collective-permute-start(bf16[144,384]{1,0:T(8,128)(2,1)} %get-tuple-element.37), channel_id=1, source_target_pairs={{0,2},{1,3},{2,0},{3,1},{4,6},{5,7},{6,4},{7,5},{8,10},{9,11},{10,... | collective-permute-start | bytes 331784 | tf_op jit(solution)/shard_map/ppermute | solution.py:109
  11.3 0.0 copy-done.1
  11.3 0.0 copy-done.2
  11.3 0.0 copy-done.4
  11.3 0.0 copy-done.9
  11.3 0.0 copy-done.5
  11.3 0.0 copy-start.10
  11.3 0.0 copy-start.11
  11.3 1.9 %shard_map.166 = (f32[3,128,512]{2,1,0:T(8,128)S(1)}, f32[128,512]{1,0:T(8,128)}) custom-call(s32[32]{0:T(128)S(1)} %copy-done.5, bf16[3,128,512]{2,1,0:T(8,128)(2,1)S(1)} %bitcast.8, bf16[128,512]{1,0:T(8,128)(2,1)S(1)} %copy-done.4, f32[128,512]{1,0:T(8,128)S(1)} %copy-done.1, f32[24,512]{1,0:T(8,128)S(1)} %copy-done.9), custom_call_target="tpu_custom_call" | custom-call | flops 2000000000 | bytes 835584 | tf_op jit(solution)/shard_map/pallas_call | solution.py:461
  13.2 0.0 copy-start.3
  13.2 0.0 collective-permute-done
  13.2 0.0 collective-permute-done.2
  13.2 1.6 %collective-permute-done.3.refs_0_.refs_2_ = bf16[144,384]{1,0:T(8,128)(2,1)S(1)} collective-permute-done((bf16[144,384]{1,0:T(8,128)(2,1)}, bf16[144,384]{1,0:T(8,128)(2,1)S(1)}, u32[]{:S(2)}, u32[]{:S(2)}) %collective-permute-start.3) | collective-permute-done | bytes 110624 | tf_op jit(solution)/shard_map/ppermute | solution.py:109
  14.9 0.1 collective-permute-start.4
  15.0 0.0 copy-done.10
  15.0 0.0 copy-done.11
  15.0 0.0 copy-done.3
  15.0 0.0 copy-start
  15.0 0.0 copy-start.6
  15.0 0.0 copy-start.7
  15.0 0.0 copy-start.8
  15.0 1.3 %shard_map.167 = (f32[256,256]{1,0:T(8,128)S(1)}, bf16[128,1152]{1,0:T(8,128)(2,1)S(1)}, bf16[128,1152]{1,0:T(8,128)(2,1)S(1)}) custom-call(f32[64,128]{1,0:T(8,128)S(1)} %copy-done.10, f32[16,128]{1,0:T(8,128)S(1)} %copy-done.11, bf16[144,384]{1,0:T(8,128)(2,1)S(1)} %collective-permute-done.3.refs_0_.refs_2_, bf16[128,1152]{1,0:T(8,128)(2,1)S(1)} %copy-done.3, ...), custom_call_target="tpu_custom_call" | custom-call | flops 1000000000 | bytes 741376 | tf_op jit(solution)/shard_map/pallas_call | solution.py:461
  16.3 0.0 collective-permute-done.4.refs_1_
  16.3 0.0 copy-done
  16.3 0.0 copy-done.6
  16.3 0.0 copy-done.7
  16.3 0.0 copy-done.8
  16.4 2.9 %shard_map.168 = (bf16[128,1152]{1,0:T(8,128)(2,1)S(1)}, bf16[128,1152]{1,0:T(8,128)(2,1)S(1)}, f32[32,8,128]{2,1,0:T(8,128)S(1)}) custom-call(f32[3,128,512]{2,1,0:T(8,128)S(1)} %get-tuple-element.38.part_ref, f32[128,512]{1,0:T(8,128)S(1)} %copy-done.1, f32[64,128]{1,0:T(8,128)S(1)} %copy-done.10, bf16[384,512]{1,0:T(8,128)(2,1)S(1)} %copy-done, ...), custom_call_target="tpu_custom_call" | custom-call | flops 2000000000 | bytes 3657728 | tf_op jit(solution)/shard_map/pallas_call | solution.py:461
  19.3 1.6 %collective-permute-start.5 = (bf16[128,1152]{1,0:T(8,128)(2,1)S(1)}, bf16[128,1152]{1,0:T(8,128)(2,1)S(1)}, u32[]{:S(2)}, u32[]{:S(2)}) collective-permute-start(bf16[128,1152]{1,0:T(8,128)(2,1)S(1)} %get-tuple-element.47), channel_id=1, source_target_pairs={{0,2},{1,3},{2,0},{3,1},{4,6},{5,7},{6,4},{7,5},{8,10},{9,11},{10,... | collective-permute-start | bytes 884744 | tf_op jit(solution)/shard_map/ppermute | solution.py:109
  20.8 11.8 %all_to_all.5.sums_ref = f32[32,8,128]{2,1,0:T(8,128)S(1)} all-to-all(f32[32,8,128]{2,1,0:T(8,128)S(1)} %get-tuple-element.46), channel_id=1, replica_groups=mesh['morton'=8,'sib'=4] {'morton','sib'}, dimensions={0} | all-to-all | bytes 262144 | tf_op jit(solution)/shard_map/all_to_all | solution.py:537
  32.6 0.0 collective-permute-done.5.refs_0_
  32.6 1.3 %shard_map.169 = (f32[3,128,512]{2,1,0:T(8,128)}, f32[3,1,216]{2,1,0:T(1,128)}, f32[3,1,216]{2,1,0:T(1,128)}) custom-call(f32[3,128,512]{2,1,0:T(8,128)S(1)} %get-tuple-element.38.part_ref, f32[128,512]{1,0:T(8,128)S(1)} %copy-done.1, bf16[384,512]{1,0:T(8,128)(2,1)S(1)} %copy-done, f32[32,8,128]{2,1,0:T(8,128)S(1)} %all_to_all.5.sums_ref, ...), custom_call_target="tpu_custom_call" | custom-call | flops 200000000 | bytes 2424832 | tf_op jit(solution)/shard_map/pallas_call | solution.py:461
  (2 shorter events, 0.0 us)
Async XLA Ops:
  0.6 10.6 %copy-start.1 = (f32[128,512]{1,0:T(8,128)S(1)}, f32[128,512]{1,0:T(8,128)}, u32[]{:S(2)}) copy-start(f32[128,512]{1,0:T(8,128)} %visc_ref.7) | copy-start | bytes 786436
  0.6 10.6 %copy-start.2 = (bf16[128,3,512]{2,0,1:T(8,128)(2,1)S(1)}, bf16[128,3,512]{2,0,1:T(8,128)(2,1)}, u32[]{:S(2)}) copy-start(bf16[128,3,512]{2,0,1:T(8,128)(2,1)} %param.14) | copy-start | bytes 1179652
  0.7 10.6 %copy-start.4 = (bf16[128,512]{1,0:T(8,128)(2,1)S(1)}, bf16[128,512]{1,0:T(8,128)(2,1)}, u32[]{:S(2)}) copy-start(bf16[128,512]{1,0:T(8,128)(2,1)} %press_ref) | copy-start | bytes 393220
  0.7 10.6 %copy-start.9 = (f32[24,512]{1,0:T(8,128)S(1)}, f32[24,512]{1,0:T(8,128)}, u32[]{:S(2)}) copy-start(f32[24,512]{1,0:T(8,128)} %constant.14.clone.rows_ref) | copy-start | bytes 147460
  3.2 1.9 %collective-permute-start.1 = (bf16[128,1152]{1,0:T(8,128)(2,1)}, bf16[128,1152]{1,0:T(8,128)(2,1)S(1)}, u32[]{:S(2)}, u32[]{:S(2)}) collective-permute-start(bf16[128,1152]{1,0:T(8,128)(2,1)} %get-tuple-element.31.refs_1_), channel_id=1, source_target_pairs={{0,1},{1,0},{2,3},{3,2},{4,5},{5,4},{6,7},{7,6},{8,9},{9,8},{10,11... | collective-permute-start | bytes 884744 | tf_op jit(solution)/shard_map/ppermute | solution.py:109
  3.7 9.5 %collective-permute-start = (bf16[32,1152]{1,0:T(8,128)(2,1)}, bf16[32,1152]{1,0:T(8,128)(2,1)S(1)}, u32[]{:S(2)}, u32[]{:S(2)}) collective-permute-start(bf16[32,1152]{1,0:T(8,128)(2,1)} %get-tuple-element.30), channel_id=1, source_target_pairs={{4,8},{8,4},{12,16},{16,12},{20,24},{24,20},{5,9},{9,5},{13,17},{1... | collective-permute-start | bytes 221192 | tf_op jit(solution)/shard_map/ppermute | solution.py:116
  5.1 6.2 %copy-start.5 = (s32[32]{0:T(128)S(1)}, s32[32]{0:T(128)}, u32[]{:S(2)}) copy-start(s32[32]{0:T(128)} %counts_ref.3) | copy-start | bytes 388
  5.1 8.1 %collective-permute-start.2 = (bf16[32,1152]{1,0:T(8,128)(2,1)}, bf16[32,1152]{1,0:T(8,128)(2,1)S(1)}, u32[]{:S(2)}, u32[]{:S(2)}) collective-permute-start(bf16[32,1152]{1,0:T(8,128)(2,1)} %get-tuple-element.34), channel_id=1, source_target_pairs={{0,4},{4,0},{8,12},{12,8},{16,20},{20,16},{24,28},{28,24},{1,5},{5... | collective-permute-start | bytes 221192 | tf_op jit(solution)/shard_map/ppermute | solution.py:116
  9.7 5.1 %collective-permute-start.3 = (bf16[144,384]{1,0:T(8,128)(2,1)}, bf16[144,384]{1,0:T(8,128)(2,1)S(1)}, u32[]{:S(2)}, u32[]{:S(2)}) collective-permute-start(bf16[144,384]{1,0:T(8,128)(2,1)} %get-tuple-element.37), channel_id=1, source_target_pairs={{0,2},{1,3},{2,0},{3,1},{4,6},{5,7},{6,4},{7,5},{8,10},{9,11},{10,... | collective-permute-start | bytes 331784 | tf_op jit(solution)/shard_map/ppermute | solution.py:109
  11.3 3.7 %copy-start.10 = (f32[64,128]{1,0:T(8,128)S(1)}, f32[64,128]{1,0:T(8,128)}, u32[]{:S(2)}) copy-start(f32[64,128]{1,0:T(8,128)} %constant.19.clone.box_ref) | copy-start | bytes 98308
  11.3 3.7 %copy-start.11 = (f32[16,128]{1,0:T(8,128)S(1)}, f32[16,128]{1,0:T(8,128)}, u32[]{:S(2)}) copy-start(f32[16,128]{1,0:T(8,128)} %get-tuple-element.39.spots_ref) | copy-start | bytes 24580
  13.2 1.8 %copy-start.3 = (bf16[128,1152]{1,0:T(8,128)(2,1)S(1)}, bf16[128,1152]{1,0:T(8,128)(2,1)}, u32[]{:S(2)}) copy-start(bf16[128,1152]{1,0:T(8,128)(2,1)} %get-tuple-element.31.refs_1_) | copy-start | bytes 884740
  14.9 1.4 %collective-permute-start.4 = (bf16[64,1152]{1,0:T(8,128)(2,1)S(1)}, bf16[64,1152]{1,0:T(8,128)(2,1)S(1)}, u32[]{:S(2)}, u32[]{:S(2)}) collective-permute-start(bf16[64,1152]{1,0:T(8,128)(2,1)S(1)} %constant_dynamic-update-slice_fusion.refs_0_), channel_id=1, source_target_pairs={{0,1},{1,0},{2,3},{3,2},{4,5},{5,4},{6,7},{7,6},{8,9},{9,8},{10,11... | collective-permute-start | bytes 442376 | tf_op jit(solution)/shard_map/ppermute | solution.py:109
  15.0 1.3 %copy-start = (bf16[384,512]{1,0:T(8,128)(2,1)S(1)}, bf16[384,512]{1,0:T(8,128)(2,1)}, u32[]{:S(2)}) copy-start(bf16[384,512]{1,0:T(8,128)(2,1)} %constant.22.spread_ref) | copy-start | bytes 1179652
  15.0 1.3 %copy-start.6 = (bf16[576,512]{1,0:T(8,128)(2,1)S(1)}, bf16[576,512]{1,0:T(8,128)(2,1)}, u32[]{:S(2)}) copy-start(bf16[576,512]{1,0:T(8,128)(2,1)} %constant.17.clone.basis_ref) | copy-start | bytes 1769476
  15.0 1.3 %copy-start.7 = (bf16[576,384]{1,0:T(8,128)(2,1)S(1)}, bf16[576,384]{1,0:T(8,128)(2,1)}, u32[]{:S(2)}) copy-start(bf16[576,384]{1,0:T(8,128)(2,1)} %constant.18.clone.face_basis_ref) | copy-start | bytes 1327108
  15.0 1.3 %copy-start.8 = (bf16[288,256]{1,0:T(8,128)(2,1)S(1)}, bf16[288,256]{1,0:T(8,128)(2,1)}, u32[]{:S(2)}) copy-start(bf16[288,256]{1,0:T(8,128)(2,1)} %constant.20.clone.compact_ref) | copy-start | bytes 442372
  19.3 13.4 %collective-permute-start.5 = (bf16[128,1152]{1,0:T(8,128)(2,1)S(1)}, bf16[128,1152]{1,0:T(8,128)(2,1)S(1)}, u32[]{:S(2)}, u32[]{:S(2)}) collective-permute-start(bf16[128,1152]{1,0:T(8,128)(2,1)S(1)} %get-tuple-element.47), channel_id=1, source_target_pairs={{0,2},{1,3},{2,0},{3,1},{4,6},{5,7},{6,4},{7,5},{8,10},{9,11},{10,... | collective-permute-start | bytes 884744 | tf_op jit(solution)/shard_map/ppermute | solution.py:109

commit v11 on v10

--- a/solution.py
+++ b/solution.py
@@ -14,7 +14,7 @@
 BAND = 32
 NODES = 512
 FACES = 384
-ROWS = 288
+ROWS = 224
 LANES = 128
 
 penalty = 256.0
@@ -66,20 +66,11 @@
 def basis_tables():
     points, _ = cheb_matrix()
     powers = np.stack([points**power for power in range(DEG + 1)])
-    basis = np.zeros((6, 6, 8, 8, 8, 8))
-    basis[:, :, :6] = np.einsum("xa,yb,zc->xyzabc", powers, powers, powers)
-    basis = basis.reshape(ROWS, NODES).astype(np.float32)
+    basis = np.zeros((ROWS, NODES), np.float32)
+    basis[:MOMENTS] = np.einsum("xa,yb,zc->xyzabc", powers, powers, powers).reshape(MOMENTS, NODES)
     top = np.asarray(basis.astype(jnp.bfloat16))
     rest = np.asarray((basis - top.astype(np.float32)).astype(jnp.bfloat16))
     return np.concatenate([top, rest], axis=0)
-
-
-def compact_table():
-    table = np.zeros((ROWS, 256), jnp.bfloat16)
-    for group in range(36):
-        for power in range(6):
-            table[group * 8 + power, group * 6 + power] = 1.0 / 512.0
-    return table
 
 
 def box_table(morton_count):
@@ -330,30 +321,29 @@
     move_ref[...] = move
 
 
-def shifted(tiles, geom):
-    width = tiles[0].shape
-    scale = jnp.broadcast_to(geom[3:4, :], width)
-    level = lax.broadcasted_iota(jnp.int32, width, 0)
-    depth = jnp.ones(width, f32)
-    for power in range(1, DEG + 1):
-        depth = depth * jnp.where(level >= power, scale, 1.0)
-    scales = [depth]
-    for _ in range(2 * DEG):
-        scales.append(scales[-1] * scale)
-    tiles = [tile * scales[at // 6 + at % 6] for at, tile in enumerate(tiles)]
-    along = [jnp.broadcast_to(geom[dim : dim + 1, :], width) for dim in range(3)]
-    for low in range(1, DEG + 1):
-        for power in range(DEG, low - 1, -1):
-            for other in range(6):
-                at = power * 6 + other
-                tiles[at] = tiles[at] + along[0] * tiles[at - 6]
-            for other in range(6):
-                at = other * 6 + power
-                tiles[at] = tiles[at] + along[1] * tiles[at - 1]
-    steps = [jnp.where(level >= low, along[2], 0.0) for low in range(1, DEG + 1)]
-    for step in steps:
-        tiles = [tile + step * pltpu.roll(tile, 1, 0) for tile in tiles]
-    return tiles
+def shifted(load, geom, width):
+    def rows(at):
+        return jnp.concatenate([leaf[at : at + 1, :] for leaf in geom for _ in range(3)], axis=0)
+
+    scales = [None, rows(3)]
+    for _ in range(2, 3 * DEG + 1):
+        scales.append(scales[-1] * scales[1])
+    tiles = {}
+    for ax in range(width):
+        for ay in range(width):
+            for az in range(width):
+                tile = load((ax * width + ay) * width + az)
+                degree = ax + ay + az
+                tiles[ax, ay, az] = tile * scales[degree] if degree else tile
+    for dim in (2, 1, 0):
+        along = rows(dim)
+        for first in range(width):
+            for second in range(width):
+                places = [tuple(np.insert([first, second], dim, power)) for power in range(width)]
+                for low in range(1, width):
+                    for power in range(width - 1, low - 1, -1):
+                        tiles[places[power]] = tiles[places[power]] + along * tiles[places[power - 1]]
+    return [tiles[place] for place in np.ndindex(width, width, width)]
 
 
 def split(values, parts):
@@ -365,11 +355,11 @@
 
 
 def moment_kernel(
-    part_ref, visc_ref, box_ref, spread_ref, basis_ref, face_basis_ref, compact_ref, spots_ref, *refs
+    part_ref, visc_ref, spread_ref, basis_ref, face_basis_ref, move_ref, spots_ref, *refs
 ):
     sides = lax.axis_size("sib") // 2
     window_refs, request_refs, group_refs = refs[:2], refs[2 : 1 + sides], refs[1 + sides : 1 + 2 * sides]
-    near_ref, served_refs, sums_ref, raw_ref = refs[1 + 2 * sides], refs[2 + 2 * sides : -2], refs[-2], refs[-1]
+    near_ref, served_refs, (sums_ref, raw_ref, moved_ref) = refs[1 + 2 * sides], refs[2 + 2 * sides : -3], refs[-3:]
     morton = lax.axis_index("morton")
     leaf_count = visc_ref.shape[0]
     asked = [spots_ref[...]] + [requested(ref) for ref in request_refs]
@@ -383,8 +373,10 @@
     def add_moments(who, values, table_ref):
         high, low = split(values, 2)
         raw = dot_nt(table_ref[...], high)
-        lanes = slice(3 * who * leaf_count, 3 * (who + 1) * leaf_count)
-        raw_ref[:, lanes] = raw[:ROWS] + raw[ROWS:] + dot_nt(table_ref[:ROWS, :], low)
+        raw = raw[:ROWS] + raw[ROWS:] + dot_nt(table_ref[:ROWS, :], low)
+        for comp in range(3):
+            at = (3 * who + comp) * ROWS
+            raw_ref[at : at + ROWS, :] = raw[:, comp * leaf_count : (comp + 1) * leaf_count]
 
     for who, ref in enumerate(request_refs, 1):
         weight = ref[:leaf_count].astype(f32) * (-penalty * out_scale)
@@ -396,21 +388,22 @@
         part_ref[comp] - weight * jumps[comp * leaf_count : (comp + 1) * leaf_count] for comp in range(3)
     ]
     add_moments(0, jnp.concatenate(force, axis=0), basis_ref)
-    geom = jnp.concatenate([spots[8:] for spots in asked for _ in range(3)], axis=1)
-    tiles = shifted([raw_ref[8 * at : 8 * at + 8, :] for at in range(36)], geom)
-    span = 3 * leaf_count
-    tiles = [sum(tile[:, span * who : span * (who + 1)] for who in range(sides)) for tile in tiles]
-    group = lax.broadcasted_iota(jnp.int32, (span, LANES), 0) // leaf_count
-    column = lax.broadcasted_iota(jnp.int32, (span, LANES), 1)
-    gather = jnp.where((group == column) | (group + 3 == column), 1.0, 0.0).astype(bf16)
-    summed = sum(dot(piece, gather) for piece in split(jnp.concatenate(tiles, axis=0), 3))
-    box = box_ref[pl.ds(pl.multiple_of(morton * 8, 8), 8), :]
-    both = shifted([summed[8 * at : 8 * at + 8, :] for at in range(36)], box)
-    flat = jnp.concatenate(both, axis=0).T
-    sums = sum(dot(piece, compact_ref[...]) for piece in split(flat[:8], 3))
+    tiles = shifted(
+        lambda at: raw_ref[pl.ds(at, 3 * sides, stride=ROWS), :], [spots[8:12] for spots in asked], DEG + 1
+    )
+    for at, tile in enumerate(tiles):
+        moved_ref[8 * at : 8 * at + 3 * sides, :] = tile
+    row = lax.broadcasted_iota(jnp.int32, (8, leaf_count), 0)
+    box = jnp.zeros((8, MOMENTS), f32)
+    for comp in range(3):
+        leaves = sum(moved_ref[pl.ds(3 * who + comp, MOMENTS, stride=8), :] for who in range(sides))
+        ones = jnp.where(row == comp, 1.0, 0.0).astype(bf16)
+        box = box + sum(dot_nt(ones, piece) for piece in split(leaves, 3))
+    box = jnp.concatenate([box * (1.0 / 512.0), jnp.zeros((8, 256 - MOMENTS), f32)], axis=1)
+    root = jnp.dot(box, move_ref[...], precision=highest, preferred_element_type=f32)
     blank = jnp.zeros((2, LANES), f32)
-    to_box = jnp.concatenate([sums[:3, :LANES], sums[:3, LANES:], blank], axis=0)
-    to_root = jnp.concatenate([sums[3:6, :LANES], sums[3:6, LANES:], blank], axis=0)
+    to_box = jnp.concatenate([box[:3, :LANES], box[:3, LANES:], blank], axis=0)
+    to_root = jnp.concatenate([root[:3, :LANES], root[:3, LANES:], blank], axis=0)
     sib_count = lax.axis_size("sib")
     for other in range(sums_ref.shape[0]):
         sums_ref[other] = jnp.where(morton == other // sib_count, to_box, to_root)
@@ -528,10 +521,10 @@
         2 * 10**9,
         [],
         [
-            part, viscosity, boxes, spread, basis, face_basis, jnp.asarray(compact_table()), spots,
+            part, viscosity, spread, basis, face_basis, move, spots,
             bands, swap(bands, "sib", 1), *requests, *group,
         ],
-        [pltpu.VMEM((ROWS, 3 * sides * leaf_count), f32)],
+        [pltpu.VMEM((3 * sides * ROWS, leaf_count), f32), pltpu.VMEM((8 * MOMENTS, leaf_count), f32)],
     )
     got = [swap(block, "sib", apart) for block, apart in zip(served, other_sides)]
     every = lax.all_to_all(sums, ("morton", "sib"), 0, 0, tiled=True)

time: 34.1 us -> 34.6 us (1.015)
  Pallas kernels: 9.93 us -> 10.5 us
    pallas_call x5, Pallas kernels: 9.93 us -> 10.5 us  [call(): pl.pallas_call(kernel, out_shape=[jax.ShapeDtypeStruct(shape, dtype) for...]
where the time goes in v11:
time: 34.6 us; the launch traced here: 34.5 us
  blocking collectives  11.8 us (34%)
  Pallas kernels  10.5 us (30%)
  starting transfers between devices  8.89 us (26%)
  waiting for transfers between devices  2.42 us (7%)
  between operations  0.8 us (2%)
    all_to_all x1, blocking collectives, on_device(): every = lax.all_to_all(sums, ('morton', 'sib'), 0, 0, tiled=True)  11.8 us
    pallas_call x5, Pallas kernels, call(): pl.pallas_call(kernel, out_shape=[jax.ShapeDtypeStruct(shape, dtype) for...  10.5 us
    ppermute x2, starting transfers between devices, pairs(): return lax.ppermute(block, 'morton', route)  5.27 us
    ppermute x4, starting transfers between devices, swap(): lax.ppermute(block, axis, [(at, at ^ apart) for at in range(lax.axis_size...  3.63 us
    ppermute x4, waiting for transfers between devices, swap(): lax.ppermute(block, axis, [(at, at ^ apart) for at in range(lax.axis_size...  2.41 us
  transfers between devices with their start and end apart: 6, of which 2 were waited for; matrix products, arithmetic and copies ran while one was open for 0% of the time, Pallas kernels for 9%

profile of v11, /device:TPU:0, one launch (start us, length us, event | category | flops | bytes accessed | tf_op | source)
XLA Modules:
  0.0 34.5 jit_solution(13030932078587424718)
XLA Ops:
  0.6 0.0 copy-start.1
  0.6 0.0 copy-start.2
  0.7 0.0 copy-start.4
  0.7 0.0 copy-start.8
  0.7 2.6 %shard_map.156 = (bf16[128,1152]{1,0:T(8,128)(2,1)}, bf16[32,1152]{1,0:T(8,128)(2,1)}, bf16[32,1152]{1,0:T(8,128)(2,1)}, f32[16,128]{1,0:T(8,128)}, bf16[144,384]{1,0:T(8,128)(2,1)}) custom-call(s32[32]{0:T(128)} %counts_ref.3, bf16[3,128,512]{2,1,0:T(8,128)(2,1)} %bitcast.7, f32[128,512]{1,0:T(8,128)} %visc_ref.7, s32[6,128]{1,0:T(8,128)} %bitcast.10, ...), custom_call_target="tpu_custom_call" | custom-call | flops 400000000 | bytes 1085440 | tf_op jit(solution)/shard_map/pallas_call | solution.py:454
  3.2 0.5 %collective-permute-start.1 = (bf16[128,1152]{1,0:T(8,128)(2,1)}, bf16[128,1152]{1,0:T(8,128)(2,1)S(1)}, u32[]{:S(2)}, u32[]{:S(2)}) collective-permute-start(bf16[128,1152]{1,0:T(8,128)(2,1)} %get-tuple-element.31.refs_1_), channel_id=1, source_target_pairs={{0,1},{1,0},{2,3},{3,2},{4,5},{5,4},{6,7},{7,6},{8,9},{9,8},{10,11... | collective-permute-start | bytes 884744 | tf_op jit(solution)/shard_map/ppermute | solution.py:100
  3.7 0.7 %collective-permute-start = (bf16[32,1152]{1,0:T(8,128)(2,1)}, bf16[32,1152]{1,0:T(8,128)(2,1)S(1)}, u32[]{:S(2)}, u32[]{:S(2)}) collective-permute-start(bf16[32,1152]{1,0:T(8,128)(2,1)} %get-tuple-element.30), channel_id=1, source_target_pairs={{4,8},{8,4},{12,16},{16,12},{20,24},{24,20},{5,9},{9,5},{13,17},{1... | collective-permute-start | bytes 221192 | tf_op jit(solution)/shard_map/ppermute | solution.py:107
  4.4 0.8 %collective-permute-done.1.refs_2_ = bf16[128,1152]{1,0:T(8,128)(2,1)S(1)} collective-permute-done((bf16[128,1152]{1,0:T(8,128)(2,1)}, bf16[128,1152]{1,0:T(8,128)(2,1)S(1)}, u32[]{:S(2)}, u32[]{:S(2)}) %collective-permute-start.1) | collective-permute-done | bytes 294944 | tf_op jit(solution)/shard_map/ppermute | solution.py:100
  5.1 0.0 copy-start.5
  5.1 4.6 %collective-permute-start.2 = (bf16[32,1152]{1,0:T(8,128)(2,1)}, bf16[32,1152]{1,0:T(8,128)(2,1)S(1)}, u32[]{:S(2)}, u32[]{:S(2)}) collective-permute-start(bf16[32,1152]{1,0:T(8,128)(2,1)} %get-tuple-element.34), channel_id=1, source_target_pairs={{0,4},{4,0},{8,12},{12,8},{16,20},{20,16},{24,28},{28,24},{1,5},{5... | collective-permute-start | bytes 221192 | tf_op jit(solution)/shard_map/ppermute | solution.py:107
  9.7 1.5 %collective-permute-start.3 = (bf16[144,384]{1,0:T(8,128)(2,1)}, bf16[144,384]{1,0:T(8,128)(2,1)S(1)}, u32[]{:S(2)}, u32[]{:S(2)}) collective-permute-start(bf16[144,384]{1,0:T(8,128)(2,1)} %get-tuple-element.37), channel_id=1, source_target_pairs={{0,2},{1,3},{2,0},{3,1},{4,6},{5,7},{6,4},{7,5},{8,10},{9,11},{10,... | collective-permute-start | bytes 331784 | tf_op jit(solution)/shard_map/ppermute | solution.py:100
  11.3 0.0 copy-done.1
  11.3 0.0 copy-done.2
  11.3 0.0 copy-done.4
  11.3 0.0 copy-done.8
  11.3 0.0 copy-done.5
  11.3 0.0 copy-start.9
  11.3 0.0 copy-start.10
  11.3 1.9 %shard_map.157 = (f32[3,128,512]{2,1,0:T(8,128)S(1)}, f32[128,512]{1,0:T(8,128)}) custom-call(s32[32]{0:T(128)S(1)} %copy-done.5, bf16[3,128,512]{2,1,0:T(8,128)(2,1)S(1)} %bitcast.8, bf16[128,512]{1,0:T(8,128)(2,1)S(1)} %copy-done.4, f32[128,512]{1,0:T(8,128)S(1)} %copy-done.1, f32[24,512]{1,0:T(8,128)S(1)} %copy-done.8), custom_call_target="tpu_custom_call" | custom-call | flops 2000000000 | bytes 835584 | tf_op jit(solution)/shard_map/pallas_call | solution.py:454
  13.2 0.0 copy-start.3
  13.2 0.0 collective-permute-done
  13.2 0.0 collective-permute-done.2
  13.2 1.6 %collective-permute-done.3.refs_0_.refs_2_ = bf16[144,384]{1,0:T(8,128)(2,1)S(1)} collective-permute-done((bf16[144,384]{1,0:T(8,128)(2,1)}, bf16[144,384]{1,0:T(8,128)(2,1)S(1)}, u32[]{:S(2)}, u32[]{:S(2)}) %collective-permute-start.3) | collective-permute-done | bytes 110624 | tf_op jit(solution)/shard_map/ppermute | solution.py:100
  14.9 0.1 collective-permute-start.4
  14.9 0.0 copy-done.9
  15.0 0.0 copy-done.10
  15.0 0.0 copy-done.3
  15.0 0.0 copy-start
  15.0 0.0 copy-start.6
  15.0 0.0 copy-start.7
  15.0 1.3 %shard_map.158 = (f32[256,256]{1,0:T(8,128)S(1)}, bf16[128,1152]{1,0:T(8,128)(2,1)S(1)}, bf16[128,1152]{1,0:T(8,128)(2,1)S(1)}) custom-call(f32[64,128]{1,0:T(8,128)S(1)} %copy-done.9, f32[16,128]{1,0:T(8,128)S(1)} %copy-done.10, bf16[144,384]{1,0:T(8,128)(2,1)S(1)} %collective-permute-done.3.refs_0_.refs_2_, bf16[128,1152]{1,0:T(8,128)(2,1)S(1)} %copy-done.3, ...), custom_call_target="tpu_custom_call" | custom-call | flops 1000000000 | bytes 741376 | tf_op jit(solution)/shard_map/pallas_call | solution.py:454
  16.3 0.0 collective-permute-done.4.refs_1_
  16.3 0.0 copy-done
  16.3 0.0 copy-done.6
  16.3 0.0 copy-done.7
  16.3 3.5 %shard_map.159 = (bf16[128,1152]{1,0:T(8,128)(2,1)S(1)}, bf16[128,1152]{1,0:T(8,128)(2,1)S(1)}, f32[32,8,128]{2,1,0:T(8,128)S(1)}) custom-call(f32[3,128,512]{2,1,0:T(8,128)S(1)} %get-tuple-element.38.part_ref, f32[128,512]{1,0:T(8,128)S(1)} %copy-done.1, bf16[384,512]{1,0:T(8,128)(2,1)S(1)} %copy-done, bf16[448,512]{1,0:T(8,128)(2,1)S(1)} %copy-done.6, ...), custom_call_target="tpu_custom_call" | custom-call | flops 2000000000 | bytes 3510272 | tf_op jit(solution)/shard_map/pallas_call | solution.py:454
  19.8 1.6 %collective-permute-start.5 = (bf16[128,1152]{1,0:T(8,128)(2,1)S(1)}, bf16[128,1152]{1,0:T(8,128)(2,1)S(1)}, u32[]{:S(2)}, u32[]{:S(2)}) collective-permute-start(bf16[128,1152]{1,0:T(8,128)(2,1)S(1)} %get-tuple-element.48), channel_id=1, source_target_pairs={{0,2},{1,3},{2,0},{3,1},{4,6},{5,7},{6,4},{7,5},{8,10},{9,11},{10,... | collective-permute-start | bytes 884744 | tf_op jit(solution)/shard_map/ppermute | solution.py:100
  21.4 11.8 %all_to_all.5.sums_ref = f32[32,8,128]{2,1,0:T(8,128)S(1)} all-to-all(f32[32,8,128]{2,1,0:T(8,128)S(1)} %get-tuple-element.47), channel_id=1, replica_groups=mesh['morton'=8,'sib'=4] {'morton','sib'}, dimensions={0} | all-to-all | bytes 262144 | tf_op jit(solution)/shard_map/all_to_all | solution.py:530
  33.2 0.0 collective-permute-done.5.refs_0_
  33.2 1.3 %shard_map.160 = (f32[3,128,512]{2,1,0:T(8,128)}, f32[3,1,216]{2,1,0:T(1,128)}, f32[3,1,216]{2,1,0:T(1,128)}) custom-call(f32[3,128,512]{2,1,0:T(8,128)S(1)} %get-tuple-element.38.part_ref, f32[128,512]{1,0:T(8,128)S(1)} %copy-done.1, bf16[384,512]{1,0:T(8,128)(2,1)S(1)} %copy-done, f32[32,8,128]{2,1,0:T(8,128)S(1)} %all_to_all.5.sums_ref, ...), custom_call_target="tpu_custom_call" | custom-call | flops 200000000 | bytes 2424832 | tf_op jit(solution)/shard_map/pallas_call | solution.py:454
  (2 shorter events, 0.0 us)
Async XLA Ops:
  0.6 10.6 %copy-start.1 = (f32[128,512]{1,0:T(8,128)S(1)}, f32[128,512]{1,0:T(8,128)}, u32[]{:S(2)}) copy-start(f32[128,512]{1,0:T(8,128)} %visc_ref.7) | copy-start | bytes 786436
  0.6 10.6 %copy-start.2 = (bf16[128,3,512]{2,0,1:T(8,128)(2,1)S(1)}, bf16[128,3,512]{2,0,1:T(8,128)(2,1)}, u32[]{:S(2)}) copy-start(bf16[128,3,512]{2,0,1:T(8,128)(2,1)} %param.13) | copy-start | bytes 1179652
  0.7 10.6 %copy-start.4 = (bf16[128,512]{1,0:T(8,128)(2,1)S(1)}, bf16[128,512]{1,0:T(8,128)(2,1)}, u32[]{:S(2)}) copy-start(bf16[128,512]{1,0:T(8,128)(2,1)} %press_ref) | copy-start | bytes 393220
  0.7 10.6 %copy-start.8 = (f32[24,512]{1,0:T(8,128)S(1)}, f32[24,512]{1,0:T(8,128)}, u32[]{:S(2)}) copy-start(f32[24,512]{1,0:T(8,128)} %constant.12.clone.rows_ref) | copy-start | bytes 147460
  3.2 1.9 %collective-permute-start.1 = (bf16[128,1152]{1,0:T(8,128)(2,1)}, bf16[128,1152]{1,0:T(8,128)(2,1)S(1)}, u32[]{:S(2)}, u32[]{:S(2)}) collective-permute-start(bf16[128,1152]{1,0:T(8,128)(2,1)} %get-tuple-element.31.refs_1_), channel_id=1, source_target_pairs={{0,1},{1,0},{2,3},{3,2},{4,5},{5,4},{6,7},{7,6},{8,9},{9,8},{10,11... | collective-permute-start | bytes 884744 | tf_op jit(solution)/shard_map/ppermute | solution.py:100
  3.7 9.5 %collective-permute-start = (bf16[32,1152]{1,0:T(8,128)(2,1)}, bf16[32,1152]{1,0:T(8,128)(2,1)S(1)}, u32[]{:S(2)}, u32[]{:S(2)}) collective-permute-start(bf16[32,1152]{1,0:T(8,128)(2,1)} %get-tuple-element.30), channel_id=1, source_target_pairs={{4,8},{8,4},{12,16},{16,12},{20,24},{24,20},{5,9},{9,5},{13,17},{1... | collective-permute-start | bytes 221192 | tf_op jit(solution)/shard_map/ppermute | solution.py:107
  5.1 6.2 %copy-start.5 = (s32[32]{0:T(128)S(1)}, s32[32]{0:T(128)}, u32[]{:S(2)}) copy-start(s32[32]{0:T(128)} %counts_ref.3) | copy-start | bytes 388
  5.1 8.1 %collective-permute-start.2 = (bf16[32,1152]{1,0:T(8,128)(2,1)}, bf16[32,1152]{1,0:T(8,128)(2,1)S(1)}, u32[]{:S(2)}, u32[]{:S(2)}) collective-permute-start(bf16[32,1152]{1,0:T(8,128)(2,1)} %get-tuple-element.34), channel_id=1, source_target_pairs={{0,4},{4,0},{8,12},{12,8},{16,20},{20,16},{24,28},{28,24},{1,5},{5... | collective-permute-start | bytes 221192 | tf_op jit(solution)/shard_map/ppermute | solution.py:107
  9.7 5.1 %collective-permute-start.3 = (bf16[144,384]{1,0:T(8,128)(2,1)}, bf16[144,384]{1,0:T(8,128)(2,1)S(1)}, u32[]{:S(2)}, u32[]{:S(2)}) collective-permute-start(bf16[144,384]{1,0:T(8,128)(2,1)} %get-tuple-element.37), channel_id=1, source_target_pairs={{0,2},{1,3},{2,0},{3,1},{4,6},{5,7},{6,4},{7,5},{8,10},{9,11},{10,... | collective-permute-start | bytes 331784 | tf_op jit(solution)/shard_map/ppermute | solution.py:100
  11.3 3.7 %copy-start.9 = (f32[64,128]{1,0:T(8,128)S(1)}, f32[64,128]{1,0:T(8,128)}, u32[]{:S(2)}) copy-start(f32[64,128]{1,0:T(8,128)} %constant.17.clone.box_ref) | copy-start | bytes 98308
  11.3 3.7 %copy-start.10 = (f32[16,128]{1,0:T(8,128)S(1)}, f32[16,128]{1,0:T(8,128)}, u32[]{:S(2)}) copy-start(f32[16,128]{1,0:T(8,128)} %get-tuple-element.39.spots_ref) | copy-start | bytes 24580
  13.2 1.8 %copy-start.3 = (bf16[128,1152]{1,0:T(8,128)(2,1)S(1)}, bf16[128,1152]{1,0:T(8,128)(2,1)}, u32[]{:S(2)}) copy-start(bf16[128,1152]{1,0:T(8,128)(2,1)} %get-tuple-element.31.refs_1_) | copy-start | bytes 884740
  14.9 1.4 %collective-permute-start.4 = (bf16[64,1152]{1,0:T(8,128)(2,1)S(1)}, bf16[64,1152]{1,0:T(8,128)(2,1)S(1)}, u32[]{:S(2)}, u32[]{:S(2)}) collective-permute-start(bf16[64,1152]{1,0:T(8,128)(2,1)S(1)} %constant_dynamic-update-slice_fusion.refs_0_), channel_id=1, source_target_pairs={{0,1},{1,0},{2,3},{3,2},{4,5},{5,4},{6,7},{7,6},{8,9},{9,8},{10,11... | collective-permute-start | bytes 442376 | tf_op jit(solution)/shard_map/ppermute | solution.py:100
  15.0 1.3 %copy-start = (bf16[384,512]{1,0:T(8,128)(2,1)S(1)}, bf16[384,512]{1,0:T(8,128)(2,1)}, u32[]{:S(2)}) copy-start(bf16[384,512]{1,0:T(8,128)(2,1)} %constant.19.spread_ref) | copy-start | bytes 1179652
  15.0 1.3 %copy-start.6 = (bf16[448,512]{1,0:T(8,128)(2,1)S(1)}, bf16[448,512]{1,0:T(8,128)(2,1)}, u32[]{:S(2)}) copy-start(bf16[448,512]{1,0:T(8,128)(2,1)} %constant.15.clone.basis_ref) | copy-start | bytes 1376260
  15.0 1.3 %copy-start.7 = (bf16[448,384]{1,0:T(8,128)(2,1)S(1)}, bf16[448,384]{1,0:T(8,128)(2,1)}, u32[]{:S(2)}) copy-start(bf16[448,384]{1,0:T(8,128)(2,1)} %constant.16.clone.face_basis_ref) | copy-start | bytes 1032196
  19.8 13.4 %collective-permute-start.5 = (bf16[128,1152]{1,0:T(8,128)(2,1)S(1)}, bf16[128,1152]{1,0:T(8,128)(2,1)S(1)}, u32[]{:S(2)}, u32[]{:S(2)}) collective-permute-start(bf16[128,1152]{1,0:T(8,128)(2,1)S(1)} %get-tuple-element.48), channel_id=1, source_target_pairs={{0,2},{1,3},{2,0},{3,1},{4,6},{5,7},{6,4},{7,5},{8,10},{9,11},{10,... | collective-permute-start | bytes 884744 | tf_op jit(solution)/shard_map/ppermute | solution.py:100

commit v12 on v10

--- a/solution.py
+++ b/solution.py
@@ -364,46 +364,48 @@
     return pieces
 
 
+def lane_sums(raw_ref, geoms):
+    leaf_count = geoms[0].shape[1]
+    geom = jnp.concatenate([leaf for leaf in geoms for _ in range(3)], axis=1)
+    tiles = shifted([raw_ref[8 * at : 8 * at + 8, :] for at in range(36)], geom)
+    span = 3 * leaf_count
+    tiles = [sum(tile[:, span * who : span * (who + 1)] for who in range(len(geoms))) for tile in tiles]
+    group = lax.broadcasted_iota(jnp.int32, (span, LANES), 0) // leaf_count
+    column = lax.broadcasted_iota(jnp.int32, (span, LANES), 1)
+    gather = jnp.where((group == column) | (group + 3 == column), 1.0, 0.0).astype(bf16)
+    return sum(dot(piece, gather) for piece in split(jnp.concatenate(tiles, axis=0), 3))
+
+
+def own_kernel(part_ref, basis_ref, spots_ref, summed_ref, raw_ref):
+    leaf_count = part_ref.shape[1]
+    high, low = split(part_ref[...].reshape(3 * leaf_count, NODES), 2)
+    raw = dot_nt(basis_ref[...], high)
+    raw_ref[...] = raw[:ROWS] + raw[ROWS:] + dot_nt(basis_ref[:ROWS, :], low)
+    summed_ref[...] = lane_sums(raw_ref, [spots_ref[8:, :]])
+
+
 def moment_kernel(
-    part_ref, visc_ref, box_ref, spread_ref, basis_ref, face_basis_ref, compact_ref, spots_ref, *refs
+    summed_ref, box_ref, face_basis_ref, compact_ref, spots_ref, weights_ref, *refs
 ):
     sides = lax.axis_size("sib") // 2
     window_refs, request_refs, group_refs = refs[:2], refs[2 : 1 + sides], refs[1 + sides : 1 + 2 * sides]
     near_ref, served_refs, sums_ref, raw_ref = refs[1 + 2 * sides], refs[2 + 2 * sides : -2], refs[-2], refs[-1]
     morton = lax.axis_index("morton")
-    leaf_count = visc_ref.shape[0]
+    leaf_count = spots_ref.shape[1]
     asked = [spots_ref[...]] + [requested(ref) for ref in request_refs]
     chosen = gathered(asked, window_refs, 2 * leaf_count)
-    for blocks, group_ref, out_ref in zip(chosen, group_refs, (near_ref, *served_refs)):
+    values = []
+    for blocks, group_ref, out_ref, ref in zip(
+        chosen, group_refs, (near_ref, *served_refs), (weights_ref, *request_refs)
+    ):
         for dim in range(3):
             lanes = slice(dim * FACES, (dim + 1) * FACES)
             blocks[dim] = blocks[dim] + group_ref[:, lanes]
             out_ref[:, lanes] = blocks[dim]
-
-    def add_moments(who, values, table_ref):
-        high, low = split(values, 2)
-        raw = dot_nt(table_ref[...], high)
-        lanes = slice(3 * who * leaf_count, 3 * (who + 1) * leaf_count)
-        raw_ref[:, lanes] = raw[:ROWS] + raw[ROWS:] + dot_nt(table_ref[:ROWS, :], low)
-
-    for who, ref in enumerate(request_refs, 1):
         weight = ref[:leaf_count].astype(f32) * (-penalty * out_scale)
-        weight = jnp.concatenate([weight] * 3, axis=0)
-        add_moments(who, weight * by_comp(chosen[who]).astype(f32), face_basis_ref)
-    jumps = dot(by_comp(chosen[0]), spread_ref[...])
-    weight = visc_ref[...] * (penalty * out_scale)
-    force = [
-        part_ref[comp] - weight * jumps[comp * leaf_count : (comp + 1) * leaf_count] for comp in range(3)
-    ]
-    add_moments(0, jnp.concatenate(force, axis=0), basis_ref)
-    geom = jnp.concatenate([spots[8:] for spots in asked for _ in range(3)], axis=1)
-    tiles = shifted([raw_ref[8 * at : 8 * at + 8, :] for at in range(36)], geom)
-    span = 3 * leaf_count
-    tiles = [sum(tile[:, span * who : span * (who + 1)] for who in range(sides)) for tile in tiles]
-    group = lax.broadcasted_iota(jnp.int32, (span, LANES), 0) // leaf_count
-    column = lax.broadcasted_iota(jnp.int32, (span, LANES), 1)
-    gather = jnp.where((group == column) | (group + 3 == column), 1.0, 0.0).astype(bf16)
-    summed = sum(dot(piece, gather) for piece in split(jnp.concatenate(tiles, axis=0), 3))
+        values.append(jnp.concatenate([weight] * 3, axis=0) * by_comp(blocks).astype(f32))
+    raw_ref[...] = dot_nt(face_basis_ref[...], jnp.concatenate(values, axis=0).astype(bf16))
+    summed = summed_ref[...] + lane_sums(raw_ref, [spots[8:] for spots in asked])
     box = box_ref[pl.ds(pl.multiple_of(morton * 8, 8), 8), :]
     both = shifted([summed[8 * at : 8 * at + 8, :] for at in range(36)], box)
     flat = jnp.concatenate(both, axis=0).T
@@ -477,7 +479,7 @@
     spread = jnp.asarray(spread_table().astype(np.float32)).astype(bf16)
     basis = basis_tables()
     face_basis = (basis.astype(np.float32) @ spread_table().T.astype(np.float32)).astype(jnp.bfloat16)
-    basis, face_basis = jnp.asarray(basis), jnp.asarray(face_basis)
+    basis, face_basis = jnp.asarray(basis), jnp.asarray(face_basis[:ROWS])
     boxes = jnp.asarray(box_table(morton_count))
     vel = jnp.transpose(velocity, (1, 0, 2))
     nbrs = jnp.transpose(neighbors, (1, 0))
@@ -500,6 +502,7 @@
         [vel, viscosity, nbrs, levels.reshape(1, -1), morton_keys.reshape(1, -1), boxes, pick],
         grant=60,
     )
+    weights = requests[0]
     odd = pairs(odd, 1)
     across = swap(faces, "sib", 1)
     across, requests, even, pressure = lax.optimization_barrier((across, requests, even, pressure))
@@ -513,7 +516,15 @@
         [vel, pressure, viscosity, rows],
         [pltpu.VMEM((NODES, NODES), bf16), pltpu.VMEM((256, NODES), bf16)],
     )
-    odd, even, part, requests = lax.optimization_barrier((odd, even, part, requests))
+    (summed,) = call(
+        own_kernel,
+        [((ROWS, LANES), f32)],
+        10**9,
+        [],
+        [part, basis, spots],
+        [pltpu.VMEM((ROWS, 3 * leaf_count), f32)],
+    )
+    odd, even, summed, requests = lax.optimization_barrier((odd, even, summed, requests))
     bands = jnp.concatenate([odd, even], axis=0)
     move, *group = call(
         group_kernel,
@@ -528,7 +539,7 @@
         2 * 10**9,
         [],
         [
-            part, viscosity, boxes, spread, basis, face_basis, jnp.asarray(compact_table()), spots,
+            summed, boxes, face_basis, jnp.asarray(compact_table()), spots, weights,
             bands, swap(bands, "sib", 1), *requests, *group,
         ],
         [pltpu.VMEM((ROWS, 3 * sides * leaf_count), f32)],

time: 34.1 us -> 33.7 us (0.988)
  waiting for transfers between devices: 2.41 us -> 1.16 us
  Pallas kernels: 9.93 us -> 10.4 us
  local copies, waits for them, and re-layouts: 0.08 us -> 0.48 us
    ppermute x4, waiting for transfers between devices: 2.4 us -> 1.16 us  [swap(): lax.ppermute(block, axis, [(at, at ^ apart) for at in range(lax.axis_size...]
    pallas_call x5 -> x6, Pallas kernels: 9.93 us -> 10.4 us  [call(): pl.pallas_call(kernel, out_shape=[jax.ShapeDtypeStruct(shape, dtype) for...]
    unnamed x25 -> x27, local copies, waits for them, and re-layouts: 0.07 us -> 0.46 us
    ppermute x4, starting transfers between devices: 3.63 us -> 3.28 us  [swap(): lax.ppermute(block, axis, [(at, at ^ apart) for at in range(lax.axis_size...]
  transfers between devices with their start and end apart: 6 -> 6, of which waited for: 2 -> 2; matrix products, arithmetic and copies ran while one was open for 0% -> 0% of each run, Pallas kernels for 9% -> 13%
where the time goes in v12:
time: 33.7 us; the launch traced here: 33.5 us
  blocking collectives  12.1 us (36%)
  Pallas kernels  10.4 us (31%)
  starting transfers between devices  8.57 us (25%)
  waiting for transfers between devices  1.16 us (3%)
  between operations  0.82 us (2%)
  local copies, waits for them, and re-layouts  0.48 us (1%)
    all_to_all x1, blocking collectives, on_device(): every = lax.all_to_all(sums, ('morton', 'sib'), 0, 0, tiled=True)  12.1 us
    pallas_call x6, Pallas kernels, call(): pl.pallas_call(kernel, out_shape=[jax.ShapeDtypeStruct(shape, dtype) for...  10.4 us
    ppermute x2, starting transfers between devices, pairs(): return lax.ppermute(block, 'morton', route)  5.28 us
    ppermute x4, starting transfers between devices, swap(): lax.ppermute(block, axis, [(at, at ^ apart) for at in range(lax.axis_size...  3.28 us
    ppermute x4, waiting for transfers between devices, swap(): lax.ppermute(block, axis, [(at, at ^ apart) for at in range(lax.axis_size...  1.16 us
  transfers between devices with their start and end apart: 6, of which 2 were waited for; matrix products, arithmetic and copies ran while one was open for 0% of the time, Pallas kernels for 13%

profile of v12, /device:TPU:0, one launch (start us, length us, event | category | flops | bytes accessed | tf_op | source)
XLA Modules:
  0.0 33.5 jit_solution(2637777286291796025)
XLA Ops:
  0.6 0.0 copy-start.1
  0.6 0.0 copy-start.2
  0.7 0.0 copy-start.4
  0.7 0.0 copy-start.10
  0.7 2.6 %shard_map.165 = (bf16[128,1152]{1,0:T(8,128)(2,1)}, bf16[32,1152]{1,0:T(8,128)(2,1)}, bf16[32,1152]{1,0:T(8,128)(2,1)}, f32[16,128]{1,0:T(8,128)}, bf16[144,384]{1,0:T(8,128)(2,1)}) custom-call(s32[32]{0:T(128)} %counts_ref.3, bf16[3,128,512]{2,1,0:T(8,128)(2,1)} %bitcast.7, f32[128,512]{1,0:T(8,128)} %visc_ref.5, s32[6,128]{1,0:T(8,128)} %bitcast.10, ...), custom_call_target="tpu_custom_call" | custom-call | flops 400000000 | bytes 1085440 | tf_op jit(solution)/shard_map/pallas_call | solution.py:463
  3.2 0.5 %collective-permute-start = (bf16[128,1152]{1,0:T(8,128)(2,1)}, bf16[128,1152]{1,0:T(8,128)(2,1)S(1)}, u32[]{:S(2)}, u32[]{:S(2)}) collective-permute-start(bf16[128,1152]{1,0:T(8,128)(2,1)} %get-tuple-element.30.refs_1_), channel_id=1, source_target_pairs={{0,1},{1,0},{2,3},{3,2},{4,5},{5,4},{6,7},{7,6},{8,9},{9,8},{10,11... | collective-permute-start | bytes 884744 | tf_op jit(solution)/shard_map/ppermute | solution.py:109
  3.7 0.7 %collective-permute-start.1 = (bf16[32,1152]{1,0:T(8,128)(2,1)}, bf16[32,1152]{1,0:T(8,128)(2,1)S(1)}, u32[]{:S(2)}, u32[]{:S(2)}) collective-permute-start(bf16[32,1152]{1,0:T(8,128)(2,1)} %get-tuple-element.35), channel_id=1, source_target_pairs={{4,8},{8,4},{12,16},{16,12},{20,24},{24,20},{5,9},{9,5},{13,17},{1... | collective-permute-start | bytes 221192 | tf_op jit(solution)/shard_map/ppermute | solution.py:116
  4.4 0.8 %collective-permute-done.refs_2_ = bf16[128,1152]{1,0:T(8,128)(2,1)S(1)} collective-permute-done((bf16[128,1152]{1,0:T(8,128)(2,1)}, bf16[128,1152]{1,0:T(8,128)(2,1)S(1)}, u32[]{:S(2)}, u32[]{:S(2)}) %collective-permute-start) | collective-permute-done | bytes 294944 | tf_op jit(solution)/shard_map/ppermute | solution.py:109
  5.1 0.0 copy-start.6
  5.1 0.0 copy-start.7
  5.1 0.0 copy-start.12
  5.1 4.6 %collective-permute-start.2 = (bf16[32,1152]{1,0:T(8,128)(2,1)}, bf16[32,1152]{1,0:T(8,128)(2,1)S(1)}, u32[]{:S(2)}, u32[]{:S(2)}) collective-permute-start(bf16[32,1152]{1,0:T(8,128)(2,1)} %get-tuple-element.36), channel_id=1, source_target_pairs={{0,4},{4,0},{8,12},{12,8},{16,20},{20,16},{24,28},{28,24},{1,5},{5... | collective-permute-start | bytes 221192 | tf_op jit(solution)/shard_map/ppermute | solution.py:116
  9.8 1.5 %collective-permute-start.3 = (bf16[144,384]{1,0:T(8,128)(2,1)}, bf16[144,384]{1,0:T(8,128)(2,1)S(1)}, u32[]{:S(2)}, u32[]{:S(2)}) collective-permute-start(bf16[144,384]{1,0:T(8,128)(2,1)} %get-tuple-element.38.weights_ref), channel_id=1, source_target_pairs={{0,2},{1,3},{2,0},{3,1},{4,6},{5,7},{6,4},{7,5},{8,10},{9,11},{10,... | collective-permute-start | bytes 331784 | tf_op jit(solution)/shard_map/ppermute | solution.py:109
  11.3 0.0 copy-done.1
  11.3 0.0 copy-done.2
  11.3 0.0 copy-done.4
  11.3 0.0 copy-done.10
  11.3 0.0 copy-done.6
  11.3 1.9 %shard_map.166 = (f32[3,128,512]{2,1,0:T(8,128)S(1)}, f32[128,512]{1,0:T(8,128)}) custom-call(s32[32]{0:T(128)S(1)} %copy-done.6, bf16[3,128,512]{2,1,0:T(8,128)(2,1)S(1)} %bitcast.8, bf16[128,512]{1,0:T(8,128)(2,1)S(1)} %copy-done.4, f32[128,512]{1,0:T(8,128)S(1)} %copy-done.1, f32[24,512]{1,0:T(8,128)S(1)} %copy-done.10), custom_call_target="tpu_custom_call" | custom-call | flops 2000000000 | bytes 835584 | tf_op jit(solution)/shard_map/pallas_call | solution.py:463
  13.2 0.0 copy-done.7
  13.2 0.0 copy-done.12
  13.2 0.0 copy-start.11
  13.2 1.2 %shard_map.167.summed_ref = f32[288,128]{1,0:T(8,128)S(1)} custom-call(f32[3,128,512]{2,1,0:T(8,128)S(1)} %get-tuple-element.34.part_ref, bf16[576,512]{1,0:T(8,128)(2,1)S(1)} %copy-done.7, f32[16,128]{1,0:T(8,128)S(1)} %copy-done.12), custom_call_target="tpu_custom_call" | custom-call | flops 1000000000 | bytes 1384448 | tf_op jit(solution)/shard_map/pallas_call | solution.py:463
  14.4 0.0 copy-start.3
  14.5 0.0 collective-permute-done.1
  14.5 0.0 collective-permute-done.2
  14.5 0.4 %collective-permute-done.3.refs_0_.refs_2_ = bf16[144,384]{1,0:T(8,128)(2,1)S(1)} collective-permute-done((bf16[144,384]{1,0:T(8,128)(2,1)}, bf16[144,384]{1,0:T(8,128)(2,1)S(1)}, u32[]{:S(2)}, u32[]{:S(2)}) %collective-permute-start.3) | collective-permute-done | bytes 110624 | tf_op jit(solution)/shard_map/ppermute | solution.py:109
  14.9 0.0 copy-start.5
  14.9 0.0 copy-start.8
  14.9 0.0 copy-start.9
  14.9 0.1 collective-permute-start.4
  15.0 0.0 copy-done.11
  15.0 0.4 %copy-done.3 = bf16[128,1152]{1,0:T(8,128)(2,1)S(1)} copy-done((bf16[128,1152]{1,0:T(8,128)(2,1)S(1)}, bf16[128,1152]{1,0:T(8,128)(2,1)}, u32[]{:S(2)}) %copy-start.3) | copy-done | bytes 294936
  15.4 1.3 %shard_map.168 = (f32[256,256]{1,0:T(8,128)S(1)}, bf16[128,1152]{1,0:T(8,128)(2,1)S(1)}, bf16[128,1152]{1,0:T(8,128)(2,1)S(1)}) custom-call(f32[64,128]{1,0:T(8,128)S(1)} %copy-done.11, f32[16,128]{1,0:T(8,128)S(1)} %copy-done.12, bf16[144,384]{1,0:T(8,128)(2,1)S(1)} %collective-permute-done.3.refs_0_.refs_2_, bf16[128,1152]{1,0:T(8,128)(2,1)S(1)} %copy-done.3, ...), custom_call_target="tpu_custom_call" | custom-call | flops 1000000000 | bytes 741376 | tf_op jit(solution)/shard_map/pallas_call | solution.py:463
  16.7 0.0 collective-permute-done.4.refs_1_
  16.7 0.0 copy-done.5
  16.7 0.0 copy-done.8
  16.7 0.0 copy-done.9
  16.7 0.0 copy-start
  16.7 2.1 %shard_map.169 = (bf16[128,1152]{1,0:T(8,128)(2,1)S(1)}, bf16[128,1152]{1,0:T(8,128)(2,1)S(1)}, f32[32,8,128]{2,1,0:T(8,128)S(1)}) custom-call(f32[288,128]{1,0:T(8,128)S(1)} %shard_map.167.summed_ref, f32[64,128]{1,0:T(8,128)S(1)} %copy-done.11, bf16[288,384]{1,0:T(8,128)(2,1)S(1)} %copy-done.8, bf16[288,256]{1,0:T(8,128)(2,1)S(1)} %copy-done.9, ...), custom_call_target="tpu_custom_call" | custom-call | flops 2000000000 | bytes 1662976 | tf_op jit(solution)/shard_map/pallas_call | solution.py:463
  18.9 1.2 %collective-permute-start.5 = (bf16[128,1152]{1,0:T(8,128)(2,1)S(1)}, bf16[128,1152]{1,0:T(8,128)(2,1)S(1)}, u32[]{:S(2)}, u32[]{:S(2)}) collective-permute-start(bf16[128,1152]{1,0:T(8,128)(2,1)S(1)} %get-tuple-element.47), channel_id=1, source_target_pairs={{0,2},{1,3},{2,0},{3,1},{4,6},{5,7},{6,4},{7,5},{8,10},{9,11},{10,... | collective-permute-start | bytes 884744 | tf_op jit(solution)/shard_map/ppermute | solution.py:109
  20.1 12.1 %all_to_all.5.sums_ref = f32[32,8,128]{2,1,0:T(8,128)S(1)} all-to-all(f32[32,8,128]{2,1,0:T(8,128)S(1)} %get-tuple-element.46), channel_id=1, replica_groups=mesh['morton'=8,'sib'=4] {'morton','sib'}, dimensions={0} | all-to-all | bytes 262144 | tf_op jit(solution)/shard_map/all_to_all | solution.py:548
  32.2 0.0 collective-permute-done.5.refs_0_
  32.2 0.0 copy-done
  32.2 1.3 %shard_map.170 = (f32[3,128,512]{2,1,0:T(8,128)}, f32[3,1,216]{2,1,0:T(1,128)}, f32[3,1,216]{2,1,0:T(1,128)}) custom-call(f32[3,128,512]{2,1,0:T(8,128)S(1)} %get-tuple-element.34.part_ref, f32[128,512]{1,0:T(8,128)S(1)} %copy-done.1, bf16[384,512]{1,0:T(8,128)(2,1)S(1)} %copy-done, f32[32,8,128]{2,1,0:T(8,128)S(1)} %all_to_all.5.sums_ref, ...), custom_call_target="tpu_custom_call" | custom-call | flops 200000000 | bytes 2424832 | tf_op jit(solution)/shard_map/pallas_call | solution.py:463
  (2 shorter events, 0.0 us)
Async XLA Ops:
  0.6 10.6 %copy-start.1 = (f32[128,512]{1,0:T(8,128)S(1)}, f32[128,512]{1,0:T(8,128)}, u32[]{:S(2)}) copy-start(f32[128,512]{1,0:T(8,128)} %visc_ref.5) | copy-start | bytes 786436
  0.6 10.6 %copy-start.2 = (bf16[128,3,512]{2,0,1:T(8,128)(2,1)S(1)}, bf16[128,3,512]{2,0,1:T(8,128)(2,1)}, u32[]{:S(2)}) copy-start(bf16[128,3,512]{2,0,1:T(8,128)(2,1)} %param.14) | copy-start | bytes 1179652
  0.7 10.6 %copy-start.4 = (bf16[128,512]{1,0:T(8,128)(2,1)S(1)}, bf16[128,512]{1,0:T(8,128)(2,1)}, u32[]{:S(2)}) copy-start(bf16[128,512]{1,0:T(8,128)(2,1)} %press_ref) | copy-start | bytes 393220
  0.7 10.6 %copy-start.10 = (f32[24,512]{1,0:T(8,128)S(1)}, f32[24,512]{1,0:T(8,128)}, u32[]{:S(2)}) copy-start(f32[24,512]{1,0:T(8,128)} %constant.14.clone.rows_ref) | copy-start | bytes 147460
  3.2 1.9 %collective-permute-start = (bf16[128,1152]{1,0:T(8,128)(2,1)}, bf16[128,1152]{1,0:T(8,128)(2,1)S(1)}, u32[]{:S(2)}, u32[]{:S(2)}) collective-permute-start(bf16[128,1152]{1,0:T(8,128)(2,1)} %get-tuple-element.30.refs_1_), channel_id=1, source_target_pairs={{0,1},{1,0},{2,3},{3,2},{4,5},{5,4},{6,7},{7,6},{8,9},{9,8},{10,11... | collective-permute-start | bytes 884744 | tf_op jit(solution)/shard_map/ppermute | solution.py:109
  3.7 10.8 %collective-permute-start.1 = (bf16[32,1152]{1,0:T(8,128)(2,1)}, bf16[32,1152]{1,0:T(8,128)(2,1)S(1)}, u32[]{:S(2)}, u32[]{:S(2)}) collective-permute-start(bf16[32,1152]{1,0:T(8,128)(2,1)} %get-tuple-element.35), channel_id=1, source_target_pairs={{4,8},{8,4},{12,16},{16,12},{20,24},{24,20},{5,9},{9,5},{13,17},{1... | collective-permute-start | bytes 221192 | tf_op jit(solution)/shard_map/ppermute | solution.py:116
  5.1 6.2 %copy-start.6 = (s32[32]{0:T(128)S(1)}, s32[32]{0:T(128)}, u32[]{:S(2)}) copy-start(s32[32]{0:T(128)} %counts_ref.3) | copy-start | bytes 388
  5.1 8.1 %copy-start.7 = (bf16[576,512]{1,0:T(8,128)(2,1)S(1)}, bf16[576,512]{1,0:T(8,128)(2,1)}, u32[]{:S(2)}) copy-start(bf16[576,512]{1,0:T(8,128)(2,1)} %constant.17.clone.basis_ref) | copy-start | bytes 1769476
  5.1 8.1 %copy-start.12 = (f32[16,128]{1,0:T(8,128)S(1)}, f32[16,128]{1,0:T(8,128)}, u32[]{:S(2)}) copy-start(f32[16,128]{1,0:T(8,128)} %get-tuple-element.37.spots_ref) | copy-start | bytes 24580
  5.1 9.3 %collective-permute-start.2 = (bf16[32,1152]{1,0:T(8,128)(2,1)}, bf16[32,1152]{1,0:T(8,128)(2,1)S(1)}, u32[]{:S(2)}, u32[]{:S(2)}) collective-permute-start(bf16[32,1152]{1,0:T(8,128)(2,1)} %get-tuple-element.36), channel_id=1, source_target_pairs={{0,4},{4,0},{8,12},{12,8},{16,20},{20,16},{24,28},{28,24},{1,5},{5... | collective-permute-start | bytes 221192 | tf_op jit(solution)/shard_map/ppermute | solution.py:116
  9.8 5.1 %collective-permute-start.3 = (bf16[144,384]{1,0:T(8,128)(2,1)}, bf16[144,384]{1,0:T(8,128)(2,1)S(1)}, u32[]{:S(2)}, u32[]{:S(2)}) collective-permute-start(bf16[144,384]{1,0:T(8,128)(2,1)} %get-tuple-element.38.weights_ref), channel_id=1, source_target_pairs={{0,2},{1,3},{2,0},{3,1},{4,6},{5,7},{6,4},{7,5},{8,10},{9,11},{10,... | collective-permute-start | bytes 331784 | tf_op jit(solution)/shard_map/ppermute | solution.py:109
  13.2 1.8 %copy-start.11 = (f32[64,128]{1,0:T(8,128)S(1)}, f32[64,128]{1,0:T(8,128)}, u32[]{:S(2)}) copy-start(f32[64,128]{1,0:T(8,128)} %constant.19.clone.box_ref) | copy-start | bytes 98308
  14.4 1.0 %copy-start.3 = (bf16[128,1152]{1,0:T(8,128)(2,1)S(1)}, bf16[128,1152]{1,0:T(8,128)(2,1)}, u32[]{:S(2)}) copy-start(bf16[128,1152]{1,0:T(8,128)(2,1)} %get-tuple-element.30.refs_1_) | copy-start | bytes 884740
  14.9 1.8 %copy-start.5 = (bf16[144,384]{1,0:T(8,128)(2,1)S(1)}, bf16[144,384]{1,0:T(8,128)(2,1)}, u32[]{:S(2)}) copy-start(bf16[144,384]{1,0:T(8,128)(2,1)} %get-tuple-element.38.weights_ref) | copy-start | bytes 331780
  14.9 1.8 %copy-start.8 = (bf16[288,384]{1,0:T(8,128)(2,1)S(1)}, bf16[288,384]{1,0:T(8,128)(2,1)}, u32[]{:S(2)}) copy-start(bf16[288,384]{1,0:T(8,128)(2,1)} %constant.18.clone.face_basis_ref) | copy-start | bytes 663556
  14.9 1.8 %copy-start.9 = (bf16[288,256]{1,0:T(8,128)(2,1)S(1)}, bf16[288,256]{1,0:T(8,128)(2,1)}, u32[]{:S(2)}) copy-start(bf16[288,256]{1,0:T(8,128)(2,1)} %constant.20.clone.compact_ref) | copy-start | bytes 442372
  14.9 1.8 %collective-permute-start.4 = (bf16[64,1152]{1,0:T(8,128)(2,1)S(1)}, bf16[64,1152]{1,0:T(8,128)(2,1)S(1)}, u32[]{:S(2)}, u32[]{:S(2)}) collective-permute-start(bf16[64,1152]{1,0:T(8,128)(2,1)S(1)} %constant_dynamic-update-slice_fusion.refs_0_), channel_id=1, source_target_pairs={{0,1},{1,0},{2,3},{3,2},{4,5},{5,4},{6,7},{7,6},{8,9},{9,8},{10,11... | collective-permute-start | bytes 442376 | tf_op jit(solution)/shard_map/ppermute | solution.py:109
  16.7 15.5 %copy-start = (bf16[384,512]{1,0:T(8,128)(2,1)S(1)}, bf16[384,512]{1,0:T(8,128)(2,1)}, u32[]{:S(2)}) copy-start(bf16[384,512]{1,0:T(8,128)(2,1)} %constant.22.spread_ref) | copy-start | bytes 1179652
  18.9 13.3 %collective-permute-start.5 = (bf16[128,1152]{1,0:T(8,128)(2,1)S(1)}, bf16[128,1152]{1,0:T(8,128)(2,1)S(1)}, u32[]{:S(2)}, u32[]{:S(2)}) collective-permute-start(bf16[128,1152]{1,0:T(8,128)(2,1)S(1)} %get-tuple-element.47), channel_id=1, source_target_pairs={{0,2},{1,3},{2,0},{3,1},{4,6},{5,7},{6,4},{7,5},{8,10},{9,11},{10,... | collective-permute-start | bytes 884744 | tf_op jit(solution)/shard_map/ppermute | solution.py:109

commit v13 on v12

--- a/solution.py
+++ b/solution.py
@@ -192,7 +192,7 @@
         spot = jnp.where(step == 0, piece * leaf_count + slot, 2 * leaf_count + piece * (2 * BAND) + in_band)
         spot = jnp.where((nbrs >= 0) & (piece < 2), spot, -1)
         if side == 0:
-            spots_ref[...] = jnp.concatenate([spot.astype(f32), jnp.zeros((2, leaf_count), f32), geom], axis=0)
+            spots_ref[...] = jnp.concatenate([spot.astype(f32), jnp.zeros((2, leaf_count), f32), geom[:4], box[:4]], axis=0)
             continue
         whole = jnp.right_shift(spot, 4)
         parts = [whole.astype(f32), (spot - 16 * whole).astype(f32), geom[:4]]
@@ -301,15 +301,14 @@
         part_ref[comp] = jnp.where(live, part, 0.0)
 
 
-def group_kernel(box_ref, spots_ref, *refs):
+def group_kernel(spots_ref, *refs):
     sides = lax.axis_size("sib") // 2
     request_refs, window_refs, move_ref, out_refs = refs[: sides - 1], refs[sides - 1 : sides + 1], refs[sides + 1], refs[sides + 2 :]
     chosen = gathered([spots_ref[...]] + [requested(ref) for ref in request_refs], window_refs, 0)
     for blocks, out_ref in zip(chosen, out_refs):
         for dim, block in enumerate(blocks):
             out_ref[:, dim * FACES : (dim + 1) * FACES] = block
-    morton = lax.axis_index("morton")
-    box = box_ref[pl.ds(pl.multiple_of(morton * 8, 8), 8), :]
+    box = spots_ref[12:, :]
     move = jnp.ones((256, 256), f32)
     for dim, stride in enumerate((36, 6, 1)):
         col = lax.broadcasted_iota(jnp.int32, (1, 256), 1) // stride % 6
@@ -385,7 +384,7 @@
 
 
 def moment_kernel(
-    summed_ref, box_ref, face_basis_ref, compact_ref, spots_ref, weights_ref, *refs
+    summed_ref, face_basis_ref, compact_ref, spots_ref, weights_ref, *refs
 ):
     sides = lax.axis_size("sib") // 2
     window_refs, request_refs, group_refs = refs[:2], refs[2 : 1 + sides], refs[1 + sides : 1 + 2 * sides]
@@ -406,7 +405,7 @@
         values.append(jnp.concatenate([weight] * 3, axis=0) * by_comp(blocks).astype(f32))
     raw_ref[...] = dot_nt(face_basis_ref[...], jnp.concatenate(values, axis=0).astype(bf16))
     summed = summed_ref[...] + lane_sums(raw_ref, [spots[8:] for spots in asked])
-    box = box_ref[pl.ds(pl.multiple_of(morton * 8, 8), 8), :]
+    box = spots_ref[12:, :]
     both = shifted([summed[8 * at : 8 * at + 8, :] for at in range(36)], box)
     flat = jnp.concatenate(both, axis=0).T
     sums = sum(dot(piece, compact_ref[...]) for piece in split(flat[:8], 3))
@@ -420,6 +419,17 @@
 
 def last_kernel(part_ref, visc_ref, spread_ref, sums_ref, move_ref, near_ref, *refs):
     got_refs, (force_hbm, box_hbm, root_hbm, force_ref, box_ref, root_ref, sems) = refs[:-7], refs[-7:]
+    faces = near_ref[...]
+    for got_ref in got_refs:
+        faces = faces + got_ref[...]
+    weight = visc_ref[...] * (penalty * out_scale)
+    stores = []
+    for comp in range(3):
+        lanes = [(dim * 3 + comp) * LANES for dim in range(3)]
+        jump = dot(jnp.concatenate([faces[:, at : at + LANES] for at in lanes], axis=1), spread_ref[...])
+        force_ref[comp] = part_ref[comp] - weight * jump
+        stores.append(pltpu.make_async_copy(force_ref.at[comp], force_hbm.at[comp], sems.at[comp]))
+        stores[-1].start()
     sib_count = lax.axis_size("sib")
     morton = lax.axis_index("morton")
     box = jnp.zeros(sums_ref.shape[1:], f32)
@@ -430,27 +440,17 @@
         root = root + jnp.where(morton == group, 0.0, total)
     box = jnp.concatenate([box[:3], box[3:6]], axis=1)
     root = jnp.concatenate([root[:3], root[3:6]], axis=1)
-    box8 = jnp.concatenate([box, jnp.zeros((5, 2 * LANES), f32)], axis=0)
-    root = root + jnp.dot(box8, move_ref[...], precision=highest, preferred_element_type=f32)[:3]
+    box_rows = jnp.concatenate([box, jnp.zeros((5, 2 * LANES), f32)], axis=0)
+    pieces = jnp.concatenate([piece.astype(f32) for piece in split(box_rows, 3)], axis=0).astype(bf16)
+    moved = sum(dot(pieces, table) for table in split(move_ref[...], 2))
+    root = root + (moved[:3] + moved[8:11] + moved[16:19])
     for comp in range(3):
         box_ref[comp] = box[comp : comp + 1, :MOMENTS]
         root_ref[comp] = root[comp : comp + 1, :MOMENTS]
-    stores = [
-        pltpu.make_async_copy(box_ref, box_hbm, sems.at[3]),
-        pltpu.make_async_copy(root_ref, root_hbm, sems.at[4]),
-    ]
-    for store in stores:
+    stores.append(pltpu.make_async_copy(box_ref, box_hbm, sems.at[3]))
+    stores.append(pltpu.make_async_copy(root_ref, root_hbm, sems.at[4]))
+    for store in stores[3:]:
         store.start()
-    faces = near_ref[...]
-    for got_ref in got_refs:
-        faces = faces + got_ref[...]
-    weight = visc_ref[...] * (penalty * out_scale)
-    for comp in range(3):
-        lanes = [(dim * 3 + comp) * LANES for dim in range(3)]
-        jump = dot(jnp.concatenate([faces[:, at : at + LANES] for at in lanes], axis=1), spread_ref[...])
-        force_ref[comp] = part_ref[comp] - weight * jump
-        stores.append(pltpu.make_async_copy(force_ref.at[comp], force_hbm.at[comp], sems.at[comp]))
-        stores[-1].start()
     for store in stores:
         store.wait()
 
@@ -503,11 +503,10 @@
         grant=60,
     )
     weights = requests[0]
-    odd = pairs(odd, 1)
+    even, odd = pairs(even, 0), pairs(odd, 1)
     across = swap(faces, "sib", 1)
-    across, requests, even, pressure = lax.optimization_barrier((across, requests, even, pressure))
+    across, requests, pressure = lax.optimization_barrier((across, requests, pressure))
     requests = [swap(block, "sib", apart) for block, apart in zip(requests, other_sides)]
-    even = pairs(even, 0)
     part, continuity = call(
         operator_kernel,
         [((3, leaf_count, NODES), f32), ((leaf_count, NODES), f32)],
@@ -524,14 +523,14 @@
         [part, basis, spots],
         [pltpu.VMEM((ROWS, 3 * leaf_count), f32)],
     )
-    odd, even, summed, requests = lax.optimization_barrier((odd, even, summed, requests))
+    even, odd, summed, requests = lax.optimization_barrier((even, odd, summed, requests))
     bands = jnp.concatenate([odd, even], axis=0)
     move, *group = call(
         group_kernel,
         [((256, 256), f32)] + [((leaf_count, width), bf16)] * sides,
         10**9,
         [],
-        [boxes, spots, *requests, faces, across],
+        [spots, *requests, faces, across],
     )
     near, *served, sums = call(
         moment_kernel,
@@ -539,7 +538,7 @@
         2 * 10**9,
         [],
         [
-            summed, boxes, face_basis, jnp.asarray(compact_table()), spots, weights,
+            summed, face_basis, jnp.asarray(compact_table()), spots, weights,
             bands, swap(bands, "sib", 1), *requests, *group,
         ],
         [pltpu.VMEM((ROWS, 3 * sides * leaf_count), f32)],

time: 33.7 us -> 33.9 us (level)
  blocking collectives: 12.1 us -> 14.7 us
  starting transfers between devices: 8.57 us -> 6.92 us
  waiting for transfers between devices: 1.16 us -> 0.64 us
    all_to_all x1, blocking collectives: 12.1 us -> 14.7 us  [on_device(): every = lax.all_to_all(sums, ('morton', 'sib'), 0, 0, tiled=True)]
    ppermute x2, starting transfers between devices: 5.28 us -> 3.33 us  [pairs(): return lax.ppermute(block, 'morton', route)]
    ppermute x4, waiting for transfers between devices: 1.16 us -> 0.63 us  [swap(): lax.ppermute(block, axis, [(at, at ^ apart) for at in range(lax.axis_size...]
  transfers between devices with their start and end apart: 6 -> 6, of which waited for: 2 -> 1; matrix products, arithmetic and copies ran while one was open for 0% -> 0% of each run, Pallas kernels for 13% -> 13%
where the time goes in v13:
time: 33.9 us; the launch traced here: 33.7 us
  blocking collectives  14.7 us (43%)
  Pallas kernels  10.3 us (30%)
  starting transfers between devices  6.92 us (20%)
  between operations  0.83 us (2%)
  waiting for transfers between devices  0.64 us (2%)
    all_to_all x1, blocking collectives, on_device(): every = lax.all_to_all(sums, ('morton', 'sib'), 0, 0, tiled=True)  14.7 us
    pallas_call x6, Pallas kernels, call(): pl.pallas_call(kernel, out_shape=[jax.ShapeDtypeStruct(shape, dtype) for...  10.3 us
    ppermute x4, starting transfers between devices, swap(): lax.ppermute(block, axis, [(at, at ^ apart) for at in range(lax.axis_size...  3.58 us
    ppermute x2, starting transfers between devices, pairs(): return lax.ppermute(block, 'morton', route)  3.33 us
  transfers between devices with their start and end apart: 6, of which 1 were waited for; matrix products, arithmetic and copies ran while one was open for 0% of the time, Pallas kernels for 13%

profile of v13, /device:TPU:0, one launch (start us, length us, event | category | flops | bytes accessed | tf_op | source)
XLA Modules:
  0.0 33.7 jit_solution(10068526263086096481)
XLA Ops:
  0.6 0.0 copy-start.1
  0.6 0.0 copy-start.2
  0.7 0.0 copy-start.4
  0.7 0.0 copy-start.10
  0.7 2.6 %shard_map.165 = (bf16[128,1152]{1,0:T(8,128)(2,1)}, bf16[32,1152]{1,0:T(8,128)(2,1)}, bf16[32,1152]{1,0:T(8,128)(2,1)}, f32[16,128]{1,0:T(8,128)}, bf16[144,384]{1,0:T(8,128)(2,1)}) custom-call(s32[32]{0:T(128)} %counts_ref.3, bf16[3,128,512]{2,1,0:T(8,128)(2,1)} %bitcast.7, f32[128,512]{1,0:T(8,128)} %visc_ref.5, s32[6,128]{1,0:T(8,128)} %bitcast.10, ...), custom_call_target="tpu_custom_call" | custom-call | flops 400000000 | bytes 1085440 | tf_op jit(solution)/shard_map/pallas_call | solution.py:463
  3.2 0.5 %collective-permute-start = (bf16[128,1152]{1,0:T(8,128)(2,1)}, bf16[128,1152]{1,0:T(8,128)(2,1)S(1)}, u32[]{:S(2)}, u32[]{:S(2)}) collective-permute-start(bf16[128,1152]{1,0:T(8,128)(2,1)} %get-tuple-element.29.refs_1_), channel_id=1, source_target_pairs={{0,1},{1,0},{2,3},{3,2},{4,5},{5,4},{6,7},{7,6},{8,9},{9,8},{10,11... | collective-permute-start | bytes 884744 | tf_op jit(solution)/shard_map/ppermute | solution.py:109
  3.7 2.5 %collective-permute-start.1 = (bf16[32,1152]{1,0:T(8,128)(2,1)}, bf16[32,1152]{1,0:T(8,128)(2,1)S(1)}, u32[]{:S(2)}, u32[]{:S(2)}) collective-permute-start(bf16[32,1152]{1,0:T(8,128)(2,1)} %get-tuple-element.33), channel_id=1, source_target_pairs={{0,4},{4,0},{8,12},{12,8},{16,20},{20,16},{24,28},{28,24},{1,5},{5... | collective-permute-start | bytes 221192 | tf_op jit(solution)/shard_map/ppermute | solution.py:116
  6.3 0.0 copy-start.6
  6.3 0.8 %collective-permute-start.2 = (bf16[32,1152]{1,0:T(8,128)(2,1)}, bf16[32,1152]{1,0:T(8,128)(2,1)S(1)}, u32[]{:S(2)}, u32[]{:S(2)}) collective-permute-start(bf16[32,1152]{1,0:T(8,128)(2,1)} %get-tuple-element.34), channel_id=1, source_target_pairs={{4,8},{8,4},{12,16},{16,12},{20,24},{24,20},{5,9},{9,5},{13,17},{1... | collective-permute-start | bytes 221192 | tf_op jit(solution)/shard_map/ppermute | solution.py:116
  7.0 0.0 collective-permute-done.refs_2_
  7.1 0.0 copy-start.7
  7.1 0.0 copy-start.11
  7.1 1.6 %collective-permute-start.3 = (bf16[144,384]{1,0:T(8,128)(2,1)}, bf16[144,384]{1,0:T(8,128)(2,1)S(1)}, u32[]{:S(2)}, u32[]{:S(2)}) collective-permute-start(bf16[144,384]{1,0:T(8,128)(2,1)} %get-tuple-element.36.weights_ref), channel_id=1, source_target_pairs={{0,2},{1,3},{2,0},{3,1},{4,6},{5,7},{6,4},{7,5},{8,10},{9,11},{10,... | collective-permute-start | bytes 331784 | tf_op jit(solution)/shard_map/ppermute | solution.py:109
  8.7 0.0 copy-done.1
  8.7 0.0 copy-done.2
  8.7 0.0 copy-done.4
  8.7 0.0 copy-done.10
  8.7 0.0 copy-done.6
  8.7 1.9 %shard_map.166 = (f32[3,128,512]{2,1,0:T(8,128)S(1)}, f32[128,512]{1,0:T(8,128)}) custom-call(s32[32]{0:T(128)S(1)} %copy-done.6, bf16[3,128,512]{2,1,0:T(8,128)(2,1)S(1)} %bitcast.8, bf16[128,512]{1,0:T(8,128)(2,1)S(1)} %copy-done.4, f32[128,512]{1,0:T(8,128)S(1)} %copy-done.1, f32[24,512]{1,0:T(8,128)S(1)} %copy-done.10), custom_call_target="tpu_custom_call" | custom-call | flops 2000000000 | bytes 835584 | tf_op jit(solution)/shard_map/pallas_call | solution.py:463
  10.6 0.0 copy-done.7
  10.6 0.0 copy-done.11
  10.6 1.2 %shard_map.167.summed_ref = f32[288,128]{1,0:T(8,128)S(1)} custom-call(f32[3,128,512]{2,1,0:T(8,128)S(1)} %get-tuple-element.32.part_ref, bf16[576,512]{1,0:T(8,128)(2,1)S(1)} %copy-done.7, f32[16,128]{1,0:T(8,128)S(1)} %copy-done.11), custom_call_target="tpu_custom_call" | custom-call | flops 1000000000 | bytes 1384448 | tf_op jit(solution)/shard_map/pallas_call | solution.py:463
  11.8 0.0 copy-start.3
  11.8 0.0 collective-permute-done.1
  11.9 0.0 collective-permute-done.2
  11.9 0.6 %collective-permute-done.3.refs_0_.refs_2_ = bf16[144,384]{1,0:T(8,128)(2,1)S(1)} collective-permute-done((bf16[144,384]{1,0:T(8,128)(2,1)}, bf16[144,384]{1,0:T(8,128)(2,1)S(1)}, u32[]{:S(2)}, u32[]{:S(2)}) %collective-permute-start.3) | collective-permute-done | bytes 110624 | tf_op jit(solution)/shard_map/ppermute | solution.py:109
  12.5 0.0 copy-start.5
  12.5 0.0 copy-start.8
  12.5 0.0 copy-start.9
  12.5 0.1 collective-permute-start.4
  12.6 0.2 copy-done.3
  12.8 1.3 %shard_map.168 = (f32[256,256]{1,0:T(8,128)S(1)}, bf16[128,1152]{1,0:T(8,128)(2,1)S(1)}, bf16[128,1152]{1,0:T(8,128)(2,1)S(1)}) custom-call(f32[16,128]{1,0:T(8,128)S(1)} %copy-done.11, bf16[144,384]{1,0:T(8,128)(2,1)S(1)} %collective-permute-done.3.refs_0_.refs_2_, bf16[128,1152]{1,0:T(8,128)(2,1)S(1)} %copy-done.3, ...), custom_call_target="tpu_custom_call" | custom-call | flops 1000000000 | bytes 708608 | tf_op jit(solution)/shard_map/pallas_call | solution.py:463
  14.1 0.0 collective-permute-done.4.refs_1_
  14.1 0.0 copy-done.5
  14.1 0.0 copy-done.8
  14.1 0.0 copy-done.9
  14.1 0.0 copy-start
  14.1 2.1 %shard_map.169 = (bf16[128,1152]{1,0:T(8,128)(2,1)S(1)}, bf16[128,1152]{1,0:T(8,128)(2,1)S(1)}, f32[32,8,128]{2,1,0:T(8,128)S(1)}) custom-call(f32[288,128]{1,0:T(8,128)S(1)} %shard_map.167.summed_ref, bf16[288,384]{1,0:T(8,128)(2,1)S(1)} %copy-done.8, bf16[288,256]{1,0:T(8,128)(2,1)S(1)} %copy-done.9, f32[16,128]{1,0:T(8,128)S(1)} %copy-done.11, ...), custom_call_target="tpu_custom_call" | custom-call | flops 2000000000 | bytes 1630208 | tf_op jit(solution)/shard_map/pallas_call | solution.py:463
  16.3 1.5 %collective-permute-start.5 = (bf16[128,1152]{1,0:T(8,128)(2,1)S(1)}, bf16[128,1152]{1,0:T(8,128)(2,1)S(1)}, u32[]{:S(2)}, u32[]{:S(2)}) collective-permute-start(bf16[128,1152]{1,0:T(8,128)(2,1)S(1)} %get-tuple-element.45), channel_id=1, source_target_pairs={{0,2},{1,3},{2,0},{3,1},{4,6},{5,7},{6,4},{7,5},{8,10},{9,11},{10,... | collective-permute-start | bytes 884744 | tf_op jit(solution)/shard_map/ppermute | solution.py:109
  17.7 14.7 %all_to_all.5.sums_ref = f32[32,8,128]{2,1,0:T(8,128)S(1)} all-to-all(f32[32,8,128]{2,1,0:T(8,128)S(1)} %get-tuple-element.44), channel_id=1, replica_groups=mesh['morton'=8,'sib'=4] {'morton','sib'}, dimensions={0} | all-to-all | bytes 262144 | tf_op jit(solution)/shard_map/all_to_all | solution.py:547
  32.5 0.0 collective-permute-done.5.refs_0_
  32.5 0.0 copy-done
  32.5 1.2 %shard_map.170 = (f32[3,128,512]{2,1,0:T(8,128)}, f32[3,1,216]{2,1,0:T(1,128)}, f32[3,1,216]{2,1,0:T(1,128)}) custom-call(f32[3,128,512]{2,1,0:T(8,128)S(1)} %get-tuple-element.32.part_ref, f32[128,512]{1,0:T(8,128)S(1)} %copy-done.1, bf16[384,512]{1,0:T(8,128)(2,1)S(1)} %copy-done, f32[32,8,128]{2,1,0:T(8,128)S(1)} %all_to_all.5.sums_ref, ...), custom_call_target="tpu_custom_call" | custom-call | flops 200000000 | bytes 2424832 | tf_op jit(solution)/shard_map/pallas_call | solution.py:463
  (2 shorter events, 0.0 us)
Async XLA Ops:
  0.6 8.0 %copy-start.1 = (f32[128,512]{1,0:T(8,128)S(1)}, f32[128,512]{1,0:T(8,128)}, u32[]{:S(2)}) copy-start(f32[128,512]{1,0:T(8,128)} %visc_ref.5) | copy-start | bytes 786436
  0.6 8.0 %copy-start.2 = (bf16[128,3,512]{2,0,1:T(8,128)(2,1)S(1)}, bf16[128,3,512]{2,0,1:T(8,128)(2,1)}, u32[]{:S(2)}) copy-start(bf16[128,3,512]{2,0,1:T(8,128)(2,1)} %param.14) | copy-start | bytes 1179652
  0.7 8.0 %copy-start.4 = (bf16[128,512]{1,0:T(8,128)(2,1)S(1)}, bf16[128,512]{1,0:T(8,128)(2,1)}, u32[]{:S(2)}) copy-start(bf16[128,512]{1,0:T(8,128)(2,1)} %press_ref) | copy-start | bytes 393220
  0.7 8.0 %copy-start.10 = (f32[24,512]{1,0:T(8,128)S(1)}, f32[24,512]{1,0:T(8,128)}, u32[]{:S(2)}) copy-start(f32[24,512]{1,0:T(8,128)} %constant.14.clone.rows_ref) | copy-start | bytes 147460
  3.2 3.8 %collective-permute-start = (bf16[128,1152]{1,0:T(8,128)(2,1)}, bf16[128,1152]{1,0:T(8,128)(2,1)S(1)}, u32[]{:S(2)}, u32[]{:S(2)}) collective-permute-start(bf16[128,1152]{1,0:T(8,128)(2,1)} %get-tuple-element.29.refs_1_), channel_id=1, source_target_pairs={{0,1},{1,0},{2,3},{3,2},{4,5},{5,4},{6,7},{7,6},{8,9},{9,8},{10,11... | collective-permute-start | bytes 884744 | tf_op jit(solution)/shard_map/ppermute | solution.py:109
  3.7 8.1 %collective-permute-start.1 = (bf16[32,1152]{1,0:T(8,128)(2,1)}, bf16[32,1152]{1,0:T(8,128)(2,1)S(1)}, u32[]{:S(2)}, u32[]{:S(2)}) collective-permute-start(bf16[32,1152]{1,0:T(8,128)(2,1)} %get-tuple-element.33), channel_id=1, source_target_pairs={{0,4},{4,0},{8,12},{12,8},{16,20},{20,16},{24,28},{28,24},{1,5},{5... | collective-permute-start | bytes 221192 | tf_op jit(solution)/shard_map/ppermute | solution.py:116
  6.3 2.4 %copy-start.6 = (s32[32]{0:T(128)S(1)}, s32[32]{0:T(128)}, u32[]{:S(2)}) copy-start(s32[32]{0:T(128)} %counts_ref.3) | copy-start | bytes 388
  6.3 5.6 %collective-permute-start.2 = (bf16[32,1152]{1,0:T(8,128)(2,1)}, bf16[32,1152]{1,0:T(8,128)(2,1)S(1)}, u32[]{:S(2)}, u32[]{:S(2)}) collective-permute-start(bf16[32,1152]{1,0:T(8,128)(2,1)} %get-tuple-element.34), channel_id=1, source_target_pairs={{4,8},{8,4},{12,16},{16,12},{20,24},{24,20},{5,9},{9,5},{13,17},{1... | collective-permute-start | bytes 221192 | tf_op jit(solution)/shard_map/ppermute | solution.py:116
  7.1 3.5 %copy-start.7 = (bf16[576,512]{1,0:T(8,128)(2,1)S(1)}, bf16[576,512]{1,0:T(8,128)(2,1)}, u32[]{:S(2)}) copy-start(bf16[576,512]{1,0:T(8,128)(2,1)} %constant.17.clone.basis_ref) | copy-start | bytes 1769476
  7.1 3.5 %copy-start.11 = (f32[16,128]{1,0:T(8,128)S(1)}, f32[16,128]{1,0:T(8,128)}, u32[]{:S(2)}) copy-start(f32[16,128]{1,0:T(8,128)} %get-tuple-element.35.spots_ref) | copy-start | bytes 24580
  7.1 5.4 %collective-permute-start.3 = (bf16[144,384]{1,0:T(8,128)(2,1)}, bf16[144,384]{1,0:T(8,128)(2,1)S(1)}, u32[]{:S(2)}, u32[]{:S(2)}) collective-permute-start(bf16[144,384]{1,0:T(8,128)(2,1)} %get-tuple-element.36.weights_ref), channel_id=1, source_target_pairs={{0,2},{1,3},{2,0},{3,1},{4,6},{5,7},{6,4},{7,5},{8,10},{9,11},{10,... | collective-permute-start | bytes 331784 | tf_op jit(solution)/shard_map/ppermute | solution.py:109
  11.8 1.0 %copy-start.3 = (bf16[128,1152]{1,0:T(8,128)(2,1)S(1)}, bf16[128,1152]{1,0:T(8,128)(2,1)}, u32[]{:S(2)}) copy-start(bf16[128,1152]{1,0:T(8,128)(2,1)} %get-tuple-element.29.refs_1_) | copy-start | bytes 884740
  12.5 1.6 %copy-start.5 = (bf16[144,384]{1,0:T(8,128)(2,1)S(1)}, bf16[144,384]{1,0:T(8,128)(2,1)}, u32[]{:S(2)}) copy-start(bf16[144,384]{1,0:T(8,128)(2,1)} %get-tuple-element.36.weights_ref) | copy-start | bytes 331780
  12.5 1.6 %copy-start.8 = (bf16[288,384]{1,0:T(8,128)(2,1)S(1)}, bf16[288,384]{1,0:T(8,128)(2,1)}, u32[]{:S(2)}) copy-start(bf16[288,384]{1,0:T(8,128)(2,1)} %constant.18.clone.face_basis_ref) | copy-start | bytes 663556
  12.5 1.6 %copy-start.9 = (bf16[288,256]{1,0:T(8,128)(2,1)S(1)}, bf16[288,256]{1,0:T(8,128)(2,1)}, u32[]{:S(2)}) copy-start(bf16[288,256]{1,0:T(8,128)(2,1)} %constant.20.clone.compact_ref) | copy-start | bytes 442372
  12.5 1.5 %collective-permute-start.4 = (bf16[64,1152]{1,0:T(8,128)(2,1)S(1)}, bf16[64,1152]{1,0:T(8,128)(2,1)S(1)}, u32[]{:S(2)}, u32[]{:S(2)}) collective-permute-start(bf16[64,1152]{1,0:T(8,128)(2,1)S(1)} %constant_dynamic-update-slice_fusion.refs_0_), channel_id=1, source_target_pairs={{0,1},{1,0},{2,3},{3,2},{4,5},{5,4},{6,7},{7,6},{8,9},{9,8},{10,11... | collective-permute-start | bytes 442376 | tf_op jit(solution)/shard_map/ppermute | solution.py:109
  14.1 18.4 %copy-start = (bf16[384,512]{1,0:T(8,128)(2,1)S(1)}, bf16[384,512]{1,0:T(8,128)(2,1)}, u32[]{:S(2)}) copy-start(bf16[384,512]{1,0:T(8,128)(2,1)} %constant.22.spread_ref) | copy-start | bytes 1179652
  16.3 16.2 %collective-permute-start.5 = (bf16[128,1152]{1,0:T(8,128)(2,1)S(1)}, bf16[128,1152]{1,0:T(8,128)(2,1)S(1)}, u32[]{:S(2)}, u32[]{:S(2)}) collective-permute-start(bf16[128,1152]{1,0:T(8,128)(2,1)S(1)} %get-tuple-element.45), channel_id=1, source_target_pairs={{0,2},{1,3},{2,0},{3,1},{4,6},{5,7},{6,4},{7,5},{8,10},{9,11},{10,... | collective-permute-start | bytes 884744 | tf_op jit(solution)/shard_map/ppermute | solution.py:109

commit v14 on v13

--- a/solution.py
+++ b/solution.py
@@ -375,16 +375,15 @@
     return sum(dot(piece, gather) for piece in split(jnp.concatenate(tiles, axis=0), 3))
 
 
-def own_kernel(part_ref, basis_ref, spots_ref, summed_ref, raw_ref):
+def own_kernel(part_ref, basis_ref, faces_ref, raw_ref):
     leaf_count = part_ref.shape[1]
     high, low = split(part_ref[...].reshape(3 * leaf_count, NODES), 2)
     raw = dot_nt(basis_ref[...], high)
     raw_ref[...] = raw[:ROWS] + raw[ROWS:] + dot_nt(basis_ref[:ROWS, :], low)
-    summed_ref[...] = lane_sums(raw_ref, [spots_ref[8:, :]])
 
 
 def moment_kernel(
-    summed_ref, face_basis_ref, compact_ref, spots_ref, weights_ref, *refs
+    own_ref, face_basis_ref, compact_ref, spots_ref, weights_ref, *refs
 ):
     sides = lax.axis_size("sib") // 2
     window_refs, request_refs, group_refs = refs[:2], refs[2 : 1 + sides], refs[1 + sides : 1 + 2 * sides]
@@ -403,8 +402,11 @@
             out_ref[:, lanes] = blocks[dim]
         weight = ref[:leaf_count].astype(f32) * (-penalty * out_scale)
         values.append(jnp.concatenate([weight] * 3, axis=0) * by_comp(blocks).astype(f32))
-    raw_ref[...] = dot_nt(face_basis_ref[...], jnp.concatenate(values, axis=0).astype(bf16))
-    summed = summed_ref[...] + lane_sums(raw_ref, [spots[8:] for spots in asked])
+    raw = dot_nt(face_basis_ref[...], jnp.concatenate(values, axis=0).astype(bf16))
+    span = 3 * leaf_count
+    raw_ref[:, :span] = raw[:, :span] + own_ref[...]
+    raw_ref[:, span:] = raw[:, span:]
+    summed = lane_sums(raw_ref, [spots[8:] for spots in asked])
     box = spots_ref[12:, :]
     both = shifted([summed[8 * at : 8 * at + 8, :] for at in range(36)], box)
     flat = jnp.concatenate(both, axis=0).T
@@ -515,15 +517,14 @@
         [vel, pressure, viscosity, rows],
         [pltpu.VMEM((NODES, NODES), bf16), pltpu.VMEM((256, NODES), bf16)],
     )
-    (summed,) = call(
+    (own_raw,) = call(
         own_kernel,
-        [((ROWS, LANES), f32)],
+        [((ROWS, 3 * leaf_count), f32)],
         10**9,
         [],
-        [part, basis, spots],
-        [pltpu.VMEM((ROWS, 3 * leaf_count), f32)],
-    )
-    even, odd, summed, requests = lax.optimization_barrier((even, odd, summed, requests))
+        [part, basis, faces],
+    )
+    even, odd, own_raw, requests = lax.optimization_barrier((even, odd, own_raw, requests))
     bands = jnp.concatenate([odd, even], axis=0)
     move, *group = call(
         group_kernel,
@@ -538,7 +539,7 @@
         2 * 10**9,
         [],
         [
-            summed, face_basis, jnp.asarray(compact_table()), spots, weights,
+            own_raw, face_basis, jnp.asarray(compact_table()), spots, weights,
             bands, swap(bands, "sib", 1), *requests, *group,
         ],
         [pltpu.VMEM((ROWS, 3 * sides * leaf_count), f32)],

time: 33.9 us -> 34.2 us (level)
  waiting for transfers between devices: 0.64 us -> 1.24 us
  Pallas kernels: 10.3 us -> 9.77 us
  local copies, waits for them, and re-layouts: 0.26 us -> 0.67 us
    ppermute x4, waiting for transfers between devices: 0.63 us -> 1.23 us  [swap(): lax.ppermute(block, axis, [(at, at ^ apart) for at in range(lax.axis_size...]
    pallas_call x6, Pallas kernels: 10.3 us -> 9.77 us  [call(): pl.pallas_call(kernel, out_shape=[jax.ShapeDtypeStruct(shape, dtype) for...]
    unnamed x25, local copies, waits for them, and re-layouts: 0.24 us -> 0.66 us
  transfers between devices with their start and end apart: 6 -> 6, of which waited for: 1 -> 1; matrix products, arithmetic and copies ran while one was open for 0% -> 0% of each run, Pallas kernels for 13% -> 11%
where the time goes in v14:
time: 34.2 us; the launch traced here: 33.9 us
  blocking collectives  14.4 us (42%)
  Pallas kernels  9.77 us (29%)
  starting transfers between devices  7.03 us (21%)
  waiting for transfers between devices  1.24 us (4%)
  between operations  0.81 us (2%)
  local copies, waits for them, and re-layouts  0.67 us (2%)
    all_to_all x1, blocking collectives, on_device(): every = lax.all_to_all(sums, ('morton', 'sib'), 0, 0, tiled=True)  14.4 us
    pallas_call x6, Pallas kernels, call(): pl.pallas_call(kernel, out_shape=[jax.ShapeDtypeStruct(shape, dtype) for...  9.77 us
    ppermute x4, starting transfers between devices, swap(): lax.ppermute(block, axis, [(at, at ^ apart) for at in range(lax.axis_size...  3.7 us
    ppermute x2, starting transfers between devices, pairs(): return lax.ppermute(block, 'morton', route)  3.33 us
    ppermute x4, waiting for transfers between devices, swap(): lax.ppermute(block, axis, [(at, at ^ apart) for at in range(lax.axis_size...  1.23 us
  transfers between devices with their start and end apart: 6, of which 1 were waited for; matrix products, arithmetic and copies ran while one was open for 0% of the time, Pallas kernels for 11%

profile of v14, /device:TPU:0, one launch (start us, length us, event | category | flops | bytes accessed | tf_op | source)
XLA Modules:
  0.0 33.9 jit_solution(10253550533083453243)
XLA Ops:
  0.6 0.0 copy-start.1
  0.6 0.0 copy-start.2
  0.7 0.0 copy-start.4
  0.7 0.0 copy-start.10
  0.7 2.6 %shard_map.165 = (bf16[128,1152]{1,0:T(8,128)(2,1)}, bf16[32,1152]{1,0:T(8,128)(2,1)}, bf16[32,1152]{1,0:T(8,128)(2,1)}, f32[16,128]{1,0:T(8,128)}, bf16[144,384]{1,0:T(8,128)(2,1)}) custom-call(s32[32]{0:T(128)} %counts_ref.3, bf16[3,128,512]{2,1,0:T(8,128)(2,1)} %bitcast.7, f32[128,512]{1,0:T(8,128)} %visc_ref.5, s32[6,128]{1,0:T(8,128)} %bitcast.10, ...), custom_call_target="tpu_custom_call" | custom-call | flops 400000000 | bytes 1085440 | tf_op jit(solution)/shard_map/pallas_call | solution.py:465
  3.2 0.5 %collective-permute-start = (bf16[128,1152]{1,0:T(8,128)(2,1)}, bf16[128,1152]{1,0:T(8,128)(2,1)S(1)}, u32[]{:S(2)}, u32[]{:S(2)}) collective-permute-start(bf16[128,1152]{1,0:T(8,128)(2,1)} %get-tuple-element.29.faces_ref.refs_1_), channel_id=1, source_target_pairs={{0,1},{1,0},{2,3},{3,2},{4,5},{5,4},{6,7},{7,6},{8,9},{9,8},{10,11... | collective-permute-start | bytes 884744 | tf_op jit(solution)/shard_map/ppermute | solution.py:109
  3.7 2.5 %collective-permute-start.1 = (bf16[32,1152]{1,0:T(8,128)(2,1)}, bf16[32,1152]{1,0:T(8,128)(2,1)S(1)}, u32[]{:S(2)}, u32[]{:S(2)}) collective-permute-start(bf16[32,1152]{1,0:T(8,128)(2,1)} %get-tuple-element.33), channel_id=1, source_target_pairs={{0,4},{4,0},{8,12},{12,8},{16,20},{20,16},{24,28},{28,24},{1,5},{5... | collective-permute-start | bytes 221192 | tf_op jit(solution)/shard_map/ppermute | solution.py:116
  6.3 0.0 copy-start.6
  6.3 0.8 %collective-permute-start.2 = (bf16[32,1152]{1,0:T(8,128)(2,1)}, bf16[32,1152]{1,0:T(8,128)(2,1)S(1)}, u32[]{:S(2)}, u32[]{:S(2)}) collective-permute-start(bf16[32,1152]{1,0:T(8,128)(2,1)} %get-tuple-element.34), channel_id=1, source_target_pairs={{4,8},{8,4},{12,16},{16,12},{20,24},{24,20},{5,9},{9,5},{13,17},{1... | collective-permute-start | bytes 221192 | tf_op jit(solution)/shard_map/ppermute | solution.py:116
  7.0 0.0 collective-permute-done.refs_2_
  7.1 0.0 copy-start.3
  7.1 0.0 copy-start.7
  7.1 1.6 %collective-permute-start.3 = (bf16[144,384]{1,0:T(8,128)(2,1)}, bf16[144,384]{1,0:T(8,128)(2,1)S(1)}, u32[]{:S(2)}, u32[]{:S(2)}) collective-permute-start(bf16[144,384]{1,0:T(8,128)(2,1)} %get-tuple-element.35.weights_ref), channel_id=1, source_target_pairs={{0,2},{1,3},{2,0},{3,1},{4,6},{5,7},{6,4},{7,5},{8,10},{9,11},{10,... | collective-permute-start | bytes 331784 | tf_op jit(solution)/shard_map/ppermute | solution.py:109
  8.7 0.0 copy-done.1
  8.7 0.0 copy-done.2
  8.7 0.0 copy-done.4
  8.7 0.0 copy-done.10
  8.7 0.0 copy-done.6
  8.7 1.9 %shard_map.166 = (f32[3,128,512]{2,1,0:T(8,128)S(1)}, f32[128,512]{1,0:T(8,128)}) custom-call(s32[32]{0:T(128)S(1)} %copy-done.6, bf16[3,128,512]{2,1,0:T(8,128)(2,1)S(1)} %bitcast.8, bf16[128,512]{1,0:T(8,128)(2,1)S(1)} %copy-done.4, f32[128,512]{1,0:T(8,128)S(1)} %copy-done.1, f32[24,512]{1,0:T(8,128)S(1)} %copy-done.10), custom_call_target="tpu_custom_call" | custom-call | flops 2000000000 | bytes 835584 | tf_op jit(solution)/shard_map/pallas_call | solution.py:465
  10.6 0.0 copy-done.3
  10.6 0.0 copy-done.7
  10.6 0.6 %shard_map.167.own_ref = f32[288,384]{1,0:T(8,128)S(1)} custom-call(f32[3,128,512]{2,1,0:T(8,128)S(1)} %get-tuple-element.32.part_ref, bf16[576,512]{1,0:T(8,128)(2,1)S(1)} %copy-done.7, bf16[128,1152]{1,0:T(8,128)(2,1)S(1)} %copy-done.3), custom_call_target="tpu_custom_call" | custom-call | flops 1000000000 | bytes 1671168 | tf_op jit(solution)/shard_map/pallas_call | solution.py:465
  11.2 0.0 collective-permute-done.1
  11.3 0.0 collective-permute-done.2
  11.3 1.2 %collective-permute-done.3.refs_0_.refs_2_ = bf16[144,384]{1,0:T(8,128)(2,1)S(1)} collective-permute-done((bf16[144,384]{1,0:T(8,128)(2,1)}, bf16[144,384]{1,0:T(8,128)(2,1)S(1)}, u32[]{:S(2)}, u32[]{:S(2)}) %collective-permute-start.3) | collective-permute-done | bytes 110624 | tf_op jit(solution)/shard_map/ppermute | solution.py:109
  12.5 0.0 copy-start.11
  12.5 0.1 collective-permute-start.4
  12.6 0.6 %copy-done.11 = f32[16,128]{1,0:T(8,128)S(1)} copy-done((f32[16,128]{1,0:T(8,128)S(1)}, f32[16,128]{1,0:T(8,128)}, u32[]{:S(2)}) %copy-start.11) | copy-done | bytes 8216
  13.2 0.0 copy-start.5
  13.2 0.0 copy-start.8
  13.2 0.0 copy-start.9
  13.2 1.3 %shard_map.168 = (f32[256,256]{1,0:T(8,128)S(1)}, bf16[128,1152]{1,0:T(8,128)(2,1)S(1)}, bf16[128,1152]{1,0:T(8,128)(2,1)S(1)}) custom-call(f32[16,128]{1,0:T(8,128)S(1)} %copy-done.11, bf16[144,384]{1,0:T(8,128)(2,1)S(1)} %collective-permute-done.3.refs_0_.refs_2_, bf16[128,1152]{1,0:T(8,128)(2,1)S(1)} %copy-done.3, ...), custom_call_target="tpu_custom_call" | custom-call | flops 1000000000 | bytes 708608 | tf_op jit(solution)/shard_map/pallas_call | solution.py:465
  14.5 0.0 collective-permute-done.4.refs_1_
  14.5 0.0 copy-done.5
  14.5 0.0 copy-done.8
  14.5 0.0 copy-done.9
  14.5 0.0 copy-start
  14.5 2.2 %shard_map.169 = (bf16[128,1152]{1,0:T(8,128)(2,1)S(1)}, bf16[128,1152]{1,0:T(8,128)(2,1)S(1)}, f32[32,8,128]{2,1,0:T(8,128)S(1)}) custom-call(f32[288,384]{1,0:T(8,128)S(1)} %shard_map.167.own_ref, bf16[288,384]{1,0:T(8,128)(2,1)S(1)} %copy-done.8, bf16[288,256]{1,0:T(8,128)(2,1)S(1)} %copy-done.9, f32[16,128]{1,0:T(8,128)S(1)} %copy-done.11, ...), custom_call_target="tpu_custom_call" | custom-call | flops 2000000000 | bytes 1925120 | tf_op jit(solution)/shard_map/pallas_call | solution.py:465
  16.7 1.6 %collective-permute-start.5 = (bf16[128,1152]{1,0:T(8,128)(2,1)S(1)}, bf16[128,1152]{1,0:T(8,128)(2,1)S(1)}, u32[]{:S(2)}, u32[]{:S(2)}) collective-permute-start(bf16[128,1152]{1,0:T(8,128)(2,1)S(1)} %get-tuple-element.45), channel_id=1, source_target_pairs={{0,2},{1,3},{2,0},{3,1},{4,6},{5,7},{6,4},{7,5},{8,10},{9,11},{10,... | collective-permute-start | bytes 884744 | tf_op jit(solution)/shard_map/ppermute | solution.py:109
  18.3 14.4 %all_to_all.5.sums_ref = f32[32,8,128]{2,1,0:T(8,128)S(1)} all-to-all(f32[32,8,128]{2,1,0:T(8,128)S(1)} %get-tuple-element.44), channel_id=1, replica_groups=mesh['morton'=8,'sib'=4] {'morton','sib'}, dimensions={0} | all-to-all | bytes 262144 | tf_op jit(solution)/shard_map/all_to_all | solution.py:548
  32.7 0.0 collective-permute-done.5.refs_0_
  32.7 0.0 copy-done
  32.7 1.2 %shard_map.170 = (f32[3,128,512]{2,1,0:T(8,128)}, f32[3,1,216]{2,1,0:T(1,128)}, f32[3,1,216]{2,1,0:T(1,128)}) custom-call(f32[3,128,512]{2,1,0:T(8,128)S(1)} %get-tuple-element.32.part_ref, f32[128,512]{1,0:T(8,128)S(1)} %copy-done.1, bf16[384,512]{1,0:T(8,128)(2,1)S(1)} %copy-done, f32[32,8,128]{2,1,0:T(8,128)S(1)} %all_to_all.5.sums_ref, ...), custom_call_target="tpu_custom_call" | custom-call | flops 200000000 | bytes 2424832 | tf_op jit(solution)/shard_map/pallas_call | solution.py:465
  (2 shorter events, 0.0 us)
Async XLA Ops:
  0.6 8.0 %copy-start.1 = (f32[128,512]{1,0:T(8,128)S(1)}, f32[128,512]{1,0:T(8,128)}, u32[]{:S(2)}) copy-start(f32[128,512]{1,0:T(8,128)} %visc_ref.5) | copy-start | bytes 786436
  0.6 8.0 %copy-start.2 = (bf16[128,3,512]{2,0,1:T(8,128)(2,1)S(1)}, bf16[128,3,512]{2,0,1:T(8,128)(2,1)}, u32[]{:S(2)}) copy-start(bf16[128,3,512]{2,0,1:T(8,128)(2,1)} %param.14) | copy-start | bytes 1179652
  0.7 8.0 %copy-start.4 = (bf16[128,512]{1,0:T(8,128)(2,1)S(1)}, bf16[128,512]{1,0:T(8,128)(2,1)}, u32[]{:S(2)}) copy-start(bf16[128,512]{1,0:T(8,128)(2,1)} %press_ref) | copy-start | bytes 393220
  0.7 8.0 %copy-start.10 = (f32[24,512]{1,0:T(8,128)S(1)}, f32[24,512]{1,0:T(8,128)}, u32[]{:S(2)}) copy-start(f32[24,512]{1,0:T(8,128)} %constant.14.clone.rows_ref) | copy-start | bytes 147460
  3.2 3.8 %collective-permute-start = (bf16[128,1152]{1,0:T(8,128)(2,1)}, bf16[128,1152]{1,0:T(8,128)(2,1)S(1)}, u32[]{:S(2)}, u32[]{:S(2)}) collective-permute-start(bf16[128,1152]{1,0:T(8,128)(2,1)} %get-tuple-element.29.faces_ref.refs_1_), channel_id=1, source_target_pairs={{0,1},{1,0},{2,3},{3,2},{4,5},{5,4},{6,7},{7,6},{8,9},{9,8},{10,11... | collective-permute-start | bytes 884744 | tf_op jit(solution)/shard_map/ppermute | solution.py:109
  3.7 7.5 %collective-permute-start.1 = (bf16[32,1152]{1,0:T(8,128)(2,1)}, bf16[32,1152]{1,0:T(8,128)(2,1)S(1)}, u32[]{:S(2)}, u32[]{:S(2)}) collective-permute-start(bf16[32,1152]{1,0:T(8,128)(2,1)} %get-tuple-element.33), channel_id=1, source_target_pairs={{0,4},{4,0},{8,12},{12,8},{16,20},{20,16},{24,28},{28,24},{1,5},{5... | collective-permute-start | bytes 221192 | tf_op jit(solution)/shard_map/ppermute | solution.py:116
  6.3 2.4 %copy-start.6 = (s32[32]{0:T(128)S(1)}, s32[32]{0:T(128)}, u32[]{:S(2)}) copy-start(s32[32]{0:T(128)} %counts_ref.3) | copy-start | bytes 388
  6.3 5.0 %collective-permute-start.2 = (bf16[32,1152]{1,0:T(8,128)(2,1)}, bf16[32,1152]{1,0:T(8,128)(2,1)S(1)}, u32[]{:S(2)}, u32[]{:S(2)}) collective-permute-start(bf16[32,1152]{1,0:T(8,128)(2,1)} %get-tuple-element.34), channel_id=1, source_target_pairs={{4,8},{8,4},{12,16},{16,12},{20,24},{24,20},{5,9},{9,5},{13,17},{1... | collective-permute-start | bytes 221192 | tf_op jit(solution)/shard_map/ppermute | solution.py:116
  7.1 3.5 %copy-start.3 = (bf16[128,1152]{1,0:T(8,128)(2,1)S(1)}, bf16[128,1152]{1,0:T(8,128)(2,1)}, u32[]{:S(2)}) copy-start(bf16[128,1152]{1,0:T(8,128)(2,1)} %get-tuple-element.29.faces_ref.refs_1_) | copy-start | bytes 884740
  7.1 3.5 %copy-start.7 = (bf16[576,512]{1,0:T(8,128)(2,1)S(1)}, bf16[576,512]{1,0:T(8,128)(2,1)}, u32[]{:S(2)}) copy-start(bf16[576,512]{1,0:T(8,128)(2,1)} %constant.17.clone.basis_ref) | copy-start | bytes 1769476
  7.1 5.4 %collective-permute-start.3 = (bf16[144,384]{1,0:T(8,128)(2,1)}, bf16[144,384]{1,0:T(8,128)(2,1)S(1)}, u32[]{:S(2)}, u32[]{:S(2)}) collective-permute-start(bf16[144,384]{1,0:T(8,128)(2,1)} %get-tuple-element.35.weights_ref), channel_id=1, source_target_pairs={{0,2},{1,3},{2,0},{3,1},{4,6},{5,7},{6,4},{7,5},{8,10},{9,11},{10,... | collective-permute-start | bytes 331784 | tf_op jit(solution)/shard_map/ppermute | solution.py:109
  12.5 0.7 %copy-start.11 = (f32[16,128]{1,0:T(8,128)S(1)}, f32[16,128]{1,0:T(8,128)}, u32[]{:S(2)}) copy-start(f32[16,128]{1,0:T(8,128)} %get-tuple-element.37.spots_ref) | copy-start | bytes 24580
  12.5 2.0 %collective-permute-start.4 = (bf16[64,1152]{1,0:T(8,128)(2,1)S(1)}, bf16[64,1152]{1,0:T(8,128)(2,1)S(1)}, u32[]{:S(2)}, u32[]{:S(2)}) collective-permute-start(bf16[64,1152]{1,0:T(8,128)(2,1)S(1)} %constant_dynamic-update-slice_fusion.refs_0_), channel_id=1, source_target_pairs={{0,1},{1,0},{2,3},{3,2},{4,5},{5,4},{6,7},{7,6},{8,9},{9,8},{10,11... | collective-permute-start | bytes 442376 | tf_op jit(solution)/shard_map/ppermute | solution.py:109
  13.2 1.3 %copy-start.5 = (bf16[144,384]{1,0:T(8,128)(2,1)S(1)}, bf16[144,384]{1,0:T(8,128)(2,1)}, u32[]{:S(2)}) copy-start(bf16[144,384]{1,0:T(8,128)(2,1)} %get-tuple-element.35.weights_ref) | copy-start | bytes 331780
  13.2 1.3 %copy-start.8 = (bf16[288,384]{1,0:T(8,128)(2,1)S(1)}, bf16[288,384]{1,0:T(8,128)(2,1)}, u32[]{:S(2)}) copy-start(bf16[288,384]{1,0:T(8,128)(2,1)} %constant.18.clone.face_basis_ref) | copy-start | bytes 663556
  13.2 1.3 %copy-start.9 = (bf16[288,256]{1,0:T(8,128)(2,1)S(1)}, bf16[288,256]{1,0:T(8,128)(2,1)}, u32[]{:S(2)}) copy-start(bf16[288,256]{1,0:T(8,128)(2,1)} %constant.20.clone.compact_ref) | copy-start | bytes 442372
  14.5 18.2 %copy-start = (bf16[384,512]{1,0:T(8,128)(2,1)S(1)}, bf16[384,512]{1,0:T(8,128)(2,1)}, u32[]{:S(2)}) copy-start(bf16[384,512]{1,0:T(8,128)(2,1)} %constant.22.spread_ref) | copy-start | bytes 1179652
  16.7 16.0 %collective-permute-start.5 = (bf16[128,1152]{1,0:T(8,128)(2,1)S(1)}, bf16[128,1152]{1,0:T(8,128)(2,1)S(1)}, u32[]{:S(2)}, u32[]{:S(2)}) collective-permute-start(bf16[128,1152]{1,0:T(8,128)(2,1)S(1)} %get-tuple-element.45), channel_id=1, source_target_pairs={{0,2},{1,3},{2,0},{3,1},{4,6},{5,7},{6,4},{7,5},{8,10},{9,11},{10,... | collective-permute-start | bytes 884744 | tf_op jit(solution)/shard_map/ppermute | solution.py:109

commit v15 on v14

--- a/solution.py
+++ b/solution.py
@@ -375,7 +375,7 @@
     return sum(dot(piece, gather) for piece in split(jnp.concatenate(tiles, axis=0), 3))
 
 
-def own_kernel(part_ref, basis_ref, faces_ref, raw_ref):
+def own_kernel(part_ref, basis_ref, faces_ref, spots_ref, raw_ref):
     leaf_count = part_ref.shape[1]
     high, low = split(part_ref[...].reshape(3 * leaf_count, NODES), 2)
     raw = dot_nt(basis_ref[...], high)
@@ -505,10 +505,11 @@
         grant=60,
     )
     weights = requests[0]
-    even, odd = pairs(even, 0), pairs(odd, 1)
+    odd = pairs(odd, 1)
     across = swap(faces, "sib", 1)
-    across, requests, pressure = lax.optimization_barrier((across, requests, pressure))
+    across, requests, even, pressure = lax.optimization_barrier((across, requests, even, pressure))
     requests = [swap(block, "sib", apart) for block, apart in zip(requests, other_sides)]
+    even = pairs(even, 0)
     part, continuity = call(
         operator_kernel,
         [((3, leaf_count, NODES), f32), ((leaf_count, NODES), f32)],
@@ -522,9 +523,9 @@
         [((ROWS, 3 * leaf_count), f32)],
         10**9,
         [],
-        [part, basis, faces],
-    )
-    even, odd, own_raw, requests = lax.optimization_barrier((even, odd, own_raw, requests))
+        [part, basis, faces, spots],
+    )
+    odd, even, own_raw, requests = lax.optimization_barrier((odd, even, own_raw, requests))
     bands = jnp.concatenate([odd, even], axis=0)
     move, *group = call(
         group_kernel,

time: 34.2 us -> 33.3 us (0.974)
  blocking collectives: 14.4 us -> 11.8 us
  starting transfers between devices: 7.03 us -> 8.92 us
  waiting for transfers between devices: 1.24 us -> 1.84 us
  local copies, waits for them, and re-layouts: 0.67 us -> 0.08 us
    all_to_all x1, blocking collectives: 14.4 us -> 11.8 us  [on_device(): every = lax.all_to_all(sums, ('morton', 'sib'), 0, 0, tiled=True)]
    ppermute x2, starting transfers between devices: 3.33 us -> 5.29 us  [pairs(): return lax.ppermute(block, 'morton', route)]
    ppermute x4, waiting for transfers between devices: 1.23 us -> 1.83 us  [swap(): lax.ppermute(block, axis, [(at, at ^ apart) for at in range(lax.axis_size...]
    unnamed x25, local copies, waits for them, and re-layouts: 0.66 us -> 0.06 us
  transfers between devices with their start and end apart: 6 -> 6, of which waited for: 1 -> 3; matrix products, arithmetic and copies ran while one was open for 0% -> 0% of each run, Pallas kernels for 11% -> 11%
where the time goes in v15:
time: 33.3 us; the launch traced here: 33.2 us
  blocking collectives  11.8 us (35%)
  Pallas kernels  9.77 us (29%)
  starting transfers between devices  8.92 us (27%)
  waiting for transfers between devices  1.84 us (6%)
  between operations  0.78 us (2%)
    all_to_all x1, blocking collectives, on_device(): every = lax.all_to_all(sums, ('morton', 'sib'), 0, 0, tiled=True)  11.8 us
    pallas_call x6, Pallas kernels, call(): pl.pallas_call(kernel, out_shape=[jax.ShapeDtypeStruct(shape, dtype) for...  9.77 us
    ppermute x2, starting transfers between devices, pairs(): return lax.ppermute(block, 'morton', route)  5.29 us
    ppermute x4, starting transfers between devices, swap(): lax.ppermute(block, axis, [(at, at ^ apart) for at in range(lax.axis_size...  3.63 us
    ppermute x4, waiting for transfers between devices, swap(): lax.ppermute(block, axis, [(at, at ^ apart) for at in range(lax.axis_size...  1.83 us
  transfers between devices with their start and end apart: 6, of which 3 were waited for; matrix products, arithmetic and copies ran while one was open for 0% of the time, Pallas kernels for 11%

profile of v15, /device:TPU:0, one launch (start us, length us, event | category | flops | bytes accessed | tf_op | source)
XLA Modules:
  0.0 33.2 jit_solution(2509583009745374657)
XLA Ops:
  0.6 0.0 copy-start.1
  0.6 0.0 copy-start.2
  0.7 0.0 copy-start.4
  0.7 0.0 copy-start.10
  0.7 2.6 %shard_map.165 = (bf16[128,1152]{1,0:T(8,128)(2,1)}, bf16[32,1152]{1,0:T(8,128)(2,1)}, bf16[32,1152]{1,0:T(8,128)(2,1)}, f32[16,128]{1,0:T(8,128)}, bf16[144,384]{1,0:T(8,128)(2,1)}) custom-call(s32[32]{0:T(128)} %counts_ref.3, bf16[3,128,512]{2,1,0:T(8,128)(2,1)} %bitcast.7, f32[128,512]{1,0:T(8,128)} %visc_ref.5, s32[6,128]{1,0:T(8,128)} %bitcast.10, ...), custom_call_target="tpu_custom_call" | custom-call | flops 400000000 | bytes 1085440 | tf_op jit(solution)/shard_map/pallas_call | solution.py:465
  3.2 0.5 %collective-permute-start = (bf16[128,1152]{1,0:T(8,128)(2,1)}, bf16[128,1152]{1,0:T(8,128)(2,1)S(1)}, u32[]{:S(2)}, u32[]{:S(2)}) collective-permute-start(bf16[128,1152]{1,0:T(8,128)(2,1)} %get-tuple-element.30.faces_ref.refs_1_), channel_id=1, source_target_pairs={{0,1},{1,0},{2,3},{3,2},{4,5},{5,4},{6,7},{7,6},{8,9},{9,8},{10,11... | collective-permute-start | bytes 884744 | tf_op jit(solution)/shard_map/ppermute | solution.py:109
  3.7 0.7 %collective-permute-start.1 = (bf16[32,1152]{1,0:T(8,128)(2,1)}, bf16[32,1152]{1,0:T(8,128)(2,1)S(1)}, u32[]{:S(2)}, u32[]{:S(2)}) collective-permute-start(bf16[32,1152]{1,0:T(8,128)(2,1)} %get-tuple-element.35), channel_id=1, source_target_pairs={{4,8},{8,4},{12,16},{16,12},{20,24},{24,20},{5,9},{9,5},{13,17},{1... | collective-permute-start | bytes 221192 | tf_op jit(solution)/shard_map/ppermute | solution.py:116
  4.4 0.8 %collective-permute-done.refs_2_ = bf16[128,1152]{1,0:T(8,128)(2,1)S(1)} collective-permute-done((bf16[128,1152]{1,0:T(8,128)(2,1)}, bf16[128,1152]{1,0:T(8,128)(2,1)S(1)}, u32[]{:S(2)}, u32[]{:S(2)}) %collective-permute-start) | collective-permute-done | bytes 294944 | tf_op jit(solution)/shard_map/ppermute | solution.py:109
  5.1 0.0 copy-start.6
  5.1 0.0 copy-start.3
  5.1 0.0 copy-start.7
  5.1 0.0 copy-start.11
  5.1 4.6 %collective-permute-start.2 = (bf16[32,1152]{1,0:T(8,128)(2,1)}, bf16[32,1152]{1,0:T(8,128)(2,1)S(1)}, u32[]{:S(2)}, u32[]{:S(2)}) collective-permute-start(bf16[32,1152]{1,0:T(8,128)(2,1)} %get-tuple-element.36), channel_id=1, source_target_pairs={{0,4},{4,0},{8,12},{12,8},{16,20},{20,16},{24,28},{28,24},{1,5},{5... | collective-permute-start | bytes 221192 | tf_op jit(solution)/shard_map/ppermute | solution.py:116
  9.8 1.5 %collective-permute-start.3 = (bf16[144,384]{1,0:T(8,128)(2,1)}, bf16[144,384]{1,0:T(8,128)(2,1)S(1)}, u32[]{:S(2)}, u32[]{:S(2)}) collective-permute-start(bf16[144,384]{1,0:T(8,128)(2,1)} %get-tuple-element.38.weights_ref), channel_id=1, source_target_pairs={{0,2},{1,3},{2,0},{3,1},{4,6},{5,7},{6,4},{7,5},{8,10},{9,11},{10,... | collective-permute-start | bytes 331784 | tf_op jit(solution)/shard_map/ppermute | solution.py:109
  11.3 0.0 copy-done.1
  11.3 0.0 copy-done.2
  11.3 0.0 copy-done.4
  11.3 0.0 copy-done.10
  11.3 0.0 copy-done.6
  11.3 1.9 %shard_map.166 = (f32[3,128,512]{2,1,0:T(8,128)S(1)}, f32[128,512]{1,0:T(8,128)}) custom-call(s32[32]{0:T(128)S(1)} %copy-done.6, bf16[3,128,512]{2,1,0:T(8,128)(2,1)S(1)} %bitcast.8, bf16[128,512]{1,0:T(8,128)(2,1)S(1)} %copy-done.4, f32[128,512]{1,0:T(8,128)S(1)} %copy-done.1, f32[24,512]{1,0:T(8,128)S(1)} %copy-done.10), custom_call_target="tpu_custom_call" | custom-call | flops 2000000000 | bytes 835584 | tf_op jit(solution)/shard_map/pallas_call | solution.py:465
  13.2 0.0 copy-done.3
  13.2 0.0 copy-done.7
  13.2 0.0 copy-done.11
  13.2 0.6 %shard_map.167.own_ref = f32[288,384]{1,0:T(8,128)S(1)} custom-call(f32[3,128,512]{2,1,0:T(8,128)S(1)} %get-tuple-element.34.part_ref, bf16[576,512]{1,0:T(8,128)(2,1)S(1)} %copy-done.7, bf16[128,1152]{1,0:T(8,128)(2,1)S(1)} %copy-done.3, f32[16,128]{1,0:T(8,128)S(1)} %copy-done.11), custom_call_target="tpu_custom_call" | custom-call | flops 1000000000 | bytes 1679360 | tf_op jit(solution)/shard_map/pallas_call | solution.py:465
  13.9 0.0 collective-permute-done.1
  13.9 0.0 collective-permute-done.2
  13.9 1.0 %collective-permute-done.3.refs_0_.refs_2_ = bf16[144,384]{1,0:T(8,128)(2,1)S(1)} collective-permute-done((bf16[144,384]{1,0:T(8,128)(2,1)}, bf16[144,384]{1,0:T(8,128)(2,1)S(1)}, u32[]{:S(2)}, u32[]{:S(2)}) %collective-permute-start.3) | collective-permute-done | bytes 110624 | tf_op jit(solution)/shard_map/ppermute | solution.py:109
  14.9 0.0 copy-start.5
  14.9 0.0 copy-start.8
  14.9 0.0 copy-start.9
  14.9 0.1 collective-permute-start.4
  15.0 1.3 %shard_map.168 = (f32[256,256]{1,0:T(8,128)S(1)}, bf16[128,1152]{1,0:T(8,128)(2,1)S(1)}, bf16[128,1152]{1,0:T(8,128)(2,1)S(1)}) custom-call(f32[16,128]{1,0:T(8,128)S(1)} %copy-done.11, bf16[144,384]{1,0:T(8,128)(2,1)S(1)} %collective-permute-done.3.refs_0_.refs_2_, bf16[128,1152]{1,0:T(8,128)(2,1)S(1)} %copy-done.3, ...), custom_call_target="tpu_custom_call" | custom-call | flops 1000000000 | bytes 708608 | tf_op jit(solution)/shard_map/pallas_call | solution.py:465
  16.3 0.1 collective-permute-done.4.refs_1_
  16.4 0.0 copy-done.5
  16.4 0.0 copy-done.8
  16.4 0.0 copy-done.9
  16.4 0.0 copy-start
  16.4 2.2 %shard_map.169 = (bf16[128,1152]{1,0:T(8,128)(2,1)S(1)}, bf16[128,1152]{1,0:T(8,128)(2,1)S(1)}, f32[32,8,128]{2,1,0:T(8,128)S(1)}) custom-call(f32[288,384]{1,0:T(8,128)S(1)} %shard_map.167.own_ref, bf16[288,384]{1,0:T(8,128)(2,1)S(1)} %copy-done.8, bf16[288,256]{1,0:T(8,128)(2,1)S(1)} %copy-done.9, f32[16,128]{1,0:T(8,128)S(1)} %copy-done.11, ...), custom_call_target="tpu_custom_call" | custom-call | flops 2000000000 | bytes 1925120 | tf_op jit(solution)/shard_map/pallas_call | solution.py:465
  18.6 1.6 %collective-permute-start.5 = (bf16[128,1152]{1,0:T(8,128)(2,1)S(1)}, bf16[128,1152]{1,0:T(8,128)(2,1)S(1)}, u32[]{:S(2)}, u32[]{:S(2)}) collective-permute-start(bf16[128,1152]{1,0:T(8,128)(2,1)S(1)} %get-tuple-element.47), channel_id=1, source_target_pairs={{0,2},{1,3},{2,0},{3,1},{4,6},{5,7},{6,4},{7,5},{8,10},{9,11},{10,... | collective-permute-start | bytes 884744 | tf_op jit(solution)/shard_map/ppermute | solution.py:109
  20.2 11.8 %all_to_all.5.sums_ref = f32[32,8,128]{2,1,0:T(8,128)S(1)} all-to-all(f32[32,8,128]{2,1,0:T(8,128)S(1)} %get-tuple-element.46), channel_id=1, replica_groups=mesh['morton'=8,'sib'=4] {'morton','sib'}, dimensions={0} | all-to-all | bytes 262144 | tf_op jit(solution)/shard_map/all_to_all | solution.py:549
  32.0 0.0 collective-permute-done.5.refs_0_
  32.0 0.0 copy-done
  32.0 1.2 %shard_map.170 = (f32[3,128,512]{2,1,0:T(8,128)}, f32[3,1,216]{2,1,0:T(1,128)}, f32[3,1,216]{2,1,0:T(1,128)}) custom-call(f32[3,128,512]{2,1,0:T(8,128)S(1)} %get-tuple-element.34.part_ref, f32[128,512]{1,0:T(8,128)S(1)} %copy-done.1, bf16[384,512]{1,0:T(8,128)(2,1)S(1)} %copy-done, f32[32,8,128]{2,1,0:T(8,128)S(1)} %all_to_all.5.sums_ref, ...), custom_call_target="tpu_custom_call" | custom-call | flops 200000000 | bytes 2424832 | tf_op jit(solution)/shard_map/pallas_call | solution.py:465
  (2 shorter events, 0.0 us)
Async XLA Ops:
  0.6 10.7 %copy-start.1 = (f32[128,512]{1,0:T(8,128)S(1)}, f32[128,512]{1,0:T(8,128)}, u32[]{:S(2)}) copy-start(f32[128,512]{1,0:T(8,128)} %visc_ref.5) | copy-start | bytes 786436
  0.6 10.7 %copy-start.2 = (bf16[128,3,512]{2,0,1:T(8,128)(2,1)S(1)}, bf16[128,3,512]{2,0,1:T(8,128)(2,1)}, u32[]{:S(2)}) copy-start(bf16[128,3,512]{2,0,1:T(8,128)(2,1)} %param.14) | copy-start | bytes 1179652
  0.7 10.6 %copy-start.4 = (bf16[128,512]{1,0:T(8,128)(2,1)S(1)}, bf16[128,512]{1,0:T(8,128)(2,1)}, u32[]{:S(2)}) copy-start(bf16[128,512]{1,0:T(8,128)(2,1)} %press_ref) | copy-start | bytes 393220
  0.7 10.6 %copy-start.10 = (f32[24,512]{1,0:T(8,128)S(1)}, f32[24,512]{1,0:T(8,128)}, u32[]{:S(2)}) copy-start(f32[24,512]{1,0:T(8,128)} %constant.14.clone.rows_ref) | copy-start | bytes 147460
  3.2 1.9 %collective-permute-start = (bf16[128,1152]{1,0:T(8,128)(2,1)}, bf16[128,1152]{1,0:T(8,128)(2,1)S(1)}, u32[]{:S(2)}, u32[]{:S(2)}) collective-permute-start(bf16[128,1152]{1,0:T(8,128)(2,1)} %get-tuple-element.30.faces_ref.refs_1_), channel_id=1, source_target_pairs={{0,1},{1,0},{2,3},{3,2},{4,5},{5,4},{6,7},{7,6},{8,9},{9,8},{10,11... | collective-permute-start | bytes 884744 | tf_op jit(solution)/shard_map/ppermute | solution.py:109
  3.7 10.2 %collective-permute-start.1 = (bf16[32,1152]{1,0:T(8,128)(2,1)}, bf16[32,1152]{1,0:T(8,128)(2,1)S(1)}, u32[]{:S(2)}, u32[]{:S(2)}) collective-permute-start(bf16[32,1152]{1,0:T(8,128)(2,1)} %get-tuple-element.35), channel_id=1, source_target_pairs={{4,8},{8,4},{12,16},{16,12},{20,24},{24,20},{5,9},{9,5},{13,17},{1... | collective-permute-start | bytes 221192 | tf_op jit(solution)/shard_map/ppermute | solution.py:116
  5.1 6.2 %copy-start.6 = (s32[32]{0:T(128)S(1)}, s32[32]{0:T(128)}, u32[]{:S(2)}) copy-start(s32[32]{0:T(128)} %counts_ref.3) | copy-start | bytes 388
  5.1 8.1 %copy-start.3 = (bf16[128,1152]{1,0:T(8,128)(2,1)S(1)}, bf16[128,1152]{1,0:T(8,128)(2,1)}, u32[]{:S(2)}) copy-start(bf16[128,1152]{1,0:T(8,128)(2,1)} %get-tuple-element.30.faces_ref.refs_1_) | copy-start | bytes 884740
  5.1 8.1 %copy-start.7 = (bf16[576,512]{1,0:T(8,128)(2,1)S(1)}, bf16[576,512]{1,0:T(8,128)(2,1)}, u32[]{:S(2)}) copy-start(bf16[576,512]{1,0:T(8,128)(2,1)} %constant.17.clone.basis_ref) | copy-start | bytes 1769476
  5.1 8.1 %copy-start.11 = (f32[16,128]{1,0:T(8,128)S(1)}, f32[16,128]{1,0:T(8,128)}, u32[]{:S(2)}) copy-start(f32[16,128]{1,0:T(8,128)} %get-tuple-element.37.spots_ref) | copy-start | bytes 24580
  5.1 8.8 %collective-permute-start.2 = (bf16[32,1152]{1,0:T(8,128)(2,1)}, bf16[32,1152]{1,0:T(8,128)(2,1)S(1)}, u32[]{:S(2)}, u32[]{:S(2)}) collective-permute-start(bf16[32,1152]{1,0:T(8,128)(2,1)} %get-tuple-element.36), channel_id=1, source_target_pairs={{0,4},{4,0},{8,12},{12,8},{16,20},{20,16},{24,28},{28,24},{1,5},{5... | collective-permute-start | bytes 221192 | tf_op jit(solution)/shard_map/ppermute | solution.py:116
  9.8 5.1 %collective-permute-start.3 = (bf16[144,384]{1,0:T(8,128)(2,1)}, bf16[144,384]{1,0:T(8,128)(2,1)S(1)}, u32[]{:S(2)}, u32[]{:S(2)}) collective-permute-start(bf16[144,384]{1,0:T(8,128)(2,1)} %get-tuple-element.38.weights_ref), channel_id=1, source_target_pairs={{0,2},{1,3},{2,0},{3,1},{4,6},{5,7},{6,4},{7,5},{8,10},{9,11},{10,... | collective-permute-start | bytes 331784 | tf_op jit(solution)/shard_map/ppermute | solution.py:109
  14.9 1.5 %copy-start.5 = (bf16[144,384]{1,0:T(8,128)(2,1)S(1)}, bf16[144,384]{1,0:T(8,128)(2,1)}, u32[]{:S(2)}) copy-start(bf16[144,384]{1,0:T(8,128)(2,1)} %get-tuple-element.38.weights_ref) | copy-start | bytes 331780
  14.9 1.5 %copy-start.8 = (bf16[288,384]{1,0:T(8,128)(2,1)S(1)}, bf16[288,384]{1,0:T(8,128)(2,1)}, u32[]{:S(2)}) copy-start(bf16[288,384]{1,0:T(8,128)(2,1)} %constant.18.clone.face_basis_ref) | copy-start | bytes 663556
  14.9 1.5 %copy-start.9 = (bf16[288,256]{1,0:T(8,128)(2,1)S(1)}, bf16[288,256]{1,0:T(8,128)(2,1)}, u32[]{:S(2)}) copy-start(bf16[288,256]{1,0:T(8,128)(2,1)} %constant.20.clone.compact_ref) | copy-start | bytes 442372
  14.9 1.4 %collective-permute-start.4 = (bf16[64,1152]{1,0:T(8,128)(2,1)S(1)}, bf16[64,1152]{1,0:T(8,128)(2,1)S(1)}, u32[]{:S(2)}, u32[]{:S(2)}) collective-permute-start(bf16[64,1152]{1,0:T(8,128)(2,1)S(1)} %constant_dynamic-update-slice_fusion.refs_0_), channel_id=1, source_target_pairs={{0,1},{1,0},{2,3},{3,2},{4,5},{5,4},{6,7},{7,6},{8,9},{9,8},{10,11... | collective-permute-start | bytes 442376 | tf_op jit(solution)/shard_map/ppermute | solution.py:109
  16.4 15.6 %copy-start = (bf16[384,512]{1,0:T(8,128)(2,1)S(1)}, bf16[384,512]{1,0:T(8,128)(2,1)}, u32[]{:S(2)}) copy-start(bf16[384,512]{1,0:T(8,128)(2,1)} %constant.22.spread_ref) | copy-start | bytes 1179652
  18.6 13.4 %collective-permute-start.5 = (bf16[128,1152]{1,0:T(8,128)(2,1)S(1)}, bf16[128,1152]{1,0:T(8,128)(2,1)S(1)}, u32[]{:S(2)}, u32[]{:S(2)}) collective-permute-start(bf16[128,1152]{1,0:T(8,128)(2,1)S(1)} %get-tuple-element.47), channel_id=1, source_target_pairs={{0,2},{1,3},{2,0},{3,1},{4,6},{5,7},{6,4},{7,5},{8,10},{9,11},{10,... | collective-permute-start | bytes 884744 | tf_op jit(solution)/shard_map/ppermute | solution.py:109

commit v16 on v15

--- a/solution.py
+++ b/solution.py
@@ -127,36 +127,35 @@
 
 
 def pack_kernel(
-    counts_ref, vel_ref, visc_ref, nbrs_ref, levels_ref, keys_ref, box_ref, pick_ref,
-    faces_ref, even_ref, odd_ref, spots_ref, *request_refs,
+    counts_ref, vel_hbm, visc_hbm, nbrs_hbm, levels_hbm, keys_hbm, box_hbm, pick_hbm, *refs
 ):
+    sides = lax.axis_size("sib") // 2
+    out_hbms, refs = refs[: 3 + sides], refs[3 + sides :]
+    faces_ref, even_ref, odd_ref, spots_ref, *request_refs = refs[: 3 + sides]
+    vel_ref, visc_ref, nbrs_ref, levels_ref, keys_ref, box_ref, pick_ref, in_sems, out_sems = refs[3 + sides :]
     sib_count = lax.axis_size("sib")
     morton = lax.axis_index("morton")
     sib = lax.axis_index("sib")
     own = morton * sib_count + sib
     leaf_count = faces_ref.shape[0]
-    fields = jnp.concatenate([vel_ref[0], vel_ref[1], vel_ref[2], visc_ref[...].astype(bf16)], axis=0)
-    picked = dot(fields, pick_ref[...])
-    for dim in range(3):
-        block = picked[3 * leaf_count :, dim * LANES : (dim + 1) * LANES]
-        block = pltpu.roll(block, LANES // 2, 1).astype(bf16)
-        for request_ref in request_refs:
-            request_ref[:leaf_count, dim * LANES : (dim + 1) * LANES] = block
-    picked = picked[: 3 * leaf_count].astype(bf16)
-    for comp in range(3):
-        for dim in range(3):
-            lane = (dim * 3 + comp) * LANES
-            rows = picked[comp * leaf_count : (comp + 1) * leaf_count]
-            faces_ref[:, lane : lane + LANES] = rows[:, dim * LANES : (dim + 1) * LANES]
-    first = counts_ref[own] - BAND
-    row = lax.broadcasted_iota(jnp.int32, (BAND, leaf_count), 0)
-    col = lax.broadcasted_iota(jnp.int32, (BAND, leaf_count), 1)
-    last_rows = jnp.where(col == row + first, 1.0, 0.0).astype(bf16)
-    high = dot(last_rows, faces_ref[...]).astype(bf16)
-    low = faces_ref[:BAND, :]
-    is_odd = jnp.bitwise_and(morton, 1) == 1
-    even_ref[...] = jnp.where(is_odd, low, high)
-    odd_ref[...] = jnp.where(is_odd, high, low)
+    box_rows = box_hbm.at[pl.ds(pl.multiple_of(morton * 8, 8), 8), :]
+    loads = [
+        pltpu.make_async_copy(source, target, in_sems.at[at])
+        for at, (source, target) in enumerate(
+            [
+                (vel_hbm, vel_ref), (pick_hbm, pick_ref), (visc_hbm, visc_ref), (nbrs_hbm, nbrs_ref),
+                (levels_hbm, levels_ref), (keys_hbm, keys_ref), (box_rows, box_ref),
+            ]
+        )
+    ]
+    stores = [
+        pltpu.make_async_copy(source, target, out_sems.at[at])
+        for at, (source, target) in enumerate(zip((faces_ref, even_ref, odd_ref, spots_ref, *request_refs), out_hbms))
+    ]
+    for load in loads:
+        load.start()
+    for load in loads[3:]:
+        load.wait()
 
     nbrs = nbrs_ref[...]
     target = jnp.maximum(nbrs, 0)
@@ -171,7 +170,7 @@
         band_start = jnp.where(owner_sib == other, counts_ref[below + other] - BAND, band_start)
     below_at = BAND * jnp.bitwise_and(morton, 1)
     in_band = jnp.where(step < 0, slot - band_start + below_at, slot + BAND - below_at)
-    box = box_ref[pl.ds(pl.multiple_of(morton * 8, 8), 8), :]
+    box = box_ref[...]
     shift_bits = 3 * (LMAX - levels_ref[...])
     anchor = jnp.left_shift(jnp.right_shift(keys_ref[...], shift_bits), shift_bits)
     span = jnp.left_shift(jnp.ones_like(shift_bits), LMAX - levels_ref[...]).astype(f32)
@@ -199,6 +198,38 @@
         request_ref = request_refs[side - 1]
         request_ref[leaf_count:, :LANES] = jnp.concatenate(parts, axis=0).astype(bf16)
         request_ref[leaf_count:, LANES:] = jnp.zeros((16, FACES - LANES), bf16)
+    stores[3].start()
+
+    for load in loads[:3]:
+        load.wait()
+    fields = jnp.concatenate([vel_ref[0], vel_ref[1], vel_ref[2], visc_ref[...].astype(bf16)], axis=0)
+    picked = dot(fields, pick_ref[...])
+    for comp in range(3):
+        rows = picked[comp * leaf_count : (comp + 1) * leaf_count].astype(bf16)
+        for dim in range(3):
+            lane = (dim * 3 + comp) * LANES
+            faces_ref[:, lane : lane + LANES] = rows[:, dim * LANES : (dim + 1) * LANES]
+    stores[0].start()
+    first = counts_ref[own] - BAND
+    row = lax.broadcasted_iota(jnp.int32, (BAND, leaf_count), 0)
+    col = lax.broadcasted_iota(jnp.int32, (BAND, leaf_count), 1)
+    last_rows = jnp.where(col == row + first, 1.0, 0.0).astype(bf16)
+    high = dot(last_rows, faces_ref[...]).astype(bf16)
+    low = faces_ref[:BAND, :]
+    is_odd = jnp.bitwise_and(morton, 1) == 1
+    even_ref[...] = jnp.where(is_odd, low, high)
+    odd_ref[...] = jnp.where(is_odd, high, low)
+    for store in stores[1:3]:
+        store.start()
+    for dim in range(3):
+        block = picked[3 * leaf_count :, dim * LANES : (dim + 1) * LANES]
+        block = pltpu.roll(block, LANES // 2, 1).astype(bf16)
+        for request_ref in request_refs:
+            request_ref[:leaf_count, dim * LANES : (dim + 1) * LANES] = block
+    for store in stores[4:]:
+        store.start()
+    for store in stores:
+        store.wait()
 
 
 def gathered(asked, window_refs, start):
@@ -502,6 +533,26 @@
         4 * 10**8,
         [counts],
         [vel, viscosity, nbrs, levels.reshape(1, -1), morton_keys.reshape(1, -1), boxes, pick],
+        [
+            pltpu.VMEM((leaf_count, width), bf16),
+            pltpu.VMEM((BAND, width), bf16),
+            pltpu.VMEM((BAND, width), bf16),
+            pltpu.VMEM((16, leaf_count), f32),
+        ]
+        + [pltpu.VMEM((leaf_count + 16, FACES), bf16)] * (sides - 1)
+        + [
+            pltpu.VMEM(vel.shape, bf16),
+            pltpu.VMEM(viscosity.shape, f32),
+            pltpu.VMEM(nbrs.shape, jnp.int32),
+            pltpu.VMEM((1, leaf_count), jnp.int32),
+            pltpu.VMEM((1, leaf_count), jnp.int32),
+            pltpu.VMEM((8, LANES), f32),
+            pltpu.VMEM(pick.shape, bf16),
+            pltpu.SemaphoreType.DMA((7,)),
+            pltpu.SemaphoreType.DMA((3 + sides,)),
+        ],
+        place=pltpu.HBM,
+        outs=[pltpu.HBM] * (3 + sides),
         grant=60,
     )
     weights = requests[0]

time: 33.3 us -> 34.3 us (1.030)
  Pallas kernels: 9.77 us -> 10.6 us
    pallas_call x6, Pallas kernels: 9.77 us -> 10.6 us  [call(): pl.pallas_call(kernel, out_shape=[jax.ShapeDtypeStruct(shape, dtype) for...]
where the time goes in v16:
time: 34.3 us; the launch traced here: 34.1 us
  blocking collectives  11.8 us (34%)
  Pallas kernels  10.6 us (31%)
  starting transfers between devices  9.01 us (26%)
  waiting for transfers between devices  1.82 us (5%)
  between operations  0.79 us (2%)
    all_to_all x1, blocking collectives, on_device(): every = lax.all_to_all(sums, ('morton', 'sib'), 0, 0, tiled=True)  11.8 us
    pallas_call x6, Pallas kernels, call(): pl.pallas_call(kernel, out_shape=[jax.ShapeDtypeStruct(shape, dtype) for...  10.6 us
    ppermute x2, starting transfers between devices, pairs(): return lax.ppermute(block, 'morton', route)  5.31 us
    ppermute x4, starting transfers between devices, swap(): lax.ppermute(block, axis, [(at, at ^ apart) for at in range(lax.axis_size...  3.7 us
    ppermute x4, waiting for transfers between devices, swap(): lax.ppermute(block, axis, [(at, at ^ apart) for at in range(lax.axis_size...  1.82 us
  transfers between devices with their start and end apart: 6, of which 3 were waited for; matrix products, arithmetic and copies ran while one was open for 0% of the time, Pallas kernels for 11%

profile of v16, /device:TPU:0, one launch (start us, length us, event | category | flops | bytes accessed | tf_op | source)
XLA Modules:
  0.0 34.1 jit_solution(9424412780252371379)
XLA Ops:
  0.6 0.0 copy-start.1
  0.6 0.0 copy-start.2
  0.7 0.0 copy-start.4
  0.7 0.0 copy-start.10
  0.7 3.4 %shard_map.165 = (bf16[128,1152]{1,0:T(8,128)(2,1)}, bf16[32,1152]{1,0:T(8,128)(2,1)}, bf16[32,1152]{1,0:T(8,128)(2,1)}, f32[16,128]{1,0:T(8,128)}, bf16[144,384]{1,0:T(8,128)(2,1)}) custom-call(s32[32]{0:T(128)} %counts_ref.3, bf16[3,128,512]{2,1,0:T(8,128)(2,1)} %bitcast.7, f32[128,512]{1,0:T(8,128)} %visc_ref.3, s32[6,128]{1,0:T(8,128)} %bitcast.10, ...), custom_call_target="tpu_custom_call" | custom-call | flops 400000000 | bytes 1085440 | tf_op jit(solution)/shard_map/pallas_call | solution.py:496
  4.0 0.5 %collective-permute-start = (bf16[128,1152]{1,0:T(8,128)(2,1)}, bf16[128,1152]{1,0:T(8,128)(2,1)S(1)}, u32[]{:S(2)}, u32[]{:S(2)}) collective-permute-start(bf16[128,1152]{1,0:T(8,128)(2,1)} %get-tuple-element.30.faces_ref.refs_1_), channel_id=1, source_target_pairs={{0,1},{1,0},{2,3},{3,2},{4,5},{5,4},{6,7},{7,6},{8,9},{9,8},{10,11... | collective-permute-start | bytes 884744 | tf_op jit(solution)/shard_map/ppermute | solution.py:109
  4.6 0.7 %collective-permute-start.1 = (bf16[32,1152]{1,0:T(8,128)(2,1)}, bf16[32,1152]{1,0:T(8,128)(2,1)S(1)}, u32[]{:S(2)}, u32[]{:S(2)}) collective-permute-start(bf16[32,1152]{1,0:T(8,128)(2,1)} %get-tuple-element.35), channel_id=1, source_target_pairs={{4,8},{8,4},{12,16},{16,12},{20,24},{24,20},{5,9},{9,5},{13,17},{1... | collective-permute-start | bytes 221192 | tf_op jit(solution)/shard_map/ppermute | solution.py:116
  5.2 0.8 %collective-permute-done.refs_2_ = bf16[128,1152]{1,0:T(8,128)(2,1)S(1)} collective-permute-done((bf16[128,1152]{1,0:T(8,128)(2,1)}, bf16[128,1152]{1,0:T(8,128)(2,1)S(1)}, u32[]{:S(2)}, u32[]{:S(2)}) %collective-permute-start) | collective-permute-done | bytes 294944 | tf_op jit(solution)/shard_map/ppermute | solution.py:109
  6.0 0.0 copy-start.6
  6.0 0.0 copy-start.3
  6.0 0.0 copy-start.7
  6.0 0.0 copy-start.11
  6.0 4.7 %collective-permute-start.2 = (bf16[32,1152]{1,0:T(8,128)(2,1)}, bf16[32,1152]{1,0:T(8,128)(2,1)S(1)}, u32[]{:S(2)}, u32[]{:S(2)}) collective-permute-start(bf16[32,1152]{1,0:T(8,128)(2,1)} %get-tuple-element.36), channel_id=1, source_target_pairs={{0,4},{4,0},{8,12},{12,8},{16,20},{20,16},{24,28},{28,24},{1,5},{5... | collective-permute-start | bytes 221192 | tf_op jit(solution)/shard_map/ppermute | solution.py:116
  10.6 1.5 %collective-permute-start.3 = (bf16[144,384]{1,0:T(8,128)(2,1)}, bf16[144,384]{1,0:T(8,128)(2,1)S(1)}, u32[]{:S(2)}, u32[]{:S(2)}) collective-permute-start(bf16[144,384]{1,0:T(8,128)(2,1)} %get-tuple-element.38.weights_ref), channel_id=1, source_target_pairs={{0,2},{1,3},{2,0},{3,1},{4,6},{5,7},{6,4},{7,5},{8,10},{9,11},{10,... | collective-permute-start | bytes 331784 | tf_op jit(solution)/shard_map/ppermute | solution.py:109
  12.2 0.0 copy-done.1
  12.2 0.0 copy-done.2
  12.2 0.0 copy-done.4
  12.2 0.0 copy-done.10
  12.2 0.0 copy-done.6
  12.2 1.9 %shard_map.166 = (f32[3,128,512]{2,1,0:T(8,128)S(1)}, f32[128,512]{1,0:T(8,128)}) custom-call(s32[32]{0:T(128)S(1)} %copy-done.6, bf16[3,128,512]{2,1,0:T(8,128)(2,1)S(1)} %bitcast.8, bf16[128,512]{1,0:T(8,128)(2,1)S(1)} %copy-done.4, f32[128,512]{1,0:T(8,128)S(1)} %copy-done.1, f32[24,512]{1,0:T(8,128)S(1)} %copy-done.10), custom_call_target="tpu_custom_call" | custom-call | flops 2000000000 | bytes 835584 | tf_op jit(solution)/shard_map/pallas_call | solution.py:496
  14.1 0.0 copy-done.3
  14.1 0.0 copy-done.7
  14.1 0.0 copy-done.11
  14.1 0.6 %shard_map.167.own_ref = f32[288,384]{1,0:T(8,128)S(1)} custom-call(f32[3,128,512]{2,1,0:T(8,128)S(1)} %get-tuple-element.34.part_ref, bf16[576,512]{1,0:T(8,128)(2,1)S(1)} %copy-done.7, bf16[128,1152]{1,0:T(8,128)(2,1)S(1)} %copy-done.3, f32[16,128]{1,0:T(8,128)S(1)} %copy-done.11), custom_call_target="tpu_custom_call" | custom-call | flops 1000000000 | bytes 1679360 | tf_op jit(solution)/shard_map/pallas_call | solution.py:496
  14.8 0.0 collective-permute-done.1
  14.8 0.0 collective-permute-done.2
  14.8 1.0 %collective-permute-done.3.refs_0_.refs_2_ = bf16[144,384]{1,0:T(8,128)(2,1)S(1)} collective-permute-done((bf16[144,384]{1,0:T(8,128)(2,1)}, bf16[144,384]{1,0:T(8,128)(2,1)S(1)}, u32[]{:S(2)}, u32[]{:S(2)}) %collective-permute-start.3) | collective-permute-done | bytes 110624 | tf_op jit(solution)/shard_map/ppermute | solution.py:109
  15.8 0.0 copy-start.5
  15.8 0.0 copy-start.8
  15.8 0.0 copy-start.9
  15.8 0.1 collective-permute-start.4
  15.9 1.3 %shard_map.168 = (f32[256,256]{1,0:T(8,128)S(1)}, bf16[128,1152]{1,0:T(8,128)(2,1)S(1)}, bf16[128,1152]{1,0:T(8,128)(2,1)S(1)}) custom-call(f32[16,128]{1,0:T(8,128)S(1)} %copy-done.11, bf16[144,384]{1,0:T(8,128)(2,1)S(1)} %collective-permute-done.3.refs_0_.refs_2_, bf16[128,1152]{1,0:T(8,128)(2,1)S(1)} %copy-done.3, ...), custom_call_target="tpu_custom_call" | custom-call | flops 1000000000 | bytes 708608 | tf_op jit(solution)/shard_map/pallas_call | solution.py:496
  17.2 0.1 collective-permute-done.4.refs_1_
  17.2 0.0 copy-done.5
  17.2 0.0 copy-done.8
  17.2 0.0 copy-done.9
  17.3 0.0 copy-start
  17.3 2.2 %shard_map.169 = (bf16[128,1152]{1,0:T(8,128)(2,1)S(1)}, bf16[128,1152]{1,0:T(8,128)(2,1)S(1)}, f32[32,8,128]{2,1,0:T(8,128)S(1)}) custom-call(f32[288,384]{1,0:T(8,128)S(1)} %shard_map.167.own_ref, bf16[288,384]{1,0:T(8,128)(2,1)S(1)} %copy-done.8, bf16[288,256]{1,0:T(8,128)(2,1)S(1)} %copy-done.9, f32[16,128]{1,0:T(8,128)S(1)} %copy-done.11, ...), custom_call_target="tpu_custom_call" | custom-call | flops 2000000000 | bytes 1925120 | tf_op jit(solution)/shard_map/pallas_call | solution.py:496
  19.4 1.6 %collective-permute-start.5 = (bf16[128,1152]{1,0:T(8,128)(2,1)S(1)}, bf16[128,1152]{1,0:T(8,128)(2,1)S(1)}, u32[]{:S(2)}, u32[]{:S(2)}) collective-permute-start(bf16[128,1152]{1,0:T(8,128)(2,1)S(1)} %get-tuple-element.47), channel_id=1, source_target_pairs={{0,2},{1,3},{2,0},{3,1},{4,6},{5,7},{6,4},{7,5},{8,10},{9,11},{10,... | collective-permute-start | bytes 884744 | tf_op jit(solution)/shard_map/ppermute | solution.py:109
  21.0 11.8 %all_to_all.5.sums_ref = f32[32,8,128]{2,1,0:T(8,128)S(1)} all-to-all(f32[32,8,128]{2,1,0:T(8,128)S(1)} %get-tuple-element.46), channel_id=1, replica_groups=mesh['morton'=8,'sib'=4] {'morton','sib'}, dimensions={0} | all-to-all | bytes 262144 | tf_op jit(solution)/shard_map/all_to_all | solution.py:600
  32.8 0.0 collective-permute-done.5.refs_0_
  32.8 0.0 copy-done
  32.8 1.2 %shard_map.170 = (f32[3,128,512]{2,1,0:T(8,128)}, f32[3,1,216]{2,1,0:T(1,128)}, f32[3,1,216]{2,1,0:T(1,128)}) custom-call(f32[3,128,512]{2,1,0:T(8,128)S(1)} %get-tuple-element.34.part_ref, f32[128,512]{1,0:T(8,128)S(1)} %copy-done.1, bf16[384,512]{1,0:T(8,128)(2,1)S(1)} %copy-done, f32[32,8,128]{2,1,0:T(8,128)S(1)} %all_to_all.5.sums_ref, ...), custom_call_target="tpu_custom_call" | custom-call | flops 200000000 | bytes 2424832 | tf_op jit(solution)/shard_map/pallas_call | solution.py:496
  (2 shorter events, 0.0 us)
Async XLA Ops:
  0.6 11.5 %copy-start.1 = (f32[128,512]{1,0:T(8,128)S(1)}, f32[128,512]{1,0:T(8,128)}, u32[]{:S(2)}) copy-start(f32[128,512]{1,0:T(8,128)} %visc_ref.3) | copy-start | bytes 786436
  0.6 11.5 %copy-start.2 = (bf16[128,3,512]{2,0,1:T(8,128)(2,1)S(1)}, bf16[128,3,512]{2,0,1:T(8,128)(2,1)}, u32[]{:S(2)}) copy-start(bf16[128,3,512]{2,0,1:T(8,128)(2,1)} %param.14) | copy-start | bytes 1179652
  0.7 11.5 %copy-start.4 = (bf16[128,512]{1,0:T(8,128)(2,1)S(1)}, bf16[128,512]{1,0:T(8,128)(2,1)}, u32[]{:S(2)}) copy-start(bf16[128,512]{1,0:T(8,128)(2,1)} %press_ref) | copy-start | bytes 393220
  0.7 11.5 %copy-start.10 = (f32[24,512]{1,0:T(8,128)S(1)}, f32[24,512]{1,0:T(8,128)}, u32[]{:S(2)}) copy-start(f32[24,512]{1,0:T(8,128)} %constant.14.clone.rows_ref) | copy-start | bytes 147460
  4.0 1.9 %collective-permute-start = (bf16[128,1152]{1,0:T(8,128)(2,1)}, bf16[128,1152]{1,0:T(8,128)(2,1)S(1)}, u32[]{:S(2)}, u32[]{:S(2)}) collective-permute-start(bf16[128,1152]{1,0:T(8,128)(2,1)} %get-tuple-element.30.faces_ref.refs_1_), channel_id=1, source_target_pairs={{0,1},{1,0},{2,3},{3,2},{4,5},{5,4},{6,7},{7,6},{8,9},{9,8},{10,11... | collective-permute-start | bytes 884744 | tf_op jit(solution)/shard_map/ppermute | solution.py:109
  4.6 10.2 %collective-permute-start.1 = (bf16[32,1152]{1,0:T(8,128)(2,1)}, bf16[32,1152]{1,0:T(8,128)(2,1)S(1)}, u32[]{:S(2)}, u32[]{:S(2)}) collective-permute-start(bf16[32,1152]{1,0:T(8,128)(2,1)} %get-tuple-element.35), channel_id=1, source_target_pairs={{4,8},{8,4},{12,16},{16,12},{20,24},{24,20},{5,9},{9,5},{13,17},{1... | collective-permute-start | bytes 221192 | tf_op jit(solution)/shard_map/ppermute | solution.py:116
  6.0 6.2 %copy-start.6 = (s32[32]{0:T(128)S(1)}, s32[32]{0:T(128)}, u32[]{:S(2)}) copy-start(s32[32]{0:T(128)} %counts_ref.3) | copy-start | bytes 388
  6.0 8.1 %copy-start.3 = (bf16[128,1152]{1,0:T(8,128)(2,1)S(1)}, bf16[128,1152]{1,0:T(8,128)(2,1)}, u32[]{:S(2)}) copy-start(bf16[128,1152]{1,0:T(8,128)(2,1)} %get-tuple-element.30.faces_ref.refs_1_) | copy-start | bytes 884740
  6.0 8.1 %copy-start.7 = (bf16[576,512]{1,0:T(8,128)(2,1)S(1)}, bf16[576,512]{1,0:T(8,128)(2,1)}, u32[]{:S(2)}) copy-start(bf16[576,512]{1,0:T(8,128)(2,1)} %constant.17.clone.basis_ref) | copy-start | bytes 1769476
  6.0 8.1 %copy-start.11 = (f32[16,128]{1,0:T(8,128)S(1)}, f32[16,128]{1,0:T(8,128)}, u32[]{:S(2)}) copy-start(f32[16,128]{1,0:T(8,128)} %get-tuple-element.37.spots_ref) | copy-start | bytes 24580
  6.0 8.8 %collective-permute-start.2 = (bf16[32,1152]{1,0:T(8,128)(2,1)}, bf16[32,1152]{1,0:T(8,128)(2,1)S(1)}, u32[]{:S(2)}, u32[]{:S(2)}) collective-permute-start(bf16[32,1152]{1,0:T(8,128)(2,1)} %get-tuple-element.36), channel_id=1, source_target_pairs={{0,4},{4,0},{8,12},{12,8},{16,20},{20,16},{24,28},{28,24},{1,5},{5... | collective-permute-start | bytes 221192 | tf_op jit(solution)/shard_map/ppermute | solution.py:116
  10.6 5.1 %collective-permute-start.3 = (bf16[144,384]{1,0:T(8,128)(2,1)}, bf16[144,384]{1,0:T(8,128)(2,1)S(1)}, u32[]{:S(2)}, u32[]{:S(2)}) collective-permute-start(bf16[144,384]{1,0:T(8,128)(2,1)} %get-tuple-element.38.weights_ref), channel_id=1, source_target_pairs={{0,2},{1,3},{2,0},{3,1},{4,6},{5,7},{6,4},{7,5},{8,10},{9,11},{10,... | collective-permute-start | bytes 331784 | tf_op jit(solution)/shard_map/ppermute | solution.py:109
  15.8 1.5 %copy-start.5 = (bf16[144,384]{1,0:T(8,128)(2,1)S(1)}, bf16[144,384]{1,0:T(8,128)(2,1)}, u32[]{:S(2)}) copy-start(bf16[144,384]{1,0:T(8,128)(2,1)} %get-tuple-element.38.weights_ref) | copy-start | bytes 331780
  15.8 1.5 %copy-start.8 = (bf16[288,384]{1,0:T(8,128)(2,1)S(1)}, bf16[288,384]{1,0:T(8,128)(2,1)}, u32[]{:S(2)}) copy-start(bf16[288,384]{1,0:T(8,128)(2,1)} %constant.18.clone.face_basis_ref) | copy-start | bytes 663556
  15.8 1.5 %copy-start.9 = (bf16[288,256]{1,0:T(8,128)(2,1)S(1)}, bf16[288,256]{1,0:T(8,128)(2,1)}, u32[]{:S(2)}) copy-start(bf16[288,256]{1,0:T(8,128)(2,1)} %constant.20.clone.compact_ref) | copy-start | bytes 442372
  15.8 1.4 %collective-permute-start.4 = (bf16[64,1152]{1,0:T(8,128)(2,1)S(1)}, bf16[64,1152]{1,0:T(8,128)(2,1)S(1)}, u32[]{:S(2)}, u32[]{:S(2)}) collective-permute-start(bf16[64,1152]{1,0:T(8,128)(2,1)S(1)} %constant_dynamic-update-slice_fusion.refs_0_), channel_id=1, source_target_pairs={{0,1},{1,0},{2,3},{3,2},{4,5},{5,4},{6,7},{7,6},{8,9},{9,8},{10,11... | collective-permute-start | bytes 442376 | tf_op jit(solution)/shard_map/ppermute | solution.py:109
  17.3 15.6 %copy-start = (bf16[384,512]{1,0:T(8,128)(2,1)S(1)}, bf16[384,512]{1,0:T(8,128)(2,1)}, u32[]{:S(2)}) copy-start(bf16[384,512]{1,0:T(8,128)(2,1)} %constant.22.spread_ref) | copy-start | bytes 1179652
  19.4 13.4 %collective-permute-start.5 = (bf16[128,1152]{1,0:T(8,128)(2,1)S(1)}, bf16[128,1152]{1,0:T(8,128)(2,1)S(1)}, u32[]{:S(2)}, u32[]{:S(2)}) collective-permute-start(bf16[128,1152]{1,0:T(8,128)(2,1)S(1)} %get-tuple-element.47), channel_id=1, source_target_pairs={{0,2},{1,3},{2,0},{3,1},{4,6},{5,7},{6,4},{7,5},{8,10},{9,11},{10,... | collective-permute-start | bytes 884744 | tf_op jit(solution)/shard_map/ppermute | solution.py:109

commit v17 on v15

--- a/solution.py
+++ b/solution.py
@@ -82,27 +82,23 @@
     return table
 
 
-def box_table(morton_count):
-    bits = morton_count.bit_length() - 1
-    key_bits = 3 * LMAX - bits
-    table = np.zeros((morton_count, 8, LANES), np.float32)
-    for morton in range(morton_count):
-        base = morton << key_bits
-        lows, sides = [], []
-        for offset in (2, 1, 0):
-            free = max(0, min(LMAX, (key_bits - offset + 2) // 3))
-            cell = sum(((base >> (3 * bit + offset)) & 1) << bit for bit in range(LMAX))
-            sides.append(2.0**free / 2.0**LMAX)
-            lows.append(cell / 2.0**LMAX)
-        scale = 0.5 * max(sides)
-        for dim in range(3):
-            center = lows[dim] + 0.5 * sides[dim]
-            table[morton, dim, 3:6] = (center - 0.5) / 0.5
-            table[morton, 4 + dim] = center
-        table[morton, 3] = 1.0
-        table[morton, 3, 3:6] = scale / 0.5
-        table[morton, 7] = 1.0 / scale
-    return table.reshape(morton_count * 8, LANES)
+def box_rows():
+    morton = lax.axis_index("morton")
+    key_bits = 3 * LMAX - (lax.axis_size("morton").bit_length() - 1)
+    base = jnp.full((1, LANES), morton, jnp.int32) << key_bits
+    lane = lax.broadcasted_iota(jnp.int32, (1, LANES), 1)
+    to_root = (lane >= 3) & (lane < 6)
+    sides = [2.0 ** max(0, min(LMAX, (key_bits - offset + 2) // 3)) / 2.0**LMAX for offset in (2, 1, 0)]
+    scale = 0.5 * max(sides)
+    centers = []
+    for side, offset in zip(sides, (2, 1, 0)):
+        cell = jnp.zeros_like(base)
+        for bit in range(LMAX):
+            cell = cell + jnp.left_shift(jnp.bitwise_and(jnp.right_shift(base, 3 * bit + offset), 1), bit)
+        centers.append(cell.astype(f32) * (1.0 / 2.0**LMAX) + 0.5 * side)
+    shifts = [jnp.where(to_root, (center - 0.5) * 2.0, 0.0) for center in centers]
+    ratio = jnp.where(to_root, scale * 2.0, 1.0)
+    return jnp.concatenate(shifts + [ratio] + centers + [jnp.full((1, LANES), 1.0 / scale, f32)], axis=0)
 
 
 def swap(block, axis, apart):
@@ -127,7 +123,7 @@
 
 
 def pack_kernel(
-    counts_ref, vel_ref, visc_ref, nbrs_ref, levels_ref, keys_ref, box_ref, pick_ref,
+    counts_ref, vel_ref, visc_ref, nbrs_ref, levels_ref, keys_ref,
     faces_ref, even_ref, odd_ref, spots_ref, *request_refs,
 ):
     sib_count = lax.axis_size("sib")
@@ -136,7 +132,18 @@
     own = morton * sib_count + sib
     leaf_count = faces_ref.shape[0]
     fields = jnp.concatenate([vel_ref[0], vel_ref[1], vel_ref[2], visc_ref[...].astype(bf16)], axis=0)
-    picked = dot(fields, pick_ref[...])
+    lane = lax.broadcasted_iota(jnp.int32, (1, FACES), 1)
+    first_at, second_at = jnp.bitwise_and(jnp.right_shift(lane, 3), 7), jnp.bitwise_and(lane, 7)
+    end_at = 7 * jnp.bitwise_and(jnp.right_shift(lane, 6), 1)
+    taken = jnp.where(
+        lane < LANES,
+        64 * end_at + 8 * first_at + second_at,
+        jnp.where(
+            lane < 2 * LANES, 64 * first_at + 8 * end_at + second_at, 64 * first_at + 8 * second_at + end_at
+        ),
+    )
+    node = lax.broadcasted_iota(jnp.int32, (NODES, FACES), 0)
+    picked = dot(fields, jnp.where(node == taken, 1.0, 0.0).astype(bf16))
     for dim in range(3):
         block = picked[3 * leaf_count :, dim * LANES : (dim + 1) * LANES]
         block = pltpu.roll(block, LANES // 2, 1).astype(bf16)
@@ -171,7 +178,7 @@
         band_start = jnp.where(owner_sib == other, counts_ref[below + other] - BAND, band_start)
     below_at = BAND * jnp.bitwise_and(morton, 1)
     in_band = jnp.where(step < 0, slot - band_start + below_at, slot + BAND - below_at)
-    box = box_ref[pl.ds(pl.multiple_of(morton * 8, 8), 8), :]
+    box = box_rows()
     shift_bits = 3 * (LMAX - levels_ref[...])
     anchor = jnp.left_shift(jnp.right_shift(keys_ref[...], shift_bits), shift_bits)
     span = jnp.left_shift(jnp.ones_like(shift_bits), LMAX - levels_ref[...]).astype(f32)
@@ -477,12 +484,10 @@
     leaf_count = velocity.shape[0]
     morton_count = lax.axis_size("morton")
     rows = jnp.asarray(derivative_rows().astype(np.float32))
-    pick = jnp.asarray(face_table().astype(np.float32)).astype(bf16)
     spread = jnp.asarray(spread_table().astype(np.float32)).astype(bf16)
     basis = basis_tables()
     face_basis = (basis.astype(np.float32) @ spread_table().T.astype(np.float32)).astype(jnp.bfloat16)
     basis, face_basis = jnp.asarray(basis), jnp.asarray(face_basis[:ROWS])
-    boxes = jnp.asarray(box_table(morton_count))
     vel = jnp.transpose(velocity, (1, 0, 2))
     nbrs = jnp.transpose(neighbors, (1, 0))
 
@@ -501,7 +506,7 @@
         + [((leaf_count + 16, FACES), bf16)] * (sides - 1),
         4 * 10**8,
         [counts],
-        [vel, viscosity, nbrs, levels.reshape(1, -1), morton_keys.reshape(1, -1), boxes, pick],
+        [vel, viscosity, nbrs, levels.reshape(1, -1), morton_keys.reshape(1, -1)],
         grant=60,
     )
     weights = requests[0]

time: 33.3 us -> 33.2 us (level)
  transfers between devices with their start and end apart: 6 -> 6, of which waited for: 3 -> 3; matrix products, arithmetic and copies ran while one was open for 0% -> 0% of each run, Pallas kernels for 11% -> 12%
where the time goes in v17:
time: 33.2 us; the launch traced here: 33 us
  blocking collectives  11.8 us (36%)
  Pallas kernels  9.63 us (29%)
  starting transfers between devices  8.92 us (27%)
  waiting for transfers between devices  1.85 us (6%)
  between operations  0.78 us (2%)
    all_to_all x1, blocking collectives, on_device(): every = lax.all_to_all(sums, ('morton', 'sib'), 0, 0, tiled=True)  11.8 us
    pallas_call x6, Pallas kernels, call(): pl.pallas_call(kernel, out_shape=[jax.ShapeDtypeStruct(shape, dtype) for...  9.63 us
    ppermute x2, starting transfers between devices, pairs(): return lax.ppermute(block, 'morton', route)  5.29 us
    ppermute x4, starting transfers between devices, swap(): lax.ppermute(block, axis, [(at, at ^ apart) for at in range(lax.axis_size...  3.63 us
    ppermute x4, waiting for transfers between devices, swap(): lax.ppermute(block, axis, [(at, at ^ apart) for at in range(lax.axis_size...  1.84 us
  transfers between devices with their start and end apart: 6, of which 3 were waited for; matrix products, arithmetic and copies ran while one was open for 0% of the time, Pallas kernels for 12%

profile of v17, /device:TPU:0, one launch (start us, length us, event | category | flops | bytes accessed | tf_op | source)
XLA Modules:
  0.0 33.0 jit_solution(10109949339845249328)
XLA Ops:
  0.6 0.0 copy-start.1
  0.6 0.0 copy-start.2
  0.7 0.0 copy-start.4
  0.7 0.0 copy-start.10
  0.7 2.4 %shard_map.147 = (bf16[128,1152]{1,0:T(8,128)(2,1)}, bf16[32,1152]{1,0:T(8,128)(2,1)}, bf16[32,1152]{1,0:T(8,128)(2,1)}, f32[16,128]{1,0:T(8,128)}, bf16[144,384]{1,0:T(8,128)(2,1)}) custom-call(s32[32]{0:T(128)} %counts_ref.3, bf16[3,128,512]{2,1,0:T(8,128)(2,1)} %bitcast.7, f32[128,512]{1,0:T(8,128)} %visc_ref.5, s32[6,128]{1,0:T(8,128)} %bitcast.10, ...), custom_call_target="tpu_custom_call" | custom-call | flops 400000000 | bytes 659456 | tf_op jit(solution)/shard_map/pallas_call | solution.py:472
  3.1 0.5 %collective-permute-start = (bf16[128,1152]{1,0:T(8,128)(2,1)}, bf16[128,1152]{1,0:T(8,128)(2,1)S(1)}, u32[]{:S(2)}, u32[]{:S(2)}) collective-permute-start(bf16[128,1152]{1,0:T(8,128)(2,1)} %get-tuple-element.30.faces_ref.refs_1_), channel_id=1, source_target_pairs={{0,1},{1,0},{2,3},{3,2},{4,5},{5,4},{6,7},{7,6},{8,9},{9,8},{10,11... | collective-permute-start | bytes 884744 | tf_op jit(solution)/shard_map/ppermute | solution.py:105
  3.5 0.7 %collective-permute-start.1 = (bf16[32,1152]{1,0:T(8,128)(2,1)}, bf16[32,1152]{1,0:T(8,128)(2,1)S(1)}, u32[]{:S(2)}, u32[]{:S(2)}) collective-permute-start(bf16[32,1152]{1,0:T(8,128)(2,1)} %get-tuple-element.35), channel_id=1, source_target_pairs={{4,8},{8,4},{12,16},{16,12},{20,24},{24,20},{5,9},{9,5},{13,17},{1... | collective-permute-start | bytes 221192 | tf_op jit(solution)/shard_map/ppermute | solution.py:112
  4.2 0.8 %collective-permute-done.refs_2_ = bf16[128,1152]{1,0:T(8,128)(2,1)S(1)} collective-permute-done((bf16[128,1152]{1,0:T(8,128)(2,1)}, bf16[128,1152]{1,0:T(8,128)(2,1)S(1)}, u32[]{:S(2)}, u32[]{:S(2)}) %collective-permute-start) | collective-permute-done | bytes 294944 | tf_op jit(solution)/shard_map/ppermute | solution.py:105
  5.0 0.0 copy-start.6
  5.0 0.0 copy-start.3
  5.0 0.0 copy-start.7
  5.0 0.0 copy-start.11
  5.0 4.6 %collective-permute-start.2 = (bf16[32,1152]{1,0:T(8,128)(2,1)}, bf16[32,1152]{1,0:T(8,128)(2,1)S(1)}, u32[]{:S(2)}, u32[]{:S(2)}) collective-permute-start(bf16[32,1152]{1,0:T(8,128)(2,1)} %get-tuple-element.36), channel_id=1, source_target_pairs={{0,4},{4,0},{8,12},{12,8},{16,20},{20,16},{24,28},{28,24},{1,5},{5... | collective-permute-start | bytes 221192 | tf_op jit(solution)/shard_map/ppermute | solution.py:112
  9.6 1.5 %collective-permute-start.3 = (bf16[144,384]{1,0:T(8,128)(2,1)}, bf16[144,384]{1,0:T(8,128)(2,1)S(1)}, u32[]{:S(2)}, u32[]{:S(2)}) collective-permute-start(bf16[144,384]{1,0:T(8,128)(2,1)} %get-tuple-element.38.weights_ref), channel_id=1, source_target_pairs={{0,2},{1,3},{2,0},{3,1},{4,6},{5,7},{6,4},{7,5},{8,10},{9,11},{10,... | collective-permute-start | bytes 331784 | tf_op jit(solution)/shard_map/ppermute | solution.py:105
  11.1 0.0 copy-done.1
  11.1 0.0 copy-done.2
  11.1 0.0 copy-done.4
  11.1 0.0 copy-done.10
  11.1 0.0 copy-done.6
  11.2 1.9 %shard_map.148 = (f32[3,128,512]{2,1,0:T(8,128)S(1)}, f32[128,512]{1,0:T(8,128)}) custom-call(s32[32]{0:T(128)S(1)} %copy-done.6, bf16[3,128,512]{2,1,0:T(8,128)(2,1)S(1)} %bitcast.8, bf16[128,512]{1,0:T(8,128)(2,1)S(1)} %copy-done.4, f32[128,512]{1,0:T(8,128)S(1)} %copy-done.1, f32[24,512]{1,0:T(8,128)S(1)} %copy-done.10), custom_call_target="tpu_custom_call" | custom-call | flops 2000000000 | bytes 835584 | tf_op jit(solution)/shard_map/pallas_call | solution.py:472
  13.1 0.0 copy-done.3
  13.1 0.0 copy-done.7
  13.1 0.0 copy-done.11
  13.1 0.6 %shard_map.149.own_ref = f32[288,384]{1,0:T(8,128)S(1)} custom-call(f32[3,128,512]{2,1,0:T(8,128)S(1)} %get-tuple-element.34.part_ref, bf16[576,512]{1,0:T(8,128)(2,1)S(1)} %copy-done.7, bf16[128,1152]{1,0:T(8,128)(2,1)S(1)} %copy-done.3, f32[16,128]{1,0:T(8,128)S(1)} %copy-done.11), custom_call_target="tpu_custom_call" | custom-call | flops 1000000000 | bytes 1679360 | tf_op jit(solution)/shard_map/pallas_call | solution.py:472
  13.7 0.0 collective-permute-done.1
  13.7 0.0 collective-permute-done.2
  13.7 1.0 %collective-permute-done.3.refs_0_.refs_2_ = bf16[144,384]{1,0:T(8,128)(2,1)S(1)} collective-permute-done((bf16[144,384]{1,0:T(8,128)(2,1)}, bf16[144,384]{1,0:T(8,128)(2,1)S(1)}, u32[]{:S(2)}, u32[]{:S(2)}) %collective-permute-start.3) | collective-permute-done | bytes 110624 | tf_op jit(solution)/shard_map/ppermute | solution.py:105
  14.7 0.0 copy-start.5
  14.8 0.0 copy-start.8
  14.8 0.0 copy-start.9
  14.8 0.1 collective-permute-start.4
  14.9 1.3 %shard_map.150 = (f32[256,256]{1,0:T(8,128)S(1)}, bf16[128,1152]{1,0:T(8,128)(2,1)S(1)}, bf16[128,1152]{1,0:T(8,128)(2,1)S(1)}) custom-call(f32[16,128]{1,0:T(8,128)S(1)} %copy-done.11, bf16[144,384]{1,0:T(8,128)(2,1)S(1)} %collective-permute-done.3.refs_0_.refs_2_, bf16[128,1152]{1,0:T(8,128)(2,1)S(1)} %copy-done.3, ...), custom_call_target="tpu_custom_call" | custom-call | flops 1000000000 | bytes 708608 | tf_op jit(solution)/shard_map/pallas_call | solution.py:472
  16.1 0.1 collective-permute-done.4.refs_1_
  16.2 0.0 copy-done.5
  16.2 0.0 copy-done.8
  16.2 0.0 copy-done.9
  16.2 0.0 copy-start
  16.2 2.2 %shard_map.151 = (bf16[128,1152]{1,0:T(8,128)(2,1)S(1)}, bf16[128,1152]{1,0:T(8,128)(2,1)S(1)}, f32[32,8,128]{2,1,0:T(8,128)S(1)}) custom-call(f32[288,384]{1,0:T(8,128)S(1)} %shard_map.149.own_ref, bf16[288,384]{1,0:T(8,128)(2,1)S(1)} %copy-done.8, bf16[288,256]{1,0:T(8,128)(2,1)S(1)} %copy-done.9, f32[16,128]{1,0:T(8,128)S(1)} %copy-done.11, ...), custom_call_target="tpu_custom_call" | custom-call | flops 2000000000 | bytes 1925120 | tf_op jit(solution)/shard_map/pallas_call | solution.py:472
  18.4 1.6 %collective-permute-start.5 = (bf16[128,1152]{1,0:T(8,128)(2,1)S(1)}, bf16[128,1152]{1,0:T(8,128)(2,1)S(1)}, u32[]{:S(2)}, u32[]{:S(2)}) collective-permute-start(bf16[128,1152]{1,0:T(8,128)(2,1)S(1)} %get-tuple-element.47), channel_id=1, source_target_pairs={{0,2},{1,3},{2,0},{3,1},{4,6},{5,7},{6,4},{7,5},{8,10},{9,11},{10,... | collective-permute-start | bytes 884744 | tf_op jit(solution)/shard_map/ppermute | solution.py:105
  20.0 11.8 %all_to_all.5.sums_ref = f32[32,8,128]{2,1,0:T(8,128)S(1)} all-to-all(f32[32,8,128]{2,1,0:T(8,128)S(1)} %get-tuple-element.46), channel_id=1, replica_groups=mesh['morton'=8,'sib'=4] {'morton','sib'}, dimensions={0} | all-to-all | bytes 262144 | tf_op jit(solution)/shard_map/all_to_all | solution.py:554
  31.8 0.0 collective-permute-done.5.refs_0_
  31.8 0.0 copy-done
  31.8 1.2 %shard_map.152 = (f32[3,128,512]{2,1,0:T(8,128)}, f32[3,1,216]{2,1,0:T(1,128)}, f32[3,1,216]{2,1,0:T(1,128)}) custom-call(f32[3,128,512]{2,1,0:T(8,128)S(1)} %get-tuple-element.34.part_ref, f32[128,512]{1,0:T(8,128)S(1)} %copy-done.1, bf16[384,512]{1,0:T(8,128)(2,1)S(1)} %copy-done, f32[32,8,128]{2,1,0:T(8,128)S(1)} %all_to_all.5.sums_ref, ...), custom_call_target="tpu_custom_call" | custom-call | flops 200000000 | bytes 2424832 | tf_op jit(solution)/shard_map/pallas_call | solution.py:472
  (2 shorter events, 0.0 us)
Async XLA Ops:
  0.6 10.5 %copy-start.1 = (f32[128,512]{1,0:T(8,128)S(1)}, f32[128,512]{1,0:T(8,128)}, u32[]{:S(2)}) copy-start(f32[128,512]{1,0:T(8,128)} %visc_ref.5) | copy-start | bytes 786436
  0.6 10.5 %copy-start.2 = (bf16[128,3,512]{2,0,1:T(8,128)(2,1)S(1)}, bf16[128,3,512]{2,0,1:T(8,128)(2,1)}, u32[]{:S(2)}) copy-start(bf16[128,3,512]{2,0,1:T(8,128)(2,1)} %param.12) | copy-start | bytes 1179652
  0.7 10.5 %copy-start.4 = (bf16[128,512]{1,0:T(8,128)(2,1)S(1)}, bf16[128,512]{1,0:T(8,128)(2,1)}, u32[]{:S(2)}) copy-start(bf16[128,512]{1,0:T(8,128)(2,1)} %press_ref) | copy-start | bytes 393220
  0.7 10.5 %copy-start.10 = (f32[24,512]{1,0:T(8,128)S(1)}, f32[24,512]{1,0:T(8,128)}, u32[]{:S(2)}) copy-start(f32[24,512]{1,0:T(8,128)} %constant.10.clone.rows_ref) | copy-start | bytes 147460
  3.1 1.9 %collective-permute-start = (bf16[128,1152]{1,0:T(8,128)(2,1)}, bf16[128,1152]{1,0:T(8,128)(2,1)S(1)}, u32[]{:S(2)}, u32[]{:S(2)}) collective-permute-start(bf16[128,1152]{1,0:T(8,128)(2,1)} %get-tuple-element.30.faces_ref.refs_1_), channel_id=1, source_target_pairs={{0,1},{1,0},{2,3},{3,2},{4,5},{5,4},{6,7},{7,6},{8,9},{9,8},{10,11... | collective-permute-start | bytes 884744 | tf_op jit(solution)/shard_map/ppermute | solution.py:105
  3.5 10.2 %collective-permute-start.1 = (bf16[32,1152]{1,0:T(8,128)(2,1)}, bf16[32,1152]{1,0:T(8,128)(2,1)S(1)}, u32[]{:S(2)}, u32[]{:S(2)}) collective-permute-start(bf16[32,1152]{1,0:T(8,128)(2,1)} %get-tuple-element.35), channel_id=1, source_target_pairs={{4,8},{8,4},{12,16},{16,12},{20,24},{24,20},{5,9},{9,5},{13,17},{1... | collective-permute-start | bytes 221192 | tf_op jit(solution)/shard_map/ppermute | solution.py:112
  5.0 6.2 %copy-start.6 = (s32[32]{0:T(128)S(1)}, s32[32]{0:T(128)}, u32[]{:S(2)}) copy-start(s32[32]{0:T(128)} %counts_ref.3) | copy-start | bytes 388
  5.0 8.1 %copy-start.3 = (bf16[128,1152]{1,0:T(8,128)(2,1)S(1)}, bf16[128,1152]{1,0:T(8,128)(2,1)}, u32[]{:S(2)}) copy-start(bf16[128,1152]{1,0:T(8,128)(2,1)} %get-tuple-element.30.faces_ref.refs_1_) | copy-start | bytes 884740
  5.0 8.1 %copy-start.7 = (bf16[576,512]{1,0:T(8,128)(2,1)S(1)}, bf16[576,512]{1,0:T(8,128)(2,1)}, u32[]{:S(2)}) copy-start(bf16[576,512]{1,0:T(8,128)(2,1)} %constant.12.clone.basis_ref) | copy-start | bytes 1769476
  5.0 8.1 %copy-start.11 = (f32[16,128]{1,0:T(8,128)S(1)}, f32[16,128]{1,0:T(8,128)}, u32[]{:S(2)}) copy-start(f32[16,128]{1,0:T(8,128)} %get-tuple-element.37.spots_ref) | copy-start | bytes 24580
  5.0 8.8 %collective-permute-start.2 = (bf16[32,1152]{1,0:T(8,128)(2,1)}, bf16[32,1152]{1,0:T(8,128)(2,1)S(1)}, u32[]{:S(2)}, u32[]{:S(2)}) collective-permute-start(bf16[32,1152]{1,0:T(8,128)(2,1)} %get-tuple-element.36), channel_id=1, source_target_pairs={{0,4},{4,0},{8,12},{12,8},{16,20},{20,16},{24,28},{28,24},{1,5},{5... | collective-permute-start | bytes 221192 | tf_op jit(solution)/shard_map/ppermute | solution.py:112
  9.6 5.1 %collective-permute-start.3 = (bf16[144,384]{1,0:T(8,128)(2,1)}, bf16[144,384]{1,0:T(8,128)(2,1)S(1)}, u32[]{:S(2)}, u32[]{:S(2)}) collective-permute-start(bf16[144,384]{1,0:T(8,128)(2,1)} %get-tuple-element.38.weights_ref), channel_id=1, source_target_pairs={{0,2},{1,3},{2,0},{3,1},{4,6},{5,7},{6,4},{7,5},{8,10},{9,11},{10,... | collective-permute-start | bytes 331784 | tf_op jit(solution)/shard_map/ppermute | solution.py:105
  14.7 1.5 %copy-start.5 = (bf16[144,384]{1,0:T(8,128)(2,1)S(1)}, bf16[144,384]{1,0:T(8,128)(2,1)}, u32[]{:S(2)}) copy-start(bf16[144,384]{1,0:T(8,128)(2,1)} %get-tuple-element.38.weights_ref) | copy-start | bytes 331780
  14.8 1.5 %copy-start.8 = (bf16[288,384]{1,0:T(8,128)(2,1)S(1)}, bf16[288,384]{1,0:T(8,128)(2,1)}, u32[]{:S(2)}) copy-start(bf16[288,384]{1,0:T(8,128)(2,1)} %constant.13.clone.face_basis_ref) | copy-start | bytes 663556
  14.8 1.5 %copy-start.9 = (bf16[288,256]{1,0:T(8,128)(2,1)S(1)}, bf16[288,256]{1,0:T(8,128)(2,1)}, u32[]{:S(2)}) copy-start(bf16[288,256]{1,0:T(8,128)(2,1)} %constant.14.clone.compact_ref) | copy-start | bytes 442372
  14.8 1.4 %collective-permute-start.4 = (bf16[64,1152]{1,0:T(8,128)(2,1)S(1)}, bf16[64,1152]{1,0:T(8,128)(2,1)S(1)}, u32[]{:S(2)}, u32[]{:S(2)}) collective-permute-start(bf16[64,1152]{1,0:T(8,128)(2,1)S(1)} %constant_dynamic-update-slice_fusion.refs_0_), channel_id=1, source_target_pairs={{0,1},{1,0},{2,3},{3,2},{4,5},{5,4},{6,7},{7,6},{8,9},{9,8},{10,11... | collective-permute-start | bytes 442376 | tf_op jit(solution)/shard_map/ppermute | solution.py:105
  16.2 15.6 %copy-start = (bf16[384,512]{1,0:T(8,128)(2,1)S(1)}, bf16[384,512]{1,0:T(8,128)(2,1)}, u32[]{:S(2)}) copy-start(bf16[384,512]{1,0:T(8,128)(2,1)} %constant.15.spread_ref) | copy-start | bytes 1179652
  18.4 13.4 %collective-permute-start.5 = (bf16[128,1152]{1,0:T(8,128)(2,1)S(1)}, bf16[128,1152]{1,0:T(8,128)(2,1)S(1)}, u32[]{:S(2)}, u32[]{:S(2)}) collective-permute-start(bf16[128,1152]{1,0:T(8,128)(2,1)S(1)} %get-tuple-element.47), channel_id=1, source_target_pairs={{0,2},{1,3},{2,0},{3,1},{4,6},{5,7},{6,4},{7,5},{8,10},{9,11},{10,... | collective-permute-start | bytes 884744 | tf_op jit(solution)/shard_map/ppermute | solution.py:105

commit v18 on v17

--- a/solution.py
+++ b/solution.py
@@ -530,7 +530,7 @@
         [],
         [part, basis, faces, spots],
     )
-    odd, even, own_raw, requests = lax.optimization_barrier((odd, even, own_raw, requests))
+    odd, even, own_raw = lax.optimization_barrier((odd, even, own_raw))
     bands = jnp.concatenate([odd, even], axis=0)
     move, *group = call(
         group_kernel,

time: 33.2 us -> 33 us (level)
  transfers between devices with their start and end apart: 6 -> 6, of which waited for: 3 -> 2; matrix products, arithmetic and copies ran while one was open for 0% -> 0% of each run, Pallas kernels for 12% -> 12%
where the time goes in v18:
time: 33 us; the launch traced here: 32.9 us
  blocking collectives  11.8 us (36%)
  Pallas kernels  9.63 us (29%)
  starting transfers between devices  8.92 us (27%)
  waiting for transfers between devices  1.62 us (5%)
  between operations  0.82 us (2%)
    all_to_all x1, blocking collectives, on_device(): every = lax.all_to_all(sums, ('morton', 'sib'), 0, 0, tiled=True)  11.8 us
    pallas_call x6, Pallas kernels, call(): pl.pallas_call(kernel, out_shape=[jax.ShapeDtypeStruct(shape, dtype) for...  9.63 us
    ppermute x2, starting transfers between devices, pairs(): return lax.ppermute(block, 'morton', route)  5.29 us
    ppermute x4, starting transfers between devices, swap(): lax.ppermute(block, axis, [(at, at ^ apart) for at in range(lax.axis_size...  3.63 us
    ppermute x4, waiting for transfers between devices, swap(): lax.ppermute(block, axis, [(at, at ^ apart) for at in range(lax.axis_size...  1.61 us
  transfers between devices with their start and end apart: 6, of which 2 were waited for; matrix products, arithmetic and copies ran while one was open for 0% of the time, Pallas kernels for 12%

profile of v18, /device:TPU:0, one launch (start us, length us, event | category | flops | bytes accessed | tf_op | source)
XLA Modules:
  0.0 32.9 jit_solution(8429476862849055483)
XLA Ops:
  0.6 0.0 copy-start.1
  0.6 0.0 copy-start.2
  0.7 0.0 copy-start.4
  0.7 0.0 copy-start.10
  0.7 2.4 %shard_map.147 = (bf16[128,1152]{1,0:T(8,128)(2,1)}, bf16[32,1152]{1,0:T(8,128)(2,1)}, bf16[32,1152]{1,0:T(8,128)(2,1)}, f32[16,128]{1,0:T(8,128)}, bf16[144,384]{1,0:T(8,128)(2,1)}) custom-call(s32[32]{0:T(128)} %counts_ref.3, bf16[3,128,512]{2,1,0:T(8,128)(2,1)} %bitcast.7, f32[128,512]{1,0:T(8,128)} %visc_ref.5, s32[6,128]{1,0:T(8,128)} %bitcast.10, ...), custom_call_target="tpu_custom_call" | custom-call | flops 400000000 | bytes 659456 | tf_op jit(solution)/shard_map/pallas_call | solution.py:472
  3.1 0.5 %collective-permute-start = (bf16[128,1152]{1,0:T(8,128)(2,1)}, bf16[128,1152]{1,0:T(8,128)(2,1)S(1)}, u32[]{:S(2)}, u32[]{:S(2)}) collective-permute-start(bf16[128,1152]{1,0:T(8,128)(2,1)} %get-tuple-element.29.faces_ref.refs_1_), channel_id=1, source_target_pairs={{0,1},{1,0},{2,3},{3,2},{4,5},{5,4},{6,7},{7,6},{8,9},{9,8},{10,11... | collective-permute-start | bytes 884744 | tf_op jit(solution)/shard_map/ppermute | solution.py:105
  3.5 0.7 %collective-permute-start.1 = (bf16[32,1152]{1,0:T(8,128)(2,1)}, bf16[32,1152]{1,0:T(8,128)(2,1)S(1)}, u32[]{:S(2)}, u32[]{:S(2)}) collective-permute-start(bf16[32,1152]{1,0:T(8,128)(2,1)} %get-tuple-element.34), channel_id=1, source_target_pairs={{4,8},{8,4},{12,16},{16,12},{20,24},{24,20},{5,9},{9,5},{13,17},{1... | collective-permute-start | bytes 221192 | tf_op jit(solution)/shard_map/ppermute | solution.py:112
  4.2 0.8 %collective-permute-done.refs_2_ = bf16[128,1152]{1,0:T(8,128)(2,1)S(1)} collective-permute-done((bf16[128,1152]{1,0:T(8,128)(2,1)}, bf16[128,1152]{1,0:T(8,128)(2,1)S(1)}, u32[]{:S(2)}, u32[]{:S(2)}) %collective-permute-start) | collective-permute-done | bytes 294944 | tf_op jit(solution)/shard_map/ppermute | solution.py:105
  5.0 0.0 copy-start.6
  5.0 0.0 copy-start.3
  5.0 0.0 copy-start.7
  5.0 0.0 copy-start.11
  5.0 4.6 %collective-permute-start.2 = (bf16[32,1152]{1,0:T(8,128)(2,1)}, bf16[32,1152]{1,0:T(8,128)(2,1)S(1)}, u32[]{:S(2)}, u32[]{:S(2)}) collective-permute-start(bf16[32,1152]{1,0:T(8,128)(2,1)} %get-tuple-element.35), channel_id=1, source_target_pairs={{0,4},{4,0},{8,12},{12,8},{16,20},{20,16},{24,28},{28,24},{1,5},{5... | collective-permute-start | bytes 221192 | tf_op jit(solution)/shard_map/ppermute | solution.py:112
  9.6 1.5 %collective-permute-start.4 = (bf16[144,384]{1,0:T(8,128)(2,1)}, bf16[144,384]{1,0:T(8,128)(2,1)S(1)}, u32[]{:S(2)}, u32[]{:S(2)}) collective-permute-start(bf16[144,384]{1,0:T(8,128)(2,1)} %get-tuple-element.40.weights_ref), channel_id=1, source_target_pairs={{0,2},{1,3},{2,0},{3,1},{4,6},{5,7},{6,4},{7,5},{8,10},{9,11},{10,... | collective-permute-start | bytes 331784 | tf_op jit(solution)/shard_map/ppermute | solution.py:105
  11.1 0.0 copy-done.1
  11.1 0.0 copy-done.2
  11.1 0.0 copy-done.4
  11.1 0.0 copy-done.10
  11.1 0.0 copy-done.6
  11.2 1.9 %shard_map.148 = (f32[3,128,512]{2,1,0:T(8,128)S(1)}, f32[128,512]{1,0:T(8,128)}) custom-call(s32[32]{0:T(128)S(1)} %copy-done.6, bf16[3,128,512]{2,1,0:T(8,128)(2,1)S(1)} %bitcast.8, bf16[128,512]{1,0:T(8,128)(2,1)S(1)} %copy-done.4, f32[128,512]{1,0:T(8,128)S(1)} %copy-done.1, f32[24,512]{1,0:T(8,128)S(1)} %copy-done.10), custom_call_target="tpu_custom_call" | custom-call | flops 2000000000 | bytes 835584 | tf_op jit(solution)/shard_map/pallas_call | solution.py:472
  13.1 0.0 copy-done.3
  13.1 0.0 copy-done.7
  13.1 0.0 copy-done.11
  13.1 0.6 %shard_map.149.own_ref = f32[288,384]{1,0:T(8,128)S(1)} custom-call(f32[3,128,512]{2,1,0:T(8,128)S(1)} %get-tuple-element.33.part_ref, bf16[576,512]{1,0:T(8,128)(2,1)S(1)} %copy-done.7, bf16[128,1152]{1,0:T(8,128)(2,1)S(1)} %copy-done.3, f32[16,128]{1,0:T(8,128)S(1)} %copy-done.11), custom_call_target="tpu_custom_call" | custom-call | flops 1000000000 | bytes 1679360 | tf_op jit(solution)/shard_map/pallas_call | solution.py:472
  13.7 0.0 collective-permute-done.1
  13.7 0.0 collective-permute-done.2
  13.8 0.0 copy-start.5
  13.8 0.0 copy-start.8
  13.8 0.0 copy-start.9
  13.8 0.1 collective-permute-start.3
  13.9 0.8 %collective-permute-done.4.refs_0_.refs_2_ = bf16[144,384]{1,0:T(8,128)(2,1)S(1)} collective-permute-done((bf16[144,384]{1,0:T(8,128)(2,1)}, bf16[144,384]{1,0:T(8,128)(2,1)S(1)}, u32[]{:S(2)}, u32[]{:S(2)}) %collective-permute-start.4) | collective-permute-done | bytes 110624 | tf_op jit(solution)/shard_map/ppermute | solution.py:105
  14.7 1.3 %shard_map.150 = (f32[256,256]{1,0:T(8,128)S(1)}, bf16[128,1152]{1,0:T(8,128)(2,1)S(1)}, bf16[128,1152]{1,0:T(8,128)(2,1)S(1)}) custom-call(f32[16,128]{1,0:T(8,128)S(1)} %copy-done.11, bf16[144,384]{1,0:T(8,128)(2,1)S(1)} %collective-permute-done.4.refs_0_.refs_2_, bf16[128,1152]{1,0:T(8,128)(2,1)S(1)} %copy-done.3, ...), custom_call_target="tpu_custom_call" | custom-call | flops 1000000000 | bytes 708608 | tf_op jit(solution)/shard_map/pallas_call | solution.py:472
  16.0 0.0 collective-permute-done.3.refs_1_
  16.0 0.0 copy-done.5
  16.0 0.0 copy-done.8
  16.0 0.0 copy-done.9
  16.0 0.0 copy-start
  16.1 2.2 %shard_map.151 = (bf16[128,1152]{1,0:T(8,128)(2,1)S(1)}, bf16[128,1152]{1,0:T(8,128)(2,1)S(1)}, f32[32,8,128]{2,1,0:T(8,128)S(1)}) custom-call(f32[288,384]{1,0:T(8,128)S(1)} %shard_map.149.own_ref, bf16[288,384]{1,0:T(8,128)(2,1)S(1)} %copy-done.8, bf16[288,256]{1,0:T(8,128)(2,1)S(1)} %copy-done.9, f32[16,128]{1,0:T(8,128)S(1)} %copy-done.11, ...), custom_call_target="tpu_custom_call" | custom-call | flops 2000000000 | bytes 1925120 | tf_op jit(solution)/shard_map/pallas_call | solution.py:472
  18.2 1.6 %collective-permute-start.5 = (bf16[128,1152]{1,0:T(8,128)(2,1)S(1)}, bf16[128,1152]{1,0:T(8,128)(2,1)S(1)}, u32[]{:S(2)}, u32[]{:S(2)}) collective-permute-start(bf16[128,1152]{1,0:T(8,128)(2,1)S(1)} %get-tuple-element.45), channel_id=1, source_target_pairs={{0,2},{1,3},{2,0},{3,1},{4,6},{5,7},{6,4},{7,5},{8,10},{9,11},{10,... | collective-permute-start | bytes 884744 | tf_op jit(solution)/shard_map/ppermute | solution.py:105
  19.8 11.8 %all_to_all.5.sums_ref = f32[32,8,128]{2,1,0:T(8,128)S(1)} all-to-all(f32[32,8,128]{2,1,0:T(8,128)S(1)} %get-tuple-element.44), channel_id=1, replica_groups=mesh['morton'=8,'sib'=4] {'morton','sib'}, dimensions={0} | all-to-all | bytes 262144 | tf_op jit(solution)/shard_map/all_to_all | solution.py:554
  31.6 0.0 collective-permute-done.5.refs_0_
  31.6 0.0 copy-done
  31.6 1.2 %shard_map.152 = (f32[3,128,512]{2,1,0:T(8,128)}, f32[3,1,216]{2,1,0:T(1,128)}, f32[3,1,216]{2,1,0:T(1,128)}) custom-call(f32[3,128,512]{2,1,0:T(8,128)S(1)} %get-tuple-element.33.part_ref, f32[128,512]{1,0:T(8,128)S(1)} %copy-done.1, bf16[384,512]{1,0:T(8,128)(2,1)S(1)} %copy-done, f32[32,8,128]{2,1,0:T(8,128)S(1)} %all_to_all.5.sums_ref, ...), custom_call_target="tpu_custom_call" | custom-call | flops 200000000 | bytes 2424832 | tf_op jit(solution)/shard_map/pallas_call | solution.py:472
  (2 shorter events, 0.0 us)
Async XLA Ops:
  0.6 10.5 %copy-start.1 = (f32[128,512]{1,0:T(8,128)S(1)}, f32[128,512]{1,0:T(8,128)}, u32[]{:S(2)}) copy-start(f32[128,512]{1,0:T(8,128)} %visc_ref.5) | copy-start | bytes 786436
  0.6 10.5 %copy-start.2 = (bf16[128,3,512]{2,0,1:T(8,128)(2,1)S(1)}, bf16[128,3,512]{2,0,1:T(8,128)(2,1)}, u32[]{:S(2)}) copy-start(bf16[128,3,512]{2,0,1:T(8,128)(2,1)} %param.12) | copy-start | bytes 1179652
  0.7 10.5 %copy-start.4 = (bf16[128,512]{1,0:T(8,128)(2,1)S(1)}, bf16[128,512]{1,0:T(8,128)(2,1)}, u32[]{:S(2)}) copy-start(bf16[128,512]{1,0:T(8,128)(2,1)} %press_ref) | copy-start | bytes 393220
  0.7 10.5 %copy-start.10 = (f32[24,512]{1,0:T(8,128)S(1)}, f32[24,512]{1,0:T(8,128)}, u32[]{:S(2)}) copy-start(f32[24,512]{1,0:T(8,128)} %constant.10.clone.rows_ref) | copy-start | bytes 147460
  3.1 1.9 %collective-permute-start = (bf16[128,1152]{1,0:T(8,128)(2,1)}, bf16[128,1152]{1,0:T(8,128)(2,1)S(1)}, u32[]{:S(2)}, u32[]{:S(2)}) collective-permute-start(bf16[128,1152]{1,0:T(8,128)(2,1)} %get-tuple-element.29.faces_ref.refs_1_), channel_id=1, source_target_pairs={{0,1},{1,0},{2,3},{3,2},{4,5},{5,4},{6,7},{7,6},{8,9},{9,8},{10,11... | collective-permute-start | bytes 884744 | tf_op jit(solution)/shard_map/ppermute | solution.py:105
  3.5 10.2 %collective-permute-start.1 = (bf16[32,1152]{1,0:T(8,128)(2,1)}, bf16[32,1152]{1,0:T(8,128)(2,1)S(1)}, u32[]{:S(2)}, u32[]{:S(2)}) collective-permute-start(bf16[32,1152]{1,0:T(8,128)(2,1)} %get-tuple-element.34), channel_id=1, source_target_pairs={{4,8},{8,4},{12,16},{16,12},{20,24},{24,20},{5,9},{9,5},{13,17},{1... | collective-permute-start | bytes 221192 | tf_op jit(solution)/shard_map/ppermute | solution.py:112
  5.0 6.2 %copy-start.6 = (s32[32]{0:T(128)S(1)}, s32[32]{0:T(128)}, u32[]{:S(2)}) copy-start(s32[32]{0:T(128)} %counts_ref.3) | copy-start | bytes 388
  5.0 8.1 %copy-start.3 = (bf16[128,1152]{1,0:T(8,128)(2,1)S(1)}, bf16[128,1152]{1,0:T(8,128)(2,1)}, u32[]{:S(2)}) copy-start(bf16[128,1152]{1,0:T(8,128)(2,1)} %get-tuple-element.29.faces_ref.refs_1_) | copy-start | bytes 884740
  5.0 8.1 %copy-start.7 = (bf16[576,512]{1,0:T(8,128)(2,1)S(1)}, bf16[576,512]{1,0:T(8,128)(2,1)}, u32[]{:S(2)}) copy-start(bf16[576,512]{1,0:T(8,128)(2,1)} %constant.12.clone.basis_ref) | copy-start | bytes 1769476
  5.0 8.1 %copy-start.11 = (f32[16,128]{1,0:T(8,128)S(1)}, f32[16,128]{1,0:T(8,128)}, u32[]{:S(2)}) copy-start(f32[16,128]{1,0:T(8,128)} %get-tuple-element.36.spots_ref) | copy-start | bytes 24580
  5.0 8.8 %collective-permute-start.2 = (bf16[32,1152]{1,0:T(8,128)(2,1)}, bf16[32,1152]{1,0:T(8,128)(2,1)S(1)}, u32[]{:S(2)}, u32[]{:S(2)}) collective-permute-start(bf16[32,1152]{1,0:T(8,128)(2,1)} %get-tuple-element.35), channel_id=1, source_target_pairs={{0,4},{4,0},{8,12},{12,8},{16,20},{20,16},{24,28},{28,24},{1,5},{5... | collective-permute-start | bytes 221192 | tf_op jit(solution)/shard_map/ppermute | solution.py:112
  9.6 5.1 %collective-permute-start.4 = (bf16[144,384]{1,0:T(8,128)(2,1)}, bf16[144,384]{1,0:T(8,128)(2,1)S(1)}, u32[]{:S(2)}, u32[]{:S(2)}) collective-permute-start(bf16[144,384]{1,0:T(8,128)(2,1)} %get-tuple-element.40.weights_ref), channel_id=1, source_target_pairs={{0,2},{1,3},{2,0},{3,1},{4,6},{5,7},{6,4},{7,5},{8,10},{9,11},{10,... | collective-permute-start | bytes 331784 | tf_op jit(solution)/shard_map/ppermute | solution.py:105
  13.8 2.2 %copy-start.5 = (bf16[144,384]{1,0:T(8,128)(2,1)S(1)}, bf16[144,384]{1,0:T(8,128)(2,1)}, u32[]{:S(2)}) copy-start(bf16[144,384]{1,0:T(8,128)(2,1)} %get-tuple-element.40.weights_ref) | copy-start | bytes 331780
  13.8 2.2 %copy-start.8 = (bf16[288,384]{1,0:T(8,128)(2,1)S(1)}, bf16[288,384]{1,0:T(8,128)(2,1)}, u32[]{:S(2)}) copy-start(bf16[288,384]{1,0:T(8,128)(2,1)} %constant.13.clone.face_basis_ref) | copy-start | bytes 663556
  13.8 2.2 %copy-start.9 = (bf16[288,256]{1,0:T(8,128)(2,1)S(1)}, bf16[288,256]{1,0:T(8,128)(2,1)}, u32[]{:S(2)}) copy-start(bf16[288,256]{1,0:T(8,128)(2,1)} %constant.14.clone.compact_ref) | copy-start | bytes 442372
  13.8 2.2 %collective-permute-start.3 = (bf16[64,1152]{1,0:T(8,128)(2,1)S(1)}, bf16[64,1152]{1,0:T(8,128)(2,1)S(1)}, u32[]{:S(2)}, u32[]{:S(2)}) collective-permute-start(bf16[64,1152]{1,0:T(8,128)(2,1)S(1)} %constant_dynamic-update-slice_fusion.refs_0_), channel_id=1, source_target_pairs={{0,1},{1,0},{2,3},{3,2},{4,5},{5,4},{6,7},{7,6},{8,9},{9,8},{10,11... | collective-permute-start | bytes 442376 | tf_op jit(solution)/shard_map/ppermute | solution.py:105
  16.0 15.6 %copy-start = (bf16[384,512]{1,0:T(8,128)(2,1)S(1)}, bf16[384,512]{1,0:T(8,128)(2,1)}, u32[]{:S(2)}) copy-start(bf16[384,512]{1,0:T(8,128)(2,1)} %constant.15.spread_ref) | copy-start | bytes 1179652
  18.2 13.4 %collective-permute-start.5 = (bf16[128,1152]{1,0:T(8,128)(2,1)S(1)}, bf16[128,1152]{1,0:T(8,128)(2,1)S(1)}, u32[]{:S(2)}, u32[]{:S(2)}) collective-permute-start(bf16[128,1152]{1,0:T(8,128)(2,1)S(1)} %get-tuple-element.45), channel_id=1, source_target_pairs={{0,2},{1,3},{2,0},{3,1},{4,6},{5,7},{6,4},{7,5},{8,10},{9,11},{10,... | collective-permute-start | bytes 884744 | tf_op jit(solution)/shard_map/ppermute | solution.py:105

commit v19 on v18

--- a/solution.py
+++ b/solution.py
@@ -379,7 +379,7 @@
     group = lax.broadcasted_iota(jnp.int32, (span, LANES), 0) // leaf_count
     column = lax.broadcasted_iota(jnp.int32, (span, LANES), 1)
     gather = jnp.where((group == column) | (group + 3 == column), 1.0, 0.0).astype(bf16)
-    return sum(dot(piece, gather) for piece in split(jnp.concatenate(tiles, axis=0), 3))
+    return sum(dot(piece, gather) for piece in split(jnp.concatenate(tiles, axis=0), 2))
 
 
 def own_kernel(part_ref, basis_ref, faces_ref, spots_ref, raw_ref):
@@ -417,7 +417,7 @@
     box = spots_ref[12:, :]
     both = shifted([summed[8 * at : 8 * at + 8, :] for at in range(36)], box)
     flat = jnp.concatenate(both, axis=0).T
-    sums = sum(dot(piece, compact_ref[...]) for piece in split(flat[:8], 3))
+    sums = sum(dot(piece, compact_ref[...]) for piece in split(flat[:8], 2))
     blank = jnp.zeros((2, LANES), f32)
     to_box = jnp.concatenate([sums[:3, :LANES], sums[:3, LANES:], blank], axis=0)
     to_root = jnp.concatenate([sums[3:6, :LANES], sums[3:6, LANES:], blank], axis=0)

time: 33 us -> 32.9 us (level)
  no operation moved by 1% of the time
where the time goes in v19:
time: 32.9 us; the launch traced here: 32.8 us
  blocking collectives  11.8 us (36%)
  Pallas kernels  9.53 us (29%)
  starting transfers between devices  8.92 us (27%)
  waiting for transfers between devices  1.62 us (5%)
  between operations  0.82 us (2%)
    all_to_all x1, blocking collectives, on_device(): every = lax.all_to_all(sums, ('morton', 'sib'), 0, 0, tiled=True)  11.8 us
    pallas_call x6, Pallas kernels, call(): pl.pallas_call(kernel, out_shape=[jax.ShapeDtypeStruct(shape, dtype) for...  9.53 us
    ppermute x2, starting transfers between devices, pairs(): return lax.ppermute(block, 'morton', route)  5.29 us
    ppermute x4, starting transfers between devices, swap(): lax.ppermute(block, axis, [(at, at ^ apart) for at in range(lax.axis_size...  3.63 us
    ppermute x4, waiting for transfers between devices, swap(): lax.ppermute(block, axis, [(at, at ^ apart) for at in range(lax.axis_size...  1.61 us
  transfers between devices with their start and end apart: 6, of which 2 were waited for; matrix products, arithmetic and copies ran while one was open for 0% of the time, Pallas kernels for 12%

profile of v19, /device:TPU:0, one launch (start us, length us, event | category | flops | bytes accessed | tf_op | source)
XLA Modules:
  0.0 32.8 jit_solution(7260372641962008542)
XLA Ops:
  0.6 0.0 copy-start.1
  0.6 0.0 copy-start.2
  0.7 0.0 copy-start.4
  0.7 0.0 copy-start.10
  0.7 2.4 %shard_map.147 = (bf16[128,1152]{1,0:T(8,128)(2,1)}, bf16[32,1152]{1,0:T(8,128)(2,1)}, bf16[32,1152]{1,0:T(8,128)(2,1)}, f32[16,128]{1,0:T(8,128)}, bf16[144,384]{1,0:T(8,128)(2,1)}) custom-call(s32[32]{0:T(128)} %counts_ref.3, bf16[3,128,512]{2,1,0:T(8,128)(2,1)} %bitcast.7, f32[128,512]{1,0:T(8,128)} %visc_ref.5, s32[6,128]{1,0:T(8,128)} %bitcast.10, ...), custom_call_target="tpu_custom_call" | custom-call | flops 400000000 | bytes 659456 | tf_op jit(solution)/shard_map/pallas_call | solution.py:472
  3.1 0.5 %collective-permute-start = (bf16[128,1152]{1,0:T(8,128)(2,1)}, bf16[128,1152]{1,0:T(8,128)(2,1)S(1)}, u32[]{:S(2)}, u32[]{:S(2)}) collective-permute-start(bf16[128,1152]{1,0:T(8,128)(2,1)} %get-tuple-element.29.faces_ref.refs_1_), channel_id=1, source_target_pairs={{0,1},{1,0},{2,3},{3,2},{4,5},{5,4},{6,7},{7,6},{8,9},{9,8},{10,11... | collective-permute-start | bytes 884744 | tf_op jit(solution)/shard_map/ppermute | solution.py:105
  3.5 0.7 %collective-permute-start.1 = (bf16[32,1152]{1,0:T(8,128)(2,1)}, bf16[32,1152]{1,0:T(8,128)(2,1)S(1)}, u32[]{:S(2)}, u32[]{:S(2)}) collective-permute-start(bf16[32,1152]{1,0:T(8,128)(2,1)} %get-tuple-element.34), channel_id=1, source_target_pairs={{4,8},{8,4},{12,16},{16,12},{20,24},{24,20},{5,9},{9,5},{13,17},{1... | collective-permute-start | bytes 221192 | tf_op jit(solution)/shard_map/ppermute | solution.py:112
  4.2 0.8 %collective-permute-done.refs_2_ = bf16[128,1152]{1,0:T(8,128)(2,1)S(1)} collective-permute-done((bf16[128,1152]{1,0:T(8,128)(2,1)}, bf16[128,1152]{1,0:T(8,128)(2,1)S(1)}, u32[]{:S(2)}, u32[]{:S(2)}) %collective-permute-start) | collective-permute-done | bytes 294944 | tf_op jit(solution)/shard_map/ppermute | solution.py:105
  5.0 0.0 copy-start.6
  5.0 0.0 copy-start.3
  5.0 0.0 copy-start.7
  5.0 0.0 copy-start.11
  5.0 4.6 %collective-permute-start.2 = (bf16[32,1152]{1,0:T(8,128)(2,1)}, bf16[32,1152]{1,0:T(8,128)(2,1)S(1)}, u32[]{:S(2)}, u32[]{:S(2)}) collective-permute-start(bf16[32,1152]{1,0:T(8,128)(2,1)} %get-tuple-element.35), channel_id=1, source_target_pairs={{0,4},{4,0},{8,12},{12,8},{16,20},{20,16},{24,28},{28,24},{1,5},{5... | collective-permute-start | bytes 221192 | tf_op jit(solution)/shard_map/ppermute | solution.py:112
  9.6 1.5 %collective-permute-start.4 = (bf16[144,384]{1,0:T(8,128)(2,1)}, bf16[144,384]{1,0:T(8,128)(2,1)S(1)}, u32[]{:S(2)}, u32[]{:S(2)}) collective-permute-start(bf16[144,384]{1,0:T(8,128)(2,1)} %get-tuple-element.40.weights_ref), channel_id=1, source_target_pairs={{0,2},{1,3},{2,0},{3,1},{4,6},{5,7},{6,4},{7,5},{8,10},{9,11},{10,... | collective-permute-start | bytes 331784 | tf_op jit(solution)/shard_map/ppermute | solution.py:105
  11.1 0.0 copy-done.1
  11.1 0.0 copy-done.2
  11.1 0.0 copy-done.4
  11.1 0.0 copy-done.10
  11.1 0.0 copy-done.6
  11.2 1.9 %shard_map.148 = (f32[3,128,512]{2,1,0:T(8,128)S(1)}, f32[128,512]{1,0:T(8,128)}) custom-call(s32[32]{0:T(128)S(1)} %copy-done.6, bf16[3,128,512]{2,1,0:T(8,128)(2,1)S(1)} %bitcast.8, bf16[128,512]{1,0:T(8,128)(2,1)S(1)} %copy-done.4, f32[128,512]{1,0:T(8,128)S(1)} %copy-done.1, f32[24,512]{1,0:T(8,128)S(1)} %copy-done.10), custom_call_target="tpu_custom_call" | custom-call | flops 2000000000 | bytes 835584 | tf_op jit(solution)/shard_map/pallas_call | solution.py:472
  13.1 0.0 copy-done.3
  13.1 0.0 copy-done.7
  13.1 0.0 copy-done.11
  13.1 0.6 %shard_map.149.own_ref = f32[288,384]{1,0:T(8,128)S(1)} custom-call(f32[3,128,512]{2,1,0:T(8,128)S(1)} %get-tuple-element.33.part_ref, bf16[576,512]{1,0:T(8,128)(2,1)S(1)} %copy-done.7, bf16[128,1152]{1,0:T(8,128)(2,1)S(1)} %copy-done.3, f32[16,128]{1,0:T(8,128)S(1)} %copy-done.11), custom_call_target="tpu_custom_call" | custom-call | flops 1000000000 | bytes 1679360 | tf_op jit(solution)/shard_map/pallas_call | solution.py:472
  13.7 0.0 collective-permute-done.1
  13.7 0.0 collective-permute-done.2
  13.8 0.0 copy-start.5
  13.8 0.0 copy-start.8
  13.8 0.0 copy-start.9
  13.8 0.1 collective-permute-start.3
  13.9 0.8 %collective-permute-done.4.refs_0_.refs_2_ = bf16[144,384]{1,0:T(8,128)(2,1)S(1)} collective-permute-done((bf16[144,384]{1,0:T(8,128)(2,1)}, bf16[144,384]{1,0:T(8,128)(2,1)S(1)}, u32[]{:S(2)}, u32[]{:S(2)}) %collective-permute-start.4) | collective-permute-done | bytes 110624 | tf_op jit(solution)/shard_map/ppermute | solution.py:105
  14.7 1.3 %shard_map.150 = (f32[256,256]{1,0:T(8,128)S(1)}, bf16[128,1152]{1,0:T(8,128)(2,1)S(1)}, bf16[128,1152]{1,0:T(8,128)(2,1)S(1)}) custom-call(f32[16,128]{1,0:T(8,128)S(1)} %copy-done.11, bf16[144,384]{1,0:T(8,128)(2,1)S(1)} %collective-permute-done.4.refs_0_.refs_2_, bf16[128,1152]{1,0:T(8,128)(2,1)S(1)} %copy-done.3, ...), custom_call_target="tpu_custom_call" | custom-call | flops 1000000000 | bytes 708608 | tf_op jit(solution)/shard_map/pallas_call | solution.py:472
  16.0 0.0 collective-permute-done.3.refs_1_
  16.0 0.0 copy-done.5
  16.0 0.0 copy-done.8
  16.0 0.0 copy-done.9
  16.0 0.0 copy-start
  16.1 2.1 %shard_map.151 = (bf16[128,1152]{1,0:T(8,128)(2,1)S(1)}, bf16[128,1152]{1,0:T(8,128)(2,1)S(1)}, f32[32,8,128]{2,1,0:T(8,128)S(1)}) custom-call(f32[288,384]{1,0:T(8,128)S(1)} %shard_map.149.own_ref, bf16[288,384]{1,0:T(8,128)(2,1)S(1)} %copy-done.8, bf16[288,256]{1,0:T(8,128)(2,1)S(1)} %copy-done.9, f32[16,128]{1,0:T(8,128)S(1)} %copy-done.11, ...), custom_call_target="tpu_custom_call" | custom-call | flops 2000000000 | bytes 1925120 | tf_op jit(solution)/shard_map/pallas_call | solution.py:472
  18.1 1.6 %collective-permute-start.5 = (bf16[128,1152]{1,0:T(8,128)(2,1)S(1)}, bf16[128,1152]{1,0:T(8,128)(2,1)S(1)}, u32[]{:S(2)}, u32[]{:S(2)}) collective-permute-start(bf16[128,1152]{1,0:T(8,128)(2,1)S(1)} %get-tuple-element.45), channel_id=1, source_target_pairs={{0,2},{1,3},{2,0},{3,1},{4,6},{5,7},{6,4},{7,5},{8,10},{9,11},{10,... | collective-permute-start | bytes 884744 | tf_op jit(solution)/shard_map/ppermute | solution.py:105
  19.7 11.8 %all_to_all.5.sums_ref = f32[32,8,128]{2,1,0:T(8,128)S(1)} all-to-all(f32[32,8,128]{2,1,0:T(8,128)S(1)} %get-tuple-element.44), channel_id=1, replica_groups=mesh['morton'=8,'sib'=4] {'morton','sib'}, dimensions={0} | all-to-all | bytes 262144 | tf_op jit(solution)/shard_map/all_to_all | solution.py:554
  31.5 0.0 collective-permute-done.5.refs_0_
  31.5 0.0 copy-done
  31.5 1.2 %shard_map.152 = (f32[3,128,512]{2,1,0:T(8,128)}, f32[3,1,216]{2,1,0:T(1,128)}, f32[3,1,216]{2,1,0:T(1,128)}) custom-call(f32[3,128,512]{2,1,0:T(8,128)S(1)} %get-tuple-element.33.part_ref, f32[128,512]{1,0:T(8,128)S(1)} %copy-done.1, bf16[384,512]{1,0:T(8,128)(2,1)S(1)} %copy-done, f32[32,8,128]{2,1,0:T(8,128)S(1)} %all_to_all.5.sums_ref, ...), custom_call_target="tpu_custom_call" | custom-call | flops 200000000 | bytes 2424832 | tf_op jit(solution)/shard_map/pallas_call | solution.py:472
  (2 shorter events, 0.0 us)
Async XLA Ops:
  0.6 10.5 %copy-start.1 = (f32[128,512]{1,0:T(8,128)S(1)}, f32[128,512]{1,0:T(8,128)}, u32[]{:S(2)}) copy-start(f32[128,512]{1,0:T(8,128)} %visc_ref.5) | copy-start | bytes 786436
  0.6 10.5 %copy-start.2 = (bf16[128,3,512]{2,0,1:T(8,128)(2,1)S(1)}, bf16[128,3,512]{2,0,1:T(8,128)(2,1)}, u32[]{:S(2)}) copy-start(bf16[128,3,512]{2,0,1:T(8,128)(2,1)} %param.12) | copy-start | bytes 1179652
  0.7 10.5 %copy-start.4 = (bf16[128,512]{1,0:T(8,128)(2,1)S(1)}, bf16[128,512]{1,0:T(8,128)(2,1)}, u32[]{:S(2)}) copy-start(bf16[128,512]{1,0:T(8,128)(2,1)} %press_ref) | copy-start | bytes 393220
  0.7 10.5 %copy-start.10 = (f32[24,512]{1,0:T(8,128)S(1)}, f32[24,512]{1,0:T(8,128)}, u32[]{:S(2)}) copy-start(f32[24,512]{1,0:T(8,128)} %constant.10.clone.rows_ref) | copy-start | bytes 147460
  3.1 1.9 %collective-permute-start = (bf16[128,1152]{1,0:T(8,128)(2,1)}, bf16[128,1152]{1,0:T(8,128)(2,1)S(1)}, u32[]{:S(2)}, u32[]{:S(2)}) collective-permute-start(bf16[128,1152]{1,0:T(8,128)(2,1)} %get-tuple-element.29.faces_ref.refs_1_), channel_id=1, source_target_pairs={{0,1},{1,0},{2,3},{3,2},{4,5},{5,4},{6,7},{7,6},{8,9},{9,8},{10,11... | collective-permute-start | bytes 884744 | tf_op jit(solution)/shard_map/ppermute | solution.py:105
  3.5 10.2 %collective-permute-start.1 = (bf16[32,1152]{1,0:T(8,128)(2,1)}, bf16[32,1152]{1,0:T(8,128)(2,1)S(1)}, u32[]{:S(2)}, u32[]{:S(2)}) collective-permute-start(bf16[32,1152]{1,0:T(8,128)(2,1)} %get-tuple-element.34), channel_id=1, source_target_pairs={{4,8},{8,4},{12,16},{16,12},{20,24},{24,20},{5,9},{9,5},{13,17},{1... | collective-permute-start | bytes 221192 | tf_op jit(solution)/shard_map/ppermute | solution.py:112
  5.0 6.2 %copy-start.6 = (s32[32]{0:T(128)S(1)}, s32[32]{0:T(128)}, u32[]{:S(2)}) copy-start(s32[32]{0:T(128)} %counts_ref.3) | copy-start | bytes 388
  5.0 8.1 %copy-start.3 = (bf16[128,1152]{1,0:T(8,128)(2,1)S(1)}, bf16[128,1152]{1,0:T(8,128)(2,1)}, u32[]{:S(2)}) copy-start(bf16[128,1152]{1,0:T(8,128)(2,1)} %get-tuple-element.29.faces_ref.refs_1_) | copy-start | bytes 884740
  5.0 8.1 %copy-start.7 = (bf16[576,512]{1,0:T(8,128)(2,1)S(1)}, bf16[576,512]{1,0:T(8,128)(2,1)}, u32[]{:S(2)}) copy-start(bf16[576,512]{1,0:T(8,128)(2,1)} %constant.12.clone.basis_ref) | copy-start | bytes 1769476
  5.0 8.1 %copy-start.11 = (f32[16,128]{1,0:T(8,128)S(1)}, f32[16,128]{1,0:T(8,128)}, u32[]{:S(2)}) copy-start(f32[16,128]{1,0:T(8,128)} %get-tuple-element.36.spots_ref) | copy-start | bytes 24580
  5.0 8.8 %collective-permute-start.2 = (bf16[32,1152]{1,0:T(8,128)(2,1)}, bf16[32,1152]{1,0:T(8,128)(2,1)S(1)}, u32[]{:S(2)}, u32[]{:S(2)}) collective-permute-start(bf16[32,1152]{1,0:T(8,128)(2,1)} %get-tuple-element.35), channel_id=1, source_target_pairs={{0,4},{4,0},{8,12},{12,8},{16,20},{20,16},{24,28},{28,24},{1,5},{5... | collective-permute-start | bytes 221192 | tf_op jit(solution)/shard_map/ppermute | solution.py:112
  9.6 5.1 %collective-permute-start.4 = (bf16[144,384]{1,0:T(8,128)(2,1)}, bf16[144,384]{1,0:T(8,128)(2,1)S(1)}, u32[]{:S(2)}, u32[]{:S(2)}) collective-permute-start(bf16[144,384]{1,0:T(8,128)(2,1)} %get-tuple-element.40.weights_ref), channel_id=1, source_target_pairs={{0,2},{1,3},{2,0},{3,1},{4,6},{5,7},{6,4},{7,5},{8,10},{9,11},{10,... | collective-permute-start | bytes 331784 | tf_op jit(solution)/shard_map/ppermute | solution.py:105
  13.8 2.2 %copy-start.5 = (bf16[144,384]{1,0:T(8,128)(2,1)S(1)}, bf16[144,384]{1,0:T(8,128)(2,1)}, u32[]{:S(2)}) copy-start(bf16[144,384]{1,0:T(8,128)(2,1)} %get-tuple-element.40.weights_ref) | copy-start | bytes 331780
  13.8 2.2 %copy-start.8 = (bf16[288,384]{1,0:T(8,128)(2,1)S(1)}, bf16[288,384]{1,0:T(8,128)(2,1)}, u32[]{:S(2)}) copy-start(bf16[288,384]{1,0:T(8,128)(2,1)} %constant.13.clone.face_basis_ref) | copy-start | bytes 663556
  13.8 2.2 %copy-start.9 = (bf16[288,256]{1,0:T(8,128)(2,1)S(1)}, bf16[288,256]{1,0:T(8,128)(2,1)}, u32[]{:S(2)}) copy-start(bf16[288,256]{1,0:T(8,128)(2,1)} %constant.14.clone.compact_ref) | copy-start | bytes 442372
  13.8 2.2 %collective-permute-start.3 = (bf16[64,1152]{1,0:T(8,128)(2,1)S(1)}, bf16[64,1152]{1,0:T(8,128)(2,1)S(1)}, u32[]{:S(2)}, u32[]{:S(2)}) collective-permute-start(bf16[64,1152]{1,0:T(8,128)(2,1)S(1)} %constant_dynamic-update-slice_fusion.refs_0_), channel_id=1, source_target_pairs={{0,1},{1,0},{2,3},{3,2},{4,5},{5,4},{6,7},{7,6},{8,9},{9,8},{10,11... | collective-permute-start | bytes 442376 | tf_op jit(solution)/shard_map/ppermute | solution.py:105
  16.0 15.5 %copy-start = (bf16[384,512]{1,0:T(8,128)(2,1)S(1)}, bf16[384,512]{1,0:T(8,128)(2,1)}, u32[]{:S(2)}) copy-start(bf16[384,512]{1,0:T(8,128)(2,1)} %constant.15.spread_ref) | copy-start | bytes 1179652
  18.1 13.4 %collective-permute-start.5 = (bf16[128,1152]{1,0:T(8,128)(2,1)S(1)}, bf16[128,1152]{1,0:T(8,128)(2,1)S(1)}, u32[]{:S(2)}, u32[]{:S(2)}) collective-permute-start(bf16[128,1152]{1,0:T(8,128)(2,1)S(1)} %get-tuple-element.45), channel_id=1, source_target_pairs={{0,2},{1,3},{2,0},{3,1},{4,6},{5,7},{6,4},{7,5},{8,10},{9,11},{10,... | collective-permute-start | bytes 884744 | tf_op jit(solution)/shard_map/ppermute | solution.py:105
